TPU v7x, 32 devices: a whole 2x2x4 slice. The times are simulated.
32 devices in a mesh: gx: 4 (over y, core), gy: 2 (over x), gz: 4 (over z).
Axes of the slice: x: 2, y: 2, z: 4, core: 2. Of those that a mesh axis runs over, the one named last changes fastest.
Arguments:
- rhs: float32 [4, 2, 3, 162, 1024], P('gx', 'gy', None, None, 'gz'), may hold values from -6 to 6
- angles: float32 [4, 2, 3, 1024], P('gx', 'gy', None, 'gz'), may hold values from -3.140625 to 3.140625
- self_mob: float32 [486, 486], replicated, may hold values from -0.25 to 0.25
- near_mat: float32 [486, 486], replicated, may hold values from -0.25 to 0.25
- near_weight: float32 [4, 2, 8, 1024], P('gx', 'gy', None, 'gz'), may hold values from -2 to 2
- neighbours: int32 [4, 2, 8, 1024], P('gx', 'gy', None, 'gz'), may hold values from 0 to 2111, as said below
- cells: int32 [4, 2, 1024], P('gx', 'gy', 'gz'), may hold values from 0 to 191
- blob_weight: float32 [162], replicated, may hold values from -0.5 to 0.5
- skel_perm: int32 [2, 384], replicated, may hold values from 0 to 383, each once within a row
- interp: float32 [2, 192, 192], replicated, may hold values from -0.4375 to 0.4375
- sibling_ops: float32 [2, 192, 192], replicated, may hold values from -0.375 to 0.375
- root_op: float32 [192, 192], replicated, may hold values from -0.0625 to 0.0625
Outputs:
- solution: float32 [4, 2, 3, 162, 1024], P('gx', 'gy', None, None, 'gz')
- lsq_residual: float32 [], replicated
Inputs may be any that keep to these rules, and one draw needn't show every extreme that they name: `neighbours`: each id is s * 256 + j with slot s in 0..8 and j < 256; j < 64 whenever s != 4, and some id in every draw reaches j = 63 in slot 8.
All inputs are finite; a program needn't handle non-finite values.
Results may differ from a plain program's by a relative error of at most 0.0003.
Values sent between devices are 32-bit elements; how exact they have to be, the bound alone decides.
No kernel may reach another device: no remote copies, remote signals or barrier semaphores. Data moves between devices by JAX's collectives and lax.ppermute only.
A program may use at most 128 MiB of HBM per device.

v0:
```python
import jax
import jax.numpy as jnp
from jax import lax
from jax.sharding import PartitionSpec as P

highest = lax.Precision.HIGHEST
epsilon = 1e-06


def padded(shard, sides, width):
    for axis, dim in sides:
        size, length = (lax.axis_size(axis), shard.shape[dim])
        up = [(i, (i + 1) % size) for i in range(size)]
        down = [(j, i) for i, j in up]
        last = lax.slice_in_dim(shard, length - width, length, axis=dim)
        leading = lax.slice_in_dim(shard, 0, width, axis=dim)
        before = lax.ppermute(last, axis, up)
        after = lax.ppermute(leading, axis, down)
        shard = jnp.concatenate([before, shard, after], axis=dim)
    return shard


def from_partner(value, axis, stride):
    mask = 2**stride
    pairs = [(source, source ^ mask) for source in range(lax.axis_size(axis))]
    return lax.ppermute(value, axis, pairs)


def frame(angles):
    cos_yaw = jnp.cos(angles[0])
    sin_yaw = jnp.sin(angles[0])
    cos_pitch = jnp.cos(angles[1])
    sin_pitch = jnp.sin(angles[1])
    cos_roll = jnp.cos(angles[2])
    sin_roll = jnp.sin(angles[2])
    return (
        (
            cos_yaw * cos_pitch,
            cos_yaw * sin_pitch * sin_roll - sin_yaw * cos_roll,
            cos_yaw * sin_pitch * cos_roll + sin_yaw * sin_roll,
        ),
        (
            sin_yaw * cos_pitch,
            sin_yaw * sin_pitch * sin_roll + cos_yaw * cos_roll,
            sin_yaw * sin_pitch * cos_roll - cos_yaw * sin_roll,
        ),
        (-sin_pitch, cos_pitch * sin_roll, cos_pitch * cos_roll),
    )


def rotate(source, rotation, inverse):
    components = []
    for target_axis in range(3):
        summed = jnp.zeros_like(source[0])
        for source_axis in range(3):
            factor = (
                rotation[source_axis][target_axis]
                if inverse
                else rotation[target_axis][source_axis]
            )
            summed = summed + factor[None, :] * source[source_axis]
        components.append(summed)
    return jnp.stack(components)


def least_squares(beta, diag_first, below_first, above_second, diag_second, below_second):
    first_norm = jnp.sqrt(diag_first * diag_first + below_first * below_first)
    first_cos = diag_first / first_norm
    first_sin = below_first / first_norm
    top_right = first_cos * above_second + first_sin * diag_second
    lower_right = first_cos * diag_second - first_sin * above_second
    second_norm = jnp.sqrt(lower_right * lower_right + below_second * below_second)
    second_cos = lower_right / second_norm
    second_sin = below_second / second_norm
    carried = -first_sin * beta
    coef_two = second_cos * carried / second_norm
    coef_one = (first_cos * beta - top_right * coef_two) / first_norm
    return (coef_one, coef_two, jnp.abs(second_sin * carried))


def contract_last(left, right):
    return lax.dot_general(left, right, (((1,), (1,)), ((), ())), precision=highest)


def body(
    rhs,
    angles,
    self_mob,
    near_mat,
    near_weight,
    neighbours,
    cells,
    blob_weight,
    skel_perm,
    interp,
    sibling_ops,
    root_op,
):
    blob_count = blob_weight.shape[0]
    dof_count = 3 * blob_count
    box_bodies = rhs.shape[-1]
    skel_points = root_op.shape[0]
    level_count = skel_perm.shape[0]
    initial = rhs.reshape(3, blob_count, box_bodies)
    rotation = frame(angles.reshape(3, box_bodies))
    near_coef = near_weight.reshape(-1, box_bodies)
    link_ids = neighbours.reshape(-1, box_bodies)
    box_slot = link_ids // box_bodies
    body_slot = link_ids % box_bodies
    is_own = (box_slot == 4)[:, :, None]
    occupancy = (
        cells.reshape(box_bodies)[:, None] == jnp.arange(skel_points, dtype=jnp.int32)[None, :]
    ).astype(jnp.float32)
    permuter = (
        skel_perm[:, :, None] == jnp.arange(2 * skel_points, dtype=jnp.int32)[None, None, :]
    ).astype(jnp.float32)
    layer_index = lax.axis_index("gz")

    def operate(source):
        turned = rotate(source, rotation, False).reshape(dof_count, box_bodies)
        mixture = jnp.dot(self_mob, turned, precision=highest).reshape(3, blob_count, box_bodies)
        own_part = source + rotate(mixture, rotation, True)
        ghosts = padded(source[None, None], (("gx", 0), ("gy", 1)), 1)
        ghost_width = ghosts.shape[-1]
        ghost_boxes = ghosts.reshape(9, dof_count, ghost_width)
        own_rows = source.reshape(dof_count, box_bodies).T
        gathered = jnp.zeros((box_bodies, dof_count), jnp.float32)
        for link_index in range(near_coef.shape[0]):
            remote = ghost_boxes[
                box_slot[link_index], :, jnp.minimum(body_slot[link_index], ghost_width - 1)
            ]
            own_value = own_rows[body_slot[link_index]]
            gathered = gathered + near_coef[link_index][:, None] * jnp.where(
                is_own[link_index], own_value, remote
            )
        near_part = contract_last(near_mat, gathered).reshape(3, blob_count, box_bodies)
        moments = jnp.einsum("cqn,q->cn", source, blob_weight, precision=highest)
        charges = jnp.dot(moments, occupancy, precision=highest)
        partners = []
        high_flags = []
        for tree_level in range(level_count):
            partner = from_partner(charges, "gz", tree_level)
            high_side = layer_index >> tree_level & 1 == 1
            low_child = jnp.where(high_side, partner, charges)
            higher = jnp.where(high_side, charges, partner)
            joined = jnp.concatenate([low_child, higher], axis=1)
            picked = contract_last(joined, permuter[tree_level])
            charges = picked[:, :skel_points] + jnp.dot(
                picked[:, skel_points:], interp[tree_level], precision=highest
            )
            partners.append(partner)
            high_flags.append(high_side)
        root_total = lax.psum(charges, ("gx", "gy"))
        potential = jnp.dot(root_total - charges, root_op, precision=highest)
        for tree_level in reversed(range(level_count)):
            spread = jnp.concatenate(
                [potential, contract_last(potential, interp[tree_level])], axis=1
            )
            placed = jnp.dot(spread, permuter[tree_level], precision=highest)
            child_part = jnp.where(
                high_flags[tree_level], placed[:, skel_points:], placed[:, :skel_points]
            )
            potential = child_part + jnp.dot(
                partners[tree_level], sibling_ops[tree_level], precision=highest
            )
        body_values = contract_last(potential, occupancy)
        far_part = blob_weight[None, :, None] * body_values[:, None, :]
        return own_part + near_part + far_part

    def global_sum(value):
        return lax.psum(value, ("gx", "gy", "gz"))

    beta = jnp.sqrt(global_sum(jnp.sum(initial * initial)) + epsilon)
    basis_one = initial / beta
    image_one = operate(basis_one)
    diag_first = global_sum(jnp.sum(image_one * basis_one))
    residue_one = image_one - diag_first * basis_one
    below_first = jnp.sqrt(global_sum(jnp.sum(residue_one * residue_one)) + epsilon)
    basis_two = residue_one / below_first
    image_two = operate(basis_two)
    above_second, diag_second = lax.psum(
        (jnp.sum(image_two * basis_one), jnp.sum(image_two * basis_two)), ("gx", "gy", "gz")
    )
    residue_two = image_two - above_second * basis_one - diag_second * basis_two
    below_second = jnp.sqrt(global_sum(jnp.sum(residue_two * residue_two)) + epsilon)
    coef_one, coef_two, lsq_residual = least_squares(
        beta, diag_first, below_first, above_second, diag_second, below_second
    )
    result = coef_one * basis_one + coef_two * basis_two
    return (result[None, None], lsq_residual)


def solution(mesh):
    in_specs = (
        P("gx", "gy", None, None, "gz"),
        P("gx", "gy", None, "gz"),
        P(),
        P(),
        P("gx", "gy", None, "gz"),
        P("gx", "gy", None, "gz"),
        P("gx", "gy", "gz"),
        P(),
        P(),
        P(),
        P(),
        P(),
    )
    out_specs = (P("gx", "gy", None, None, "gz"), P())
    return jax.shard_map(body, mesh=mesh, in_specs=in_specs, out_specs=out_specs, check_vma=False)
```

profile of v0, /device:TPU:0, one launch (start us, length us, event | category | flops | bytes accessed | tf_op | source)
XLA Modules:
  0.0 580.7 jit_solution(11294653157665643823)
XLA Ops:
  3.5 42.2 %psum.56 = f32[]{:T(128)} all-reduce(f32[]{:T(128)} %multiply_reduce_fusion.5), channel_id=1, replica_groups=mesh['gx'=4,'gy'=2,'gz'=4] {'gx','gy','gz'}, use_global_device_ids=true, to_apply=%region_1.2 | all-reduce | flops 1 | bytes 8 | tf_op jit(solution)/shard_map/psum | solution.py:171
  81.2 14.4 %psum.57 = f32[3,192]{1,0:T(4,128)S(1)} all-reduce(f32[3,192]{1,0:T(4,128)S(1)} %slice_add_fusion.2), channel_id=1, replica_groups=mesh['gx'=4,'gy'=2,'gz'=4] {'gx','gy'}, use_global_device_ids=true, to_apply=%region_2.3 | all-reduce | flops 576 | bytes 4608 | tf_op jit(solution)/shard_map/psum | solution.py:153
  104.7 31.0 %collective-permute-done.2 = f32[3,1,3,162,256]{4,1,3,2,0:T(1,128)} collective-permute-done((f32[3,1,3,162,256]{4,1,3,2,0:T(1,128)}, f32[3,1,3,162,256]{4,1,3,2,0:T(1,128)}, u32[]{:S(2)}, u32[]{:S(2)}) %collective-permute-start.2) | collective-permute-done | bytes 1493024 | tf_op jit(solution)/shard_map/ppermute | solution.py:17
  137.3 29.6 %collective-permute-done.3 = f32[3,1,3,162,256]{4,1,3,2,0:T(1,128)} collective-permute-done((f32[3,1,3,162,256]{4,1,3,2,0:T(1,128)}, f32[3,1,3,162,256]{4,1,3,2,0:T(1,128)}, u32[]{:S(2)}, u32[]{:S(2)}) %collective-permute-start.3) | collective-permute-done | bytes 1493024 | tf_op jit(solution)/shard_map/ppermute | solution.py:18
  168.4 3.8 pad_maximum_fusion
  172.1 5.5 reshape.988
  177.6 6.0 %copy.81 = f32[9,486,256]{1,2,0:T(8,128)} copy(f32[9,486,256]{2,1,0:T(8,128)} %reshape.988) | data formatting | bytes 8957952 | tf_op jit(solution)/shard_map/reshape | solution.py:125
  183.6 3.5 gather_fusion.1
  190.6 3.5 gather_fusion.13
  194.1 3.5 gather_fusion.3
  197.7 3.5 gather_fusion.5
  201.1 3.5 gather_fusion.7
  204.7 3.5 gather_fusion.9
  208.2 14.3 %gather_fusion.15 = f32[256,486]{1,0:T(8,128)} fusion(f32[9,486,256]{1,2,0:T(8,128)} %copy.81, s32[256]{0:T(256)S(1)} %bitcast.288), kind=kCustom, calls=%fused_computation.15 | custom fusion | bytes 997376 | tf_op jit(solution)/shard_map/gather | solution.py:129
  222.6 6.0 %multiply_reduce_fusion.4 = (f32[]{:T(128)}, f32[486,256]{1,0:T(8,128)S(1)}, f32[486,256]{1,0:T(8,128)S(1)}) fusion(f32[486,256]{1,0:T(8,128)S(1)} %div.74, f32[486,256]{1,0:T(8,128)} %mul.754, f32[486]{0:T(512)S(1)} %mul.751, f32[486,256]{1,0:T(8,128)} %stack.53, f32[486,486]{1,0:T(8,128)S(1)} %copy-done, f32[256,486]{1,0:T(8,128)} %gather_fusion.14, ...), kind=kOutput, calls=%fused_computation.119 | convolution fusion | flops 729202176 | bytes 11407916 | tf_op jit(solution)/shard_map/dot_general | solution.py:82
  228.6 39.6 %psum.58 = f32[]{:T(128)} all-reduce(f32[]{:T(128)} %get-tuple-element.20), channel_id=1, replica_groups=mesh['gx'=4,'gy'=2,'gz'=4] {'gx','gy','gz'}, use_global_device_ids=true, to_apply=%region_4.5 | all-reduce | flops 1 | bytes 8 | tf_op jit(solution)/shard_map/psum | solution.py:171
  271.3 39.4 %psum.59 = f32[]{:T(128)} all-reduce(f32[]{:T(128)} %multiply_reduce_fusion.3), channel_id=1, replica_groups=mesh['gx'=4,'gy'=2,'gz'=4] {'gx','gy','gz'}, use_global_device_ids=true, to_apply=%region_6.7 | all-reduce | flops 1 | bytes 8 | tf_op jit(solution)/shard_map/psum | solution.py:171
  352.5 14.2 %psum.60 = f32[3,192]{1,0:T(4,128)S(1)} all-reduce(f32[3,192]{1,0:T(4,128)S(1)} %slice_add_fusion), channel_id=1, replica_groups=mesh['gx'=4,'gy'=2,'gz'=4] {'gx','gy'}, use_global_device_ids=true, to_apply=%region_7.8 | all-reduce | flops 576 | bytes 4608 | tf_op jit(solution)/shard_map/psum | solution.py:153
  376.8 31.0 %collective-permute-done.8 = f32[3,1,3,162,256]{4,1,3,2,0:T(1,128)} collective-permute-done((f32[3,1,3,162,256]{4,1,3,2,0:T(1,128)}, f32[3,1,3,162,256]{4,1,3,2,0:T(1,128)}, u32[]{:S(2)}, u32[]{:S(2)}) %collective-permute-start.8) | collective-permute-done | bytes 1493024 | tf_op jit(solution)/shard_map/ppermute | solution.py:17
  409.3 29.6 %collective-permute-done.9 = f32[3,1,3,162,256]{4,1,3,2,0:T(1,128)} collective-permute-done((f32[3,1,3,162,256]{4,1,3,2,0:T(1,128)}, f32[3,1,3,162,256]{4,1,3,2,0:T(1,128)}, u32[]{:S(2)}, u32[]{:S(2)}) %collective-permute-start.9) | collective-permute-done | bytes 1493024 | tf_op jit(solution)/shard_map/ppermute | solution.py:18
  440.4 3.7 pad_maximum_fusion.1
  444.1 5.5 reshape.992
  449.6 6.2 %copy.94 = f32[9,486,256]{1,2,0:T(8,128)} copy(f32[9,486,256]{2,1,0:T(8,128)} %reshape.992) | data formatting | bytes 8957952 | tf_op jit(solution)/shard_map/reshape | solution.py:125
  455.8 3.5 gather_fusion.17
  459.3 3.5 gather_fusion.19
  466.3 3.5 gather_fusion.23
  469.8 3.5 gather_fusion.25
  476.9 3.5 gather_fusion.29
  480.4 3.8 gather_fusion.31
  484.2 6.8 %multiply_reduce_fusion.2 = (f32[]{:T(128)}, f32[]{:T(128)}, f32[486,256]{1,0:T(8,128)}) fusion(f32[486,256]{1,0:T(8,128)S(1)} %div.74, f32[486,256]{1,0:T(8,128)S(1)} %copy-done.2, f32[486,256]{1,0:T(8,128)} %mul.799, f32[486]{0:T(512)S(1)} %mul.751, f32[486,486]{1,0:T(8,128)S(1)} %copy-done, f32[256,486]{1,0:T(8,128)} %gather_fusion.30, ...), kind=kOutput, calls=%fused_computation.116 | convolution fusion | flops 729451008 | bytes 11407920 | tf_op jit(solution)/shard_map/dot_general | solution.py:82
  491.0 38.5 %all-reduce = (f32[]{:T(128)}, f32[]{:T(128)}) all-reduce(f32[]{:T(128)} %get-tuple-element.9, f32[]{:T(128)} %get-tuple-element.8), channel_id=1, replica_groups=mesh['gx'=4,'gy'=2,'gz'=4] {'gx','gy','gz'}, use_global_device_ids=true, to_apply=%region_11.12 | all-reduce | flops 2 | bytes 16 | tf_op jit(solution)/shard_map/psum | solution.py:181
  535.2 41.5 %psum.63 = f32[]{:T(128)} all-reduce(f32[]{:T(128)} %multiply_reduce_fusion), channel_id=1, replica_groups=mesh['gx'=4,'gy'=2,'gz'=4] {'gx','gy','gz'}, use_global_device_ids=true, to_apply=%region_13.14 | all-reduce | flops 1 | bytes 8 | tf_op jit(solution)/shard_map/psum | solution.py:171
  (212 shorter events, 119.6 us)
Async XLA Ops:
  0.6 221.9 %copy-start = (f32[486,486]{1,0:T(8,128)S(1)}, f32[486,486]{1,0:T(8,128)}, u32[]{:S(2)}) copy-start(f32[486,486]{1,0:T(8,128)} %param.15) | copy-start | bytes 2834356
  0.6 56.0 %copy-start.6 = (f32[486,486]{1,0:T(8,128)S(1)}, f32[486,486]{1,0:T(8,128)}, u32[]{:S(2)}) copy-start(f32[486,486]{1,0:T(8,128)} %param.14) | copy-start | bytes 2834356
  0.7 58.1 %copy-start.37 = (s32[2,384]{1,0:T(2,128)S(1)}, s32[2,384]{1,0:T(2,128)}, u32[]{:S(2)}) copy-start(s32[2,384]{1,0:T(2,128)} %param.20) | copy-start | bytes 9220
  46.3 16.3 %copy-start.3 = (f32[2,192,192]{2,1,0:T(8,128)S(1)}, f32[2,192,192]{2,1,0:T(8,128)}, u32[]{:S(2)}) copy-start(f32[2,192,192]{2,1,0:T(8,128)} %param.21) | copy-start | bytes 884740
  47.5 48.3 %collective-permute-start = (f32[1,1,3,162,256]{4,3,2,1,0:T(8,128)S(1)}, f32[1,1,3,162,256]{4,3,2,1,0:T(8,128)}, u32[]{:S(2)}, u32[]{:S(2)}) collective-permute-start(f32[1,1,3,162,256]{4,3,2,1,0:T(8,128)S(1)} %copy_divide_fusion), channel_id=1, source_target_pairs={{0,8},{8,16},{16,24},{24,0},{1,9},{9,17},{17,25},{25,1},{2,10},{10... | collective-permute-start | bytes 1493000 | tf_op jit(solution)/shard_map/ppermute | solution.py:17
  47.6 48.3 %collective-permute-start.1 = (f32[1,1,3,162,256]{4,3,2,1,0:T(8,128)S(1)}, f32[1,1,3,162,256]{4,3,2,1,0:T(8,128)}, u32[]{:S(2)}, u32[]{:S(2)}) collective-permute-start(f32[1,1,3,162,256]{4,3,2,1,0:T(8,128)S(1)} %copy_divide_fusion), channel_id=1, source_target_pairs={{8,0},{16,8},{24,16},{0,24},{9,1},{17,9},{25,17},{1,25},{10,2},{18... | collective-permute-start | bytes 1493000 | tf_op jit(solution)/shard_map/ppermute | solution.py:18
  51.9 9.7 %collective-permute-start.4 = (f32[3,192]{1,0:T(4,128)}, f32[3,192]{1,0:T(4,128)S(1)}, u32[]{:S(2)}, u32[]{:S(2)}) collective-permute-start(f32[3,192]{1,0:T(4,128)} %fusion.61), channel_id=1, source_target_pairs={{0,1},{1,0},{2,3},{3,2},{4,5},{5,4},{6,7},{7,6},{8,9},{9,8},{10,11... | collective-permute-start | bytes 6920 | tf_op jit(solution)/shard_map/ppermute | solution.py:26
  59.1 43.9 %copy-start.13 = (pred[2,384,384]{2,1,0:T(32,128)(4,1)}, pred[2,384,384]{2,1,0:T(32,128)(4,1)S(1)}, u32[]{:S(2)}) copy-start(pred[2,384,384]{2,1,0:T(32,128)(4,1)S(1)} %iota_compare_fusion) | copy-start | bytes 884740
  62.9 17.7 %collective-permute-start.5 = (f32[3,192]{1,0:T(4,128)S(1)}, f32[3,192]{1,0:T(4,128)S(1)}, u32[]{:S(2)}, u32[]{:S(2)}) collective-permute-start(f32[3,192]{1,0:T(4,128)S(1)} %slice_add_fusion.3), channel_id=1, source_target_pairs={{0,2},{1,3},{2,0},{3,1},{4,6},{5,7},{6,4},{7,5},{8,10},{9,11},{10,... | collective-permute-start | bytes 6920 | tf_op jit(solution)/shard_map/ppermute | solution.py:26
  76.5 19.1 %copy-start.12 = (f32[192,192]{1,0:T(8,128)S(1)}, f32[192,192]{1,0:T(8,128)}, u32[]{:S(2)}) copy-start(f32[192,192]{1,0:T(8,128)} %param.23) | copy-start | bytes 442372
  80.5 22.0 %copy-start.10 = (f32[2,192,192]{2,1,0:T(8,128)S(1)}, f32[2,192,192]{2,1,0:T(8,128)}, u32[]{:S(2)}) copy-start(f32[2,192,192]{2,1,0:T(8,128)} %param.22) | copy-start | bytes 884740
  80.5 23.0 %copy-start.38 = (s32[1,1,256]{2,1,0:T(1,128)S(1)}, s32[1,1,256]{2,1,0:T(1,128)}, u32[]{:S(2)}) copy-start(s32[1,1,256]{2,1,0:T(1,128)} %param.18) | copy-start | bytes 3076
  99.9 35.9 %collective-permute-start.2 = (f32[3,1,3,162,256]{4,1,3,2,0:T(1,128)}, f32[3,1,3,162,256]{4,1,3,2,0:T(1,128)}, u32[]{:S(2)}, u32[]{:S(2)}) collective-permute-start(f32[3,1,3,162,256]{4,1,3,2,0:T(1,128)} %copy.77), channel_id=1, source_target_pairs={{0,4},{4,0},{1,5},{5,1},{2,6},{6,2},{3,7},{7,3},{8,12},{12,8},{9,1... | collective-permute-start | bytes 4478984 | tf_op jit(solution)/shard_map/ppermute | solution.py:17
  100.1 66.7 %collective-permute-start.3 = (f32[3,1,3,162,256]{4,1,3,2,0:T(1,128)}, f32[3,1,3,162,256]{4,1,3,2,0:T(1,128)}, u32[]{:S(2)}, u32[]{:S(2)}) collective-permute-start(f32[3,1,3,162,256]{4,1,3,2,0:T(1,128)} %copy.77), channel_id=1, source_target_pairs={{4,0},{0,4},{5,1},{1,5},{6,2},{2,6},{7,3},{3,7},{12,8},{8,12},{13,... | collective-permute-start | bytes 4478984 | tf_op jit(solution)/shard_map/ppermute | solution.py:18
  204.6 17.9 %copy-start.22 = (pred[256]{0:T(512)(128)(4,1)S(1)}, pred[256]{0:T(512)(128)(4,1)}, u32[]{:S(2)}) copy-start(pred[256]{0:T(512)(128)(4,1)} %get-tuple-element.10) | copy-start | bytes 772
  204.6 17.9 %copy-start.23 = (pred[256]{0:T(512)(128)(4,1)S(1)}, pred[256]{0:T(512)(128)(4,1)}, u32[]{:S(2)}) copy-start(pred[256]{0:T(512)(128)(4,1)} %get-tuple-element.11) | copy-start | bytes 772
  204.6 17.9 %copy-start.25 = (pred[256]{0:T(512)(128)(4,1)S(1)}, pred[256]{0:T(512)(128)(4,1)}, u32[]{:S(2)}) copy-start(pred[256]{0:T(512)(128)(4,1)} %get-tuple-element.12) | copy-start | bytes 772
  204.6 17.9 %copy-start.27 = (pred[256]{0:T(512)(128)(4,1)S(1)}, pred[256]{0:T(512)(128)(4,1)}, u32[]{:S(2)}) copy-start(pred[256]{0:T(512)(128)(4,1)} %get-tuple-element.13) | copy-start | bytes 772
  204.6 17.9 %copy-start.29 = (pred[256]{0:T(512)(128)(4,1)S(1)}, pred[256]{0:T(512)(128)(4,1)}, u32[]{:S(2)}) copy-start(pred[256]{0:T(512)(128)(4,1)} %get-tuple-element.14) | copy-start | bytes 772
  204.7 17.9 %copy-start.31 = (pred[256]{0:T(512)(128)(4,1)S(1)}, pred[256]{0:T(512)(128)(4,1)}, u32[]{:S(2)}) copy-start(pred[256]{0:T(512)(128)(4,1)} %get-tuple-element.15) | copy-start | bytes 772
  204.7 17.9 %copy-start.33 = (pred[256]{0:T(512)(128)(4,1)S(1)}, pred[256]{0:T(512)(128)(4,1)}, u32[]{:S(2)}) copy-start(pred[256]{0:T(512)(128)(4,1)} %get-tuple-element.16) | copy-start | bytes 772
  204.7 17.9 %copy-start.35 = (pred[256]{0:T(512)(128)(4,1)S(1)}, pred[256]{0:T(512)(128)(4,1)}, u32[]{:S(2)}) copy-start(pred[256]{0:T(512)(128)(4,1)} %get-tuple-element.17) | copy-start | bytes 772
  222.6 88.8 %copy-start.1 = (f32[1,1,3,162,256]{4,1,3,2,0:T(1,128)S(1)}, f32[1,1,3,162,256]{4,1,3,2,0:T(1,128)}, u32[]{:S(2)}) copy-start(f32[1,1,3,162,256]{4,1,3,2,0:T(1,128)} %param.12) | copy-start | bytes 1492996
  228.6 82.8 %copy-start.4 = (f32[486,256]{1,0:T(8,128)}, f32[486,256]{1,0:T(8,128)S(1)}, u32[]{:S(2)}) copy-start(f32[486,256]{1,0:T(8,128)S(1)} %get-tuple-element.21) | copy-start | bytes 1492996
  313.5 54.4 %collective-permute-start.6 = (f32[1,1,3,162,256]{4,3,2,1,0:T(8,128)S(1)}, f32[1,1,3,162,256]{4,3,2,1,0:T(8,128)}, u32[]{:S(2)}, u32[]{:S(2)}) collective-permute-start(f32[1,1,3,162,256]{4,3,2,1,0:T(8,128)S(1)} %fusion.51), channel_id=1, source_target_pairs={{0,8},{8,16},{16,24},{24,0},{1,9},{9,17},{17,25},{25,1},{2,10},{10... | collective-permute-start | bytes 1493000 | tf_op jit(solution)/shard_map/ppermute | solution.py:17
  313.6 54.3 %collective-permute-start.7 = (f32[1,1,3,162,256]{4,3,2,1,0:T(8,128)S(1)}, f32[1,1,3,162,256]{4,3,2,1,0:T(8,128)}, u32[]{:S(2)}, u32[]{:S(2)}) collective-permute-start(f32[1,1,3,162,256]{4,3,2,1,0:T(8,128)S(1)} %fusion.51), channel_id=1, source_target_pairs={{8,0},{16,8},{24,16},{0,24},{9,1},{17,9},{25,17},{1,25},{10,2},{18... | collective-permute-start | bytes 1493000 | tf_op jit(solution)/shard_map/ppermute | solution.py:18
  322.9 3.7 collective-permute-start.10
  328.0 23.1 %collective-permute-start.11 = (f32[3,192]{1,0:T(4,128)S(1)}, f32[3,192]{1,0:T(4,128)S(1)}, u32[]{:S(2)}, u32[]{:S(2)}) collective-permute-start(f32[3,192]{1,0:T(4,128)S(1)} %slice_add_fusion.1), channel_id=1, source_target_pairs={{0,2},{1,3},{2,0},{3,1},{4,6},{5,7},{6,4},{7,5},{8,10},{9,11},{10,... | collective-permute-start | bytes 6920 | tf_op jit(solution)/shard_map/ppermute | solution.py:26
  347.1 27.5 %copy-start.11 = (f32[2,192,192]{2,1,0:T(8,128)S(1)}, f32[2,192,192]{2,1,0:T(8,128)}, u32[]{:S(2)}) copy-start(f32[2,192,192]{2,1,0:T(8,128)} %param.22) | copy-start | bytes 884740
  349.2 26.3 %copy-start.40 = (s32[1,1,256]{2,1,0:T(1,128)S(1)}, s32[1,1,256]{2,1,0:T(1,128)}, u32[]{:S(2)}) copy-start(s32[1,1,256]{2,1,0:T(1,128)} %param.18) | copy-start | bytes 3076
  371.9 35.9 %collective-permute-start.8 = (f32[3,1,3,162,256]{4,1,3,2,0:T(1,128)}, f32[3,1,3,162,256]{4,1,3,2,0:T(1,128)}, u32[]{:S(2)}, u32[]{:S(2)}) collective-permute-start(f32[3,1,3,162,256]{4,1,3,2,0:T(1,128)} %copy.90), channel_id=1, source_target_pairs={{0,4},{4,0},{1,5},{5,1},{2,6},{6,2},{3,7},{7,3},{8,12},{12,8},{9,1... | collective-permute-start | bytes 4478984 | tf_op jit(solution)/shard_map/ppermute | solution.py:17
  372.1 66.7 %collective-permute-start.9 = (f32[3,1,3,162,256]{4,1,3,2,0:T(1,128)}, f32[3,1,3,162,256]{4,1,3,2,0:T(1,128)}, u32[]{:S(2)}, u32[]{:S(2)}) collective-permute-start(f32[3,1,3,162,256]{4,1,3,2,0:T(1,128)} %copy.90), channel_id=1, source_target_pairs={{4,0},{0,4},{5,1},{1,5},{6,2},{2,6},{7,3},{3,7},{12,8},{8,12},{13,... | collective-permute-start | bytes 4478984 | tf_op jit(solution)/shard_map/ppermute | solution.py:18
  (21 other events, 172.7 us)
where the time goes:
time: 590 us; the launch traced here: 581 us
  blocking collectives  230 us (39%)
  local copies, waits for them, and re-layouts  145 us (25%)
  waiting for transfers between devices  123 us (21%)
  other arithmetic  29.5 us (5%)
  matrix products  29.3 us (5%)
  starting transfers between devices  13.8 us (2%)
  between operations  9.99 us (2%)
    psum x4, blocking collectives, global_sum(): return lax.psum(value, ('gx', 'gy', 'gz'))  163 us
    gather x16, local copies, waits for them, and re-layouts, operate(): ghost_boxes[box_slot[link_index], :, jnp.minimum(body_slot[link_index], g...  67.2 us
    ppermute x4, waiting for transfers between devices, padded(): before = lax.ppermute(last, axis, up)  62.1 us
    ppermute x4, waiting for transfers between devices, padded(): after = lax.ppermute(leading, axis, down)  59.1 us
    psum x1, blocking collectives, body(): lax.psum((jnp.sum(image_two * basis_one), jnp.sum(image_two * basis_two))...  38.5 us
    gather x16, local copies, waits for them, and re-layouts, operate(): own_value = own_rows[body_slot[link_index]]  29.8 us
    psum x2, blocking collectives, operate(): root_total = lax.psum(charges, ('gx', 'gy'))  28.6 us
    reshape x4, local copies, waits for them, and re-layouts, operate(): ghost_boxes = ghosts.reshape(9, dof_count, ghost_width)  23.1 us
  transfers between devices with their start and end apart: 12, of which 5 were waited for; matrix products, arithmetic and copies ran while one was open for 12% of the time, Pallas kernels for 0%

commit v1 on v0

v1 whole, which is shorter than its diff:
```python
import functools

import jax
import jax.numpy as jnp
from jax import lax
from jax.experimental import pallas as pl
from jax.experimental.pallas import tpu as pltpu
from jax.sharding import PartitionSpec as P

epsilon = 1e-06
f32 = jnp.float32
bf16 = jnp.bfloat16
RIM = 64
LANES = 128


def round_up(value, unit):
    return -(-value // unit) * unit


def split(x):
    hi = x.astype(bf16)
    lo = (x - hi.astype(f32)).astype(bf16)
    return hi, lo


def mm(a, b):
    return lax.dot_general(a, b, (((1,), (0,)), ((), ())), preferred_element_type=f32)


def mt(a, b):
    return lax.dot_general(a, b, (((1,), (1,)), ((), ())), preferred_element_type=f32)


def product(dot, a, b):
    return dot(a[0], b[0]) + (dot(a[0], b[1]) + dot(a[1], b[0]))


def total(x):
    return jnp.sum(jnp.sum(x, axis=0, keepdims=True), axis=1, keepdims=True)


class Sizes:
    def __init__(self, mesh_shape, rhs, skel_perm):
        self.nx, self.ny, self.nz = (mesh_shape[a] for a in ("gx", "gy", "gz"))
        self.devices = self.nx * self.ny * self.nz
        self.blobs, self.bodies = rhs.shape[-2:]
        self.step = round_up(self.blobs, 8)
        self.rows = round_up(3 * self.step, 16)
        self.half = self.rows // 2
        self.levels = skel_perm.shape[0]
        self.skel = skel_perm.shape[1] // 2
        self.own_slots = []
        self.sources = []
        self.slot_base = []
        for slot in range(9):
            offset = ((slot // 3 - 1) % self.nx, (slot % 3 - 1) % self.ny)
            if offset == (0, 0):
                self.slot_base.append(0)
                continue
            if offset not in self.sources:
                self.sources.append(offset)
            self.slot_base.append(self.bodies + RIM * self.sources.index(offset))
        self.ghosts = round_up(max(1, len(self.sources)) * RIM, LANES)


def pieces(x, s):
    return [x[c * s.step : c * s.step + s.step] for c in range(3)]


def turn(parts, rot, inverse):
    out = []
    for target in range(3):
        acc = None
        for source in range(3):
            row = 3 * source + target if inverse else 3 * target + source
            term = rot[row : row + 1] * parts[source]
            acc = term if acc is None else acc + term
        out.append(acc)
    return out


def stacked(parts, s):
    rest = s.rows - 3 * s.step
    if rest:
        parts = list(parts) + [jnp.zeros((rest, s.bodies), f32)]
    return jnp.concatenate(parts, axis=0)


def occupancy(cells, s):
    row = lax.broadcasted_iota(jnp.int32, (s.skel, s.bodies), 0)
    return jnp.where(cells == row, 1.0, 0.0).astype(bf16)


def pack_charges(parts, weight_col, occ, s):
    moments = [jnp.sum(part * weight_col, axis=0, keepdims=True) for part in parts]
    moments = jnp.concatenate(moments + [jnp.zeros((5, s.bodies), f32)], axis=0)
    high, rest = split(moments)
    mid, low = split(moments - high.astype(f32))
    stack = jnp.concatenate([high.astype(f32), mid.astype(f32), low.astype(f32)], axis=0).astype(bf16)
    sums = mt(stack, occ)
    charges = sums[0:8] + (sums[8:16] + sums[16:24])
    tail = jnp.concatenate([charges[:, LANES:], jnp.zeros((8, 2 * LANES - s.skel), f32)], axis=1)
    row = lax.broadcasted_iota(jnp.int32, (8, LANES), 0)
    return jnp.where(row < 4, charges[:, :LANES], pltpu.roll(tail, 4, 0))


def pack_rim(x, s):
    lane = lax.broadcasted_iota(jnp.int32, (s.half, LANES), 1)
    top, bottom = x[: s.half, :LANES], x[s.half :, :LANES]
    return jnp.where(lane < RIM, top, pltpu.roll(bottom, RIM, 1))


def unpack_rims(rims, s):
    lane = lax.broadcasted_iota(jnp.int32, (s.half, LANES), 1)
    tops, bottoms = [], []
    for i in range(0, s.ghosts // RIM, 2):
        a = rims[i]
        b = rims[i + 1] if i + 1 < len(rims) else jnp.zeros_like(a)
        tops.append(jnp.where(lane < RIM, a, pltpu.roll(b, RIM, 1)))
        bottoms.append(jnp.where(lane < RIM, pltpu.roll(a, RIM, 1), b))
    return jnp.concatenate(
        [jnp.concatenate(tops, axis=1), jnp.concatenate(bottoms, axis=1)], axis=0
    )


def start_kernel(s, rhs, cells, weight, q_out, rim_out, col_out, f_out):
    f_out[...] = jnp.zeros_like(f_out)
    for c in range(3):
        f_out[c * s.step : c * s.step + s.blobs, :] = rhs[0, 0, c]
    f = f_out[...]
    wide = jnp.concatenate([weight[...], jnp.zeros((1, 2 * LANES - s.blobs), f32)], axis=1)
    col = jnp.broadcast_to(wide, (LANES, 2 * LANES)).T[: s.step]
    col_out[...] = col
    rim_out[...] = pack_rim(f, s)
    occ = occupancy(cells[0], s)
    q_out[...] = pack_charges(pieces(f, s), col[:, :1], occ, s)


def frame_rows(angles):
    cos, sin = jnp.cos(angles), jnp.sin(angles)
    cy, cp, cr = cos[0:1], cos[1:2], cos[2:3]
    sy, sp, sr = sin[0:1], sin[1:2], sin[2:3]
    return [
        cy * cp,
        cy * sp * sr - sy * cr,
        cy * sp * cr + sy * sr,
        sy * cp,
        sy * sp * sr + cy * cr,
        sy * sp * cr - cy * sr,
        -sp,
        cp * sr,
        cp * cr,
    ]


def local_part(f, s, rot, mob, own):
    parts = pieces(f, s)
    turned = stacked(turn(parts, rot, False), s)
    mixed = product(mm, mob, split(turned))
    back = turn(pieces(mixed, s), rot, True)
    return f + stacked(back, s), product(mm, split(f), own)


def expand(block, level, ups):
    if level == 0:
        return [block]
    up = ups[level - 1]
    n = up.shape[0] // 2
    both = product(mm, split(up), split(block))
    return expand(both[:n], level - 1, ups) + expand(both[n:], level - 1, ups)


def setup_kernel(
    s, ids, f_in, angles, self_mob, near_mat, near_weight, neighbours, perm, interp, sibling, root,
    loc_out, gat_out, rot_out, sh_out, sl_out, nh_out, nl_out, oh_out, ol_out, gh_out, gl_out,
    th_out, tl_out, padded, ups_ref,
):
    f = f_in[...]
    rot = jnp.concatenate(frame_rows(angles[0, 0]) + [jnp.zeros((7, s.bodies), f32)], axis=0)
    rot_out[...] = rot

    padded[...] = jnp.zeros_like(padded)
    for matrix, hi_out, lo_out in ((self_mob, sh_out, sl_out), (near_mat, nh_out, nl_out)):
        for c in range(3):
            for d in range(3):
                padded[c * s.step : c * s.step + s.blobs, d * s.step : d * s.step + s.blobs] = matrix[
                    c * s.blobs : (c + 1) * s.blobs, d * s.blobs : (d + 1) * s.blobs
                ]
        hi, lo = split(padded[...])
        hi_out[...] = hi
        lo_out[...] = lo

    links = neighbours[0, 0]
    slot = links // s.bodies
    base = jnp.zeros_like(links)
    for index, start in enumerate(s.slot_base):
        base = jnp.where(slot == index, start, base)
    column = base + links % s.bodies
    coef = near_weight[0, 0]
    for first, count, hi_out, lo_out in (
        (0, s.bodies, oh_out, ol_out),
        (s.bodies, s.ghosts, gh_out, gl_out),
    ):
        for r in range(0, count, 64):
            row = lax.broadcasted_iota(jnp.int32, (64, s.bodies), 0) + (first + r)
            acc = jnp.zeros((64, s.bodies), f32)
            for k in range(coef.shape[0]):
                acc = acc + jnp.where(column[k : k + 1] == row, coef[k : k + 1], 0.0)
            hi, lo = split(acc)
            hi_out[r : r + 64, :] = hi
            lo_out[r : r + 64, :] = lo

    loc, gat = local_part(f, s, rot, (sh_out[...], sl_out[...]), (oh_out[...], ol_out[...]))
    loc_out[...] = loc
    gat_out[...] = gat

    n = s.skel
    z = ids[1]
    ups = []
    eye_row = lax.broadcasted_iota(jnp.int32, (n, n), 0)
    eye_col = lax.broadcasted_iota(jnp.int32, (n, n), 1)
    eye = jnp.where(eye_row == eye_col, 1.0, 0.0)
    for level in range(s.levels):
        spot = lax.broadcasted_iota(jnp.int32, (2 * n, 2 * n), 0)
        onehot = jnp.where(perm[level : level + 1, :] == spot, 1.0, 0.0).astype(bf16)
        hi, lo = split(jnp.concatenate([eye, interp[level]], axis=0))
        up = mm(onehot, hi) + mm(onehot, lo)
        ups.append(up)
        ups_ref[level] = up

    def down(block, level):
        bit = (z >> level) & 1
        half = ups_ref[level, pl.ds(pl.multiple_of(bit * n, 8), n), :]
        return product(mt, split(block), split(half))

    spread = root[...]
    beside = []
    for level in reversed(range(s.levels)):
        spread = down(spread, level)
        beside = [down(block, level) for block in beside]
        beside.append(sibling[level])
    far_leaves = expand(spread, s.levels, ups)
    near_leaves = [jnp.zeros((n, n), f32) for _ in range(s.nz)]
    for level, block in zip(reversed(range(s.levels)), beside):
        sub = expand(block, level, ups)
        for leaf in range(s.nz):
            hit = (leaf >> level) == ((z >> level) ^ 1)
            near_leaves[leaf] = jnp.where(hit, near_leaves[leaf] + sub[leaf % (1 << level)], near_leaves[leaf])
    pad = jnp.zeros((2 * LANES - n, n), f32)
    for leaf in range(s.nz):
        for group, block in ((0, near_leaves[leaf] - far_leaves[leaf]), (s.nz, far_leaves[leaf])):
            hi, lo = split(jnp.concatenate([block, pad], axis=0))
            at = (group + leaf) * 2 * LANES
            th_out[at : at + 2 * LANES, :] = hi
            tl_out[at : at + 2 * LANES, :] = lo


def image(s, ids, loc, gat, rims, near, ghost, charges, far_op, cells, col):
    column = ids[0]
    chunks = []
    for leaf in range(s.nz):
        chunks.append(charges[column * s.nz + leaf])
    for leaf in range(s.nz):
        acc = charges[leaf]
        for c in range(1, s.nx * s.ny):
            acc = acc + charges[c * s.nz + leaf]
        chunks.append(acc)
    left = jnp.concatenate([x for tile in chunks for x in (tile, pltpu.roll(tile, 4, 0))], axis=1)
    potential = product(mm, split(left), far_op)
    occ = occupancy(cells[0], s)
    p_hi, p_lo = split(potential)
    p_mid, p_low = split(potential - p_hi.astype(f32))
    stack = jnp.concatenate([p_hi.astype(f32), p_mid.astype(f32), p_low.astype(f32)], axis=0).astype(bf16)
    values = mm(stack, occ)
    values = values[0:8] + (values[8:16] + values[16:24])
    far = stacked([col * values[c : c + 1] for c in range(3)], s)
    gathered = gat + product(mm, split(unpack_rims(rims, s)), ghost)
    return (loc + far) + product(mm, near, split(gathered))


def first_kernel(s, n_rims, ids, loc, gat, nh, nl, gh, gl, charges, th, tl, cells, col, *rest):
    rims, (u_out, q_out, rim_out) = rest[:n_rims], rest[n_rims:]
    weight_col = col[:, :1]
    u = image(
        s, ids, loc[...], gat[...], [r[...] for r in rims], (nh[...], nl[...]), (gh[...], gl[...]),
        charges, (th[...], tl[...]), cells, weight_col,
    )
    u_out[...] = u
    rim_out[...] = pack_rim(u, s)
    q_out[...] = pack_charges(pieces(u, s), weight_col, occupancy(cells[0], s), s)


def safe_inverse(x):
    return jnp.where(x > 0.0, 1.0 / jnp.where(x > 0.0, x, 1.0), 0.0)


def middle_kernel(s, u_in, f_in, rot, sh, sl, oh, ol, loc_out, gat_out, ortho_out, stat_out):
    u, f = u_in[...], f_in[...]
    loc, gat = local_part(u, s, rot[...], (sh[...], sl[...]), (oh[...], ol[...]))
    loc_out[...] = loc
    gat_out[...] = gat
    ff = total(f * f)
    fu = total(f * u) * safe_inverse(ff)
    ortho = u - fu * f
    ortho_out[...] = ortho
    oo = total(ortho * ortho)
    stat_out[...] = jnp.broadcast_to(
        jnp.concatenate([ff, fu, oo, jnp.zeros((5, 1), f32)], axis=0), (8, LANES)
    )


def second_kernel(
    s, n_rims, ids, loc, gat, nh, nl, gh, gl, charges, th, tl, cells, col, f_in, ortho_in, stat, *rest
):
    rims, (stat_out,) = rest[:n_rims], rest[n_rims:]
    t = image(
        s, ids, loc[...], gat[...], [r[...] for r in rims], (nh[...], nl[...]), (gh[...], gl[...]),
        charges, (th[...], tl[...]), cells, col[:, :1],
    )
    f, ortho = f_in[...], ortho_in[...]
    ff, fu, oo = (stat[i : i + 1, :1] for i in range(3))
    ft = total(f * t) * safe_inverse(ff)
    ot = total(ortho * t) * safe_inverse(oo)
    rest_t = t - ft * f - ot * ortho
    tt = total(rest_t * rest_t)
    rf, ro = jnp.sqrt(ff), jnp.sqrt(oo)
    stat_out[...] = jnp.broadcast_to(
        jnp.concatenate(
            [rf, rf * fu, ro, rf * ft, ro * ot, jnp.sqrt(tt), jnp.zeros((2, 1), f32)], axis=0
        ),
        (8, LANES),
    )


def finish_kernel(s, stats, rhs, u_in, x_out, lsq_out):
    groups = []
    for g in range(0, s.devices, LANES):
        acc = jnp.zeros((8, LANES), f32)
        lane = lax.broadcasted_iota(jnp.int32, (8, LANES), 1)
        for d in range(g, min(s.devices, g + LANES)):
            acc = acc + jnp.where(lane == d - g, stats[d], 0.0)
        groups.append(acc)
    rows = jnp.concatenate(groups, axis=1) if len(groups) > 1 else groups[0]
    f1, u1, u2, t1, t2, t3 = (rows[i : i + 1] for i in range(6))

    def along(x):
        return jnp.sum(x, axis=1, keepdims=True)

    beta = jnp.sqrt(along(f1 * f1) + epsilon)
    v = f1 / beta
    w1, w2 = u1 / beta, u2 / beta
    h11 = along(w1 * v)
    r1 = w1 - h11 * v
    h21 = jnp.sqrt(along(r1 * r1 + w2 * w2) + epsilon)
    b1, b2 = r1 / h21, w2 / h21
    z1, z2, z3 = ((t1 / beta - h11 * w1) / h21, (t2 / beta - h11 * w2) / h21, t3 / beta / h21)
    h12 = along(z1 * v)
    h22 = along(z1 * b1 + z2 * b2)
    d1, d2 = z1 - h12 * v - h22 * b1, z2 - h22 * b2
    h32 = jnp.sqrt(along(d1 * d1 + d2 * d2 + z3 * z3) + epsilon)
    first_norm = jnp.sqrt(h11 * h11 + h21 * h21)
    c1, s1 = h11 / first_norm, h21 / first_norm
    t12, t22 = c1 * h12 + s1 * h22, c1 * h22 - s1 * h12
    second_norm = jnp.sqrt(t22 * t22 + h32 * h32)
    c2, s2 = t22 / second_norm, h32 / second_norm
    g2 = -s1 * beta
    y2 = c2 * g2 / second_norm
    y1 = (c1 * beta - t12 * y2) / first_norm
    lsq_out[...] = jnp.abs(s2 * g2)
    on_u = y2 / h21 / beta
    on_f = y1 / beta - on_u * h11
    for c in range(3):
        x_out[0, 0, c] = on_f * rhs[0, 0, c] + on_u * u_in[c * s.step : c * s.step + s.blobs, :]


def call(kernel, outs, args, scalars=0, scratch=(), flops=0):
    vmem = pl.BlockSpec(memory_space=pltpu.VMEM)
    smem = pl.BlockSpec(memory_space=pltpu.SMEM)
    return pl.pallas_call(
        kernel,
        out_shape=[jax.ShapeDtypeStruct(shape, kind) for shape, kind in outs],
        in_specs=[smem] * scalars + [vmem] * (len(args) - scalars),
        out_specs=[vmem] * len(outs),
        scratch_shapes=list(scratch),
        compiler_params=pltpu.CompilerParams(vmem_limit_bytes=32 * 2**20),
        cost_estimate=pl.CostEstimate(flops=flops, bytes_accessed=2**20, transcendentals=0),
    )(*args)


def body(
    mesh_shape, rhs, angles, self_mob, near_mat, near_weight, neighbours, cells, blob_weight,
    skel_perm, interp, sibling_ops, root_op,
):
    s = Sizes(mesh_shape, rhs, skel_perm)
    full = (s.rows, s.bodies)
    square = (s.rows, s.rows)
    tile = (8, LANES)
    rim = (s.half, LANES)
    far_shape = (2 * s.nz * 2 * LANES, s.skel)
    column = lax.axis_index("gx") * s.ny + lax.axis_index("gy")
    ids = jnp.stack([column, lax.axis_index("gz")]).astype(jnp.int32)

    def fetch_rims(packed):
        out = []
        for dx, dy in s.sources:
            pairs = []
            for x in range(s.nx):
                for y in range(s.ny):
                    pairs.append((((x + dx) % s.nx) * s.ny + (y + dy) % s.ny, x * s.ny + y))
            out.append(lax.ppermute(packed, ("gx", "gy"), pairs))
        return out

    def everywhere(x):
        return lax.all_gather(x, ("gx", "gy", "gz"), axis=0, tiled=False)

    charges, packed, col, f = call(
        functools.partial(start_kernel, s),
        [(tile, f32), (rim, f32), ((s.step, LANES), f32), (full, f32)],
        [rhs, cells, blob_weight.reshape(1, -1)],
        flops=10**7,
    )
    rims = fetch_rims(packed)
    charges = everywhere(charges)
    loc, gat, rot, sh, sl, nh, nl, oh, ol, gh, gl, th, tl = call(
        functools.partial(setup_kernel, s),
        [(full, f32), (full, f32), ((16, s.bodies), f32)]
        + [(square, bf16)] * 4
        + [((s.bodies, s.bodies), bf16)] * 2
        + [((s.ghosts, s.bodies), bf16)] * 2
        + [(far_shape, bf16)] * 2,
        [ids, f, angles, self_mob, near_mat, near_weight, neighbours, skel_perm, interp, sibling_ops, root_op],
        scalars=1,
        scratch=[pltpu.VMEM(square, f32), pltpu.VMEM((s.levels, 2 * s.skel, s.skel), f32)],
        flops=10**9,
    )
    u, charges, packed = call(
        functools.partial(first_kernel, s, len(rims)),
        [(full, f32), (tile, f32), (rim, f32)],
        [ids, loc, gat, nh, nl, gh, gl, charges, th, tl, cells, col, *rims],
        scalars=1,
        flops=10**9,
    )
    rims = fetch_rims(packed)
    charges = everywhere(charges)
    loc, gat, ortho, stat = call(
        functools.partial(middle_kernel, s),
        [(full, f32), (full, f32), (full, f32), (tile, f32)],
        [u, f, rot, sh, sl, oh, ol],
        flops=10**9,
    )
    (stat,) = call(
        functools.partial(second_kernel, s, len(rims)),
        [(tile, f32)],
        [ids, loc, gat, nh, nl, gh, gl, charges, th, tl, cells, col, f, ortho, stat, *rims],
        scalars=1,
        flops=10**9,
    )
    stats = everywhere(stat)
    result, lsq = call(
        functools.partial(finish_kernel, s),
        [(rhs.shape, f32), ((1, 1), f32)],
        [stats, rhs, u],
        flops=10**7,
    )
    return result, lsq.reshape(())


def solution(mesh):
    in_specs = (
        P("gx", "gy", None, None, "gz"),
        P("gx", "gy", None, "gz"),
        P(),
        P(),
        P("gx", "gy", None, "gz"),
        P("gx", "gy", None, "gz"),
        P("gx", "gy", "gz"),
        P(),
        P(),
        P(),
        P(),
        P(),
    )
    out_specs = (P("gx", "gy", None, None, "gz"), P())
    inner = functools.partial(body, dict(mesh.shape))
    return jax.shard_map(inner, mesh=mesh, in_specs=in_specs, out_specs=out_specs, check_vma=False)
```

time: 590 us -> 230 us (0.39); the launches traced: 581 us -> 230 us
  local copies, waits for them, and re-layouts: 145 us -> 5.33 us
  waiting for transfers between devices: 123 us -> 0.03 us
  blocking collectives: 230 us -> 199 us
  other arithmetic: 29.5 us -> 0.07 us
  matrix products: 29.3 us -> 0 us
  Pallas kernels: 0 us -> 13.7 us
  between operations: 9.99 us -> 0.84 us
    psum x7 -> x0, blocking collectives: 230 us -> none  [the longest x4 163 us: global_sum(): return lax.psum(value, ('gx', 'gy', 'gz'))]
    all_gather x0 -> x3, blocking collectives: none -> 199 us  [everywhere(): return lax.all_gather(x, ('gx', 'gy', 'gz'), axis=0, tiled=False)]
    ppermute x12 -> x10, waiting for transfers between devices: 123 us -> 0.03 us  [fetch_rims(): out.append(lax.ppermute(packed, ('gx', 'gy'), pairs))]
    gather x32 -> x0, local copies, waits for them, and re-layouts: 97.1 us -> none  [the longest x16 67.2 us: operate(): ghost_boxes[box_slot[link_index], :, jnp.minimum(body_slot[link_index], g...]
    dot_general x32 -> x0, matrix products: 29.3 us -> none  [the longest x12 17.3 us: contract_last(): lax.dot_general(left, right, (((1,), (1,)), ((), ())), precision=highest)]
    reshape x8 -> x0, local copies, waits for them, and re-layouts: 26.4 us -> none  [the longest x4 23.1 us: operate(): ghost_boxes = ghosts.reshape(9, dof_count, ghost_width)]
    pallas_call x0 -> x6, Pallas kernels: none -> 13.7 us  [call(): pl.pallas_call(kernel, out_shape=[jax.ShapeDtypeStruct(shape, kind) for s...]
    concatenate x5 -> x0, other arithmetic: 10.3 us -> none  [the longest x4 10.2 us: padded(): shard = jnp.concatenate([before, shard, after], axis=dim)]
  transfers between devices with their start and end apart: 12 -> 10, of which waited for: 5 -> 0; matrix products, arithmetic and copies ran while one was open for 12% -> 0% of each run, Pallas kernels for 0% -> 3%
where the time goes in v1:
time: 230 us
  blocking collectives  199 us (87%)
  Pallas kernels  13.7 us (6%)
  starting transfers between devices  10.5 us (5%)
  local copies, waits for them, and re-layouts  5.33 us (2%)
    all_gather x3, blocking collectives, everywhere(): return lax.all_gather(x, ('gx', 'gy', 'gz'), axis=0, tiled=False)  199 us
    pallas_call x6, Pallas kernels, call(): pl.pallas_call(kernel, out_shape=[jax.ShapeDtypeStruct(shape, kind) for s...  13.7 us
    ppermute x10, starting transfers between devices, fetch_rims(): out.append(lax.ppermute(packed, ('gx', 'gy'), pairs))  10.5 us
    unnamed x25, local copies, waits for them, and re-layouts  5.33 us
  transfers between devices with their start and end apart: 10, of which 0 were waited for; matrix products, arithmetic and copies ran while one was open for 0% of the time, Pallas kernels for 3%

profile of v1, /device:TPU:0, one launch (start us, length us, event | category | flops | bytes accessed | tf_op | source)
XLA Modules:
  0.0 229.8 jit_solution(15414889626922528773)
XLA Ops:
  0.7 1.2 copy.14.rhs
  1.8 0.0 copy-start
  1.8 0.0 copy-start.4
  1.9 0.6 copy-done
  2.5 0.3 shard_map.131
  2.8 2.4 %collective-permute-start = (f32[256,128]{1,0:T(8,128)S(1)}, f32[256,128]{1,0:T(8,128)S(1)}, u32[]{:S(2)}, u32[]{:S(2)}) collective-permute-start(f32[256,128]{1,0:T(8,128)S(1)} %get-tuple-element.39), channel_id=1, source_target_pairs={{28,0},{24,4},{4,8},{0,12},{12,16},{8,20},{20,24},{16,28},{29,1},{... | collective-permute-start | bytes 393224 | tf_op jit(solution)/shard_map/ppermute | solution.py:411
  5.2 1.6 collective-permute-start.1
  6.8 0.5 collective-permute-start.2
  7.4 0.8 collective-permute-start.3
  8.1 1.0 collective-permute-start.4
  9.1 0.1 pad_add_fusion.ids
  9.2 68.3 %all-gather = f32[256,128]{1,0:T(8,128)S(1)} all-gather(f32[8,128]{1,0:T(8,128)S(1)} %get-tuple-element.35), channel_id=2, replica_groups=mesh['gx'=4,'gy'=2,'gz'=4] {'gx','gy','gz'}, dimensions={0}, use_global_device_ids=true | all-gather | bytes 135168 | tf_op jit(solution)/shard_map/all_gather | solution.py:415
  77.5 0.0 copy-start.3
  77.6 1.2 copy-done.3
  78.8 1.0 copy-done.5
  79.8 4.8 %shard_map.132 = (f32[512,256]{1,0:T(8,128)S(1)}, f32[512,256]{1,0:T(8,128)S(1)}, f32[16,256]{1,0:T(8,128)S(1)}, bf16[512,512]{1,0:T(8,128)(2,1)S(1)}, bf16[512,...) custom-call(s32[2]{0:T(128)S(1)} %pad_add_fusion.ids, ...), custom_call_target="tpu_custom_call" | custom-call | flops 1000000000 | bytes 1048576 | tf_op jit(solution)/shard_map/pallas_call | solution.py:380
  84.6 0.0 collective-permute-done.rest_0_
  84.6 0.0 collective-permute-done.2.rest_2_
  84.6 0.0 collective-permute-done.3.rest_3_
  84.6 3.1 %shard_map.133 = (f32[512,256]{1,0:T(8,128)S(1)}, f32[8,128]{1,0:T(8,128)S(1)}, f32[256,128]{1,0:T(8,128)S(1)}) custom-call(s32[2]{0:T(128)S(1)} %pad_add_fusion.ids, f32[512,256]{1,0:T(8,128)S(1)} %get-tuple-element.29.loc, f32[512,256]{1,0:T(8,128)S(1)} %get-tuple-element.30.gat, bf16[512,512]{1,0:T(8,128)(2,1)S(1)} %get-tuple-element.31.nh, ...), custom_call_target="tpu_custom_call" | custom-call | flops 1000000000 | bytes 1048576 | tf_op jit(solution)/shard_map/pallas_call | solution.py:380
  87.7 0.0 collective-permute-start.5
  87.7 2.0 collective-permute-start.6
  89.8 0.4 collective-permute-start.7
  90.2 0.9 collective-permute-start.8
  91.0 1.0 collective-permute-start.9
  92.0 64.4 %all-gather.1 = f32[256,128]{1,0:T(8,128)S(1)} all-gather(f32[8,128]{1,0:T(8,128)S(1)} %get-tuple-element.48), channel_id=3, replica_groups=mesh['gx'=4,'gy'=2,'gz'=4] {'gx','gy','gz'}, dimensions={0}, use_global_device_ids=true | all-gather | bytes 135168 | tf_op jit(solution)/shard_map/all_gather | solution.py:415
  156.4 1.0 shard_map.134
  157.4 0.0 collective-permute-done.6.rest_1_
  157.5 3.5 %shard_map.135 = f32[8,128]{1,0:T(8,128)S(1)} custom-call(s32[2]{0:T(128)S(1)} %pad_add_fusion.ids, f32[512,256]{1,0:T(8,128)S(1)} %get-tuple-element.46.loc, f32[512,256]{1,0:T(8,128)S(1)} %get-tuple-element.47.gat, bf16[512,512]{1,0:T(8,128)(2,1)S(1)} %get-tuple-element.31.nh, bf16[512,512]{1,0:T(8,128)(2,1)S(1)} %get-tuple-element.32.nl, ...), custom_call_target="tpu_custom_call" | custom-call | flops 1000000000 | bytes 1048576 | tf_op jit(solution)/shard_map/pallas_call | solution.py:380
  160.9 66.6 %all-gather.2 = f32[256,128]{1,0:T(8,128)S(1)} all-gather(f32[8,128]{1,0:T(8,128)S(1)} %shard_map.135), channel_id=4, replica_groups=mesh['gx'=4,'gy'=2,'gz'=4] {'gx','gy','gz'}, dimensions={0}, use_global_device_ids=true | all-gather | bytes 135168 | tf_op jit(solution)/shard_map/all_gather | solution.py:415
  227.5 1.0 shard_map.136
  228.5 1.3 copy.17
  (23 shorter events, 0.0 us)
Async XLA Ops:
  0.6 76.9 %copy-start.2 = (f32[486,486]{1,0:T(8,128)S(1)}, f32[486,486]{1,0:T(8,128)}, u32[]{:S(2)}) copy-start(f32[486,486]{1,0:T(8,128)} %self_mob.1) | copy-start | bytes 2834356
  0.6 1.2 copy-start.1
  0.7 8.4 %copy-start.10 = (f32[1,1,3,256]{3,1,2,0:T(1,128)S(1)}, f32[1,1,3,256]{3,1,2,0:T(1,128)}, u32[]{:S(2)}) copy-start(f32[1,1,3,256]{3,1,2,0:T(1,128)} %param.13) | copy-start | bytes 9220
  1.8 0.7 copy-start
  1.8 75.7 %copy-start.4 = (f32[2,192,192]{2,1,0:T(8,128)S(1)}, f32[2,192,192]{2,1,0:T(8,128)}, u32[]{:S(2)}) copy-start(f32[2,192,192]{2,1,0:T(8,128)} %interp.1) | copy-start | bytes 884740
  2.5 75.0 %copy-start.6 = (f32[192,192]{1,0:T(8,128)S(1)}, f32[192,192]{1,0:T(8,128)}, u32[]{:S(2)}) copy-start(f32[192,192]{1,0:T(8,128)} %root.1) | copy-start | bytes 442372
  2.8 81.8 %collective-permute-start = (f32[256,128]{1,0:T(8,128)S(1)}, f32[256,128]{1,0:T(8,128)S(1)}, u32[]{:S(2)}, u32[]{:S(2)}) collective-permute-start(f32[256,128]{1,0:T(8,128)S(1)} %get-tuple-element.39), channel_id=1, source_target_pairs={{28,0},{24,4},{4,8},{0,12},{12,16},{8,20},{20,24},{16,28},{29,1},{... | collective-permute-start | bytes 393224 | tf_op jit(solution)/shard_map/ppermute | solution.py:411
  5.2 79.4 %collective-permute-start.1 = (f32[256,128]{1,0:T(8,128)S(1)}, f32[256,128]{1,0:T(8,128)S(1)}, u32[]{:S(2)}, u32[]{:S(2)}) collective-permute-start(f32[256,128]{1,0:T(8,128)S(1)} %get-tuple-element.39), channel_id=1, source_target_pairs={{24,0},{28,4},{0,8},{4,12},{8,16},{12,20},{16,24},{20,28},{25,1},{... | collective-permute-start | bytes 393224 | tf_op jit(solution)/shard_map/ppermute | solution.py:411
  6.8 77.8 %collective-permute-start.2 = (f32[256,128]{1,0:T(8,128)S(1)}, f32[256,128]{1,0:T(8,128)S(1)}, u32[]{:S(2)}, u32[]{:S(2)}) collective-permute-start(f32[256,128]{1,0:T(8,128)S(1)} %get-tuple-element.39), channel_id=1, source_target_pairs={{4,0},{0,4},{12,8},{8,12},{20,16},{16,20},{28,24},{24,28},{5,1},{1... | collective-permute-start | bytes 393224 | tf_op jit(solution)/shard_map/ppermute | solution.py:411
  7.4 77.3 %collective-permute-start.3 = (f32[256,128]{1,0:T(8,128)S(1)}, f32[256,128]{1,0:T(8,128)S(1)}, u32[]{:S(2)}, u32[]{:S(2)}) collective-permute-start(f32[256,128]{1,0:T(8,128)S(1)} %get-tuple-element.39), channel_id=1, source_target_pairs={{12,0},{8,4},{20,8},{16,12},{28,16},{24,20},{4,24},{0,28},{13,1},{... | collective-permute-start | bytes 393224 | tf_op jit(solution)/shard_map/ppermute | solution.py:411
  8.1 76.5 %collective-permute-start.4 = (f32[256,128]{1,0:T(8,128)S(1)}, f32[256,128]{1,0:T(8,128)S(1)}, u32[]{:S(2)}, u32[]{:S(2)}) collective-permute-start(f32[256,128]{1,0:T(8,128)S(1)} %get-tuple-element.39), channel_id=1, source_target_pairs={{8,0},{12,4},{16,8},{20,12},{24,16},{28,20},{0,24},{4,28},{9,1},{1... | collective-permute-start | bytes 393224 | tf_op jit(solution)/shard_map/ppermute | solution.py:411
  9.2 68.4 %copy-start.7 = (f32[1,1,8,256]{3,2,1,0:T(8,128)S(1)}, f32[1,1,8,256]{3,2,1,0:T(8,128)}, u32[]{:S(2)}) copy-start(f32[1,1,8,256]{3,2,1,0:T(8,128)} %near_weight.1) | copy-start | bytes 24580
  9.2 68.4 %copy-start.8 = (s32[1,1,8,256]{3,2,1,0:T(8,128)S(1)}, s32[1,1,8,256]{3,2,1,0:T(8,128)}, u32[]{:S(2)}) copy-start(s32[1,1,8,256]{3,2,1,0:T(8,128)} %neighbours.1) | copy-start | bytes 24580
  9.2 68.4 %copy-start.9 = (s32[2,384]{1,0:T(2,128)S(1)}, s32[2,384]{1,0:T(2,128)}, u32[]{:S(2)}) copy-start(s32[2,384]{1,0:T(2,128)} %perm.1) | copy-start | bytes 9220
  77.5 1.2 copy-start.3
  78.8 1.0 copy-start.5
  87.7 69.7 %collective-permute-start.5 = (f32[256,128]{1,0:T(8,128)S(1)}, f32[256,128]{1,0:T(8,128)S(1)}, u32[]{:S(2)}, u32[]{:S(2)}) collective-permute-start(f32[256,128]{1,0:T(8,128)S(1)} %get-tuple-element.51), channel_id=1, source_target_pairs={{28,0},{24,4},{4,8},{0,12},{12,16},{8,20},{20,24},{16,28},{29,1},{... | collective-permute-start | bytes 393224 | tf_op jit(solution)/shard_map/ppermute | solution.py:411
  87.7 69.7 %collective-permute-start.6 = (f32[256,128]{1,0:T(8,128)S(1)}, f32[256,128]{1,0:T(8,128)S(1)}, u32[]{:S(2)}, u32[]{:S(2)}) collective-permute-start(f32[256,128]{1,0:T(8,128)S(1)} %get-tuple-element.51), channel_id=1, source_target_pairs={{24,0},{28,4},{0,8},{4,12},{8,16},{12,20},{16,24},{20,28},{25,1},{... | collective-permute-start | bytes 393224 | tf_op jit(solution)/shard_map/ppermute | solution.py:411
  89.8 67.7 %collective-permute-start.7 = (f32[256,128]{1,0:T(8,128)S(1)}, f32[256,128]{1,0:T(8,128)S(1)}, u32[]{:S(2)}, u32[]{:S(2)}) collective-permute-start(f32[256,128]{1,0:T(8,128)S(1)} %get-tuple-element.51), channel_id=1, source_target_pairs={{4,0},{0,4},{12,8},{8,12},{20,16},{16,20},{28,24},{24,28},{5,1},{1... | collective-permute-start | bytes 393224 | tf_op jit(solution)/shard_map/ppermute | solution.py:411
  90.2 67.3 %collective-permute-start.8 = (f32[256,128]{1,0:T(8,128)S(1)}, f32[256,128]{1,0:T(8,128)S(1)}, u32[]{:S(2)}, u32[]{:S(2)}) collective-permute-start(f32[256,128]{1,0:T(8,128)S(1)} %get-tuple-element.51), channel_id=1, source_target_pairs={{12,0},{8,4},{20,8},{16,12},{28,16},{24,20},{4,24},{0,28},{13,1},{... | collective-permute-start | bytes 393224 | tf_op jit(solution)/shard_map/ppermute | solution.py:411
  91.0 66.4 %collective-permute-start.9 = (f32[256,128]{1,0:T(8,128)S(1)}, f32[256,128]{1,0:T(8,128)S(1)}, u32[]{:S(2)}, u32[]{:S(2)}) collective-permute-start(f32[256,128]{1,0:T(8,128)S(1)} %get-tuple-element.51), channel_id=1, source_target_pairs={{8,0},{12,4},{16,8},{20,12},{24,16},{28,20},{0,24},{4,28},{9,1},{1... | collective-permute-start | bytes 393224 | tf_op jit(solution)/shard_map/ppermute | solution.py:411

commit v2 on v1

--- a/solution.py
+++ b/solution.py
@@ -412,7 +412,8 @@
         return out
 
     def everywhere(x):
-        return lax.all_gather(x, ("gx", "gy", "gz"), axis=0, tiled=False)
+        copies = jnp.broadcast_to(x[None], (s.devices,) + x.shape)
+        return lax.all_to_all(copies, ("gx", "gy", "gz"), 0, 0)
 
     charges, packed, col, f = call(
         functools.partial(start_kernel, s),

time: 230 us -> 100 us (0.43)
  blocking collectives: 199 us -> 12.2 us
  local copies, waits for them, and re-layouts: 5.33 us -> 47.8 us
  starting transfers between devices: 10.5 us -> 22.3 us
    all_gather x3 -> x0, blocking collectives: 199 us -> none  [everywhere(): return lax.all_gather(x, ('gx', 'gy', 'gz'), axis=0, tiled=False)]
    unnamed x25 -> x113, local copies, waits for them, and re-layouts: 5.33 us -> 46.5 us
    all_to_all x0 -> x1, blocking collectives: none -> 12.2 us  [everywhere(): return lax.all_to_all(copies, ('gx', 'gy', 'gz'), 0, 0)]
    all_to_all x0 -> x2, starting transfers between devices: none -> 12.2 us  [everywhere(): return lax.all_to_all(copies, ('gx', 'gy', 'gz'), 0, 0)]
  transfers between devices with their start and end apart: 10 -> 12, of which waited for: 0 -> 0; matrix products, arithmetic and copies ran while one was open for 0% -> 0% of each run, Pallas kernels for 3% -> 6%
where the time goes in v2:
time: 100 us; the launch traced here: 98.6 us
  local copies, waits for them, and re-layouts  47.8 us (48%)
  starting transfers between devices  22.3 us (22%)
  Pallas kernels  15.3 us (15%)
  blocking collectives  12.2 us (12%)
    unnamed x113, local copies, waits for them, and re-layouts  46.5 us
    pallas_call x6, Pallas kernels, call(): pl.pallas_call(kernel, out_shape=[jax.ShapeDtypeStruct(shape, kind) for s...  15.3 us
    all_to_all x1, blocking collectives, everywhere(): return lax.all_to_all(copies, ('gx', 'gy', 'gz'), 0, 0)  12.2 us
    all_to_all x2, starting transfers between devices, everywhere(): return lax.all_to_all(copies, ('gx', 'gy', 'gz'), 0, 0)  12.2 us
    ppermute x10, starting transfers between devices, fetch_rims(): out.append(lax.ppermute(packed, ('gx', 'gy'), pairs))  10.1 us
  transfers between devices with their start and end apart: 12, of which 0 were waited for; matrix products, arithmetic and copies ran while one was open for 0% of the time, Pallas kernels for 6%

profile of v2, /device:TPU:0, one launch (start us, length us, event | category | flops | bytes accessed | tf_op | source)
XLA Modules:
  0.0 98.6 jit_solution(18019941057259207732)
XLA Ops:
  0.6 1.1 %copy.14.rhs = f32[1,1,3,162,256]{4,3,2,1,0:T(8,128)S(1)} copy(f32[1,1,3,162,256]{4,1,3,2,0:T(1,128)} %param.12) | data formatting | bytes 995328 | tf_op args[0]
  5.4 7.4 %all-to-all-start = ((f32[32,8,128]{2,1,0:T(8,128)}), f32[32,8,128]{2,1,0:T(8,128)}, u32[]{:S(2)}, u32[]{:S(2)}) async-start(f32[32,8,128]{2,1,0:T(8,128)} %broadcast_in_dim.6), calls=%async_computation | async-start | bytes 262144 | tf_op jit(solution)/shard_map/all_to_all | solution.py:416
  12.8 1.5 %collective-permute-start = (f32[256,128]{1,0:T(8,128)}, f32[256,128]{1,0:T(8,128)}, u32[]{:S(2)}, u32[]{:S(2)}) collective-permute-start(f32[256,128]{1,0:T(8,128)} %get-tuple-element.39), channel_id=1, source_target_pairs={{28,0},{24,4},{4,8},{0,12},{12,16},{8,20},{20,24},{16,28},{29,1},{... | collective-permute-start | bytes 393224 | tf_op jit(solution)/shard_map/ppermute | solution.py:411
  14.3 1.3 %collective-permute-start.1 = (f32[256,128]{1,0:T(8,128)}, f32[256,128]{1,0:T(8,128)}, u32[]{:S(2)}, u32[]{:S(2)}) collective-permute-start(f32[256,128]{1,0:T(8,128)} %get-tuple-element.39), channel_id=1, source_target_pairs={{24,0},{28,4},{0,8},{4,12},{8,16},{12,20},{16,24},{20,28},{25,1},{... | collective-permute-start | bytes 393224 | tf_op jit(solution)/shard_map/ppermute | solution.py:411
  16.2 1.1 %collective-permute-start.3 = (f32[256,128]{1,0:T(8,128)}, f32[256,128]{1,0:T(8,128)}, u32[]{:S(2)}, u32[]{:S(2)}) collective-permute-start(f32[256,128]{1,0:T(8,128)} %get-tuple-element.39), channel_id=1, source_target_pairs={{12,0},{8,4},{20,8},{16,12},{28,16},{24,20},{4,24},{0,28},{13,1},{... | collective-permute-start | bytes 393224 | tf_op jit(solution)/shard_map/ppermute | solution.py:411
  18.6 1.0 %copy-done.4 = f32[512,256]{1,0:T(8,128)S(1)} copy-done((f32[512,256]{1,0:T(8,128)S(1)}, f32[512,256]{1,0:T(8,128)}, u32[]{:S(2)}) %copy-start.4) | copy-done | bytes 524312
  19.7 1.2 %copy-done.35 = f32[486,486]{1,0:T(8,128)S(1)} copy-done((f32[486,486]{1,0:T(8,128)S(1)}, f32[486,486]{1,0:T(8,128)}, u32[]{:S(2)}) %copy-start.35) | copy-done | bytes 944808
  20.9 1.2 %copy-done.36 = f32[486,486]{1,0:T(8,128)S(1)} copy-done((f32[486,486]{1,0:T(8,128)S(1)}, f32[486,486]{1,0:T(8,128)}, u32[]{:S(2)}) %copy-start.36) | copy-done | bytes 944808
  22.1 1.0 %copy-done.37 = f32[2,192,192]{2,1,0:T(8,128)S(1)} copy-done((f32[2,192,192]{2,1,0:T(8,128)S(1)}, f32[2,192,192]{2,1,0:T(8,128)}, u32[]{:S(2)}) %copy-start.37) | copy-done | bytes 294936
  23.1 1.0 %copy-done.38 = f32[2,192,192]{2,1,0:T(8,128)S(1)} copy-done((f32[2,192,192]{2,1,0:T(8,128)S(1)}, f32[2,192,192]{2,1,0:T(8,128)}, u32[]{:S(2)}) %copy-start.38) | copy-done | bytes 294936
  25.7 4.8 %shard_map.132 = (f32[512,256]{1,0:T(8,128)S(1)}, f32[512,256]{1,0:T(8,128)S(1)}, f32[16,256]{1,0:T(8,128)S(1)}, bf16[512,512]{1,0:T(8,128)(2,1)S(1)}, bf16[512,...) custom-call(s32[2]{0:T(128)S(1)} %pad_add_fusion.ids, ...), custom_call_target="tpu_custom_call" | custom-call | flops 1000000000 | bytes 1048576 | tf_op jit(solution)/shard_map/pallas_call | solution.py:380
  36.5 1.0 %copy-done.1 = bf16[512,512]{1,0:T(8,128)(2,1)S(1)} copy-done((bf16[512,512]{1,0:T(8,128)(2,1)S(1)}, bf16[512,512]{1,0:T(8,128)(2,1)}, u32[]{:S(2)}) %copy-start.1) | copy-done | bytes 524312
  37.5 1.0 %copy-done.17 = f32[512,256]{1,0:T(8,128)S(1)} copy-done((f32[512,256]{1,0:T(8,128)S(1)}, f32[512,256]{1,0:T(8,128)}, u32[]{:S(2)}) %copy-start.17) | copy-done | bytes 524312
  38.5 1.0 %copy-done.19 = f32[512,256]{1,0:T(8,128)S(1)} copy-done((f32[512,256]{1,0:T(8,128)S(1)}, f32[512,256]{1,0:T(8,128)}, u32[]{:S(2)}) %copy-start.19) | copy-done | bytes 524312
  40.5 3.8 %shard_map.133 = (f32[512,256]{1,0:T(8,128)S(1)}, f32[8,128]{1,0:T(8,128)S(1)}, f32[256,128]{1,0:T(8,128)S(1)}) custom-call(s32[2]{0:T(128)S(1)} %pad_add_fusion.ids, f32[512,256]{1,0:T(8,128)S(1)} %copy-done.17, f32[512,256]{1,0:T(8,128)S(1)} %copy-done.19, bf16[512,512]{1,0:T(8,128)(2,1)S(1)} %get-tuple-element.31.nh, bf16[512,512]{1,0:T(8,128)(2,1)S(1)} %copy-done.1, ...), custom_call_target="tpu_custom_call" | custom-call | flops 1000000000 | bytes 1048576 | tf_op jit(solution)/shard_map/pallas_call | solution.py:380
  46.4 4.8 %all-to-all-start.1 = ((f32[32,8,128]{2,1,0:T(8,128)}), f32[32,8,128]{2,1,0:T(8,128)}, u32[]{:S(2)}, u32[]{:S(2)}) async-start(f32[32,8,128]{2,1,0:T(8,128)} %broadcast_in_dim.7), calls=%async_computation.1 | async-start | bytes 262144 | tf_op jit(solution)/shard_map/all_to_all | solution.py:416
  51.1 1.5 %collective-permute-start.5 = (f32[256,128]{1,0:T(8,128)}, f32[256,128]{1,0:T(8,128)S(1)}, u32[]{:S(2)}, u32[]{:S(2)}) collective-permute-start(f32[256,128]{1,0:T(8,128)} %copy-done.40), channel_id=1, source_target_pairs={{28,0},{24,4},{4,8},{0,12},{12,16},{8,20},{20,24},{16,28},{29,1},{... | collective-permute-start | bytes 393224 | tf_op jit(solution)/shard_map/ppermute | solution.py:411
  52.6 1.3 %collective-permute-start.6 = (f32[256,128]{1,0:T(8,128)}, f32[256,128]{1,0:T(8,128)S(1)}, u32[]{:S(2)}, u32[]{:S(2)}) collective-permute-start(f32[256,128]{1,0:T(8,128)} %copy-done.40), channel_id=1, source_target_pairs={{24,0},{28,4},{0,8},{4,12},{8,16},{12,20},{16,24},{20,28},{25,1},{... | collective-permute-start | bytes 393224 | tf_op jit(solution)/shard_map/ppermute | solution.py:411
  54.5 1.1 %collective-permute-start.8 = (f32[256,128]{1,0:T(8,128)}, f32[256,128]{1,0:T(8,128)S(1)}, u32[]{:S(2)}, u32[]{:S(2)}) collective-permute-start(f32[256,128]{1,0:T(8,128)} %copy-done.40), channel_id=1, source_target_pairs={{12,0},{8,4},{20,8},{16,12},{28,16},{24,20},{4,24},{0,28},{13,1},{... | collective-permute-start | bytes 393224 | tf_op jit(solution)/shard_map/ppermute | solution.py:411
  56.2 1.0 %copy-done.5 = f32[512,256]{1,0:T(8,128)S(1)} copy-done((f32[512,256]{1,0:T(8,128)S(1)}, f32[512,256]{1,0:T(8,128)}, u32[]{:S(2)}) %copy-start.5) | copy-done | bytes 524312
  57.2 1.0 %copy-done.14 = f32[512,256]{1,0:T(8,128)S(1)} copy-done((f32[512,256]{1,0:T(8,128)S(1)}, f32[512,256]{1,0:T(8,128)}, u32[]{:S(2)}) %copy-start.14) | copy-done | bytes 524312
  58.3 1.0 %copy-done.45 = bf16[512,512]{1,0:T(8,128)(2,1)S(1)} copy-done((bf16[512,512]{1,0:T(8,128)(2,1)S(1)}, bf16[512,512]{1,0:T(8,128)(2,1)}, u32[]{:S(2)}) %copy-start.45) | copy-done | bytes 524312
  59.3 1.0 %copy-done.47 = bf16[512,512]{1,0:T(8,128)(2,1)S(1)} copy-done((bf16[512,512]{1,0:T(8,128)(2,1)S(1)}, bf16[512,512]{1,0:T(8,128)(2,1)}, u32[]{:S(2)}) %copy-start.47) | copy-done | bytes 524312
  69.5 1.0 %copy-done.2 = bf16[512,512]{1,0:T(8,128)(2,1)S(1)} copy-done((bf16[512,512]{1,0:T(8,128)(2,1)S(1)}, bf16[512,512]{1,0:T(8,128)(2,1)}, u32[]{:S(2)}) %copy-start.2) | copy-done | bytes 524312
  70.6 1.0 %copy-done.6 = f32[512,256]{1,0:T(8,128)S(1)} copy-done((f32[512,256]{1,0:T(8,128)S(1)}, f32[512,256]{1,0:T(8,128)}, u32[]{:S(2)}) %copy-start.6) | copy-done | bytes 524312
  71.6 1.0 %copy-done.8 = f32[512,256]{1,0:T(8,128)S(1)} copy-done((f32[512,256]{1,0:T(8,128)S(1)}, f32[512,256]{1,0:T(8,128)}, u32[]{:S(2)}) %copy-start.8) | copy-done | bytes 524312
  72.7 1.0 %copy-done.10 = f32[512,256]{1,0:T(8,128)S(1)} copy-done((f32[512,256]{1,0:T(8,128)S(1)}, f32[512,256]{1,0:T(8,128)}, u32[]{:S(2)}) %copy-start.10) | copy-done | bytes 524312
  73.7 1.0 %copy-done.12 = f32[512,256]{1,0:T(8,128)S(1)} copy-done((f32[512,256]{1,0:T(8,128)S(1)}, f32[512,256]{1,0:T(8,128)}, u32[]{:S(2)}) %copy-start.12) | copy-done | bytes 524312
  80.2 3.9 %shard_map.135 = f32[8,128]{1,0:T(8,128)S(1)} custom-call(s32[2]{0:T(128)S(1)} %pad_add_fusion.ids, f32[512,256]{1,0:T(8,128)S(1)} %copy-done.8, f32[512,256]{1,0:T(8,128)S(1)} %copy-done.10, bf16[512,512]{1,0:T(8,128)(2,1)S(1)} %get-tuple-element.31.nh, bf16[512,512]{1,0:T(8,128)(2,1)S(1)} %copy-done.2, bf16[384,256]{1,0:T(8,128)(2,1)S(1)} %get-tuple-element.33.gh, ...), custom_call_target="tpu_custom_call" | custom-call | flops 1000000000 | bytes 1048576 | tf_op jit(solution)/shard_map/pallas_call | solution.py:380
  84.1 12.2 %all_to_all.15.stats = f32[32,8,128]{2,1,0:T(8,128)S(1)} all-to-all(f32[32,8,128]{2,1,0:T(8,128)S(1)} %broadcast_in_dim.8), channel_id=1, replica_groups=mesh['gx'=4,'gy'=2,'gz'=4] {'gx','gy','gz'}, dimensions={0} | all-to-all | bytes 262144 | tf_op jit(solution)/shard_map/all_to_all | solution.py:416
  96.3 1.0 %shard_map.136 = (f32[1,1,3,162,256]{4,3,2,1,0:T(8,128)S(1)}, f32[1,1]{1,0:T(1,128)}) custom-call(f32[32,8,128]{2,1,0:T(8,128)S(1)} %all_to_all.15.stats, f32[1,1,3,162,256]{4,3,2,1,0:T(8,128)S(1)} %copy.14.rhs, f32[512,256]{1,0:T(8,128)S(1)} %copy-done.15), custom_call_target="tpu_custom_call" | custom-call | flops 10000000 | bytes 1048576 | tf_op jit(solution)/shard_map/pallas_call | solution.py:380
  97.3 1.3 %copy.17 = f32[1,1,3,162,256]{4,1,3,2,0:T(1,128)} copy(f32[1,1,3,162,256]{4,3,2,1,0:T(8,128)S(1)} %get-tuple-element.54) | data formatting | bytes 995328
  (116 shorter events, 31.9 us)
Async XLA Ops:
  0.6 1.1 %copy-start.34 = (f32[162]{0:T(256)S(1)}, f32[162]{0:T(256)}, u32[]{:S(2)}) copy-start(f32[162]{0:T(256)} %param.19) | copy-start | bytes 1948
  5.4 12.6 %copy-start.54 = (f32[1,1,3,256]{3,1,2,0:T(1,128)S(1)}, f32[1,1,3,256]{3,1,2,0:T(1,128)}, u32[]{:S(2)}) copy-start(f32[1,1,3,256]{3,1,2,0:T(1,128)} %param.13) | copy-start | bytes 9220
  5.4 31.1 %all-to-all-start = ((f32[32,8,128]{2,1,0:T(8,128)}), f32[32,8,128]{2,1,0:T(8,128)}, u32[]{:S(2)}, u32[]{:S(2)}) async-start(f32[32,8,128]{2,1,0:T(8,128)} %broadcast_in_dim.6), calls=%async_computation | async-start | bytes 262144 | tf_op jit(solution)/shard_map/all_to_all | solution.py:416
  12.8 23.6 %collective-permute-start = (f32[256,128]{1,0:T(8,128)}, f32[256,128]{1,0:T(8,128)}, u32[]{:S(2)}, u32[]{:S(2)}) collective-permute-start(f32[256,128]{1,0:T(8,128)} %get-tuple-element.39), channel_id=1, source_target_pairs={{28,0},{24,4},{4,8},{0,12},{12,16},{8,20},{20,24},{16,28},{29,1},{... | collective-permute-start | bytes 393224 | tf_op jit(solution)/shard_map/ppermute | solution.py:411
  14.3 22.1 %collective-permute-start.1 = (f32[256,128]{1,0:T(8,128)}, f32[256,128]{1,0:T(8,128)}, u32[]{:S(2)}, u32[]{:S(2)}) collective-permute-start(f32[256,128]{1,0:T(8,128)} %get-tuple-element.39), channel_id=1, source_target_pairs={{24,0},{28,4},{0,8},{4,12},{8,16},{12,20},{16,24},{20,28},{25,1},{... | collective-permute-start | bytes 393224 | tf_op jit(solution)/shard_map/ppermute | solution.py:411
  15.6 20.8 %collective-permute-start.2 = (f32[256,128]{1,0:T(8,128)}, f32[256,128]{1,0:T(8,128)}, u32[]{:S(2)}, u32[]{:S(2)}) collective-permute-start(f32[256,128]{1,0:T(8,128)} %get-tuple-element.39), channel_id=1, source_target_pairs={{4,0},{0,4},{12,8},{8,12},{20,16},{16,20},{28,24},{24,28},{5,1},{1... | collective-permute-start | bytes 393224 | tf_op jit(solution)/shard_map/ppermute | solution.py:411
  16.2 20.3 %collective-permute-start.3 = (f32[256,128]{1,0:T(8,128)}, f32[256,128]{1,0:T(8,128)}, u32[]{:S(2)}, u32[]{:S(2)}) collective-permute-start(f32[256,128]{1,0:T(8,128)} %get-tuple-element.39), channel_id=1, source_target_pairs={{12,0},{8,4},{20,8},{16,12},{28,16},{24,20},{4,24},{0,28},{13,1},{... | collective-permute-start | bytes 393224 | tf_op jit(solution)/shard_map/ppermute | solution.py:411
  17.3 19.2 %collective-permute-start.4 = (f32[256,128]{1,0:T(8,128)}, f32[256,128]{1,0:T(8,128)}, u32[]{:S(2)}, u32[]{:S(2)}) collective-permute-start(f32[256,128]{1,0:T(8,128)} %get-tuple-element.39), channel_id=1, source_target_pairs={{8,0},{12,4},{16,8},{20,12},{24,16},{28,20},{0,24},{4,28},{9,1},{1... | collective-permute-start | bytes 393224 | tf_op jit(solution)/shard_map/ppermute | solution.py:411
  18.6 1.0 %copy-start.4 = (f32[512,256]{1,0:T(8,128)S(1)}, f32[512,256]{1,0:T(8,128)}, u32[]{:S(2)}) copy-start(f32[512,256]{1,0:T(8,128)} %copy-done.3) | copy-start | bytes 1572868
  19.7 1.2 %copy-start.35 = (f32[486,486]{1,0:T(8,128)S(1)}, f32[486,486]{1,0:T(8,128)}, u32[]{:S(2)}) copy-start(f32[486,486]{1,0:T(8,128)} %self_mob.1) | copy-start | bytes 2834356
  20.9 1.2 %copy-start.36 = (f32[486,486]{1,0:T(8,128)S(1)}, f32[486,486]{1,0:T(8,128)}, u32[]{:S(2)}) copy-start(f32[486,486]{1,0:T(8,128)} %near_mat.1) | copy-start | bytes 2834356
  22.1 1.0 %copy-start.37 = (f32[2,192,192]{2,1,0:T(8,128)S(1)}, f32[2,192,192]{2,1,0:T(8,128)}, u32[]{:S(2)}) copy-start(f32[2,192,192]{2,1,0:T(8,128)} %interp.1) | copy-start | bytes 884740
  23.1 1.0 %copy-start.38 = (f32[2,192,192]{2,1,0:T(8,128)S(1)}, f32[2,192,192]{2,1,0:T(8,128)}, u32[]{:S(2)}) copy-start(f32[2,192,192]{2,1,0:T(8,128)} %sibling.1) | copy-start | bytes 884740
  36.5 1.0 %copy-start.1 = (bf16[512,512]{1,0:T(8,128)(2,1)S(1)}, bf16[512,512]{1,0:T(8,128)(2,1)}, u32[]{:S(2)}) copy-start(bf16[512,512]{1,0:T(8,128)(2,1)} %copy-done) | copy-start | bytes 1572868
  37.5 1.0 %copy-start.17 = (f32[512,256]{1,0:T(8,128)S(1)}, f32[512,256]{1,0:T(8,128)}, u32[]{:S(2)}) copy-start(f32[512,256]{1,0:T(8,128)} %copy-done.16) | copy-start | bytes 1572868
  38.5 1.0 %copy-start.19 = (f32[512,256]{1,0:T(8,128)S(1)}, f32[512,256]{1,0:T(8,128)}, u32[]{:S(2)}) copy-start(f32[512,256]{1,0:T(8,128)} %copy-done.18) | copy-start | bytes 1572868
  46.4 23.2 %all-to-all-start.1 = ((f32[32,8,128]{2,1,0:T(8,128)}), f32[32,8,128]{2,1,0:T(8,128)}, u32[]{:S(2)}, u32[]{:S(2)}) async-start(f32[32,8,128]{2,1,0:T(8,128)} %broadcast_in_dim.7), calls=%async_computation.1 | async-start | bytes 262144 | tf_op jit(solution)/shard_map/all_to_all | solution.py:416
  51.1 15.1 %collective-permute-start.5 = (f32[256,128]{1,0:T(8,128)}, f32[256,128]{1,0:T(8,128)S(1)}, u32[]{:S(2)}, u32[]{:S(2)}) collective-permute-start(f32[256,128]{1,0:T(8,128)} %copy-done.40), channel_id=1, source_target_pairs={{28,0},{24,4},{4,8},{0,12},{12,16},{8,20},{20,24},{16,28},{29,1},{... | collective-permute-start | bytes 393224 | tf_op jit(solution)/shard_map/ppermute | solution.py:411
  52.6 14.3 %collective-permute-start.6 = (f32[256,128]{1,0:T(8,128)}, f32[256,128]{1,0:T(8,128)S(1)}, u32[]{:S(2)}, u32[]{:S(2)}) collective-permute-start(f32[256,128]{1,0:T(8,128)} %copy-done.40), channel_id=1, source_target_pairs={{24,0},{28,4},{0,8},{4,12},{8,16},{12,20},{16,24},{20,28},{25,1},{... | collective-permute-start | bytes 393224 | tf_op jit(solution)/shard_map/ppermute | solution.py:411
  53.9 13.7 %collective-permute-start.7 = (f32[256,128]{1,0:T(8,128)}, f32[256,128]{1,0:T(8,128)S(1)}, u32[]{:S(2)}, u32[]{:S(2)}) collective-permute-start(f32[256,128]{1,0:T(8,128)} %copy-done.40), channel_id=1, source_target_pairs={{4,0},{0,4},{12,8},{8,12},{20,16},{16,20},{28,24},{24,28},{5,1},{1... | collective-permute-start | bytes 393224 | tf_op jit(solution)/shard_map/ppermute | solution.py:411
  54.5 13.8 %collective-permute-start.8 = (f32[256,128]{1,0:T(8,128)}, f32[256,128]{1,0:T(8,128)S(1)}, u32[]{:S(2)}, u32[]{:S(2)}) collective-permute-start(f32[256,128]{1,0:T(8,128)} %copy-done.40), channel_id=1, source_target_pairs={{12,0},{8,4},{20,8},{16,12},{28,16},{24,20},{4,24},{0,28},{13,1},{... | collective-permute-start | bytes 393224 | tf_op jit(solution)/shard_map/ppermute | solution.py:411
  55.6 13.3 %collective-permute-start.9 = (f32[256,128]{1,0:T(8,128)}, f32[256,128]{1,0:T(8,128)S(1)}, u32[]{:S(2)}, u32[]{:S(2)}) collective-permute-start(f32[256,128]{1,0:T(8,128)} %copy-done.40), channel_id=1, source_target_pairs={{8,0},{12,4},{16,8},{20,12},{24,16},{28,20},{0,24},{4,28},{9,1},{1... | collective-permute-start | bytes 393224 | tf_op jit(solution)/shard_map/ppermute | solution.py:411
  56.2 1.0 %copy-start.5 = (f32[512,256]{1,0:T(8,128)S(1)}, f32[512,256]{1,0:T(8,128)}, u32[]{:S(2)}) copy-start(f32[512,256]{1,0:T(8,128)} %copy-done.3) | copy-start | bytes 1572868
  57.2 1.0 %copy-start.14 = (f32[512,256]{1,0:T(8,128)S(1)}, f32[512,256]{1,0:T(8,128)}, u32[]{:S(2)}) copy-start(f32[512,256]{1,0:T(8,128)} %copy-done.13) | copy-start | bytes 1572868
  58.3 1.0 %copy-start.45 = (bf16[512,512]{1,0:T(8,128)(2,1)S(1)}, bf16[512,512]{1,0:T(8,128)(2,1)}, u32[]{:S(2)}) copy-start(bf16[512,512]{1,0:T(8,128)(2,1)} %copy-done.44) | copy-start | bytes 1572868
  59.3 1.0 %copy-start.47 = (bf16[512,512]{1,0:T(8,128)(2,1)S(1)}, bf16[512,512]{1,0:T(8,128)(2,1)}, u32[]{:S(2)}) copy-start(bf16[512,512]{1,0:T(8,128)(2,1)} %copy-done.46) | copy-start | bytes 1572868
  69.5 1.0 %copy-start.2 = (bf16[512,512]{1,0:T(8,128)(2,1)S(1)}, bf16[512,512]{1,0:T(8,128)(2,1)}, u32[]{:S(2)}) copy-start(bf16[512,512]{1,0:T(8,128)(2,1)} %copy-done) | copy-start | bytes 1572868
  70.6 1.0 %copy-start.6 = (f32[512,256]{1,0:T(8,128)S(1)}, f32[512,256]{1,0:T(8,128)}, u32[]{:S(2)}) copy-start(f32[512,256]{1,0:T(8,128)} %copy-done.3) | copy-start | bytes 1572868
  71.6 1.0 %copy-start.8 = (f32[512,256]{1,0:T(8,128)S(1)}, f32[512,256]{1,0:T(8,128)}, u32[]{:S(2)}) copy-start(f32[512,256]{1,0:T(8,128)} %copy-done.7) | copy-start | bytes 1572868
  72.7 1.0 %copy-start.10 = (f32[512,256]{1,0:T(8,128)S(1)}, f32[512,256]{1,0:T(8,128)}, u32[]{:S(2)}) copy-start(f32[512,256]{1,0:T(8,128)} %copy-done.9) | copy-start | bytes 1572868
  73.7 1.0 %copy-start.12 = (f32[512,256]{1,0:T(8,128)S(1)}, f32[512,256]{1,0:T(8,128)}, u32[]{:S(2)}) copy-start(f32[512,256]{1,0:T(8,128)} %copy-done.11) | copy-start | bytes 1572868
  80.2 16.1 %copy-start.15 = (f32[512,256]{1,0:T(8,128)S(1)}, f32[512,256]{1,0:T(8,128)}, u32[]{:S(2)}) copy-start(f32[512,256]{1,0:T(8,128)} %copy-done.13) | copy-start | bytes 1572868
  (35 other events, 27.0 us)

commit v3 on v1

--- a/solution.py
+++ b/solution.py
@@ -50,18 +50,27 @@
         self.half = self.rows // 2
         self.levels = skel_perm.shape[0]
         self.skel = skel_perm.shape[1] // 2
-        self.own_slots = []
-        self.sources = []
-        self.slot_base = []
-        for slot in range(9):
-            offset = ((slot // 3 - 1) % self.nx, (slot % 3 - 1) % self.ny)
-            if offset == (0, 0):
-                self.slot_base.append(0)
-                continue
-            if offset not in self.sources:
-                self.sources.append(offset)
-            self.slot_base.append(self.bodies + RIM * self.sources.index(offset))
-        self.ghosts = round_up(max(1, len(self.sources)) * RIM, LANES)
+        shifts = sorted({(dy % self.ny) for dy in (-1, 1)} - {0})
+        self.shifts = shifts
+        self.sources = [("same", dy) for dy in shifts]
+        for kind in ("other", "partner"):
+            self.sources += [(kind, dy) for dy in [0] + shifts]
+        self.ghosts = round_up(len(self.sources) * RIM, LANES)
+        self.far_tiles = self.nz + -(-self.nz // 2)
+
+    def slot_start(self, slot, parity):
+        dx, dy = slot // 3 - 1, (slot % 3 - 1) % self.ny
+        kind = "same" if dx == 0 else "partner" if dx == 1 - 2 * parity else "other"
+        if (kind, dy) == ("same", 0):
+            return 0
+        return self.bodies + RIM * self.sources.index((kind, dy))
+
+    def beside(self, kind, x):
+        if kind == "same":
+            return x
+        if kind == "partner":
+            return x ^ 1
+        return (x + 2 * (x % 2) - 1) % self.nx
 
 
 def pieces(x, s):
@@ -134,7 +143,8 @@
     col_out[...] = col
     rim_out[...] = pack_rim(f, s)
     occ = occupancy(cells[0], s)
-    q_out[...] = pack_charges(pieces(f, s), col[:, :1], occ, s)
+    charges = pack_charges(pieces(f, s), col[:, :1], occ, s)
+    q_out[...] = jnp.broadcast_to(charges[None], q_out.shape)
 
 
 def frame_rows(angles):
@@ -167,14 +177,15 @@
         return [block]
     up = ups[level - 1]
     n = up.shape[0] // 2
-    both = product(mm, split(up), split(block))
-    return expand(both[:n], level - 1, ups) + expand(both[n:], level - 1, ups)
+    block = split(block)
+    low, high = (product(mt, block, split(half)) for half in (up[:n], up[n:]))
+    return expand(low, level - 1, ups) + expand(high, level - 1, ups)
 
 
 def setup_kernel(
     s, ids, f_in, angles, self_mob, near_mat, near_weight, neighbours, perm, interp, sibling, root,
     loc_out, gat_out, rot_out, sh_out, sl_out, nh_out, nl_out, oh_out, ol_out, gh_out, gl_out,
-    th_out, tl_out, padded, ups_ref,
+    far_out, padded, ups_ref,
 ):
     f = f_in[...]
     rot = jnp.concatenate(frame_rows(angles[0, 0]) + [jnp.zeros((7, s.bodies), f32)], axis=0)
@@ -194,7 +205,9 @@
     links = neighbours[0, 0]
     slot = links // s.bodies
     base = jnp.zeros_like(links)
-    for index, start in enumerate(s.slot_base):
+    odd = (ids[0] // s.ny) % 2
+    for index in range(9):
+        start = jnp.where(odd == 1, s.slot_start(index, 1), s.slot_start(index, 0))
         base = jnp.where(slot == index, start, base)
     column = base + links % s.bodies
     coef = near_weight[0, 0]
@@ -229,66 +242,100 @@
         ups.append(up)
         ups_ref[level] = up
 
-    def down(block, level):
+    def down(block, level, dot):
         bit = (z >> level) & 1
         half = ups_ref[level, pl.ds(pl.multiple_of(bit * n, 8), n), :]
-        return product(mt, split(block), split(half))
+        return product(dot, split(half), split(block))
 
     spread = root[...]
     beside = []
     for level in reversed(range(s.levels)):
-        spread = down(spread, level)
-        beside = [down(block, level) for block in beside]
-        beside.append(sibling[level])
+        last = level == s.levels - 1
+        spread = down(spread, level, mt if last else mm)
+        beside = [down(block, level, mt if fresh else mm) for block, fresh in beside]
+        beside = [(block, False) for block in beside] + [(sibling[level], True)]
     far_leaves = expand(spread, s.levels, ups)
     near_leaves = [jnp.zeros((n, n), f32) for _ in range(s.nz)]
-    for level, block in zip(reversed(range(s.levels)), beside):
-        sub = expand(block, level, ups)
+    for level, (block, fresh) in zip(reversed(range(s.levels)), beside):
+        sub = expand(block.T if fresh else block, level, ups)
         for leaf in range(s.nz):
             hit = (leaf >> level) == ((z >> level) ^ 1)
             near_leaves[leaf] = jnp.where(hit, near_leaves[leaf] + sub[leaf % (1 << level)], near_leaves[leaf])
-    pad = jnp.zeros((2 * LANES - n, n), f32)
+    tail = n - LANES
+    far_out[...] = jnp.zeros_like(far_out)
+    own = [a - b for a, b in zip(near_leaves, far_leaves)]
+    for group, blocks in enumerate((own, far_leaves)):
+        for leaf, block in enumerate(blocks):
+            at = (group * s.far_tiles + leaf) * LANES
+            far_out[:, at : at + LANES] = block[:, :LANES]
+            at = (group * s.far_tiles + s.nz + leaf // 2) * LANES + leaf % 2 * RIM
+            far_out[:, at : at + tail] = block[:, LANES:]
+
+
+def merge_kernel(s, ids, tiles, out):
+    acc = tiles[0]
+    for c in range(1, s.nx * s.ny):
+        acc = acc + tiles[c]
+    own = tiles[ids[0]]
     for leaf in range(s.nz):
-        for group, block in ((0, near_leaves[leaf] - far_leaves[leaf]), (s.nz, far_leaves[leaf])):
-            hi, lo = split(jnp.concatenate([block, pad], axis=0))
-            at = (group + leaf) * 2 * LANES
-            th_out[at : at + 2 * LANES, :] = hi
-            tl_out[at : at + 2 * LANES, :] = lo
-
-
-def image(s, ids, loc, gat, rims, near, ghost, charges, far_op, cells, col):
-    column = ids[0]
-    chunks = []
-    for leaf in range(s.nz):
-        chunks.append(charges[column * s.nz + leaf])
-    for leaf in range(s.nz):
-        acc = charges[leaf]
-        for c in range(1, s.nx * s.ny):
-            acc = acc + charges[c * s.nz + leaf]
-        chunks.append(acc)
-    left = jnp.concatenate([x for tile in chunks for x in (tile, pltpu.roll(tile, 4, 0))], axis=1)
-    potential = product(mm, split(left), far_op)
-    occ = occupancy(cells[0], s)
-    p_hi, p_lo = split(potential)
-    p_mid, p_low = split(potential - p_hi.astype(f32))
-    stack = jnp.concatenate([p_hi.astype(f32), p_mid.astype(f32), p_low.astype(f32)], axis=0).astype(bf16)
-    values = mm(stack, occ)
-    values = values[0:8] + (values[8:16] + values[16:24])
-    far = stacked([col * values[c : c + 1] for c in range(3)], s)
+        out[leaf, 0] = own
+        out[leaf, 1] = acc
+
+
+def far_potential(s, charges, far_op):
+    rows = []
+    for group in range(2):
+        tiles = [charges[leaf, group] for leaf in range(s.nz)]
+        rows += tiles
+        for leaf in range(0, s.nz, 2):
+            pair = tiles[leaf]
+            if leaf + 1 < s.nz:
+                lane = lax.broadcasted_iota(jnp.int32, (8, LANES), 1)
+                pair = jnp.where(lane < RIM, pair, pltpu.roll(tiles[leaf + 1], RIM, 1))
+            rows.append(pltpu.roll(pair, 4, 0))
+    columns = [[], [], []]
+    for r in range(0, s.skel, 64):
+        acc = [None] * 3
+        for index, row in enumerate(rows):
+            block = far_op[r : r + 64, index * LANES : (index + 1) * LANES]
+            for c in range(3):
+                term = block * row[c : c + 1]
+                acc[c] = term if acc[c] is None else acc[c] + term
+        for c in range(3):
+            columns[c].append(jnp.sum(acc[c], axis=1, keepdims=True))
+    return columns
+
+
+def far_values(s, charges, far_op, cells):
+    columns = far_potential(s, charges, far_op)
+    out = []
+    for c in range(3):
+        acc = jnp.zeros((1, s.bodies), f32)
+        for index, r in enumerate(range(0, s.skel, 64)):
+            row = lax.broadcasted_iota(jnp.int32, (64, s.bodies), 0) + r
+            acc = acc + jnp.sum(jnp.where(cells == row, columns[c][index], 0.0), axis=0, keepdims=True)
+        out.append(acc)
+    return out
+
+
+def image(s, loc, gat, rims, near, ghost, charges, far_op, cells, col):
+    values = far_values(s, charges, far_op, cells[0])
+    far = stacked([col * value for value in values], s)
     gathered = gat + product(mm, split(unpack_rims(rims, s)), ghost)
     return (loc + far) + product(mm, near, split(gathered))
 
 
-def first_kernel(s, n_rims, ids, loc, gat, nh, nl, gh, gl, charges, th, tl, cells, col, *rest):
+def first_kernel(s, n_rims, loc, gat, nh, nl, gh, gl, charges, far_op, cells, col, *rest):
     rims, (u_out, q_out, rim_out) = rest[:n_rims], rest[n_rims:]
     weight_col = col[:, :1]
     u = image(
-        s, ids, loc[...], gat[...], [r[...] for r in rims], (nh[...], nl[...]), (gh[...], gl[...]),
-        charges, (th[...], tl[...]), cells, weight_col,
+        s, loc[...], gat[...], [r[...] for r in rims], (nh[...], nl[...]), (gh[...], gl[...]),
+        charges, far_op, cells, weight_col,
     )
     u_out[...] = u
     rim_out[...] = pack_rim(u, s)
-    q_out[...] = pack_charges(pieces(u, s), weight_col, occupancy(cells[0], s), s)
+    charges = pack_charges(pieces(u, s), weight_col, occupancy(cells[0], s), s)
+    q_out[...] = jnp.broadcast_to(charges[None], q_out.shape)
 
 
 def safe_inverse(x):
@@ -311,12 +358,12 @@
 
 
 def second_kernel(
-    s, n_rims, ids, loc, gat, nh, nl, gh, gl, charges, th, tl, cells, col, f_in, ortho_in, stat, *rest
+    s, n_rims, loc, gat, nh, nl, gh, gl, charges, far_op, cells, col, f_in, ortho_in, stat, *rest
 ):
     rims, (stat_out,) = rest[:n_rims], rest[n_rims:]
     t = image(
-        s, ids, loc[...], gat[...], [r[...] for r in rims], (nh[...], nl[...]), (gh[...], gl[...]),
-        charges, (th[...], tl[...]), cells, col[:, :1],
+        s, loc[...], gat[...], [r[...] for r in rims], (nh[...], nl[...]), (gh[...], gl[...]),
+        charges, far_op, cells, col[:, :1],
     )
     f, ortho = f_in[...], ortho_in[...]
     ff, fu, oo = (stat[i : i + 1, :1] for i in range(3))
@@ -325,21 +372,31 @@
     rest_t = t - ft * f - ot * ortho
     tt = total(rest_t * rest_t)
     rf, ro = jnp.sqrt(ff), jnp.sqrt(oo)
-    stat_out[...] = jnp.broadcast_to(
-        jnp.concatenate(
-            [rf, rf * fu, ro, rf * ft, ro * ot, jnp.sqrt(tt), jnp.zeros((2, 1), f32)], axis=0
-        ),
-        (8, LANES),
-    )
+    stats = jnp.concatenate(
+        [rf, rf * fu, ro, rf * ft, ro * ot, jnp.sqrt(tt), jnp.zeros((2, 1), f32)], axis=0
+    )
+    stat_out[...] = jnp.broadcast_to(jnp.broadcast_to(stats, (8, LANES))[None], stat_out.shape)
+
+
+def spread_kernel(s, ids, tiles, out):
+    count = s.nx * s.ny
+    lane = lax.broadcasted_iota(jnp.int32, (8, LANES), 1)
+    groups = s.devices // min(s.devices, LANES)
+    per = count // groups
+    for g in range(groups):
+        acc = jnp.zeros((8, LANES), f32)
+        for d in range(per):
+            acc = acc + jnp.where(lane == d * s.nz + ids[1], tiles[g * per + d], 0.0)
+        for leaf in range(s.nz):
+            out[leaf, g] = acc
 
 
 def finish_kernel(s, stats, rhs, u_in, x_out, lsq_out):
     groups = []
-    for g in range(0, s.devices, LANES):
-        acc = jnp.zeros((8, LANES), f32)
-        lane = lax.broadcasted_iota(jnp.int32, (8, LANES), 1)
-        for d in range(g, min(s.devices, g + LANES)):
-            acc = acc + jnp.where(lane == d - g, stats[d], 0.0)
+    for g in range(stats.shape[1]):
+        acc = stats[0, g]
+        for leaf in range(1, s.nz):
+            acc = acc + stats[leaf, g]
         groups.append(acc)
     rows = jnp.concatenate(groups, axis=1) if len(groups) > 1 else groups[0]
     f1, u1, u2, t1, t2, t3 = (rows[i : i + 1] for i in range(6))
@@ -397,38 +454,59 @@
     square = (s.rows, s.rows)
     tile = (8, LANES)
     rim = (s.half, LANES)
-    far_shape = (2 * s.nz * 2 * LANES, s.skel)
+    far_shape = (s.skel, 2 * s.far_tiles * LANES)
     column = lax.axis_index("gx") * s.ny + lax.axis_index("gy")
     ids = jnp.stack([column, lax.axis_index("gz")]).astype(jnp.int32)
 
+    def fetch(x, kind, dy):
+        pairs = []
+        for gx in range(s.nx):
+            for gy in range(s.ny):
+                pairs.append((s.beside(kind, gx) * s.ny + (gy + dy) % s.ny, gx * s.ny + gy))
+        return lax.ppermute(x, ("gx", "gy"), pairs)
+
     def fetch_rims(packed):
-        out = []
-        for dx, dy in s.sources:
-            pairs = []
-            for x in range(s.nx):
-                for y in range(s.ny):
-                    pairs.append((((x + dx) % s.nx) * s.ny + (y + dy) % s.ny, x * s.ny + y))
-            out.append(lax.ppermute(packed, ("gx", "gy"), pairs))
-        return out
-
-    def everywhere(x):
-        return lax.all_gather(x, ("gx", "gy", "gz"), axis=0, tiled=False)
+        rims = {}
+        for dy in s.shifts:
+            rims["same", dy] = fetch(packed, "same", dy)
+        for dy in s.shifts:
+            rims["other", dy] = fetch(packed, "other", dy)
+        rims["other", 0] = fetch(packed, "other", 0)
+        rims["partner", 0] = fetch(packed, "partner", 0)
+        for dy in s.shifts:
+            rims["partner", dy] = fetch(rims["same", dy], "partner", 0)
+        return [rims[key] for key in s.sources]
+
+    def over_plane(x):
+        return lax.all_to_all(x, ("gx", "gy"), 0, 0)
+
+    def over_layers(x):
+        return lax.all_to_all(x, "gz", 0, 0)
+
+    planes = (s.nx * s.ny,) + tile
+
+    def share_charges(tiles):
+        (merged,) = call(
+            functools.partial(merge_kernel, s), [((s.nz, 2) + tile, f32)], [ids, over_plane(tiles)], scalars=1
+        )
+        return over_layers(merged)
 
     charges, packed, col, f = call(
         functools.partial(start_kernel, s),
-        [(tile, f32), (rim, f32), ((s.step, LANES), f32), (full, f32)],
+        [(planes, f32), (rim, f32), ((s.step, LANES), f32), (full, f32)],
         [rhs, cells, blob_weight.reshape(1, -1)],
         flops=10**7,
     )
     rims = fetch_rims(packed)
-    charges = everywhere(charges)
-    loc, gat, rot, sh, sl, nh, nl, oh, ol, gh, gl, th, tl = call(
+    charges = share_charges(charges)
+    f, charges = lax.optimization_barrier((f, charges))
+    loc, gat, rot, sh, sl, nh, nl, oh, ol, gh, gl, far_op = call(
         functools.partial(setup_kernel, s),
         [(full, f32), (full, f32), ((16, s.bodies), f32)]
         + [(square, bf16)] * 4
         + [((s.bodies, s.bodies), bf16)] * 2
         + [((s.ghosts, s.bodies), bf16)] * 2
-        + [(far_shape, bf16)] * 2,
+        + [(far_shape, f32)],
         [ids, f, angles, self_mob, near_mat, near_weight, neighbours, skel_perm, interp, sibling_ops, root_op],
         scalars=1,
         scratch=[pltpu.VMEM(square, f32), pltpu.VMEM((s.levels, 2 * s.skel, s.skel), f32)],
@@ -436,13 +514,13 @@
     )
     u, charges, packed = call(
         functools.partial(first_kernel, s, len(rims)),
-        [(full, f32), (tile, f32), (rim, f32)],
-        [ids, loc, gat, nh, nl, gh, gl, charges, th, tl, cells, col, *rims],
-        scalars=1,
+        [(full, f32), (planes, f32), (rim, f32)],
+        [loc, gat, nh, nl, gh, gl, charges, far_op, cells, col, *rims],
         flops=10**9,
     )
     rims = fetch_rims(packed)
-    charges = everywhere(charges)
+    charges = share_charges(charges)
+    u, charges = lax.optimization_barrier((u, charges))
     loc, gat, ortho, stat = call(
         functools.partial(middle_kernel, s),
         [(full, f32), (full, f32), (full, f32), (tile, f32)],
@@ -451,16 +529,18 @@
     )
     (stat,) = call(
         functools.partial(second_kernel, s, len(rims)),
-        [(tile, f32)],
-        [ids, loc, gat, nh, nl, gh, gl, charges, th, tl, cells, col, f, ortho, stat, *rims],
-        scalars=1,
+        [(planes, f32)],
+        [loc, gat, nh, nl, gh, gl, charges, far_op, cells, col, f, ortho, stat, *rims],
         flops=10**9,
     )
-    stats = everywhere(stat)
+    groups = s.devices // min(s.devices, LANES)
+    (stats,) = call(
+        functools.partial(spread_kernel, s), [((s.nz, groups) + tile, f32)], [ids, over_plane(stat)], scalars=1
+    )
     result, lsq = call(
         functools.partial(finish_kernel, s),
         [(rhs.shape, f32), ((1, 1), f32)],
-        [stats, rhs, u],
+        [over_layers(stats), rhs, u],
         flops=10**7,
     )
     return result, lsq.reshape(())

time: 230 us -> 92.9 us (0.40)
  blocking collectives: 199 us -> 22.3 us
  local copies, waits for them, and re-layouts: 5.33 us -> 20.1 us
  waiting for transfers between devices: 0.03 us -> 11.1 us
  starting transfers between devices: 10.5 us -> 19.8 us
  Pallas kernels: 13.7 us -> 17.6 us
    all_gather x3 -> x0, blocking collectives: 199 us -> none  [everywhere(): return lax.all_gather(x, ('gx', 'gy', 'gz'), axis=0, tiled=False)]
    all_to_all x0 -> x3, blocking collectives: none -> 22.3 us  [the longest x2 14.3 us: over_plane(): return lax.all_to_all(x, ('gx', 'gy'), 0, 0)]
    unnamed x25 -> x59, local copies, waits for them, and re-layouts: 5.33 us -> 20.1 us
    all_to_all x0 -> x3, starting transfers between devices: none -> 11.5 us  [the longest x2 8.13 us: over_layers(): return lax.all_to_all(x, 'gz', 0, 0)]
    all_to_all x0 -> x3, waiting for transfers between devices: none -> 11.1 us  [the longest x2 6.52 us: over_layers(): return lax.all_to_all(x, 'gz', 0, 0)]
    pallas_call x6 -> x9, Pallas kernels: 13.7 us -> 17.6 us  [call(): pl.pallas_call(kernel, out_shape=[jax.ShapeDtypeStruct(shape, kind) for s...]
  transfers between devices with their start and end apart: 10 -> 13, of which waited for: 0 -> 3; matrix products, arithmetic and copies ran while one was open for 0% -> 0% of each run, Pallas kernels for 3% -> 9%
where the time goes in v3:
time: 92.9 us; the launch traced here: 91.8 us
  blocking collectives  22.3 us (24%)
  local copies, waits for them, and re-layouts  20.1 us (22%)
  starting transfers between devices  19.8 us (21%)
  Pallas kernels  17.6 us (19%)
  waiting for transfers between devices  11.1 us (12%)
    unnamed x59, local copies, waits for them, and re-layouts  20.1 us
    pallas_call x9, Pallas kernels, call(): pl.pallas_call(kernel, out_shape=[jax.ShapeDtypeStruct(shape, kind) for s...  17.6 us
    all_to_all x2, blocking collectives, over_plane(): return lax.all_to_all(x, ('gx', 'gy'), 0, 0)  14.3 us
    ppermute x10, starting transfers between devices, fetch(): return lax.ppermute(x, ('gx', 'gy'), pairs)  8.33 us
    all_to_all x2, starting transfers between devices, over_layers(): return lax.all_to_all(x, 'gz', 0, 0)  8.13 us
    all_to_all x1, blocking collectives, over_layers(): return lax.all_to_all(x, 'gz', 0, 0)  7.96 us
    all_to_all x2, waiting for transfers between devices, over_layers(): return lax.all_to_all(x, 'gz', 0, 0)  6.52 us
    all_to_all x1, waiting for transfers between devices, over_plane(): return lax.all_to_all(x, ('gx', 'gy'), 0, 0)  4.6 us
  transfers between devices with their start and end apart: 13, of which 3 were waited for; matrix products, arithmetic and copies ran while one was open for 0% of the time, Pallas kernels for 9%

profile of v3, /device:TPU:0, one launch (start us, length us, event | category | flops | bytes accessed | tf_op | source)
XLA Modules:
  0.0 91.8 jit_solution(11083863721974737044)
XLA Ops:
  0.7 1.1 %copy.14.rhs = f32[1,1,3,162,256]{4,3,2,1,0:T(8,128)S(1)} copy(f32[1,1,3,162,256]{4,1,3,2,0:T(1,128)} %param.12) | data formatting | bytes 995328 | tf_op args[0]
  3.1 0.9 %shard_map.131 = (f32[8,8,128]{2,1,0:T(8,128)}, f32[256,128]{1,0:T(8,128)}, f32[168,128]{1,0:T(8,128)S(1)}, f32[512,256]{1,0:T(8,128)S(1)}) custom-call(f32[1,1,3,162,256]{4,3,2,1,0:T(8,128)S(1)} %copy.14.rhs, s32[1,1,256]{2,1,0:T(1,128)S(1)} %copy-done.6, f32[1,162]{1,0:T(1,128)S(1)} %bitcast.4), custom_call_target="tpu_custom_call" | custom-call | flops 10000000 | bytes 1048576 | tf_op jit(solution)/shard_map/pallas_call | solution.py:437
  4.9 2.9 %collective-permute-start = (f32[256,128]{1,0:T(8,128)}, f32[256,128]{1,0:T(8,128)S(1)}, u32[]{:S(2)}, u32[]{:S(2)}) collective-permute-start(f32[256,128]{1,0:T(8,128)} %get-tuple-element.43), channel_id=1, source_target_pairs={{4,0},{0,4},{12,8},{8,12},{20,16},{16,20},{28,24},{24,28},{5,1},{1... | collective-permute-start | bytes 393224 | tf_op jit(solution)/shard_map/ppermute | solution.py:466
  7.8 3.3 %all-to-all-start = ((f32[8,8,128]{2,1,0:T(8,128)}), f32[8,8,128]{2,1,0:T(8,128)S(1)}, u32[]{:S(2)}, u32[]{:S(2)}) async-start(f32[8,8,128]{2,1,0:T(8,128)} %get-tuple-element.32), calls=%async_computation | async-start | bytes 65536 | tf_op jit(solution)/shard_map/all_to_all | solution.py:481
  11.2 4.6 %all-to-all-done.tiles = f32[8,8,128]{2,1,0:T(8,128)S(1)} async-done(((f32[8,8,128]{2,1,0:T(8,128)}), f32[8,8,128]{2,1,0:T(8,128)S(1)}, u32[]{:S(2)}, u32[]{:S(2)}) %all-to-all-start) | async-done | bytes 32800 | tf_op jit(solution)/shard_map/all_to_all | solution.py:481
  15.8 1.2 %shard_map.132 = f32[4,2,8,128]{3,2,1,0:T(8,128)} custom-call(s32[2]{0:T(128)S(1)} %pad_add_fusion.ids, f32[8,8,128]{2,1,0:T(8,128)S(1)} %all-to-all-done.tiles), custom_call_target="tpu_custom_call" | custom-call | bytes 1048576 | tf_op jit(solution)/shard_map/pallas_call | solution.py:437
  17.0 4.9 %all-to-all-start.1 = ((f32[4,2,8,128]{3,2,1,0:T(8,128)}), f32[4,2,8,128]{3,2,1,0:T(8,128)S(1)}, u32[]{:S(2)}, u32[]{:S(2)}) async-start(f32[4,2,8,128]{3,2,1,0:T(8,128)} %shard_map.132), calls=%async_computation.1 | async-start | bytes 65536 | tf_op jit(solution)/shard_map/all_to_all | solution.py:484
  21.8 1.8 %collective-permute-start.2 = (f32[256,128]{1,0:T(8,128)}, f32[256,128]{1,0:T(8,128)}, u32[]{:S(2)}, u32[]{:S(2)}) collective-permute-start(f32[256,128]{1,0:T(8,128)} %get-tuple-element.43), channel_id=1, source_target_pairs={{28,0},{24,4},{20,8},{16,12},{12,16},{8,20},{4,24},{0,28},{29,1},{... | collective-permute-start | bytes 393224 | tf_op jit(solution)/shard_map/ppermute | solution.py:466
  24.2 3.3 %all-to-all-done.1.charges = f32[4,2,8,128]{3,2,1,0:T(8,128)S(1)} async-done(((f32[4,2,8,128]{3,2,1,0:T(8,128)}), f32[4,2,8,128]{3,2,1,0:T(8,128)S(1)}, u32[]{:S(2)}, u32[]{:S(2)}) %all-to-all-start.1) | async-done | bytes 32800 | tf_op jit(solution)/shard_map/all_to_all | solution.py:484
  27.5 1.0 %copy-done.1 = f32[512,256]{1,0:T(8,128)S(1)} copy-done((f32[512,256]{1,0:T(8,128)S(1)}, f32[512,256]{1,0:T(8,128)}, u32[]{:S(2)}) %copy-start.1) | copy-done | bytes 524312
  28.5 1.2 %copy-done.9 = f32[486,486]{1,0:T(8,128)S(1)} copy-done((f32[486,486]{1,0:T(8,128)S(1)}, f32[486,486]{1,0:T(8,128)}, u32[]{:S(2)}) %copy-start.9) | copy-done | bytes 944808
  29.8 1.2 %copy-done.10 = f32[486,486]{1,0:T(8,128)S(1)} copy-done((f32[486,486]{1,0:T(8,128)S(1)}, f32[486,486]{1,0:T(8,128)}, u32[]{:S(2)}) %copy-start.10) | copy-done | bytes 944808
  31.0 1.0 %copy-done.11 = f32[2,192,192]{2,1,0:T(8,128)S(1)} copy-done((f32[2,192,192]{2,1,0:T(8,128)S(1)}, f32[2,192,192]{2,1,0:T(8,128)}, u32[]{:S(2)}) %copy-start.11) | copy-done | bytes 294936
  32.0 1.0 %copy-done.12 = f32[2,192,192]{2,1,0:T(8,128)S(1)} copy-done((f32[2,192,192]{2,1,0:T(8,128)S(1)}, f32[2,192,192]{2,1,0:T(8,128)}, u32[]{:S(2)}) %copy-start.12) | copy-done | bytes 294936
  33.0 0.9 %copy-done.13 = f32[192,192]{1,0:T(8,128)S(1)} copy-done((f32[192,192]{1,0:T(8,128)S(1)}, f32[192,192]{1,0:T(8,128)}, u32[]{:S(2)}) %copy-start.13) | copy-done | bytes 147480
  33.9 4.7 %shard_map.133 = (f32[512,256]{1,0:T(8,128)S(1)}, f32[512,256]{1,0:T(8,128)S(1)}, f32[16,256]{1,0:T(8,128)S(1)}, bf16[512,512]{1,0:T(8,128)(2,1)S(1)}, bf16[512,...) custom-call(s32[2]{0:T(128)S(1)} %pad_add_fusion.ids, ...), custom_call_target="tpu_custom_call" | custom-call | flops 1000000000 | bytes 1048576 | tf_op jit(solution)/shard_map/pallas_call | solution.py:437
  40.2 3.8 %shard_map.134 = (f32[512,256]{1,0:T(8,128)S(1)}, f32[8,8,128]{2,1,0:T(8,128)S(1)}, f32[256,128]{1,0:T(8,128)}) custom-call(f32[512,256]{1,0:T(8,128)S(1)} %get-tuple-element.34.loc, f32[512,256]{1,0:T(8,128)S(1)} %get-tuple-element.35.gat, bf16[512,512]{1,0:T(8,128)(2,1)S(1)} %get-tuple-element.36.nh, bf16[512,512]{1,0:T(8,128)(2,1)S(1)} %get-tuple-element.37.nl, ...), custom_call_target="tpu_custom_call" | custom-call | flops 1000000000 | bytes 1048576 | tf_op jit(solution)/shard_map/pallas_call | solution.py:437
  45.5 7.2 %all_to_all.30.tiles = f32[8,8,128]{2,1,0:T(8,128)S(1)} all-to-all(f32[8,8,128]{2,1,0:T(8,128)S(1)} %get-tuple-element.45), channel_id=1, replica_groups=mesh['gx'=4,'gy'=2,'gz'=4] {'gx','gy'}, dimensions={0} | all-to-all | bytes 65536 | tf_op jit(solution)/shard_map/all_to_all | solution.py:481
  52.7 1.2 %shard_map.135 = f32[4,2,8,128]{3,2,1,0:T(8,128)} custom-call(s32[2]{0:T(128)S(1)} %pad_add_fusion.ids, f32[8,8,128]{2,1,0:T(8,128)S(1)} %all_to_all.30.tiles), custom_call_target="tpu_custom_call" | custom-call | bytes 1048576 | tf_op jit(solution)/shard_map/pallas_call | solution.py:437
  53.8 3.3 %all-to-all-start.3 = ((f32[4,2,8,128]{3,2,1,0:T(8,128)}), f32[4,2,8,128]{3,2,1,0:T(8,128)S(1)}, u32[]{:S(2)}, u32[]{:S(2)}) async-start(f32[4,2,8,128]{3,2,1,0:T(8,128)} %shard_map.135), calls=%async_computation.3 | async-start | bytes 65536 | tf_op jit(solution)/shard_map/all_to_all | solution.py:484
  57.5 1.6 %collective-permute-start.7 = (f32[256,128]{1,0:T(8,128)}, f32[256,128]{1,0:T(8,128)}, u32[]{:S(2)}, u32[]{:S(2)}) collective-permute-start(f32[256,128]{1,0:T(8,128)} %get-tuple-element.57), channel_id=1, source_target_pairs={{28,0},{24,4},{20,8},{16,12},{12,16},{8,20},{4,24},{0,28},{29,1},{... | collective-permute-start | bytes 393224 | tf_op jit(solution)/shard_map/ppermute | solution.py:466
  59.5 3.2 %all-to-all-done.3.charges = f32[4,2,8,128]{3,2,1,0:T(8,128)S(1)} async-done(((f32[4,2,8,128]{3,2,1,0:T(8,128)}), f32[4,2,8,128]{3,2,1,0:T(8,128)S(1)}, u32[]{:S(2)}, u32[]{:S(2)}) %all-to-all-start.3) | async-done | bytes 32800 | tf_op jit(solution)/shard_map/all_to_all | solution.py:484
  62.7 1.0 %copy-done.2 = f32[512,256]{1,0:T(8,128)S(1)} copy-done((f32[512,256]{1,0:T(8,128)S(1)}, f32[512,256]{1,0:T(8,128)}, u32[]{:S(2)}) %copy-start.2) | copy-done | bytes 524312
  63.8 1.0 %copy-done.5 = f32[512,256]{1,0:T(8,128)S(1)} copy-done((f32[512,256]{1,0:T(8,128)S(1)}, f32[512,256]{1,0:T(8,128)}, u32[]{:S(2)}) %copy-start.5) | copy-done | bytes 524312
  64.8 1.0 %copy-done.18 = bf16[512,512]{1,0:T(8,128)(2,1)S(1)} copy-done((bf16[512,512]{1,0:T(8,128)(2,1)S(1)}, bf16[512,512]{1,0:T(8,128)(2,1)}, u32[]{:S(2)}) %copy-start.18) | copy-done | bytes 524312
  65.9 1.0 %copy-done.20 = bf16[512,512]{1,0:T(8,128)(2,1)S(1)} copy-done((bf16[512,512]{1,0:T(8,128)(2,1)S(1)}, bf16[512,512]{1,0:T(8,128)(2,1)}, u32[]{:S(2)}) %copy-start.20) | copy-done | bytes 524312
  69.4 1.0 %shard_map.136 = (f32[512,256]{1,0:T(8,128)S(1)}, f32[512,256]{1,0:T(8,128)S(1)}, f32[512,256]{1,0:T(8,128)S(1)}, f32[8,128]{1,0:T(8,128)S(1)}) custom-call(f32[512,256]{1,0:T(8,128)S(1)} %copy-done.5, f32[512,256]{1,0:T(8,128)S(1)} %copy-done.2, f32[16,256]{1,0:T(8,128)S(1)} %copy-done.26, bf16[512,512]{1,0:T(8,128)(2,1)S(1)} %copy-done.18, ...), custom_call_target="tpu_custom_call" | custom-call | flops 1000000000 | bytes 1048576 | tf_op jit(solution)/shard_map/pallas_call | solution.py:437
  70.5 3.4 %shard_map.137 = f32[8,8,128]{2,1,0:T(8,128)S(1)} custom-call(f32[512,256]{1,0:T(8,128)S(1)} %get-tuple-element.52.loc, f32[512,256]{1,0:T(8,128)S(1)} %get-tuple-element.53.gat, bf16[512,512]{1,0:T(8,128)(2,1)S(1)} %get-tuple-element.36.nh, bf16[512,512]{1,0:T(8,128)(2,1)S(1)} %get-tuple-element.37.nl, bf16[384,256]{1,0:T(8,128)(2,1)S(1)} %get-tuple-element.38.gh, ...), custom_call_target="tpu_custom_call" | custom-call | flops 1000000000 | bytes 1048576 | tf_op jit(solution)/shard_map/pallas_call | solution.py:437
  73.9 7.1 %all_to_all.31.tiles = f32[8,8,128]{2,1,0:T(8,128)S(1)} all-to-all(f32[8,8,128]{2,1,0:T(8,128)S(1)} %shard_map.137), channel_id=1, replica_groups=mesh['gx'=4,'gy'=2,'gz'=4] {'gx','gy'}, dimensions={0} | all-to-all | bytes 65536 | tf_op jit(solution)/shard_map/all_to_all | solution.py:481
  81.6 8.0 %all_to_all.32.stats = f32[4,1,8,128]{3,2,1,0:T(8,128)S(1)} all-to-all(f32[4,1,8,128]{3,2,1,0:T(8,128)S(1)} %shard_map.138), channel_id=1, replica_groups=mesh['gx'=4,'gy'=2,'gz'=4] {'gz'}, dimensions={0} | all-to-all | bytes 32768 | tf_op jit(solution)/shard_map/all_to_all | solution.py:484
  89.5 1.0 %shard_map.139 = (f32[1,1,3,162,256]{4,3,2,1,0:T(8,128)S(1)}, f32[1,1]{1,0:T(1,128)}) custom-call(f32[4,1,8,128]{3,2,1,0:T(8,128)S(1)} %all_to_all.32.stats, f32[1,1,3,162,256]{4,3,2,1,0:T(8,128)S(1)} %copy.14.rhs, f32[512,256]{1,0:T(8,128)S(1)} %copy-done.5), custom_call_target="tpu_custom_call" | custom-call | flops 10000000 | bytes 1048576 | tf_op jit(solution)/shard_map/pallas_call | solution.py:437
  90.5 1.3 %copy.17 = f32[1,1,3,162,256]{4,1,3,2,0:T(1,128)} copy(f32[1,1,3,162,256]{4,3,2,1,0:T(8,128)S(1)} %get-tuple-element.60) | data formatting | bytes 995328
  (66 shorter events, 9.9 us)
Async XLA Ops:
  0.6 23.5 %copy-start.27 = (f32[1,1,3,256]{3,1,2,0:T(1,128)S(1)}, f32[1,1,3,256]{3,1,2,0:T(1,128)}, u32[]{:S(2)}) copy-start(f32[1,1,3,256]{3,1,2,0:T(1,128)} %param.13) | copy-start | bytes 9220
  0.6 26.8 %copy-start.14 = (f32[1,1,8,256]{3,2,1,0:T(8,128)S(1)}, f32[1,1,8,256]{3,2,1,0:T(8,128)}, u32[]{:S(2)}) copy-start(f32[1,1,8,256]{3,2,1,0:T(8,128)} %near_weight.1) | copy-start | bytes 24580
  0.7 26.8 %copy-start.15 = (s32[1,1,8,256]{3,2,1,0:T(8,128)S(1)}, s32[1,1,8,256]{3,2,1,0:T(8,128)}, u32[]{:S(2)}) copy-start(s32[1,1,8,256]{3,2,1,0:T(8,128)} %neighbours.1) | copy-start | bytes 24580
  0.7 26.8 %copy-start.16 = (s32[2,384]{1,0:T(2,128)S(1)}, s32[2,384]{1,0:T(2,128)}, u32[]{:S(2)}) copy-start(s32[2,384]{1,0:T(2,128)} %perm.1) | copy-start | bytes 9220
  4.9 18.8 %collective-permute-start = (f32[256,128]{1,0:T(8,128)}, f32[256,128]{1,0:T(8,128)S(1)}, u32[]{:S(2)}, u32[]{:S(2)}) collective-permute-start(f32[256,128]{1,0:T(8,128)} %get-tuple-element.43), channel_id=1, source_target_pairs={{4,0},{0,4},{12,8},{8,12},{20,16},{16,20},{28,24},{24,28},{5,1},{1... | collective-permute-start | bytes 393224 | tf_op jit(solution)/shard_map/ppermute | solution.py:466
  7.8 8.0 %all-to-all-start = ((f32[8,8,128]{2,1,0:T(8,128)}), f32[8,8,128]{2,1,0:T(8,128)S(1)}, u32[]{:S(2)}, u32[]{:S(2)}) async-start(f32[8,8,128]{2,1,0:T(8,128)} %get-tuple-element.32), calls=%async_computation | async-start | bytes 65536 | tf_op jit(solution)/shard_map/all_to_all | solution.py:481
  17.0 10.5 %all-to-all-start.1 = ((f32[4,2,8,128]{3,2,1,0:T(8,128)}), f32[4,2,8,128]{3,2,1,0:T(8,128)S(1)}, u32[]{:S(2)}, u32[]{:S(2)}) async-start(f32[4,2,8,128]{3,2,1,0:T(8,128)} %shard_map.132), calls=%async_computation.1 | async-start | bytes 65536 | tf_op jit(solution)/shard_map/all_to_all | solution.py:484
  21.8 18.4 %collective-permute-start.1 = (f32[256,128]{1,0:T(8,128)}, f32[256,128]{1,0:T(8,128)S(1)}, u32[]{:S(2)}, u32[]{:S(2)}) collective-permute-start(f32[256,128]{1,0:T(8,128)} %get-tuple-element.43), channel_id=1, source_target_pairs={{24,0},{28,4},{16,8},{20,12},{8,16},{12,20},{0,24},{4,28},{25,1},{... | collective-permute-start | bytes 393224 | tf_op jit(solution)/shard_map/ppermute | solution.py:466
  21.8 18.4 %collective-permute-start.2 = (f32[256,128]{1,0:T(8,128)}, f32[256,128]{1,0:T(8,128)}, u32[]{:S(2)}, u32[]{:S(2)}) collective-permute-start(f32[256,128]{1,0:T(8,128)} %get-tuple-element.43), channel_id=1, source_target_pairs={{28,0},{24,4},{20,8},{16,12},{12,16},{8,20},{4,24},{0,28},{29,1},{... | collective-permute-start | bytes 393224 | tf_op jit(solution)/shard_map/ppermute | solution.py:466
  23.7 16.6 %collective-permute-start.3 = (f32[256,128]{1,0:T(8,128)}, f32[256,128]{1,0:T(8,128)}, u32[]{:S(2)}, u32[]{:S(2)}) collective-permute-start(f32[256,128]{1,0:T(8,128)} %get-tuple-element.43), channel_id=1, source_target_pairs={{8,0},{12,4},{0,8},{4,12},{24,16},{28,20},{16,24},{20,28},{9,1},{1... | collective-permute-start | bytes 393224 | tf_op jit(solution)/shard_map/ppermute | solution.py:466
  23.7 16.6 %collective-permute-start.4 = (f32[256,128]{1,0:T(8,128)S(1)}, f32[256,128]{1,0:T(8,128)}, u32[]{:S(2)}, u32[]{:S(2)}) collective-permute-start(f32[256,128]{1,0:T(8,128)S(1)} %collective-permute-done.rest_0_), channel_id=1, source_target_pairs={{8,0},{12,4},{0,8},{4,12},{24,16},{28,20},{16,24},{20,28},{9,1},{1... | collective-permute-start | bytes 393224 | tf_op jit(solution)/shard_map/ppermute | solution.py:466
  27.5 1.0 %copy-start.1 = (f32[512,256]{1,0:T(8,128)S(1)}, f32[512,256]{1,0:T(8,128)}, u32[]{:S(2)}) copy-start(f32[512,256]{1,0:T(8,128)} %copy-done) | copy-start | bytes 1572868
  28.5 1.2 %copy-start.9 = (f32[486,486]{1,0:T(8,128)S(1)}, f32[486,486]{1,0:T(8,128)}, u32[]{:S(2)}) copy-start(f32[486,486]{1,0:T(8,128)} %self_mob.1) | copy-start | bytes 2834356
  29.7 1.2 %copy-start.10 = (f32[486,486]{1,0:T(8,128)S(1)}, f32[486,486]{1,0:T(8,128)}, u32[]{:S(2)}) copy-start(f32[486,486]{1,0:T(8,128)} %near_mat.1) | copy-start | bytes 2834356
  31.0 1.0 %copy-start.11 = (f32[2,192,192]{2,1,0:T(8,128)S(1)}, f32[2,192,192]{2,1,0:T(8,128)}, u32[]{:S(2)}) copy-start(f32[2,192,192]{2,1,0:T(8,128)} %interp.1) | copy-start | bytes 884740
  32.0 1.0 %copy-start.12 = (f32[2,192,192]{2,1,0:T(8,128)S(1)}, f32[2,192,192]{2,1,0:T(8,128)}, u32[]{:S(2)}) copy-start(f32[2,192,192]{2,1,0:T(8,128)} %sibling.1) | copy-start | bytes 884740
  32.9 0.9 %copy-start.13 = (f32[192,192]{1,0:T(8,128)S(1)}, f32[192,192]{1,0:T(8,128)}, u32[]{:S(2)}) copy-start(f32[192,192]{1,0:T(8,128)} %root.1) | copy-start | bytes 442372
  33.9 6.4 %copy-start.7 = (s32[1,1,256]{2,1,0:T(1,128)S(1)}, s32[1,1,256]{2,1,0:T(1,128)}, u32[]{:S(2)}) copy-start(s32[1,1,256]{2,1,0:T(1,128)} %cells.5) | copy-start | bytes 3076
  40.2 3.8 %copy-start.21 = (bf16[256,256]{1,0:T(8,128)(2,1)}, bf16[256,256]{1,0:T(8,128)(2,1)S(1)}, u32[]{:S(2)}) copy-start(bf16[256,256]{1,0:T(8,128)(2,1)S(1)} %get-tuple-element.50.oh) | copy-start | bytes 393220
  40.2 3.8 %copy-start.23 = (bf16[256,256]{1,0:T(8,128)(2,1)}, bf16[256,256]{1,0:T(8,128)(2,1)S(1)}, u32[]{:S(2)}) copy-start(bf16[256,256]{1,0:T(8,128)(2,1)S(1)} %get-tuple-element.51.ol) | copy-start | bytes 393220
  40.2 3.8 %copy-start.25 = (f32[16,256]{1,0:T(8,128)}, f32[16,256]{1,0:T(8,128)S(1)}, u32[]{:S(2)}) copy-start(f32[16,256]{1,0:T(8,128)S(1)} %get-tuple-element.47.rot) | copy-start | bytes 49156
  44.8 14.2 %collective-permute-start.5 = (f32[256,128]{1,0:T(8,128)}, f32[256,128]{1,0:T(8,128)S(1)}, u32[]{:S(2)}, u32[]{:S(2)}) collective-permute-start(f32[256,128]{1,0:T(8,128)} %get-tuple-element.57), channel_id=1, source_target_pairs={{4,0},{0,4},{12,8},{8,12},{20,16},{16,20},{28,24},{24,28},{5,1},{1... | collective-permute-start | bytes 393224 | tf_op jit(solution)/shard_map/ppermute | solution.py:466
  53.8 8.9 %all-to-all-start.3 = ((f32[4,2,8,128]{3,2,1,0:T(8,128)}), f32[4,2,8,128]{3,2,1,0:T(8,128)S(1)}, u32[]{:S(2)}, u32[]{:S(2)}) async-start(f32[4,2,8,128]{3,2,1,0:T(8,128)} %shard_map.135), calls=%async_computation.3 | async-start | bytes 65536 | tf_op jit(solution)/shard_map/all_to_all | solution.py:484
  57.1 13.3 %collective-permute-start.6 = (f32[256,128]{1,0:T(8,128)}, f32[256,128]{1,0:T(8,128)S(1)}, u32[]{:S(2)}, u32[]{:S(2)}) collective-permute-start(f32[256,128]{1,0:T(8,128)} %get-tuple-element.57), channel_id=1, source_target_pairs={{24,0},{28,4},{16,8},{20,12},{8,16},{12,20},{0,24},{4,28},{25,1},{... | collective-permute-start | bytes 393224 | tf_op jit(solution)/shard_map/ppermute | solution.py:466
  57.5 13.0 %collective-permute-start.7 = (f32[256,128]{1,0:T(8,128)}, f32[256,128]{1,0:T(8,128)}, u32[]{:S(2)}, u32[]{:S(2)}) collective-permute-start(f32[256,128]{1,0:T(8,128)} %get-tuple-element.57), channel_id=1, source_target_pairs={{28,0},{24,4},{20,8},{16,12},{12,16},{8,20},{4,24},{0,28},{29,1},{... | collective-permute-start | bytes 393224 | tf_op jit(solution)/shard_map/ppermute | solution.py:466
  59.0 11.4 %collective-permute-start.8 = (f32[256,128]{1,0:T(8,128)}, f32[256,128]{1,0:T(8,128)}, u32[]{:S(2)}, u32[]{:S(2)}) collective-permute-start(f32[256,128]{1,0:T(8,128)} %get-tuple-element.57), channel_id=1, source_target_pairs={{8,0},{12,4},{0,8},{4,12},{24,16},{28,20},{16,24},{20,28},{9,1},{1... | collective-permute-start | bytes 393224 | tf_op jit(solution)/shard_map/ppermute | solution.py:466
  59.0 11.4 %collective-permute-start.9 = (f32[256,128]{1,0:T(8,128)S(1)}, f32[256,128]{1,0:T(8,128)}, u32[]{:S(2)}, u32[]{:S(2)}) collective-permute-start(f32[256,128]{1,0:T(8,128)S(1)} %collective-permute-done.5.rest_0_), channel_id=1, source_target_pairs={{8,0},{12,4},{0,8},{4,12},{24,16},{28,20},{16,24},{20,28},{9,1},{1... | collective-permute-start | bytes 393224 | tf_op jit(solution)/shard_map/ppermute | solution.py:466
  62.7 1.0 %copy-start.2 = (f32[512,256]{1,0:T(8,128)S(1)}, f32[512,256]{1,0:T(8,128)}, u32[]{:S(2)}) copy-start(f32[512,256]{1,0:T(8,128)} %copy-done) | copy-start | bytes 1572868
  63.8 1.0 %copy-start.5 = (f32[512,256]{1,0:T(8,128)S(1)}, f32[512,256]{1,0:T(8,128)}, u32[]{:S(2)}) copy-start(f32[512,256]{1,0:T(8,128)} %copy-done.4) | copy-start | bytes 1572868
  64.8 1.0 %copy-start.18 = (bf16[512,512]{1,0:T(8,128)(2,1)S(1)}, bf16[512,512]{1,0:T(8,128)(2,1)}, u32[]{:S(2)}) copy-start(bf16[512,512]{1,0:T(8,128)(2,1)} %copy-done.17) | copy-start | bytes 1572868
  65.9 1.0 %copy-start.20 = (bf16[512,512]{1,0:T(8,128)(2,1)S(1)}, bf16[512,512]{1,0:T(8,128)(2,1)}, u32[]{:S(2)}) copy-start(bf16[512,512]{1,0:T(8,128)(2,1)} %copy-done.19) | copy-start | bytes 1572868
  69.4 1.0 %copy-start.3 = (f32[512,256]{1,0:T(8,128)S(1)}, f32[512,256]{1,0:T(8,128)}, u32[]{:S(2)}) copy-start(f32[512,256]{1,0:T(8,128)} %copy-done) | copy-start | bytes 1572868
  (9 other events, 7.2 us)

commit v4 on v3

--- a/solution.py
+++ b/solution.py
@@ -48,6 +48,9 @@
         self.step = round_up(self.blobs, 8)
         self.rows = round_up(3 * self.step, 16)
         self.half = self.rows // 2
+        self.message = self.half + 8
+        self.direct = (self.nx, self.ny) == (4, 2)
+        self.groups = -(-self.devices // LANES)
         self.levels = skel_perm.shape[0]
         self.skel = skel_perm.shape[1] // 2
         shifts = sorted({(dy % self.ny) for dy in (-1, 1)} - {0})
@@ -133,7 +136,12 @@
     )
 
 
-def start_kernel(s, rhs, cells, weight, q_out, rim_out, col_out, f_out):
+def pack_message(x, weight_col, cells, s):
+    charges = pack_charges(pieces(x, s), weight_col, occupancy(cells, s), s)
+    return jnp.concatenate([pack_rim(x, s), charges], axis=0)
+
+
+def start_kernel(s, rhs, cells, weight, message_out, col_out, f_out):
     f_out[...] = jnp.zeros_like(f_out)
     for c in range(3):
         f_out[c * s.step : c * s.step + s.blobs, :] = rhs[0, 0, c]
@@ -141,10 +149,7 @@
     wide = jnp.concatenate([weight[...], jnp.zeros((1, 2 * LANES - s.blobs), f32)], axis=1)
     col = jnp.broadcast_to(wide, (LANES, 2 * LANES)).T[: s.step]
     col_out[...] = col
-    rim_out[...] = pack_rim(f, s)
-    occ = occupancy(cells[0], s)
-    charges = pack_charges(pieces(f, s), col[:, :1], occ, s)
-    q_out[...] = jnp.broadcast_to(charges[None], q_out.shape)
+    message_out[...] = pack_message(f, col[:, :1], cells[0], s)
 
 
 def frame_rows(angles):
@@ -172,14 +177,12 @@
     return f + stacked(back, s), product(mm, split(f), own)
 
 
-def expand(block, level, ups):
+def expand(block, level, halves):
     if level == 0:
         return [block]
-    up = ups[level - 1]
-    n = up.shape[0] // 2
     block = split(block)
-    low, high = (product(mt, block, split(half)) for half in (up[:n], up[n:]))
-    return expand(low, level - 1, ups) + expand(high, level - 1, ups)
+    near, far = (product(mt, block, split(half)) for half in halves[level - 1])
+    return expand(near, level - 1, halves) + expand(far, level - 1, halves)
 
 
 def setup_kernel(
@@ -230,7 +233,7 @@
 
     n = s.skel
     z = ids[1]
-    ups = []
+    halves = []
     eye_row = lax.broadcasted_iota(jnp.int32, (n, n), 0)
     eye_col = lax.broadcasted_iota(jnp.int32, (n, n), 1)
     eye = jnp.where(eye_row == eye_col, 1.0, 0.0)
@@ -238,29 +241,25 @@
         spot = lax.broadcasted_iota(jnp.int32, (2 * n, 2 * n), 0)
         onehot = jnp.where(perm[level : level + 1, :] == spot, 1.0, 0.0).astype(bf16)
         hi, lo = split(jnp.concatenate([eye, interp[level]], axis=0))
-        up = mm(onehot, hi) + mm(onehot, lo)
-        ups.append(up)
-        ups_ref[level] = up
+        ups_ref[level] = mm(onehot, hi) + mm(onehot, lo)
+        bit = (z >> level) & 1
+        halves.append(
+            [ups_ref[level, pl.ds(pl.multiple_of(side * n, 8), n), :] for side in (bit, 1 - bit)]
+        )
 
     def down(block, level, dot):
-        bit = (z >> level) & 1
-        half = ups_ref[level, pl.ds(pl.multiple_of(bit * n, 8), n), :]
-        return product(dot, split(half), split(block))
+        return product(dot, split(halves[level][0]), split(block))
 
     spread = root[...]
     beside = []
     for level in reversed(range(s.levels)):
-        last = level == s.levels - 1
-        spread = down(spread, level, mt if last else mm)
-        beside = [down(block, level, mt if fresh else mm) for block, fresh in beside]
-        beside = [(block, False) for block in beside] + [(sibling[level], True)]
-    far_leaves = expand(spread, s.levels, ups)
-    near_leaves = [jnp.zeros((n, n), f32) for _ in range(s.nz)]
-    for level, (block, fresh) in zip(reversed(range(s.levels)), beside):
-        sub = expand(block.T if fresh else block, level, ups)
-        for leaf in range(s.nz):
-            hit = (leaf >> level) == ((z >> level) ^ 1)
-            near_leaves[leaf] = jnp.where(hit, near_leaves[leaf] + sub[leaf % (1 << level)], near_leaves[leaf])
+        spread = down(spread, level, mt if level == s.levels - 1 else mm)
+        beside = [(down(block, level, mt if fresh else mm), False) for block, fresh in beside]
+        beside.append((sibling[level], True))
+    far_leaves = expand(spread, s.levels, halves)
+    near_leaves = [jnp.zeros((n, n), f32)]
+    for level, (block, fresh) in enumerate(reversed(beside)):
+        near_leaves += expand(block.T if fresh else block, level, halves)
     tail = n - LANES
     far_out[...] = jnp.zeros_like(far_out)
     own = [a - b for a, b in zip(near_leaves, far_leaves)]
@@ -272,20 +271,27 @@
             far_out[:, at : at + tail] = block[:, LANES:]
 
 
-def merge_kernel(s, ids, tiles, out):
-    acc = tiles[0]
-    for c in range(1, s.nx * s.ny):
-        acc = acc + tiles[c]
-    own = tiles[ids[0]]
-    for leaf in range(s.nz):
-        out[leaf, 0] = own
-        out[leaf, 1] = acc
+def half_kernel(s, *refs):
+    *messages, out = refs
+    acc = messages[0][s.half :, :]
+    for message in messages[1:]:
+        acc = acc + message[s.half :, :]
+    out[...] = acc
+
+
+def layer_kernel(s, message, *refs):
+    *sums, out = refs
+    acc = sums[0][...]
+    for part in sums[1:]:
+        acc = acc + part[...]
+    out[0] = message[s.half :, :]
+    out[1] = acc
 
 
 def far_potential(s, charges, far_op):
     rows = []
     for group in range(2):
-        tiles = [charges[leaf, group] for leaf in range(s.nz)]
+        tiles = [layer[group] for layer in charges]
         rows += tiles
         for leaf in range(0, s.nz, 2):
             pair = tiles[leaf]
@@ -318,24 +324,24 @@
     return out
 
 
-def image(s, loc, gat, rims, near, ghost, charges, far_op, cells, col):
-    values = far_values(s, charges, far_op, cells[0])
-    far = stacked([col * value for value in values], s)
-    gathered = gat + product(mm, split(unpack_rims(rims, s)), ghost)
-    return (loc + far) + product(mm, near, split(gathered))
-
-
-def first_kernel(s, n_rims, loc, gat, nh, nl, gh, gl, charges, far_op, cells, col, *rest):
-    rims, (u_out, q_out, rim_out) = rest[:n_rims], rest[n_rims:]
+def near_kernel(s, loc, gat, nh, nl, gh, gl, *refs):
+    *messages, out = refs
+    rims = [message[: s.half, :] for message in messages]
+    gathered = gat[...] + product(mm, split(unpack_rims(rims, s)), (gh[...], gl[...]))
+    out[...] = loc[...] + product(mm, (nh[...], nl[...]), split(gathered))
+
+
+def with_far(s, part, layers, far_op, cells, col):
+    values = far_values(s, layers, far_op, cells[0])
+    return part[...] + stacked([col * value for value in values], s)
+
+
+def first_kernel(s, part, far_op, cells, col, *refs):
+    *layers, u_out, message_out = refs
     weight_col = col[:, :1]
-    u = image(
-        s, loc[...], gat[...], [r[...] for r in rims], (nh[...], nl[...]), (gh[...], gl[...]),
-        charges, far_op, cells, weight_col,
-    )
+    u = with_far(s, part, layers, far_op, cells, weight_col)
     u_out[...] = u
-    rim_out[...] = pack_rim(u, s)
-    charges = pack_charges(pieces(u, s), weight_col, occupancy(cells[0], s), s)
-    q_out[...] = jnp.broadcast_to(charges[None], q_out.shape)
+    message_out[...] = pack_message(u, weight_col, cells[0], s)
 
 
 def safe_inverse(x):
@@ -357,14 +363,9 @@
     )
 
 
-def second_kernel(
-    s, n_rims, loc, gat, nh, nl, gh, gl, charges, far_op, cells, col, f_in, ortho_in, stat, *rest
-):
-    rims, (stat_out,) = rest[:n_rims], rest[n_rims:]
-    t = image(
-        s, loc[...], gat[...], [r[...] for r in rims], (nh[...], nl[...]), (gh[...], gl[...]),
-        charges, far_op, cells, col[:, :1],
-    )
+def second_kernel(s, ids, part, far_op, cells, col, f_in, ortho_in, stat, *refs):
+    *layers, stat_out = refs
+    t = with_far(s, part, layers, far_op, cells, col[:, :1])
     f, ortho = f_in[...], ortho_in[...]
     ff, fu, oo = (stat[i : i + 1, :1] for i in range(3))
     ft = total(f * t) * safe_inverse(ff)
@@ -375,28 +376,19 @@
     stats = jnp.concatenate(
         [rf, rf * fu, ro, rf * ft, ro * ot, jnp.sqrt(tt), jnp.zeros((2, 1), f32)], axis=0
     )
-    stat_out[...] = jnp.broadcast_to(jnp.broadcast_to(stats, (8, LANES))[None], stat_out.shape)
-
-
-def spread_kernel(s, ids, tiles, out):
-    count = s.nx * s.ny
-    lane = lax.broadcasted_iota(jnp.int32, (8, LANES), 1)
-    groups = s.devices // min(s.devices, LANES)
-    per = count // groups
-    for g in range(groups):
-        acc = jnp.zeros((8, LANES), f32)
-        for d in range(per):
-            acc = acc + jnp.where(lane == d * s.nz + ids[1], tiles[g * per + d], 0.0)
-        for leaf in range(s.nz):
-            out[leaf, g] = acc
-
-
-def finish_kernel(s, stats, rhs, u_in, x_out, lsq_out):
+    device = ids[0] * s.nz + ids[1]
+    for g in range(s.groups):
+        lane = lax.broadcasted_iota(jnp.int32, (8, LANES), 1) + g * LANES
+        stat_out[g] = jnp.where(lane == device, stats, 0.0)
+
+
+def finish_kernel(s, rhs, u_in, *refs):
+    *stats, x_out, lsq_out = refs
     groups = []
-    for g in range(stats.shape[1]):
-        acc = stats[0, g]
-        for leaf in range(1, s.nz):
-            acc = acc + stats[leaf, g]
+    for g in range(s.groups):
+        acc = stats[0][g]
+        for part in stats[1:]:
+            acc = acc + part[g]
         groups.append(acc)
     rows = jnp.concatenate(groups, axis=1) if len(groups) > 1 else groups[0]
     f1, u1, u2, t1, t2, t3 = (rows[i : i + 1] for i in range(6))
@@ -440,7 +432,7 @@
         in_specs=[smem] * scalars + [vmem] * (len(args) - scalars),
         out_specs=[vmem] * len(outs),
         scratch_shapes=list(scratch),
-        compiler_params=pltpu.CompilerParams(vmem_limit_bytes=32 * 2**20),
+        compiler_params=pltpu.CompilerParams(vmem_limit_bytes=16 * 2**20),
         cost_estimate=pl.CostEstimate(flops=flops, bytes_accessed=2**20, transcendentals=0),
     )(*args)
 
@@ -453,7 +445,6 @@
     full = (s.rows, s.bodies)
     square = (s.rows, s.rows)
     tile = (8, LANES)
-    rim = (s.half, LANES)
     far_shape = (s.skel, 2 * s.far_tiles * LANES)
     column = lax.axis_index("gx") * s.ny + lax.axis_index("gy")
     ids = jnp.stack([column, lax.axis_index("gz")]).astype(jnp.int32)
@@ -465,41 +456,48 @@
                 pairs.append((s.beside(kind, gx) * s.ny + (gy + dy) % s.ny, gx * s.ny + gy))
         return lax.ppermute(x, ("gx", "gy"), pairs)
 
-    def fetch_rims(packed):
-        rims = {}
+    def fetch_layers(x):
+        return [x] + [
+            lax.ppermute(x, "gz", [(z ^ k, z) for z in range(s.nz)]) for k in range(1, s.nz)
+        ]
+
+    def fetch_messages(message):
+        got = {}
         for dy in s.shifts:
-            rims["same", dy] = fetch(packed, "same", dy)
+            got["same", dy] = fetch(message, "same", dy)
         for dy in s.shifts:
-            rims["other", dy] = fetch(packed, "other", dy)
-        rims["other", 0] = fetch(packed, "other", 0)
-        rims["partner", 0] = fetch(packed, "partner", 0)
+            got["other", dy] = fetch(message, "other", dy)
+        got["other", 0] = fetch(message, "other", 0)
+        got["partner", 0] = fetch(message, "partner", 0)
         for dy in s.shifts:
-            rims["partner", dy] = fetch(rims["same", dy], "partner", 0)
-        return [rims[key] for key in s.sources]
-
-    def over_plane(x):
-        return lax.all_to_all(x, ("gx", "gy"), 0, 0)
-
-    def over_layers(x):
-        return lax.all_to_all(x, "gz", 0, 0)
-
-    planes = (s.nx * s.ny,) + tile
-
-    def share_charges(tiles):
-        (merged,) = call(
-            functools.partial(merge_kernel, s), [((s.nz, 2) + tile, f32)], [ids, over_plane(tiles)], scalars=1
-        )
-        return over_layers(merged)
-
-    charges, packed, col, f = call(
+            got["partner", dy] = fetch(got["same", dy], "partner", 0)
+        return got
+
+    def share_charges(message, got):
+        if s.direct:
+            quarter = [message] + [got[key] for key in s.sources if key[0] != "partner"]
+            (half,) = call(functools.partial(half_kernel, s), [(tile, f32)], quarter)
+            sums = [half, fetch(half, "partner", 0)]
+        else:
+            sums = [lax.psum(message[s.half :], ("gx", "gy"))]
+        (pair,) = call(functools.partial(layer_kernel, s), [((2,) + tile, f32)], [message] + sums)
+        return fetch_layers(pair)
+
+    def near_part(loc, gat, got):
+        return call(
+            functools.partial(near_kernel, s),
+            [(full, f32)],
+            [loc, gat, nh, nl, gh, gl] + [got[key] for key in s.sources],
+            flops=10**9,
+        )[0]
+
+    message, col, f = call(
         functools.partial(start_kernel, s),
-        [(planes, f32), (rim, f32), ((s.step, LANES), f32), (full, f32)],
+        [((s.message, LANES), f32), ((s.step, LANES), f32), (full, f32)],
         [rhs, cells, blob_weight.reshape(1, -1)],
         flops=10**7,
     )
-    rims = fetch_rims(packed)
-    charges = share_charges(charges)
-    f, charges = lax.optimization_barrier((f, charges))
+    got = fetch_messages(message)
     loc, gat, rot, sh, sl, nh, nl, oh, ol, gh, gl, far_op = call(
         functools.partial(setup_kernel, s),
         [(full, f32), (full, f32), ((16, s.bodies), f32)]
@@ -510,37 +508,41 @@
         [ids, f, angles, self_mob, near_mat, near_weight, neighbours, skel_perm, interp, sibling_ops, root_op],
         scalars=1,
         scratch=[pltpu.VMEM(square, f32), pltpu.VMEM((s.levels, 2 * s.skel, s.skel), f32)],
-        flops=10**9,
-    )
-    u, charges, packed = call(
-        functools.partial(first_kernel, s, len(rims)),
-        [(full, f32), (planes, f32), (rim, f32)],
-        [loc, gat, nh, nl, gh, gl, charges, far_op, cells, col, *rims],
-        flops=10**9,
-    )
-    rims = fetch_rims(packed)
-    charges = share_charges(charges)
-    u, charges = lax.optimization_barrier((u, charges))
+        flops=5 * 10**9,
+    )
+    part = near_part(loc, gat, got)
+    layers = share_charges(message, got)
+    u, message = call(
+        functools.partial(first_kernel, s),
+        [(full, f32), ((s.message, LANES), f32)],
+        [part, far_op, cells, col, *layers],
+        flops=10**8,
+    )
+    got = fetch_messages(message)
     loc, gat, ortho, stat = call(
         functools.partial(middle_kernel, s),
         [(full, f32), (full, f32), (full, f32), (tile, f32)],
         [u, f, rot, sh, sl, oh, ol],
         flops=10**9,
     )
-    (stat,) = call(
-        functools.partial(second_kernel, s, len(rims)),
-        [(planes, f32)],
-        [loc, gat, nh, nl, gh, gl, charges, far_op, cells, col, f, ortho, stat, *rims],
-        flops=10**9,
-    )
-    groups = s.devices // min(s.devices, LANES)
+    part = near_part(loc, gat, got)
+    layers = share_charges(message, got)
     (stats,) = call(
-        functools.partial(spread_kernel, s), [((s.nz, groups) + tile, f32)], [ids, over_plane(stat)], scalars=1
-    )
+        functools.partial(second_kernel, s),
+        [((s.groups,) + tile, f32)],
+        [ids, part, far_op, cells, col, f, ortho, stat, *layers],
+        scalars=1,
+        flops=10**8,
+    )
+    if s.direct:
+        stats = stats + fetch(stats, "partner", 0)
+        stats = stats + fetch(stats, "same", 1) + fetch(stats, "other", 0) + fetch(stats, "other", 1)
+    else:
+        stats = lax.psum(stats, ("gx", "gy"))
     result, lsq = call(
         functools.partial(finish_kernel, s),
         [(rhs.shape, f32), ((1, 1), f32)],
-        [over_layers(stats), rhs, u],
+        [rhs, u, *fetch_layers(stats)],
         flops=10**7,
     )
     return result, lsq.reshape(())

time: 92.9 us -> 73.4 us (0.79)
  blocking collectives: 22.3 us -> 0 us
  waiting for transfers between devices: 11.1 us -> 24.5 us
  local copies, waits for them, and re-layouts: 20.1 us -> 8.64 us
  starting transfers between devices: 19.8 us -> 26.2 us
  Pallas kernels: 17.6 us -> 12.9 us
    all_to_all x3 -> x0, blocking collectives: 22.3 us -> none  [the longest x2 14.3 us: over_plane(): return lax.all_to_all(x, ('gx', 'gy'), 0, 0)]
    ppermute x10 -> x16, waiting for transfers between devices: 0.03 us -> 16 us  [fetch(): return lax.ppermute(x, ('gx', 'gy'), pairs)]
    ppermute x0 -> x9, starting transfers between devices: none -> 13.3 us  [fetch_layers(): lax.ppermute(x, 'gz', [(z ^ k, z) for z in range(s.nz)])]
    unnamed x59 -> x27, local copies, waits for them, and re-layouts: 20.1 us -> 8.64 us
    all_to_all x3 -> x0, starting transfers between devices: 11.5 us -> none  [the longest x2 8.13 us: over_layers(): return lax.all_to_all(x, 'gz', 0, 0)]
    all_to_all x3 -> x0, waiting for transfers between devices: 11.1 us -> none  [the longest x2 6.52 us: over_layers(): return lax.all_to_all(x, 'gz', 0, 0)]
    ppermute x0 -> x9, waiting for transfers between devices: none -> 8.44 us  [fetch_layers(): lax.ppermute(x, 'gz', [(z ^ k, z) for z in range(s.nz)])]
    pallas_call x9 -> x12, Pallas kernels: 17.6 us -> 12.9 us  [call(): pl.pallas_call(kernel, out_shape=[jax.ShapeDtypeStruct(shape, kind) for s...]
  transfers between devices with their start and end apart: 13 -> 25, of which waited for: 3 -> 12; matrix products, arithmetic and copies ran while one was open for 0% -> 0% of each run, Pallas kernels for 9% -> 13%
where the time goes in v4:
time: 73.4 us; the launch traced here: 73.1 us
  starting transfers between devices  26.2 us (36%)
  waiting for transfers between devices  24.5 us (33%)
  Pallas kernels  12.9 us (18%)
  local copies, waits for them, and re-layouts  8.64 us (12%)
  between operations  0.83 us (1%)
    ppermute x16, waiting for transfers between devices, fetch(): return lax.ppermute(x, ('gx', 'gy'), pairs)  16 us
    ppermute x9, starting transfers between devices, fetch_layers(): lax.ppermute(x, 'gz', [(z ^ k, z) for z in range(s.nz)])  13.3 us
    pallas_call x12, Pallas kernels, call(): pl.pallas_call(kernel, out_shape=[jax.ShapeDtypeStruct(shape, kind) for s...  12.9 us
    ppermute x16, starting transfers between devices, fetch(): return lax.ppermute(x, ('gx', 'gy'), pairs)  12.9 us
    unnamed x27, local copies, waits for them, and re-layouts  8.64 us
    ppermute x9, waiting for transfers between devices, fetch_layers(): lax.ppermute(x, 'gz', [(z ^ k, z) for z in range(s.nz)])  8.44 us
  transfers between devices with their start and end apart: 25, of which 12 were waited for; matrix products, arithmetic and copies ran while one was open for 0% of the time, Pallas kernels for 13%

profile of v4, /device:TPU:0, one launch (start us, length us, event | category | flops | bytes accessed | tf_op | source)
XLA Modules:
  0.0 73.1 jit_solution(7585229537035242346)
XLA Ops:
  0.7 1.2 %copy.16.rhs = f32[1,1,3,162,256]{4,3,2,1,0:T(8,128)S(1)} copy(f32[1,1,3,162,256]{4,1,3,2,0:T(1,128)} %param.12) | data formatting | bytes 995328 | tf_op args[0]
  3.5 2.9 %collective-permute-start = (f32[264,128]{1,0:T(8,128)S(1)}, f32[264,128]{1,0:T(8,128)S(1)}, u32[]{:S(2)}, u32[]{:S(2)}) collective-permute-start(f32[264,128]{1,0:T(8,128)S(1)} %get-tuple-element.32.refs_0_.message), channel_id=1, source_target_pairs={{4,0},{0,4},{12,8},{8,12},{20,16},{16,20},{28,24},{24,28},{5,1},{1... | collective-permute-start | bytes 405512 | tf_op jit(solution)/shard_map/ppermute | solution.py:457
  8.2 1.9 %collective-permute-done.refs_0_.refs_1_ = f32[264,128]{1,0:T(8,128)S(1)} collective-permute-done((f32[264,128]{1,0:T(8,128)S(1)}, f32[264,128]{1,0:T(8,128)S(1)}, u32[]{:S(2)}, u32[]{:S(2)}) %collective-permute-start) | collective-permute-done | bytes 135200 | tf_op jit(solution)/shard_map/ppermute | solution.py:457
  10.1 5.0 %collective-permute-done.1.refs_1_.refs_2_ = f32[264,128]{1,0:T(8,128)S(1)} collective-permute-done((f32[264,128]{1,0:T(8,128)S(1)}, f32[264,128]{1,0:T(8,128)S(1)}, u32[]{:S(2)}, u32[]{:S(2)}) %collective-permute-start.1) | collective-permute-done | bytes 135200 | tf_op jit(solution)/shard_map/ppermute | solution.py:457
  15.8 1.2 %copy-done.4 = f32[486,486]{1,0:T(8,128)S(1)} copy-done((f32[486,486]{1,0:T(8,128)S(1)}, f32[486,486]{1,0:T(8,128)}, u32[]{:S(2)}) %copy-start.4) | copy-done | bytes 944808
  17.0 1.0 %copy-done.5 = f32[2,192,192]{2,1,0:T(8,128)S(1)} copy-done((f32[2,192,192]{2,1,0:T(8,128)S(1)}, f32[2,192,192]{2,1,0:T(8,128)}, u32[]{:S(2)}) %copy-start.5) | copy-done | bytes 294936
  18.0 1.0 %copy-done.6 = f32[2,192,192]{2,1,0:T(8,128)S(1)} copy-done((f32[2,192,192]{2,1,0:T(8,128)S(1)}, f32[2,192,192]{2,1,0:T(8,128)}, u32[]{:S(2)}) %copy-start.6) | copy-done | bytes 294936
  19.0 0.9 %copy-done.7 = f32[192,192]{1,0:T(8,128)S(1)} copy-done((f32[192,192]{1,0:T(8,128)S(1)}, f32[192,192]{1,0:T(8,128)}, u32[]{:S(2)}) %copy-start.7) | copy-done | bytes 147480
  20.6 4.7 %shard_map.132 = (f32[512,256]{1,0:T(8,128)S(1)}, f32[512,256]{1,0:T(8,128)S(1)}, f32[16,256]{1,0:T(8,128)S(1)}, bf16[512,512]{1,0:T(8,128)(2,1)S(1)}, bf16[512,...) custom-call(s32[2]{0:T(128)S(1)} %pad_add_fusion.ids, ...), custom_call_target="tpu_custom_call" | custom-call | flops 5000000000 | bytes 1048576 | tf_op jit(solution)/shard_map/pallas_call | solution.py:429
  25.3 1.6 %collective-permute-start.6 = (f32[2,8,128]{2,1,0:T(8,128)S(1)}, f32[2,8,128]{2,1,0:T(8,128)S(1)}, u32[]{:S(2)}, u32[]{:S(2)}) collective-permute-start(f32[2,8,128]{2,1,0:T(8,128)S(1)} %shard_map.135.refs_0_), channel_id=1, source_target_pairs={{1,0},{0,1},{3,2},{2,3},{5,4},{4,5},{7,6},{6,7},{9,8},{8,9},{11,10... | collective-permute-start | bytes 24584 | tf_op jit(solution)/shard_map/ppermute | solution.py:461
  26.9 2.6 %collective-permute-start.7 = (f32[2,8,128]{2,1,0:T(8,128)S(1)}, f32[2,8,128]{2,1,0:T(8,128)S(1)}, u32[]{:S(2)}, u32[]{:S(2)}) collective-permute-start(f32[2,8,128]{2,1,0:T(8,128)S(1)} %shard_map.135.refs_0_), channel_id=1, source_target_pairs={{2,0},{3,1},{0,2},{1,3},{6,4},{7,5},{4,6},{5,7},{10,8},{11,9},{8,1... | collective-permute-start | bytes 24584 | tf_op jit(solution)/shard_map/ppermute | solution.py:461
  29.8 1.9 %shard_map.133.part = f32[512,256]{1,0:T(8,128)S(1)} custom-call(f32[512,256]{1,0:T(8,128)S(1)} %get-tuple-element.26.loc, f32[512,256]{1,0:T(8,128)S(1)} %get-tuple-element.27.gat, bf16[512,512]{1,0:T(8,128)(2,1)S(1)} %get-tuple-element.28.nh, bf16[512,512]{1,0:T(8,128)(2,1)S(1)} %get-tuple-element.29.nl, bf16[384,256]{1,0:T(8,128)(2,1)S(1)} %get-tuple-element.30.gh, ...), custom_call_target="tpu_custom_call" | custom-call | flops 1000000000 | bytes 1048576 | tf_op jit(solution)/shard_map/pallas_call | solution.py:429
  31.7 3.3 %collective-permute-done.8.refs_3_ = f32[2,8,128]{2,1,0:T(8,128)S(1)} collective-permute-done((f32[2,8,128]{2,1,0:T(8,128)S(1)}, f32[2,8,128]{2,1,0:T(8,128)S(1)}, u32[]{:S(2)}, u32[]{:S(2)}) %collective-permute-start.8) | collective-permute-done | bytes 8224 | tf_op jit(solution)/shard_map/ppermute | solution.py:461
  35.7 3.1 %collective-permute-start.11 = (f32[264,128]{1,0:T(8,128)S(1)}, f32[264,128]{1,0:T(8,128)S(1)}, u32[]{:S(2)}, u32[]{:S(2)}) collective-permute-start(f32[264,128]{1,0:T(8,128)S(1)} %get-tuple-element.43.refs_0_.message), channel_id=1, source_target_pairs={{28,0},{24,4},{20,8},{16,12},{12,16},{8,20},{4,24},{0,28},{29,1},{... | collective-permute-start | bytes 405512 | tf_op jit(solution)/shard_map/ppermute | solution.py:457
  38.8 2.5 %collective-permute-done.9.refs_0_.refs_1_ = f32[264,128]{1,0:T(8,128)S(1)} collective-permute-done((f32[264,128]{1,0:T(8,128)S(1)}, f32[264,128]{1,0:T(8,128)S(1)}, u32[]{:S(2)}, u32[]{:S(2)}) %collective-permute-start.9) | collective-permute-done | bytes 135200 | tf_op jit(solution)/shard_map/ppermute | solution.py:457
  41.3 1.0 %collective-permute-done.10.refs_1_.refs_2_ = f32[264,128]{1,0:T(8,128)S(1)} collective-permute-done((f32[264,128]{1,0:T(8,128)S(1)}, f32[264,128]{1,0:T(8,128)S(1)}, u32[]{:S(2)}, u32[]{:S(2)}) %collective-permute-start.10) | collective-permute-done | bytes 135200 | tf_op jit(solution)/shard_map/ppermute | solution.py:457
  43.0 1.3 %collective-permute-start.14 = (f32[8,128]{1,0:T(8,128)S(1)}, f32[8,128]{1,0:T(8,128)S(1)}, u32[]{:S(2)}, u32[]{:S(2)}) collective-permute-start(f32[8,128]{1,0:T(8,128)S(1)} %shard_map.139.refs_0_), channel_id=1, source_target_pairs={{8,0},{12,4},{0,8},{4,12},{24,16},{28,20},{16,24},{20,28},{9,1},{1... | collective-permute-start | bytes 12296 | tf_op jit(solution)/shard_map/ppermute | solution.py:457
  44.3 1.1 %shard_map.137 = (f32[512,256]{1,0:T(8,128)S(1)}, f32[512,256]{1,0:T(8,128)S(1)}, f32[512,256]{1,0:T(8,128)S(1)}, f32[8,128]{1,0:T(8,128)S(1)}) custom-call(f32[512,256]{1,0:T(8,128)S(1)} %get-tuple-element.35.u_in, f32[512,256]{1,0:T(8,128)S(1)} %get-tuple-element.25.f_in, f32[16,256]{1,0:T(8,128)S(1)} %get-tuple-element.36.rot, ...), custom_call_target="tpu_custom_call" | custom-call | flops 1000000000 | bytes 1048576 | tf_op jit(solution)/shard_map/pallas_call | solution.py:429
  45.5 0.9 %collective-permute-start.16 = (f32[2,8,128]{2,1,0:T(8,128)S(1)}, f32[2,8,128]{2,1,0:T(8,128)S(1)}, u32[]{:S(2)}, u32[]{:S(2)}) collective-permute-start(f32[2,8,128]{2,1,0:T(8,128)S(1)} %shard_map.140.refs_0_), channel_id=1, source_target_pairs={{2,0},{3,1},{0,2},{1,3},{6,4},{7,5},{4,6},{5,7},{10,8},{11,9},{8,1... | collective-permute-start | bytes 24584 | tf_op jit(solution)/shard_map/ppermute | solution.py:461
  46.3 3.5 %collective-permute-start.17 = (f32[2,8,128]{2,1,0:T(8,128)S(1)}, f32[2,8,128]{2,1,0:T(8,128)S(1)}, u32[]{:S(2)}, u32[]{:S(2)}) collective-permute-start(f32[2,8,128]{2,1,0:T(8,128)S(1)} %shard_map.140.refs_0_), channel_id=1, source_target_pairs={{3,0},{2,1},{1,2},{0,3},{7,4},{6,5},{5,6},{4,7},{11,8},{10,9},{9,1... | collective-permute-start | bytes 24584 | tf_op jit(solution)/shard_map/ppermute | solution.py:461
  49.9 1.9 %shard_map.138.part = f32[512,256]{1,0:T(8,128)S(1)} custom-call(f32[512,256]{1,0:T(8,128)S(1)} %get-tuple-element.41.loc, f32[512,256]{1,0:T(8,128)S(1)} %get-tuple-element.42.gat, bf16[512,512]{1,0:T(8,128)(2,1)S(1)} %get-tuple-element.28.nh, bf16[512,512]{1,0:T(8,128)(2,1)S(1)} %get-tuple-element.29.nl, bf16[384,256]{1,0:T(8,128)(2,1)S(1)} %get-tuple-element.30.gh, ...), custom_call_target="tpu_custom_call" | custom-call | flops 1000000000 | bytes 1048576 | tf_op jit(solution)/shard_map/pallas_call | solution.py:429
  51.8 1.5 %shard_map.141 = f32[1,8,128]{2,1,0:T(8,128)S(1)} custom-call(s32[2]{0:T(128)S(1)} %pad_add_fusion.ids, f32[512,256]{1,0:T(8,128)S(1)} %shard_map.138.part, f32[192,1536]{1,0:T(8,128)S(1)} %get-tuple-element.33.far_op, s32[1,1,256]{2,1,0:T(1,128)S(1)} %copy-done.1, f32[168,128]{1,0:T(8,128)S(1)} %get-tuple-element.34.col, ...), custom_call_target="tpu_custom_call" | custom-call | flops 100000000 | bytes 1048576 | tf_op jit(solution)/shard_map/pallas_call | solution.py:429
  53.3 1.2 %collective-permute-done.18 = f32[1,8,128]{2,1,0:T(8,128)S(1)} collective-permute-done((f32[1,8,128]{2,1,0:T(8,128)S(1)}, f32[1,8,128]{2,1,0:T(8,128)S(1)}, u32[]{:S(2)}, u32[]{:S(2)}) %collective-permute-start.18) | collective-permute-done | bytes 4128 | tf_op jit(solution)/shard_map/ppermute | solution.py:457
  54.5 1.9 %collective-permute-start.21 = (f32[1,8,128]{2,1,0:T(8,128)S(1)}, f32[1,8,128]{2,1,0:T(8,128)S(1)}, u32[]{:S(2)}, u32[]{:S(2)}) collective-permute-start(f32[1,8,128]{2,1,0:T(8,128)S(1)} %add.16), channel_id=1, source_target_pairs={{28,0},{24,4},{20,8},{16,12},{12,16},{8,20},{4,24},{0,28},{29,1},{... | collective-permute-start | bytes 12296 | tf_op jit(solution)/shard_map/ppermute | solution.py:457
  56.4 1.3 %collective-permute-start.20 = (f32[1,8,128]{2,1,0:T(8,128)S(1)}, f32[1,8,128]{2,1,0:T(8,128)S(1)}, u32[]{:S(2)}, u32[]{:S(2)}) collective-permute-start(f32[1,8,128]{2,1,0:T(8,128)S(1)} %add.16), channel_id=1, source_target_pairs={{24,0},{28,4},{16,8},{20,12},{8,16},{12,20},{0,24},{4,28},{25,1},{... | collective-permute-start | bytes 12296 | tf_op jit(solution)/shard_map/ppermute | solution.py:457
  58.4 1.1 %collective-permute-done.20 = f32[1,8,128]{2,1,0:T(8,128)S(1)} collective-permute-done((f32[1,8,128]{2,1,0:T(8,128)S(1)}, f32[1,8,128]{2,1,0:T(8,128)S(1)}, u32[]{:S(2)}, u32[]{:S(2)}) %collective-permute-start.20) | collective-permute-done | bytes 4128 | tf_op jit(solution)/shard_map/ppermute | solution.py:457
  59.5 1.8 %collective-permute-done.19 = f32[1,8,128]{2,1,0:T(8,128)S(1)} collective-permute-done((f32[1,8,128]{2,1,0:T(8,128)S(1)}, f32[1,8,128]{2,1,0:T(8,128)S(1)}, u32[]{:S(2)}, u32[]{:S(2)}) %collective-permute-start.19) | collective-permute-done | bytes 4128 | tf_op jit(solution)/shard_map/ppermute | solution.py:457
  61.6 3.8 %collective-permute-start.23 = (f32[1,8,128]{2,1,0:T(8,128)S(1)}, f32[1,8,128]{2,1,0:T(8,128)S(1)}, u32[]{:S(2)}, u32[]{:S(2)}) collective-permute-start(f32[1,8,128]{2,1,0:T(8,128)S(1)} %add_add_fusion.refs_0_), channel_id=1, source_target_pairs={{2,0},{3,1},{0,2},{1,3},{6,4},{7,5},{4,6},{5,7},{10,8},{11,9},{8,1... | collective-permute-start | bytes 12296 | tf_op jit(solution)/shard_map/ppermute | solution.py:461
  65.7 1.3 %collective-permute-done.23.refs_2_ = f32[1,8,128]{2,1,0:T(8,128)S(1)} collective-permute-done((f32[1,8,128]{2,1,0:T(8,128)S(1)}, f32[1,8,128]{2,1,0:T(8,128)S(1)}, u32[]{:S(2)}, u32[]{:S(2)}) %collective-permute-start.23) | collective-permute-done | bytes 4128 | tf_op jit(solution)/shard_map/ppermute | solution.py:461
  67.0 3.8 %collective-permute-done.24.refs_3_ = f32[1,8,128]{2,1,0:T(8,128)S(1)} collective-permute-done((f32[1,8,128]{2,1,0:T(8,128)S(1)}, f32[1,8,128]{2,1,0:T(8,128)S(1)}, u32[]{:S(2)}, u32[]{:S(2)}) %collective-permute-start.24) | collective-permute-done | bytes 4128 | tf_op jit(solution)/shard_map/ppermute | solution.py:461
  70.8 1.0 %shard_map.142 = (f32[1,1,3,162,256]{4,3,2,1,0:T(8,128)S(1)}, f32[1,1]{1,0:T(1,128)}) custom-call(f32[1,1,3,162,256]{4,3,2,1,0:T(8,128)S(1)} %copy.16.rhs, f32[512,256]{1,0:T(8,128)S(1)} %get-tuple-element.35.u_in, f32[1,8,128]{2,1,0:T(8,128)S(1)} %add_add_fusion.refs_0_, f32[1,8,128]{2,1,0:T(8,128)S(1)} %collective-permute-done.22.refs_1_, ...), custom_call_target="tpu_custom_call" | custom-call | flops 10000000 | bytes 1048576 | tf_op jit(solution)/shard_map/pallas_call | solution.py:429
  71.8 1.3 %copy.17 = f32[1,1,3,162,256]{4,1,3,2,0:T(1,128)} copy(f32[1,1,3,162,256]{4,3,2,1,0:T(8,128)S(1)} %get-tuple-element.48) | data formatting | bytes 995328
  (60 shorter events, 7.7 us)
Async XLA Ops:
  0.6 7.5 %copy-start.11 = (f32[1,1,3,256]{3,1,2,0:T(1,128)S(1)}, f32[1,1,3,256]{3,1,2,0:T(1,128)}, u32[]{:S(2)}) copy-start(f32[1,1,3,256]{3,1,2,0:T(1,128)} %param.13) | copy-start | bytes 9220
  0.6 15.1 %copy-start.3 = (f32[486,486]{1,0:T(8,128)S(1)}, f32[486,486]{1,0:T(8,128)}, u32[]{:S(2)}) copy-start(f32[486,486]{1,0:T(8,128)} %self_mob.1) | copy-start | bytes 2834356
  0.7 15.1 %copy-start.8 = (f32[1,1,8,256]{3,2,1,0:T(8,128)S(1)}, f32[1,1,8,256]{3,2,1,0:T(8,128)}, u32[]{:S(2)}) copy-start(f32[1,1,8,256]{3,2,1,0:T(8,128)} %near_weight.1) | copy-start | bytes 24580
  0.7 15.1 %copy-start.10 = (s32[2,384]{1,0:T(2,128)S(1)}, s32[2,384]{1,0:T(2,128)}, u32[]{:S(2)}) copy-start(s32[2,384]{1,0:T(2,128)} %perm.1) | copy-start | bytes 9220
  3.5 6.6 %collective-permute-start = (f32[264,128]{1,0:T(8,128)S(1)}, f32[264,128]{1,0:T(8,128)S(1)}, u32[]{:S(2)}, u32[]{:S(2)}) collective-permute-start(f32[264,128]{1,0:T(8,128)S(1)} %get-tuple-element.32.refs_0_.message), channel_id=1, source_target_pairs={{4,0},{0,4},{12,8},{8,12},{20,16},{16,20},{28,24},{24,28},{5,1},{1... | collective-permute-start | bytes 405512 | tf_op jit(solution)/shard_map/ppermute | solution.py:457
  6.4 8.7 %collective-permute-start.1 = (f32[264,128]{1,0:T(8,128)S(1)}, f32[264,128]{1,0:T(8,128)S(1)}, u32[]{:S(2)}, u32[]{:S(2)}) collective-permute-start(f32[264,128]{1,0:T(8,128)S(1)} %get-tuple-element.32.refs_0_.message), channel_id=1, source_target_pairs={{24,0},{28,4},{16,8},{20,12},{8,16},{12,20},{0,24},{4,28},{25,1},{... | collective-permute-start | bytes 405512 | tf_op jit(solution)/shard_map/ppermute | solution.py:457
  7.1 8.0 %collective-permute-start.2 = (f32[264,128]{1,0:T(8,128)S(1)}, f32[264,128]{1,0:T(8,128)S(1)}, u32[]{:S(2)}, u32[]{:S(2)}) collective-permute-start(f32[264,128]{1,0:T(8,128)S(1)} %get-tuple-element.32.refs_0_.message), channel_id=1, source_target_pairs={{28,0},{24,4},{20,8},{16,12},{12,16},{8,20},{4,24},{0,28},{29,1},{... | collective-permute-start | bytes 405512 | tf_op jit(solution)/shard_map/ppermute | solution.py:457
  7.7 22.0 %collective-permute-start.3 = (f32[264,128]{1,0:T(8,128)S(1)}, f32[264,128]{1,0:T(8,128)S(1)}, u32[]{:S(2)}, u32[]{:S(2)}) collective-permute-start(f32[264,128]{1,0:T(8,128)S(1)} %get-tuple-element.32.refs_0_.message), channel_id=1, source_target_pairs={{8,0},{12,4},{0,8},{4,12},{24,16},{28,20},{16,24},{20,28},{9,1},{1... | collective-permute-start | bytes 405512 | tf_op jit(solution)/shard_map/ppermute | solution.py:457
  15.2 10.1 %collective-permute-start.5 = (f32[8,128]{1,0:T(8,128)S(1)}, f32[8,128]{1,0:T(8,128)S(1)}, u32[]{:S(2)}, u32[]{:S(2)}) collective-permute-start(f32[8,128]{1,0:T(8,128)S(1)} %shard_map.134.refs_0_), channel_id=1, source_target_pairs={{8,0},{12,4},{0,8},{4,12},{24,16},{28,20},{16,24},{20,28},{9,1},{1... | collective-permute-start | bytes 12296 | tf_op jit(solution)/shard_map/ppermute | solution.py:457
  15.3 14.4 %collective-permute-start.4 = (f32[264,128]{1,0:T(8,128)S(1)}, f32[264,128]{1,0:T(8,128)S(1)}, u32[]{:S(2)}, u32[]{:S(2)}) collective-permute-start(f32[264,128]{1,0:T(8,128)S(1)} %collective-permute-done.refs_0_.refs_1_), channel_id=1, source_target_pairs={{8,0},{12,4},{0,8},{4,12},{24,16},{28,20},{16,24},{20,28},{9,1},{1... | collective-permute-start | bytes 405512 | tf_op jit(solution)/shard_map/ppermute | solution.py:457
  15.7 1.2 %copy-start.4 = (f32[486,486]{1,0:T(8,128)S(1)}, f32[486,486]{1,0:T(8,128)}, u32[]{:S(2)}) copy-start(f32[486,486]{1,0:T(8,128)} %near_mat.1) | copy-start | bytes 2834356
  18.0 1.0 %copy-start.6 = (f32[2,192,192]{2,1,0:T(8,128)S(1)}, f32[2,192,192]{2,1,0:T(8,128)}, u32[]{:S(2)}) copy-start(f32[2,192,192]{2,1,0:T(8,128)} %sibling.1) | copy-start | bytes 884740
  25.3 6.3 %collective-permute-start.6 = (f32[2,8,128]{2,1,0:T(8,128)S(1)}, f32[2,8,128]{2,1,0:T(8,128)S(1)}, u32[]{:S(2)}, u32[]{:S(2)}) collective-permute-start(f32[2,8,128]{2,1,0:T(8,128)S(1)} %shard_map.135.refs_0_), channel_id=1, source_target_pairs={{1,0},{0,1},{3,2},{2,3},{5,4},{4,5},{7,6},{6,7},{9,8},{8,9},{11,10... | collective-permute-start | bytes 24584 | tf_op jit(solution)/shard_map/ppermute | solution.py:461
  26.9 4.7 %collective-permute-start.7 = (f32[2,8,128]{2,1,0:T(8,128)S(1)}, f32[2,8,128]{2,1,0:T(8,128)S(1)}, u32[]{:S(2)}, u32[]{:S(2)}) collective-permute-start(f32[2,8,128]{2,1,0:T(8,128)S(1)} %shard_map.135.refs_0_), channel_id=1, source_target_pairs={{2,0},{3,1},{0,2},{1,3},{6,4},{7,5},{4,6},{5,7},{10,8},{11,9},{8,1... | collective-permute-start | bytes 24584 | tf_op jit(solution)/shard_map/ppermute | solution.py:461
  29.5 5.4 %collective-permute-start.8 = (f32[2,8,128]{2,1,0:T(8,128)S(1)}, f32[2,8,128]{2,1,0:T(8,128)S(1)}, u32[]{:S(2)}, u32[]{:S(2)}) collective-permute-start(f32[2,8,128]{2,1,0:T(8,128)S(1)} %shard_map.135.refs_0_), channel_id=1, source_target_pairs={{3,0},{2,1},{1,2},{0,3},{7,4},{6,5},{5,6},{4,7},{11,8},{10,9},{9,1... | collective-permute-start | bytes 24584 | tf_op jit(solution)/shard_map/ppermute | solution.py:461
  29.7 5.2 %copy-start.1 = (s32[1,1,256]{2,1,0:T(1,128)S(1)}, s32[1,1,256]{2,1,0:T(1,128)}, u32[]{:S(2)}) copy-start(s32[1,1,256]{2,1,0:T(1,128)} %cells.5) | copy-start | bytes 3076
  35.6 5.8 %collective-permute-start.9 = (f32[264,128]{1,0:T(8,128)S(1)}, f32[264,128]{1,0:T(8,128)S(1)}, u32[]{:S(2)}, u32[]{:S(2)}) collective-permute-start(f32[264,128]{1,0:T(8,128)S(1)} %get-tuple-element.43.refs_0_.message), channel_id=1, source_target_pairs={{4,0},{0,4},{12,8},{8,12},{20,16},{16,20},{28,24},{24,28},{5,1},{1... | collective-permute-start | bytes 405512 | tf_op jit(solution)/shard_map/ppermute | solution.py:457
  35.6 6.8 %collective-permute-start.10 = (f32[264,128]{1,0:T(8,128)S(1)}, f32[264,128]{1,0:T(8,128)S(1)}, u32[]{:S(2)}, u32[]{:S(2)}) collective-permute-start(f32[264,128]{1,0:T(8,128)S(1)} %get-tuple-element.43.refs_0_.message), channel_id=1, source_target_pairs={{24,0},{28,4},{16,8},{20,12},{8,16},{12,20},{0,24},{4,28},{25,1},{... | collective-permute-start | bytes 405512 | tf_op jit(solution)/shard_map/ppermute | solution.py:457
  35.7 7.4 %collective-permute-start.11 = (f32[264,128]{1,0:T(8,128)S(1)}, f32[264,128]{1,0:T(8,128)S(1)}, u32[]{:S(2)}, u32[]{:S(2)}) collective-permute-start(f32[264,128]{1,0:T(8,128)S(1)} %get-tuple-element.43.refs_0_.message), channel_id=1, source_target_pairs={{28,0},{24,4},{20,8},{16,12},{12,16},{8,20},{4,24},{0,28},{29,1},{... | collective-permute-start | bytes 405512 | tf_op jit(solution)/shard_map/ppermute | solution.py:457
  38.8 11.1 %collective-permute-start.12 = (f32[264,128]{1,0:T(8,128)S(1)}, f32[264,128]{1,0:T(8,128)S(1)}, u32[]{:S(2)}, u32[]{:S(2)}) collective-permute-start(f32[264,128]{1,0:T(8,128)S(1)} %get-tuple-element.43.refs_0_.message), channel_id=1, source_target_pairs={{8,0},{12,4},{0,8},{4,12},{24,16},{28,20},{16,24},{20,28},{9,1},{1... | collective-permute-start | bytes 405512 | tf_op jit(solution)/shard_map/ppermute | solution.py:457
  41.3 8.5 %collective-permute-start.13 = (f32[264,128]{1,0:T(8,128)S(1)}, f32[264,128]{1,0:T(8,128)S(1)}, u32[]{:S(2)}, u32[]{:S(2)}) collective-permute-start(f32[264,128]{1,0:T(8,128)S(1)} %collective-permute-done.9.refs_0_.refs_1_), channel_id=1, source_target_pairs={{8,0},{12,4},{0,8},{4,12},{24,16},{28,20},{16,24},{20,28},{9,1},{1... | collective-permute-start | bytes 405512 | tf_op jit(solution)/shard_map/ppermute | solution.py:457
  43.0 2.4 %collective-permute-start.14 = (f32[8,128]{1,0:T(8,128)S(1)}, f32[8,128]{1,0:T(8,128)S(1)}, u32[]{:S(2)}, u32[]{:S(2)}) collective-permute-start(f32[8,128]{1,0:T(8,128)S(1)} %shard_map.139.refs_0_), channel_id=1, source_target_pairs={{8,0},{12,4},{0,8},{4,12},{24,16},{28,20},{16,24},{20,28},{9,1},{1... | collective-permute-start | bytes 12296 | tf_op jit(solution)/shard_map/ppermute | solution.py:457
  45.4 6.3 %collective-permute-start.15 = (f32[2,8,128]{2,1,0:T(8,128)S(1)}, f32[2,8,128]{2,1,0:T(8,128)S(1)}, u32[]{:S(2)}, u32[]{:S(2)}) collective-permute-start(f32[2,8,128]{2,1,0:T(8,128)S(1)} %shard_map.140.refs_0_), channel_id=1, source_target_pairs={{1,0},{0,1},{3,2},{2,3},{5,4},{4,5},{7,6},{6,7},{9,8},{8,9},{11,10... | collective-permute-start | bytes 24584 | tf_op jit(solution)/shard_map/ppermute | solution.py:461
  45.5 6.3 %collective-permute-start.16 = (f32[2,8,128]{2,1,0:T(8,128)S(1)}, f32[2,8,128]{2,1,0:T(8,128)S(1)}, u32[]{:S(2)}, u32[]{:S(2)}) collective-permute-start(f32[2,8,128]{2,1,0:T(8,128)S(1)} %shard_map.140.refs_0_), channel_id=1, source_target_pairs={{2,0},{3,1},{0,2},{1,3},{6,4},{7,5},{4,6},{5,7},{10,8},{11,9},{8,1... | collective-permute-start | bytes 24584 | tf_op jit(solution)/shard_map/ppermute | solution.py:461
  46.3 5.4 %collective-permute-start.17 = (f32[2,8,128]{2,1,0:T(8,128)S(1)}, f32[2,8,128]{2,1,0:T(8,128)S(1)}, u32[]{:S(2)}, u32[]{:S(2)}) collective-permute-start(f32[2,8,128]{2,1,0:T(8,128)S(1)} %shard_map.140.refs_0_), channel_id=1, source_target_pairs={{3,0},{2,1},{1,2},{0,3},{7,4},{6,5},{5,6},{4,7},{11,8},{10,9},{9,1... | collective-permute-start | bytes 24584 | tf_op jit(solution)/shard_map/ppermute | solution.py:461
  53.3 1.2 %collective-permute-start.18 = (f32[1,8,128]{2,1,0:T(8,128)S(1)}, f32[1,8,128]{2,1,0:T(8,128)S(1)}, u32[]{:S(2)}, u32[]{:S(2)}) collective-permute-start(f32[1,8,128]{2,1,0:T(8,128)S(1)} %shard_map.141), channel_id=1, source_target_pairs={{8,0},{12,4},{0,8},{4,12},{24,16},{28,20},{16,24},{20,28},{9,1},{1... | collective-permute-start | bytes 12296 | tf_op jit(solution)/shard_map/ppermute | solution.py:457
  54.5 3.9 %collective-permute-start.21 = (f32[1,8,128]{2,1,0:T(8,128)S(1)}, f32[1,8,128]{2,1,0:T(8,128)S(1)}, u32[]{:S(2)}, u32[]{:S(2)}) collective-permute-start(f32[1,8,128]{2,1,0:T(8,128)S(1)} %add.16), channel_id=1, source_target_pairs={{28,0},{24,4},{20,8},{16,12},{12,16},{8,20},{4,24},{0,28},{29,1},{... | collective-permute-start | bytes 12296 | tf_op jit(solution)/shard_map/ppermute | solution.py:457
  56.4 3.0 %collective-permute-start.20 = (f32[1,8,128]{2,1,0:T(8,128)S(1)}, f32[1,8,128]{2,1,0:T(8,128)S(1)}, u32[]{:S(2)}, u32[]{:S(2)}) collective-permute-start(f32[1,8,128]{2,1,0:T(8,128)S(1)} %add.16), channel_id=1, source_target_pairs={{24,0},{28,4},{16,8},{20,12},{8,16},{12,20},{0,24},{4,28},{25,1},{... | collective-permute-start | bytes 12296 | tf_op jit(solution)/shard_map/ppermute | solution.py:457
  57.7 3.6 %collective-permute-start.19 = (f32[1,8,128]{2,1,0:T(8,128)S(1)}, f32[1,8,128]{2,1,0:T(8,128)S(1)}, u32[]{:S(2)}, u32[]{:S(2)}) collective-permute-start(f32[1,8,128]{2,1,0:T(8,128)S(1)} %add.16), channel_id=1, source_target_pairs={{4,0},{0,4},{12,8},{8,12},{20,16},{16,20},{28,24},{24,28},{5,1},{1... | collective-permute-start | bytes 12296 | tf_op jit(solution)/shard_map/ppermute | solution.py:457
  61.3 4.4 %collective-permute-start.22 = (f32[1,8,128]{2,1,0:T(8,128)S(1)}, f32[1,8,128]{2,1,0:T(8,128)S(1)}, u32[]{:S(2)}, u32[]{:S(2)}) collective-permute-start(f32[1,8,128]{2,1,0:T(8,128)S(1)} %add_add_fusion.refs_0_), channel_id=1, source_target_pairs={{1,0},{0,1},{3,2},{2,3},{5,4},{4,5},{7,6},{6,7},{9,8},{8,9},{11,10... | collective-permute-start | bytes 12296 | tf_op jit(solution)/shard_map/ppermute | solution.py:461
  61.6 5.4 %collective-permute-start.23 = (f32[1,8,128]{2,1,0:T(8,128)S(1)}, f32[1,8,128]{2,1,0:T(8,128)S(1)}, u32[]{:S(2)}, u32[]{:S(2)}) collective-permute-start(f32[1,8,128]{2,1,0:T(8,128)S(1)} %add_add_fusion.refs_0_), channel_id=1, source_target_pairs={{2,0},{3,1},{0,2},{1,3},{6,4},{7,5},{4,6},{5,7},{10,8},{11,9},{8,1... | collective-permute-start | bytes 12296 | tf_op jit(solution)/shard_map/ppermute | solution.py:461
  65.4 5.4 %collective-permute-start.24 = (f32[1,8,128]{2,1,0:T(8,128)S(1)}, f32[1,8,128]{2,1,0:T(8,128)S(1)}, u32[]{:S(2)}, u32[]{:S(2)}) collective-permute-start(f32[1,8,128]{2,1,0:T(8,128)S(1)} %add_add_fusion.refs_0_), channel_id=1, source_target_pairs={{3,0},{2,1},{1,2},{0,3},{7,4},{6,5},{5,6},{4,7},{11,8},{10,9},{9,1... | collective-permute-start | bytes 12296 | tf_op jit(solution)/shard_map/ppermute | solution.py:461
  (5 other events, 4.0 us)

commit v5 on v4

--- a/solution.py
+++ b/solution.py
@@ -141,15 +141,25 @@
     return jnp.concatenate([pack_rim(x, s), charges], axis=0)
 
 
-def start_kernel(s, rhs, cells, weight, message_out, col_out, f_out):
+def begin(sources, targets, sems):
+    moves = [pltpu.make_async_copy(a, b, sems.at[i]) for i, (a, b) in enumerate(zip(sources, targets))]
+    for move in moves:
+        move.start()
+    return moves
+
+
+def start_kernel(s, rhs, cells, weight, message_out, col_out, cells_out, f_out, raw, wide, sems):
+    moves = begin((weight, cells, rhs), (wide, cells_out, raw), sems)
     f_out[...] = jnp.zeros_like(f_out)
+    moves[0].wait()
+    row = jnp.concatenate([wide[...], jnp.zeros((1, 2 * LANES - s.blobs), f32)], axis=1)
+    col = jnp.broadcast_to(row, (LANES, 2 * LANES)).T[: s.step]
+    col_out[...] = col
+    for move in moves[1:]:
+        move.wait()
     for c in range(3):
-        f_out[c * s.step : c * s.step + s.blobs, :] = rhs[0, 0, c]
-    f = f_out[...]
-    wide = jnp.concatenate([weight[...], jnp.zeros((1, 2 * LANES - s.blobs), f32)], axis=1)
-    col = jnp.broadcast_to(wide, (LANES, 2 * LANES)).T[: s.step]
-    col_out[...] = col
-    message_out[...] = pack_message(f, col[:, :1], cells[0], s)
+        f_out[c * s.step : c * s.step + s.blobs, :] = raw[c * s.blobs : (c + 1) * s.blobs, 0, :]
+    message_out[...] = pack_message(f_out[...], col[:, :1], cells_out[0], s)
 
 
 def frame_rows(angles):
@@ -186,24 +196,25 @@
 
 
 def setup_kernel(
-    s, ids, f_in, angles, self_mob, near_mat, near_weight, neighbours, perm, interp, sibling, root,
+    s, ids, f_in, *refs
+):
+    count = 9
+    sources, refs = refs[:count], refs[count:]
+    copies, refs = refs[-1 - count :], refs[: -1 - count]
+    copies, sems = copies[:-1], copies[-1]
+    setup(s, ids, f_in, begin(sources, copies, sems), *copies, *refs)
+
+
+def setup(
+    s, ids, f_in, moves, angles, near_weight, neighbours, self_mob, near_mat, perm, interp, sibling, root,
     loc_out, gat_out, rot_out, sh_out, sl_out, nh_out, nl_out, oh_out, ol_out, gh_out, gl_out,
     far_out, padded, ups_ref,
 ):
     f = f_in[...]
-    rot = jnp.concatenate(frame_rows(angles[0, 0]) + [jnp.zeros((7, s.bodies), f32)], axis=0)
+    for move in moves[:3]:
+        move.wait()
+    rot = jnp.concatenate(frame_rows(angles[:, 0, :]) + [jnp.zeros((7, s.bodies), f32)], axis=0)
     rot_out[...] = rot
-
-    padded[...] = jnp.zeros_like(padded)
-    for matrix, hi_out, lo_out in ((self_mob, sh_out, sl_out), (near_mat, nh_out, nl_out)):
-        for c in range(3):
-            for d in range(3):
-                padded[c * s.step : c * s.step + s.blobs, d * s.step : d * s.step + s.blobs] = matrix[
-                    c * s.blobs : (c + 1) * s.blobs, d * s.blobs : (d + 1) * s.blobs
-                ]
-        hi, lo = split(padded[...])
-        hi_out[...] = hi
-        lo_out[...] = lo
 
     links = neighbours[0, 0]
     slot = links // s.bodies
@@ -227,6 +238,19 @@
             hi_out[r : r + 64, :] = hi
             lo_out[r : r + 64, :] = lo
 
+    for move in moves[3:]:
+        move.wait()
+    padded[...] = jnp.zeros_like(padded)
+    for matrix, hi_out, lo_out in ((self_mob, sh_out, sl_out), (near_mat, nh_out, nl_out)):
+        for c in range(3):
+            for d in range(3):
+                padded[c * s.step : c * s.step + s.blobs, d * s.step : d * s.step + s.blobs] = matrix[
+                    c * s.blobs : (c + 1) * s.blobs, d * s.blobs : (d + 1) * s.blobs
+                ]
+        hi, lo = split(padded[...])
+        hi_out[...] = hi
+        lo_out[...] = lo
+
     loc, gat = local_part(f, s, rot, (sh_out[...], sl_out[...]), (oh_out[...], ol_out[...]))
     loc_out[...] = loc
     gat_out[...] = gat
@@ -272,7 +296,7 @@
 
 
 def half_kernel(s, *refs):
-    *messages, out = refs
+    *messages, _, out = refs
     acc = messages[0][s.half :, :]
     for message in messages[1:]:
         acc = acc + message[s.half :, :]
@@ -363,7 +387,7 @@
     )
 
 
-def second_kernel(s, ids, part, far_op, cells, col, f_in, ortho_in, stat, *refs):
+def second_kernel(s, part, far_op, cells, col, f_in, ortho_in, stat, *refs):
     *layers, stat_out = refs
     t = with_far(s, part, layers, far_op, cells, col[:, :1])
     f, ortho = f_in[...], ortho_in[...]
@@ -376,19 +400,16 @@
     stats = jnp.concatenate(
         [rf, rf * fu, ro, rf * ft, ro * ot, jnp.sqrt(tt), jnp.zeros((2, 1), f32)], axis=0
     )
-    device = ids[0] * s.nz + ids[1]
+    stat_out[...] = jnp.broadcast_to(jnp.broadcast_to(stats, (8, LANES))[None], stat_out.shape)
+
+
+def finish_kernel(s, f_in, u_in, stats, x_out, lsq_out, raw, sem):
+    groups = []
     for g in range(s.groups):
         lane = lax.broadcasted_iota(jnp.int32, (8, LANES), 1) + g * LANES
-        stat_out[g] = jnp.where(lane == device, stats, 0.0)
-
-
-def finish_kernel(s, rhs, u_in, *refs):
-    *stats, x_out, lsq_out = refs
-    groups = []
-    for g in range(s.groups):
-        acc = stats[0][g]
-        for part in stats[1:]:
-            acc = acc + part[g]
+        acc = jnp.zeros((8, LANES), f32)
+        for d in range(g * LANES, min(s.devices, (g + 1) * LANES)):
+            acc = acc + jnp.where(lane == d, stats[d], 0.0)
         groups.append(acc)
     rows = jnp.concatenate(groups, axis=1) if len(groups) > 1 else groups[0]
     f1, u1, u2, t1, t2, t3 = (rows[i : i + 1] for i in range(6))
@@ -420,17 +441,24 @@
     on_u = y2 / h21 / beta
     on_f = y1 / beta - on_u * h11
     for c in range(3):
-        x_out[0, 0, c] = on_f * rhs[0, 0, c] + on_u * u_in[c * s.step : c * s.step + s.blobs, :]
-
-
-def call(kernel, outs, args, scalars=0, scratch=(), flops=0):
+        part = slice(c * s.step, c * s.step + s.blobs)
+        raw[c * s.blobs : (c + 1) * s.blobs, 0, :] = on_f * f_in[part, :] + on_u * u_in[part, :]
+    move = pltpu.make_async_copy(raw, x_out, sem)
+    move.start()
+    move.wait()
+
+
+def call(kernel, outs, args, scalars=0, far_args=0, far_outs=0, scratch=(), flops=0):
     vmem = pl.BlockSpec(memory_space=pltpu.VMEM)
     smem = pl.BlockSpec(memory_space=pltpu.SMEM)
+    hbm = pl.BlockSpec(memory_space=pltpu.HBM)
+    near_args = len(args) - far_args
+    args = args[:near_args] + [pltpu.with_memory_space_constraint(x, pltpu.HBM) for x in args[near_args:]]
     return pl.pallas_call(
         kernel,
         out_shape=[jax.ShapeDtypeStruct(shape, kind) for shape, kind in outs],
-        in_specs=[smem] * scalars + [vmem] * (len(args) - scalars),
-        out_specs=[vmem] * len(outs),
+        in_specs=[smem] * scalars + [vmem] * (near_args - scalars) + [hbm] * far_args,
+        out_specs=[hbm] * far_outs + [vmem] * (len(outs) - far_outs),
         scratch_shapes=list(scratch),
         compiler_params=pltpu.CompilerParams(vmem_limit_bytes=16 * 2**20),
         cost_estimate=pl.CostEstimate(flops=flops, bytes_accessed=2**20, transcendentals=0),
@@ -473,10 +501,10 @@
             got["partner", dy] = fetch(got["same", dy], "partner", 0)
         return got
 
-    def share_charges(message, got):
+    def share_charges(message, got, after):
         if s.direct:
             quarter = [message] + [got[key] for key in s.sources if key[0] != "partner"]
-            (half,) = call(functools.partial(half_kernel, s), [(tile, f32)], quarter)
+            (half,) = call(functools.partial(half_kernel, s), [(tile, f32)], quarter + [after])
             sums = [half, fetch(half, "partner", 0)]
         else:
             sums = [lax.psum(message[s.half :], ("gx", "gy"))]
@@ -491,13 +519,21 @@
             flops=10**9,
         )[0]
 
-    message, col, f = call(
+    flat = (3 * s.blobs, 1, s.bodies)
+    small = (1, s.blobs)
+    message, col, cells, f = call(
         functools.partial(start_kernel, s),
-        [((s.message, LANES), f32), ((s.step, LANES), f32), (full, f32)],
-        [rhs, cells, blob_weight.reshape(1, -1)],
+        [((s.message, LANES), f32), ((s.step, LANES), f32), (cells.shape, jnp.int32), (full, f32)],
+        [rhs.reshape(flat), cells, blob_weight.reshape(small)],
+        far_args=3,
+        scratch=[pltpu.VMEM(flat, f32), pltpu.VMEM(small, f32), pltpu.SemaphoreType.DMA((3,))],
         flops=10**7,
     )
     got = fetch_messages(message)
+    operators = [
+        angles.reshape(3, 1, s.bodies), near_weight, neighbours, self_mob, near_mat, skel_perm, interp,
+        sibling_ops, root_op,
+    ]
     loc, gat, rot, sh, sl, nh, nl, oh, ol, gh, gl, far_op = call(
         functools.partial(setup_kernel, s),
         [(full, f32), (full, f32), ((16, s.bodies), f32)]
@@ -505,13 +541,16 @@
         + [((s.bodies, s.bodies), bf16)] * 2
         + [((s.ghosts, s.bodies), bf16)] * 2
         + [(far_shape, f32)],
-        [ids, f, angles, self_mob, near_mat, near_weight, neighbours, skel_perm, interp, sibling_ops, root_op],
+        [ids, f] + operators,
         scalars=1,
-        scratch=[pltpu.VMEM(square, f32), pltpu.VMEM((s.levels, 2 * s.skel, s.skel), f32)],
+        far_args=len(operators),
+        scratch=[pltpu.VMEM(square, f32), pltpu.VMEM((s.levels, 2 * s.skel, s.skel), f32)]
+        + [pltpu.VMEM(x.shape, x.dtype) for x in operators]
+        + [pltpu.SemaphoreType.DMA((len(operators),))],
         flops=5 * 10**9,
     )
     part = near_part(loc, gat, got)
-    layers = share_charges(message, got)
+    layers = share_charges(message, got, rot)
     u, message = call(
         functools.partial(first_kernel, s),
         [(full, f32), ((s.message, LANES), f32)],
@@ -526,26 +565,23 @@
         flops=10**9,
     )
     part = near_part(loc, gat, got)
-    layers = share_charges(message, got)
+    layers = share_charges(message, got, stat)
     (stats,) = call(
         functools.partial(second_kernel, s),
-        [((s.groups,) + tile, f32)],
-        [ids, part, far_op, cells, col, f, ortho, stat, *layers],
-        scalars=1,
+        [((s.devices,) + tile, f32)],
+        [part, far_op, cells, col, f, ortho, stat, *layers],
         flops=10**8,
     )
-    if s.direct:
-        stats = stats + fetch(stats, "partner", 0)
-        stats = stats + fetch(stats, "same", 1) + fetch(stats, "other", 0) + fetch(stats, "other", 1)
-    else:
-        stats = lax.psum(stats, ("gx", "gy"))
+    stats = lax.all_to_all(stats, ("gx", "gy", "gz"), 0, 0)
     result, lsq = call(
         functools.partial(finish_kernel, s),
-        [(rhs.shape, f32), ((1, 1), f32)],
-        [rhs, u, *fetch_layers(stats)],
+        [(flat, f32), ((1, 1), f32)],
+        [f, u, stats],
+        far_outs=1,
+        scratch=[pltpu.VMEM(flat, f32), pltpu.SemaphoreType.DMA],
         flops=10**7,
     )
-    return result, lsq.reshape(())
+    return result.reshape(rhs.shape), lsq.reshape(())
 
 
 def solution(mesh):

time: 73.4 us -> 59.8 us (0.81)
  blocking collectives: 0 us -> 11.8 us
  waiting for transfers between devices: 24.5 us -> 12.8 us
  local copies, waits for them, and re-layouts: 8.64 us -> 0 us
  starting transfers between devices: 26.2 us -> 18.5 us
  Pallas kernels: 12.9 us -> 15.8 us
    all_to_all x0 -> x1, blocking collectives: none -> 11.8 us  [body(): stats = lax.all_to_all(stats, ('gx', 'gy', 'gz'), 0, 0)]
    unnamed x27 -> x0, local copies, waits for them, and re-layouts: 8.64 us -> none
    ppermute x16 -> x12, waiting for transfers between devices: 16 us -> 9.3 us  [fetch(): return lax.ppermute(x, ('gx', 'gy'), pairs)]
    ppermute x9 -> x6, waiting for transfers between devices: 8.44 us -> 3.52 us  [fetch_layers(): lax.ppermute(x, 'gz', [(z ^ k, z) for z in range(s.nz)])]
    ppermute x9 -> x6, starting transfers between devices: 13.3 us -> 8.77 us  [fetch_layers(): lax.ppermute(x, 'gz', [(z ^ k, z) for z in range(s.nz)])]
    ppermute x16 -> x12, starting transfers between devices: 12.9 us -> 9.69 us  [fetch(): return lax.ppermute(x, ('gx', 'gy'), pairs)]
    pallas_call x12, Pallas kernels: 12.9 us -> 15.8 us  [call(): pl.pallas_call(kernel, out_shape=[jax.ShapeDtypeStruct(shape, kind) for s...]
  transfers between devices with their start and end apart: 25 -> 18, of which waited for: 12 -> 6; matrix products, arithmetic and copies ran while one was open for 0% -> 0% of each run, Pallas kernels for 13% -> 18%
where the time goes in v5:
time: 59.8 us; the launch traced here: 59.6 us
  starting transfers between devices  18.5 us (31%)
  Pallas kernels  15.8 us (26%)
  waiting for transfers between devices  12.8 us (21%)
  blocking collectives  11.8 us (20%)
  between operations  0.74 us (1%)
    pallas_call x12, Pallas kernels, call(): pl.pallas_call(kernel, out_shape=[jax.ShapeDtypeStruct(shape, kind) for s...  15.8 us
    all_to_all x1, blocking collectives, body(): stats = lax.all_to_all(stats, ('gx', 'gy', 'gz'), 0, 0)  11.8 us
    ppermute x12, starting transfers between devices, fetch(): return lax.ppermute(x, ('gx', 'gy'), pairs)  9.69 us
    ppermute x12, waiting for transfers between devices, fetch(): return lax.ppermute(x, ('gx', 'gy'), pairs)  9.3 us
    ppermute x6, starting transfers between devices, fetch_layers(): lax.ppermute(x, 'gz', [(z ^ k, z) for z in range(s.nz)])  8.77 us
    ppermute x6, waiting for transfers between devices, fetch_layers(): lax.ppermute(x, 'gz', [(z ^ k, z) for z in range(s.nz)])  3.52 us
  transfers between devices with their start and end apart: 18, of which 6 were waited for; matrix products, arithmetic and copies ran while one was open for 0% of the time, Pallas kernels for 18%

profile of v5, /device:TPU:0, one launch (start us, length us, event | category | flops | bytes accessed | tf_op | source)
XLA Modules:
  0.0 59.6 jit_solution(14779721842590429129)
XLA Ops:
  0.6 1.4 %shard_map.131 = (f32[264,128]{1,0:T(8,128)S(1)}, f32[168,128]{1,0:T(8,128)S(1)}, s32[1,1,256]{2,1,0:T(1,128)S(1)}, f32[512,256]{1,0:T(8,128)S(1)}) custom-call(f32[486,1,256]{2,1,0:T(1,128)} %bitcast.9, s32[1,1,256]{2,1,0:T(1,128)} %cells.1, f32[1,162]{1,0:T(1,128)} %bitcast.10), custom_call_target="tpu_custom_call" | custom-call | flops 10000000 | bytes 1048576 | tf_op jit(solution)/shard_map/pallas_call | solution.py:457
  2.1 3.0 %collective-permute-start = (f32[264,128]{1,0:T(8,128)S(1)}, f32[264,128]{1,0:T(8,128)S(1)}, u32[]{:S(2)}, u32[]{:S(2)}) collective-permute-start(f32[264,128]{1,0:T(8,128)S(1)} %get-tuple-element.33.refs_0_.message), channel_id=1, source_target_pairs={{4,0},{0,4},{12,8},{8,12},{20,16},{16,20},{28,24},{24,28},{5,1},{1... | collective-permute-start | bytes 405512 | tf_op jit(solution)/shard_map/ppermute | solution.py:485
  5.1 0.7 %collective-permute-start.1 = (f32[264,128]{1,0:T(8,128)S(1)}, f32[264,128]{1,0:T(8,128)S(1)}, u32[]{:S(2)}, u32[]{:S(2)}) collective-permute-start(f32[264,128]{1,0:T(8,128)S(1)} %get-tuple-element.33.refs_0_.message), channel_id=1, source_target_pairs={{24,0},{28,4},{16,8},{20,12},{8,16},{12,20},{0,24},{4,28},{25,1},{... | collective-permute-start | bytes 405512 | tf_op jit(solution)/shard_map/ppermute | solution.py:485
  5.7 0.6 collective-permute-start.2
  6.3 0.4 collective-permute-start.3
  6.7 0.1 pad_add_fusion.ids
  6.8 2.0 %collective-permute-done.refs_0_.refs_1_ = f32[264,128]{1,0:T(8,128)S(1)} collective-permute-done((f32[264,128]{1,0:T(8,128)S(1)}, f32[264,128]{1,0:T(8,128)S(1)}, u32[]{:S(2)}, u32[]{:S(2)}) %collective-permute-start) | collective-permute-done | bytes 135200 | tf_op jit(solution)/shard_map/ppermute | solution.py:485
  8.7 0.0 collective-permute-start.4
  8.7 5.9 %shard_map.132 = (f32[512,256]{1,0:T(8,128)S(1)}, f32[512,256]{1,0:T(8,128)S(1)}, f32[16,256]{1,0:T(8,128)S(1)}, bf16[512,512]{1,0:T(8,128)(2,1)S(1)}, bf16[512,...) custom-call(s32[2]{0:T(128)S(1)} %pad_add_fusion.ids, ...), custom_call_target="tpu_custom_call" | custom-call | flops 5000000000 | bytes 1048576 | tf_op jit(solution)/shard_map/pallas_call | solution.py:457
  14.7 0.6 collective-permute-start.5
  15.3 0.8 %collective-permute-done.5.refs_1_ = f32[8,128]{1,0:T(8,128)S(1)} collective-permute-done((f32[8,128]{1,0:T(8,128)S(1)}, f32[8,128]{1,0:T(8,128)S(1)}, u32[]{:S(2)}, u32[]{:S(2)}) %collective-permute-start.5) | collective-permute-done | bytes 4128 | tf_op jit(solution)/shard_map/ppermute | solution.py:485
  16.1 1.7 %collective-permute-start.6 = (f32[2,8,128]{2,1,0:T(8,128)S(1)}, f32[2,8,128]{2,1,0:T(8,128)S(1)}, u32[]{:S(2)}, u32[]{:S(2)}) collective-permute-start(f32[2,8,128]{2,1,0:T(8,128)S(1)} %shard_map.135.refs_0_), channel_id=1, source_target_pairs={{1,0},{0,1},{3,2},{2,3},{5,4},{4,5},{7,6},{6,7},{9,8},{8,9},{11,10... | collective-permute-start | bytes 24584 | tf_op jit(solution)/shard_map/ppermute | solution.py:489
  17.8 2.6 %collective-permute-start.7 = (f32[2,8,128]{2,1,0:T(8,128)S(1)}, f32[2,8,128]{2,1,0:T(8,128)S(1)}, u32[]{:S(2)}, u32[]{:S(2)}) collective-permute-start(f32[2,8,128]{2,1,0:T(8,128)S(1)} %shard_map.135.refs_0_), channel_id=1, source_target_pairs={{2,0},{3,1},{0,2},{1,3},{6,4},{7,5},{4,6},{5,7},{10,8},{11,9},{8,1... | collective-permute-start | bytes 24584 | tf_op jit(solution)/shard_map/ppermute | solution.py:489
  20.4 0.0 collective-permute-start.8
  20.5 1.9 %shard_map.133.part = f32[512,256]{1,0:T(8,128)S(1)} custom-call(f32[512,256]{1,0:T(8,128)S(1)} %get-tuple-element.27.loc, f32[512,256]{1,0:T(8,128)S(1)} %get-tuple-element.28.gat, bf16[512,512]{1,0:T(8,128)(2,1)S(1)} %get-tuple-element.29.nh, bf16[512,512]{1,0:T(8,128)(2,1)S(1)} %get-tuple-element.30.nl, bf16[384,256]{1,0:T(8,128)(2,1)S(1)} %get-tuple-element.31.gh, ...), custom_call_target="tpu_custom_call" | custom-call | flops 1000000000 | bytes 1048576 | tf_op jit(solution)/shard_map/pallas_call | solution.py:457
  22.4 3.5 %collective-permute-done.8.refs_3_ = f32[2,8,128]{2,1,0:T(8,128)S(1)} collective-permute-done((f32[2,8,128]{2,1,0:T(8,128)S(1)}, f32[2,8,128]{2,1,0:T(8,128)S(1)}, u32[]{:S(2)}, u32[]{:S(2)}) %collective-permute-start.8) | collective-permute-done | bytes 8224 | tf_op jit(solution)/shard_map/ppermute | solution.py:489
  25.9 0.6 %shard_map.136 = (f32[512,256]{1,0:T(8,128)S(1)}, f32[264,128]{1,0:T(8,128)S(1)}) custom-call(f32[512,256]{1,0:T(8,128)S(1)} %shard_map.133.part, f32[192,1536]{1,0:T(8,128)S(1)} %get-tuple-element.34.far_op, s32[1,1,256]{2,1,0:T(1,128)S(1)} %get-tuple-element.35.cells, f32[168,128]{1,0:T(8,128)S(1)} %get-tuple-element.36.col, ...), custom_call_target="tpu_custom_call" | custom-call | flops 100000000 | bytes 1048576 | tf_op jit(solution)/shard_map/pallas_call | solution.py:457
  26.5 2.3 %collective-permute-start.9 = (f32[264,128]{1,0:T(8,128)S(1)}, f32[264,128]{1,0:T(8,128)S(1)}, u32[]{:S(2)}, u32[]{:S(2)}) collective-permute-start(f32[264,128]{1,0:T(8,128)S(1)} %get-tuple-element.45.refs_0_.message), channel_id=1, source_target_pairs={{4,0},{0,4},{12,8},{8,12},{20,16},{16,20},{28,24},{24,28},{5,1},{1... | collective-permute-start | bytes 405512 | tf_op jit(solution)/shard_map/ppermute | solution.py:485
  28.8 1.2 %collective-permute-start.11 = (f32[264,128]{1,0:T(8,128)S(1)}, f32[264,128]{1,0:T(8,128)S(1)}, u32[]{:S(2)}, u32[]{:S(2)}) collective-permute-start(f32[264,128]{1,0:T(8,128)S(1)} %get-tuple-element.45.refs_0_.message), channel_id=1, source_target_pairs={{28,0},{24,4},{20,8},{16,12},{12,16},{8,20},{4,24},{0,28},{29,1},{... | collective-permute-start | bytes 405512 | tf_op jit(solution)/shard_map/ppermute | solution.py:485
  30.1 0.7 %collective-permute-start.12 = (f32[264,128]{1,0:T(8,128)S(1)}, f32[264,128]{1,0:T(8,128)S(1)}, u32[]{:S(2)}, u32[]{:S(2)}) collective-permute-start(f32[264,128]{1,0:T(8,128)S(1)} %get-tuple-element.45.refs_0_.message), channel_id=1, source_target_pairs={{8,0},{12,4},{0,8},{4,12},{24,16},{28,20},{16,24},{20,28},{9,1},{1... | collective-permute-start | bytes 405512 | tf_op jit(solution)/shard_map/ppermute | solution.py:485
  30.8 1.0 %collective-permute-done.9.refs_0_.refs_1_ = f32[264,128]{1,0:T(8,128)S(1)} collective-permute-done((f32[264,128]{1,0:T(8,128)S(1)}, f32[264,128]{1,0:T(8,128)S(1)}, u32[]{:S(2)}, u32[]{:S(2)}) %collective-permute-start.9) | collective-permute-done | bytes 135200 | tf_op jit(solution)/shard_map/ppermute | solution.py:485
  31.8 1.0 %shard_map.137 = (f32[512,256]{1,0:T(8,128)S(1)}, f32[512,256]{1,0:T(8,128)S(1)}, f32[512,256]{1,0:T(8,128)S(1)}, f32[8,128]{1,0:T(8,128)S(1)}) custom-call(f32[512,256]{1,0:T(8,128)S(1)} %get-tuple-element.38.u_in, f32[512,256]{1,0:T(8,128)S(1)} %get-tuple-element.26.f_in, f32[16,256]{1,0:T(8,128)S(1)} %get-tuple-element.37.refs_4_.rot, ...), custom_call_target="tpu_custom_call" | custom-call | flops 1000000000 | bytes 1048576 | tf_op jit(solution)/shard_map/pallas_call | solution.py:457
  32.8 4.4 %collective-permute-done.10.refs_1_.refs_2_ = f32[264,128]{1,0:T(8,128)S(1)} collective-permute-done((f32[264,128]{1,0:T(8,128)S(1)}, f32[264,128]{1,0:T(8,128)S(1)}, u32[]{:S(2)}, u32[]{:S(2)}) %collective-permute-start.10) | collective-permute-done | bytes 135200 | tf_op jit(solution)/shard_map/ppermute | solution.py:485
  37.3 0.2 collective-permute-start.14
  37.5 1.0 %collective-permute-done.14.refs_1_ = f32[8,128]{1,0:T(8,128)S(1)} collective-permute-done((f32[8,128]{1,0:T(8,128)S(1)}, f32[8,128]{1,0:T(8,128)S(1)}, u32[]{:S(2)}, u32[]{:S(2)}) %collective-permute-start.14) | collective-permute-done | bytes 4128 | tf_op jit(solution)/shard_map/ppermute | solution.py:485
  38.5 0.9 %collective-permute-start.16 = (f32[2,8,128]{2,1,0:T(8,128)S(1)}, f32[2,8,128]{2,1,0:T(8,128)S(1)}, u32[]{:S(2)}, u32[]{:S(2)}) collective-permute-start(f32[2,8,128]{2,1,0:T(8,128)S(1)} %shard_map.140.refs_0_), channel_id=1, source_target_pairs={{2,0},{3,1},{0,2},{1,3},{6,4},{7,5},{4,6},{5,7},{10,8},{11,9},{8,1... | collective-permute-start | bytes 24584 | tf_op jit(solution)/shard_map/ppermute | solution.py:489
  39.4 3.5 %collective-permute-start.17 = (f32[2,8,128]{2,1,0:T(8,128)S(1)}, f32[2,8,128]{2,1,0:T(8,128)S(1)}, u32[]{:S(2)}, u32[]{:S(2)}) collective-permute-start(f32[2,8,128]{2,1,0:T(8,128)S(1)} %shard_map.140.refs_0_), channel_id=1, source_target_pairs={{3,0},{2,1},{1,2},{0,3},{7,4},{6,5},{5,6},{4,7},{11,8},{10,9},{9,1... | collective-permute-start | bytes 24584 | tf_op jit(solution)/shard_map/ppermute | solution.py:489
  42.9 1.9 %shard_map.138.part = f32[512,256]{1,0:T(8,128)S(1)} custom-call(f32[512,256]{1,0:T(8,128)S(1)} %get-tuple-element.43.loc, f32[512,256]{1,0:T(8,128)S(1)} %get-tuple-element.44.gat, bf16[512,512]{1,0:T(8,128)(2,1)S(1)} %get-tuple-element.29.nh, bf16[512,512]{1,0:T(8,128)(2,1)S(1)} %get-tuple-element.30.nl, bf16[384,256]{1,0:T(8,128)(2,1)S(1)} %get-tuple-element.31.gh, ...), custom_call_target="tpu_custom_call" | custom-call | flops 1000000000 | bytes 1048576 | tf_op jit(solution)/shard_map/pallas_call | solution.py:457
  44.8 0.0 collective-permute-done.17.refs_3_
  44.8 1.0 %shard_map.141 = f32[32,8,128]{2,1,0:T(8,128)S(1)} custom-call(f32[512,256]{1,0:T(8,128)S(1)} %shard_map.138.part, f32[192,1536]{1,0:T(8,128)S(1)} %get-tuple-element.34.far_op, s32[1,1,256]{2,1,0:T(1,128)S(1)} %get-tuple-element.35.cells, f32[168,128]{1,0:T(8,128)S(1)} %get-tuple-element.36.col, f32[512,256]{1,0:T(8,128)S(1)} %get-tuple-element.26.f_in, ...), custom_call_target="tpu_custom_call" | custom-call | flops 100000000 | bytes 1048576 | tf_op jit(solution)/shard_map/pallas_call | solution.py:457
  45.8 11.8 %all_to_all.5.stats = f32[32,8,128]{2,1,0:T(8,128)S(1)} all-to-all(f32[32,8,128]{2,1,0:T(8,128)S(1)} %shard_map.141), channel_id=1, replica_groups=mesh['gx'=4,'gy'=2,'gz'=4] {'gx','gy','gz'}, dimensions={0} | all-to-all | bytes 262144 | tf_op jit(solution)/shard_map/all_to_all | solution.py:575
  57.6 2.0 %shard_map.142 = (f32[486,1,256]{2,1,0:T(1,128)}, f32[1,1]{1,0:T(1,128)}) custom-call(f32[512,256]{1,0:T(8,128)S(1)} %get-tuple-element.26.f_in, f32[512,256]{1,0:T(8,128)S(1)} %get-tuple-element.38.u_in, f32[32,8,128]{2,1,0:T(8,128)S(1)} %all_to_all.5.stats), custom_call_target="tpu_custom_call" | custom-call | flops 10000000 | bytes 1048576 | tf_op jit(solution)/shard_map/pallas_call | solution.py:457
  (18 shorter events, 0.1 us)
Async XLA Ops:
  2.1 6.7 %collective-permute-start = (f32[264,128]{1,0:T(8,128)S(1)}, f32[264,128]{1,0:T(8,128)S(1)}, u32[]{:S(2)}, u32[]{:S(2)}) collective-permute-start(f32[264,128]{1,0:T(8,128)S(1)} %get-tuple-element.33.refs_0_.message), channel_id=1, source_target_pairs={{4,0},{0,4},{12,8},{8,12},{20,16},{16,20},{28,24},{24,28},{5,1},{1... | collective-permute-start | bytes 405512 | tf_op jit(solution)/shard_map/ppermute | solution.py:485
  5.1 9.6 %collective-permute-start.1 = (f32[264,128]{1,0:T(8,128)S(1)}, f32[264,128]{1,0:T(8,128)S(1)}, u32[]{:S(2)}, u32[]{:S(2)}) collective-permute-start(f32[264,128]{1,0:T(8,128)S(1)} %get-tuple-element.33.refs_0_.message), channel_id=1, source_target_pairs={{24,0},{28,4},{16,8},{20,12},{8,16},{12,20},{0,24},{4,28},{25,1},{... | collective-permute-start | bytes 405512 | tf_op jit(solution)/shard_map/ppermute | solution.py:485
  5.7 8.9 %collective-permute-start.2 = (f32[264,128]{1,0:T(8,128)S(1)}, f32[264,128]{1,0:T(8,128)S(1)}, u32[]{:S(2)}, u32[]{:S(2)}) collective-permute-start(f32[264,128]{1,0:T(8,128)S(1)} %get-tuple-element.33.refs_0_.message), channel_id=1, source_target_pairs={{28,0},{24,4},{20,8},{16,12},{12,16},{8,20},{4,24},{0,28},{29,1},{... | collective-permute-start | bytes 405512 | tf_op jit(solution)/shard_map/ppermute | solution.py:485
  6.3 14.2 %collective-permute-start.3 = (f32[264,128]{1,0:T(8,128)S(1)}, f32[264,128]{1,0:T(8,128)S(1)}, u32[]{:S(2)}, u32[]{:S(2)}) collective-permute-start(f32[264,128]{1,0:T(8,128)S(1)} %get-tuple-element.33.refs_0_.message), channel_id=1, source_target_pairs={{8,0},{12,4},{0,8},{4,12},{24,16},{28,20},{16,24},{20,28},{9,1},{1... | collective-permute-start | bytes 405512 | tf_op jit(solution)/shard_map/ppermute | solution.py:485
  8.7 11.8 %collective-permute-start.4 = (f32[264,128]{1,0:T(8,128)S(1)}, f32[264,128]{1,0:T(8,128)S(1)}, u32[]{:S(2)}, u32[]{:S(2)}) collective-permute-start(f32[264,128]{1,0:T(8,128)S(1)} %collective-permute-done.refs_0_.refs_1_), channel_id=1, source_target_pairs={{8,0},{12,4},{0,8},{4,12},{24,16},{28,20},{16,24},{20,28},{9,1},{1... | collective-permute-start | bytes 405512 | tf_op jit(solution)/shard_map/ppermute | solution.py:485
  14.7 1.4 %collective-permute-start.5 = (f32[8,128]{1,0:T(8,128)S(1)}, f32[8,128]{1,0:T(8,128)S(1)}, u32[]{:S(2)}, u32[]{:S(2)}) collective-permute-start(f32[8,128]{1,0:T(8,128)S(1)} %shard_map.134.refs_0_), channel_id=1, source_target_pairs={{8,0},{12,4},{0,8},{4,12},{24,16},{28,20},{16,24},{20,28},{9,1},{1... | collective-permute-start | bytes 12296 | tf_op jit(solution)/shard_map/ppermute | solution.py:485
  16.1 6.3 %collective-permute-start.6 = (f32[2,8,128]{2,1,0:T(8,128)S(1)}, f32[2,8,128]{2,1,0:T(8,128)S(1)}, u32[]{:S(2)}, u32[]{:S(2)}) collective-permute-start(f32[2,8,128]{2,1,0:T(8,128)S(1)} %shard_map.135.refs_0_), channel_id=1, source_target_pairs={{1,0},{0,1},{3,2},{2,3},{5,4},{4,5},{7,6},{6,7},{9,8},{8,9},{11,10... | collective-permute-start | bytes 24584 | tf_op jit(solution)/shard_map/ppermute | solution.py:489
  17.8 4.6 %collective-permute-start.7 = (f32[2,8,128]{2,1,0:T(8,128)S(1)}, f32[2,8,128]{2,1,0:T(8,128)S(1)}, u32[]{:S(2)}, u32[]{:S(2)}) collective-permute-start(f32[2,8,128]{2,1,0:T(8,128)S(1)} %shard_map.135.refs_0_), channel_id=1, source_target_pairs={{2,0},{3,1},{0,2},{1,3},{6,4},{7,5},{4,6},{5,7},{10,8},{11,9},{8,1... | collective-permute-start | bytes 24584 | tf_op jit(solution)/shard_map/ppermute | solution.py:489
  20.4 5.4 %collective-permute-start.8 = (f32[2,8,128]{2,1,0:T(8,128)S(1)}, f32[2,8,128]{2,1,0:T(8,128)S(1)}, u32[]{:S(2)}, u32[]{:S(2)}) collective-permute-start(f32[2,8,128]{2,1,0:T(8,128)S(1)} %shard_map.135.refs_0_), channel_id=1, source_target_pairs={{3,0},{2,1},{1,2},{0,3},{7,4},{6,5},{5,6},{4,7},{11,8},{10,9},{9,1... | collective-permute-start | bytes 24584 | tf_op jit(solution)/shard_map/ppermute | solution.py:489
  26.5 5.3 %collective-permute-start.9 = (f32[264,128]{1,0:T(8,128)S(1)}, f32[264,128]{1,0:T(8,128)S(1)}, u32[]{:S(2)}, u32[]{:S(2)}) collective-permute-start(f32[264,128]{1,0:T(8,128)S(1)} %get-tuple-element.45.refs_0_.message), channel_id=1, source_target_pairs={{4,0},{0,4},{12,8},{8,12},{20,16},{16,20},{28,24},{24,28},{5,1},{1... | collective-permute-start | bytes 405512 | tf_op jit(solution)/shard_map/ppermute | solution.py:485
  28.8 8.5 %collective-permute-start.10 = (f32[264,128]{1,0:T(8,128)S(1)}, f32[264,128]{1,0:T(8,128)S(1)}, u32[]{:S(2)}, u32[]{:S(2)}) collective-permute-start(f32[264,128]{1,0:T(8,128)S(1)} %get-tuple-element.45.refs_0_.message), channel_id=1, source_target_pairs={{24,0},{28,4},{16,8},{20,12},{8,16},{12,20},{0,24},{4,28},{25,1},{... | collective-permute-start | bytes 405512 | tf_op jit(solution)/shard_map/ppermute | solution.py:485
  28.8 8.5 %collective-permute-start.11 = (f32[264,128]{1,0:T(8,128)S(1)}, f32[264,128]{1,0:T(8,128)S(1)}, u32[]{:S(2)}, u32[]{:S(2)}) collective-permute-start(f32[264,128]{1,0:T(8,128)S(1)} %get-tuple-element.45.refs_0_.message), channel_id=1, source_target_pairs={{28,0},{24,4},{20,8},{16,12},{12,16},{8,20},{4,24},{0,28},{29,1},{... | collective-permute-start | bytes 405512 | tf_op jit(solution)/shard_map/ppermute | solution.py:485
  30.1 12.9 %collective-permute-start.12 = (f32[264,128]{1,0:T(8,128)S(1)}, f32[264,128]{1,0:T(8,128)S(1)}, u32[]{:S(2)}, u32[]{:S(2)}) collective-permute-start(f32[264,128]{1,0:T(8,128)S(1)} %get-tuple-element.45.refs_0_.message), channel_id=1, source_target_pairs={{8,0},{12,4},{0,8},{4,12},{24,16},{28,20},{16,24},{20,28},{9,1},{1... | collective-permute-start | bytes 405512 | tf_op jit(solution)/shard_map/ppermute | solution.py:485
  31.8 11.1 %collective-permute-start.13 = (f32[264,128]{1,0:T(8,128)S(1)}, f32[264,128]{1,0:T(8,128)S(1)}, u32[]{:S(2)}, u32[]{:S(2)}) collective-permute-start(f32[264,128]{1,0:T(8,128)S(1)} %collective-permute-done.9.refs_0_.refs_1_), channel_id=1, source_target_pairs={{8,0},{12,4},{0,8},{4,12},{24,16},{28,20},{16,24},{20,28},{9,1},{1... | collective-permute-start | bytes 405512 | tf_op jit(solution)/shard_map/ppermute | solution.py:485
  37.3 1.2 %collective-permute-start.14 = (f32[8,128]{1,0:T(8,128)S(1)}, f32[8,128]{1,0:T(8,128)S(1)}, u32[]{:S(2)}, u32[]{:S(2)}) collective-permute-start(f32[8,128]{1,0:T(8,128)S(1)} %shard_map.139.refs_0_), channel_id=1, source_target_pairs={{8,0},{12,4},{0,8},{4,12},{24,16},{28,20},{16,24},{20,28},{9,1},{1... | collective-permute-start | bytes 12296 | tf_op jit(solution)/shard_map/ppermute | solution.py:485
  38.5 6.3 %collective-permute-start.15 = (f32[2,8,128]{2,1,0:T(8,128)S(1)}, f32[2,8,128]{2,1,0:T(8,128)S(1)}, u32[]{:S(2)}, u32[]{:S(2)}) collective-permute-start(f32[2,8,128]{2,1,0:T(8,128)S(1)} %shard_map.140.refs_0_), channel_id=1, source_target_pairs={{1,0},{0,1},{3,2},{2,3},{5,4},{4,5},{7,6},{6,7},{9,8},{8,9},{11,10... | collective-permute-start | bytes 24584 | tf_op jit(solution)/shard_map/ppermute | solution.py:489
  38.5 6.3 %collective-permute-start.16 = (f32[2,8,128]{2,1,0:T(8,128)S(1)}, f32[2,8,128]{2,1,0:T(8,128)S(1)}, u32[]{:S(2)}, u32[]{:S(2)}) collective-permute-start(f32[2,8,128]{2,1,0:T(8,128)S(1)} %shard_map.140.refs_0_), channel_id=1, source_target_pairs={{2,0},{3,1},{0,2},{1,3},{6,4},{7,5},{4,6},{5,7},{10,8},{11,9},{8,1... | collective-permute-start | bytes 24584 | tf_op jit(solution)/shard_map/ppermute | solution.py:489
  39.4 5.4 %collective-permute-start.17 = (f32[2,8,128]{2,1,0:T(8,128)S(1)}, f32[2,8,128]{2,1,0:T(8,128)S(1)}, u32[]{:S(2)}, u32[]{:S(2)}) collective-permute-start(f32[2,8,128]{2,1,0:T(8,128)S(1)} %shard_map.140.refs_0_), channel_id=1, source_target_pairs={{3,0},{2,1},{1,2},{0,3},{7,4},{6,5},{5,6},{4,7},{11,8},{10,9},{9,1... | collective-permute-start | bytes 24584 | tf_op jit(solution)/shard_map/ppermute | solution.py:489

commit v6 on v5

--- a/solution.py
+++ b/solution.py
@@ -50,7 +50,6 @@
         self.half = self.rows // 2
         self.message = self.half + 8
         self.direct = (self.nx, self.ny) == (4, 2)
-        self.groups = -(-self.devices // LANES)
         self.levels = skel_perm.shape[0]
         self.skel = skel_perm.shape[1] // 2
         shifts = sorted({(dy % self.ny) for dy in (-1, 1)} - {0})
@@ -187,12 +186,23 @@
     return f + stacked(back, s), product(mm, split(f), own)
 
 
-def expand(block, level, halves):
-    if level == 0:
-        return [block]
-    block = split(block)
-    near, far = (product(mt, block, split(half)) for half in halves[level - 1])
-    return expand(near, level - 1, halves) + expand(far, level - 1, halves)
+def product_many(dot, blocks, b):
+    rows = blocks[0].shape[0]
+    out = product(dot, split(jnp.concatenate(blocks, axis=0)), split(b))
+    return [out[i * rows : (i + 1) * rows] for i in range(len(blocks))]
+
+
+def expand_once(groups, halves):
+    flat = [block for group in groups for block in group]
+    sides = [product_many(mt, flat, half) for half in halves]
+    out, at = [], 0
+    for group in groups:
+        spread = []
+        for i in range(at, at + len(group)):
+            spread += [sides[0][i], sides[1][i]]
+        at += len(group)
+        out.append(spread)
+    return out
 
 
 def setup_kernel(
@@ -258,14 +268,12 @@
     n = s.skel
     z = ids[1]
     halves = []
-    eye_row = lax.broadcasted_iota(jnp.int32, (n, n), 0)
-    eye_col = lax.broadcasted_iota(jnp.int32, (n, n), 1)
-    eye = jnp.where(eye_row == eye_col, 1.0, 0.0)
+    spot = lax.broadcasted_iota(jnp.int32, (2 * n, n), 0)
     for level in range(s.levels):
-        spot = lax.broadcasted_iota(jnp.int32, (2 * n, 2 * n), 0)
-        onehot = jnp.where(perm[level : level + 1, :] == spot, 1.0, 0.0).astype(bf16)
-        hi, lo = split(jnp.concatenate([eye, interp[level]], axis=0))
-        ups_ref[level] = mm(onehot, hi) + mm(onehot, lo)
+        kept = jnp.where(perm[level : level + 1, :n] == spot, 1.0, 0.0)
+        moved = jnp.where(perm[level : level + 1, n:] == spot, 1.0, 0.0).astype(bf16)
+        hi, lo = split(interp[level])
+        ups_ref[level] = kept + (mm(moved, hi) + mm(moved, lo))
         bit = (z >> level) & 1
         halves.append(
             [ups_ref[level, pl.ds(pl.multiple_of(side * n, 8), n), :] for side in (bit, 1 - bit)]
@@ -280,10 +288,15 @@
         spread = down(spread, level, mt if level == s.levels - 1 else mm)
         beside = [(down(block, level, mt if fresh else mm), False) for block, fresh in beside]
         beside.append((sibling[level], True))
-    far_leaves = expand(spread, s.levels, halves)
+    beside = [block.T if fresh else block for block, fresh in reversed(beside)]
+    leaves = [[spread]]
+    for level in reversed(range(s.levels)):
+        leaves = expand_once(leaves, halves[level])
+        leaves.append([beside[level]])
+    far_leaves, *sub = leaves
     near_leaves = [jnp.zeros((n, n), f32)]
-    for level, (block, fresh) in enumerate(reversed(beside)):
-        near_leaves += expand(block.T if fresh else block, level, halves)
+    for blocks in reversed(sub):
+        near_leaves += blocks
     tail = n - LANES
     far_out[...] = jnp.zeros_like(far_out)
     own = [a - b for a, b in zip(near_leaves, far_leaves)]
@@ -304,7 +317,7 @@
 
 
 def layer_kernel(s, message, *refs):
-    *sums, out = refs
+    *sums, _, out = refs
     acc = sums[0][...]
     for part in sums[1:]:
         acc = acc + part[...]
@@ -348,11 +361,15 @@
     return out
 
 
-def near_kernel(s, loc, gat, nh, nl, gh, gl, *refs):
-    *messages, out = refs
+def gather_kernel(s, gat, gh, gl, *refs):
+    *messages, _, hi_out, lo_out = refs
     rims = [message[: s.half, :] for message in messages]
     gathered = gat[...] + product(mm, split(unpack_rims(rims, s)), (gh[...], gl[...]))
-    out[...] = loc[...] + product(mm, (nh[...], nl[...]), split(gathered))
+    hi_out[...], lo_out[...] = split(gathered)
+
+
+def near_kernel(s, loc, nh, nl, hi, lo, out):
+    out[...] = loc[...] + product(mm, (nh[...], nl[...]), (hi[...], lo[...]))
 
 
 def with_far(s, part, layers, far_op, cells, col):
@@ -397,21 +414,19 @@
     rest_t = t - ft * f - ot * ortho
     tt = total(rest_t * rest_t)
     rf, ro = jnp.sqrt(ff), jnp.sqrt(oo)
-    stats = jnp.concatenate(
-        [rf, rf * fu, ro, rf * ft, ro * ot, jnp.sqrt(tt), jnp.zeros((2, 1), f32)], axis=0
-    )
-    stat_out[...] = jnp.broadcast_to(jnp.broadcast_to(stats, (8, LANES))[None], stat_out.shape)
+    lane = lax.broadcasted_iota(jnp.int32, (1, LANES), 1)
+    stats = jnp.zeros((1, LANES), f32)
+    for index, value in enumerate((rf, rf * fu, ro, rf * ft, ro * ot, jnp.sqrt(tt))):
+        stats = jnp.where(lane == index, value, stats)
+    stat_out[:, 0, :] = jnp.broadcast_to(stats, (s.devices, LANES))
 
 
 def finish_kernel(s, f_in, u_in, stats, x_out, lsq_out, raw, sem):
-    groups = []
-    for g in range(s.groups):
-        lane = lax.broadcasted_iota(jnp.int32, (8, LANES), 1) + g * LANES
-        acc = jnp.zeros((8, LANES), f32)
-        for d in range(g * LANES, min(s.devices, (g + 1) * LANES)):
-            acc = acc + jnp.where(lane == d, stats[d], 0.0)
-        groups.append(acc)
-    rows = jnp.concatenate(groups, axis=1) if len(groups) > 1 else groups[0]
+    rows = stats[:, 0, :]
+    rest = round_up(s.devices, LANES) - s.devices
+    if rest:
+        rows = jnp.concatenate([rows, jnp.zeros((rest, LANES), f32)], axis=0)
+    rows = rows.T
     f1, u1, u2, t1, t2, t3 = (rows[i : i + 1] for i in range(6))
 
     def along(x):
@@ -497,26 +512,36 @@
             got["other", dy] = fetch(message, "other", dy)
         got["other", 0] = fetch(message, "other", 0)
         got["partner", 0] = fetch(message, "partner", 0)
+        return got
+
+    def forward_messages(got, after):
         for dy in s.shifts:
-            got["partner", dy] = fetch(got["same", dy], "partner", 0)
-        return got
-
-    def share_charges(message, got, after):
+            ready, _ = lax.optimization_barrier((got["same", dy], after))
+            got["partner", dy] = fetch(ready, "partner", 0)
+
+    def share(message, got, gat, after):
+        forward_messages(got, after)
         if s.direct:
             quarter = [message] + [got[key] for key in s.sources if key[0] != "partner"]
             (half,) = call(functools.partial(half_kernel, s), [(tile, f32)], quarter + [after])
             sums = [half, fetch(half, "partner", 0)]
         else:
-            sums = [lax.psum(message[s.half :], ("gx", "gy"))]
-        (pair,) = call(functools.partial(layer_kernel, s), [((2,) + tile, f32)], [message] + sums)
-        return fetch_layers(pair)
-
-    def near_part(loc, gat, got):
+            half = lax.psum(message[s.half :], ("gx", "gy"))
+            sums = [half]
+        gathered = call(
+            functools.partial(gather_kernel, s),
+            [(full, bf16), (full, bf16)],
+            [gat, gh, gl] + [got[key] for key in s.sources] + [half],
+            flops=10**9,
+        )
+        (pair,) = call(
+            functools.partial(layer_kernel, s), [((2,) + tile, f32)], [message] + sums + [gathered[1]]
+        )
+        return gathered, fetch_layers(pair)
+
+    def near_part(loc, gathered):
         return call(
-            functools.partial(near_kernel, s),
-            [(full, f32)],
-            [loc, gat, nh, nl, gh, gl] + [got[key] for key in s.sources],
-            flops=10**9,
+            functools.partial(near_kernel, s), [(full, f32)], [loc, nh, nl, *gathered], flops=10**9
         )[0]
 
     flat = (3 * s.blobs, 1, s.bodies)
@@ -549,8 +574,8 @@
         + [pltpu.SemaphoreType.DMA((len(operators),))],
         flops=5 * 10**9,
     )
-    part = near_part(loc, gat, got)
-    layers = share_charges(message, got, rot)
+    gathered, layers = share(message, got, gat, rot)
+    part = near_part(loc, gathered)
     u, message = call(
         functools.partial(first_kernel, s),
         [(full, f32), ((s.message, LANES), f32)],
@@ -564,11 +589,11 @@
         [u, f, rot, sh, sl, oh, ol],
         flops=10**9,
     )
-    part = near_part(loc, gat, got)
-    layers = share_charges(message, got, stat)
+    gathered, layers = share(message, got, gat, stat)
+    part = near_part(loc, gathered)
     (stats,) = call(
         functools.partial(second_kernel, s),
-        [((s.devices,) + tile, f32)],
+        [((s.devices, 1, LANES), f32)],
         [part, far_op, cells, col, f, ortho, stat, *layers],
         flops=10**8,
     )

time: 59.8 us -> 57.1 us (0.955)
  Pallas kernels: 15.8 us -> 14 us
  starting transfers between devices: 18.5 us -> 17.2 us
  waiting for transfers between devices: 12.8 us -> 13.5 us
    ppermute x6, waiting for transfers between devices: 3.52 us -> 5.89 us  [fetch_layers(): lax.ppermute(x, 'gz', [(z ^ k, z) for z in range(s.nz)])]
    pallas_call x12 -> x14, Pallas kernels: 15.8 us -> 14 us  [call(): pl.pallas_call(kernel, out_shape=[jax.ShapeDtypeStruct(shape, kind) for s...]
    ppermute x12, waiting for transfers between devices: 9.3 us -> 7.65 us  [fetch(): return lax.ppermute(x, ('gx', 'gy'), pairs)]
    ppermute x12, starting transfers between devices: 9.69 us -> 8.42 us  [fetch(): return lax.ppermute(x, ('gx', 'gy'), pairs)]
  transfers between devices with their start and end apart: 18 -> 18, of which waited for: 6 -> 8; matrix products, arithmetic and copies ran while one was open for 0% -> 0% of each run, Pallas kernels for 18% -> 16%
where the time goes in v6:
time: 57.1 us; the launch traced here: 56.8 us
  starting transfers between devices  17.2 us (30%)
  Pallas kernels  14 us (25%)
  waiting for transfers between devices  13.5 us (24%)
  blocking collectives  11.3 us (20%)
  between operations  0.75 us (1%)
    pallas_call x14, Pallas kernels, call(): pl.pallas_call(kernel, out_shape=[jax.ShapeDtypeStruct(shape, kind) for s...  14 us
    all_to_all x1, blocking collectives, body(): stats = lax.all_to_all(stats, ('gx', 'gy', 'gz'), 0, 0)  11.3 us
    ppermute x6, starting transfers between devices, fetch_layers(): lax.ppermute(x, 'gz', [(z ^ k, z) for z in range(s.nz)])  8.77 us
    ppermute x12, starting transfers between devices, fetch(): return lax.ppermute(x, ('gx', 'gy'), pairs)  8.42 us
    ppermute x12, waiting for transfers between devices, fetch(): return lax.ppermute(x, ('gx', 'gy'), pairs)  7.65 us
    ppermute x6, waiting for transfers between devices, fetch_layers(): lax.ppermute(x, 'gz', [(z ^ k, z) for z in range(s.nz)])  5.89 us
  transfers between devices with their start and end apart: 18, of which 8 were waited for; matrix products, arithmetic and copies ran while one was open for 0% of the time, Pallas kernels for 16%

profile of v6, /device:TPU:0, one launch (start us, length us, event | category | flops | bytes accessed | tf_op | source)
XLA Modules:
  0.0 56.8 jit_solution(13139581091598186671)
XLA Ops:
  0.6 1.4 %shard_map.131 = (f32[264,128]{1,0:T(8,128)S(1)}, f32[168,128]{1,0:T(8,128)S(1)}, s32[1,1,256]{2,1,0:T(1,128)S(1)}, f32[512,256]{1,0:T(8,128)S(1)}) custom-call(f32[486,1,256]{2,1,0:T(1,128)} %bitcast.9, s32[1,1,256]{2,1,0:T(1,128)} %cells.1, f32[1,162]{1,0:T(1,128)} %bitcast.10), custom_call_target="tpu_custom_call" | custom-call | flops 10000000 | bytes 1048576 | tf_op jit(solution)/shard_map/pallas_call | solution.py:472
  2.1 3.0 %collective-permute-start = (f32[264,128]{1,0:T(8,128)S(1)}, f32[264,128]{1,0:T(8,128)S(1)}, u32[]{:S(2)}, u32[]{:S(2)}) collective-permute-start(f32[264,128]{1,0:T(8,128)S(1)} %get-tuple-element.39.refs_0_.message), channel_id=1, source_target_pairs={{4,0},{0,4},{12,8},{8,12},{20,16},{16,20},{28,24},{24,28},{5,1},{1... | collective-permute-start | bytes 405512 | tf_op jit(solution)/shard_map/ppermute | solution.py:500
  5.1 0.7 %collective-permute-start.1 = (f32[264,128]{1,0:T(8,128)S(1)}, f32[264,128]{1,0:T(8,128)S(1)}, u32[]{:S(2)}, u32[]{:S(2)}) collective-permute-start(f32[264,128]{1,0:T(8,128)S(1)} %get-tuple-element.39.refs_0_.message), channel_id=1, source_target_pairs={{24,0},{28,4},{16,8},{20,12},{8,16},{12,20},{0,24},{4,28},{25,1},{... | collective-permute-start | bytes 405512 | tf_op jit(solution)/shard_map/ppermute | solution.py:500
  5.7 0.6 %collective-permute-start.2 = (f32[264,128]{1,0:T(8,128)S(1)}, f32[264,128]{1,0:T(8,128)S(1)}, u32[]{:S(2)}, u32[]{:S(2)}) collective-permute-start(f32[264,128]{1,0:T(8,128)S(1)} %get-tuple-element.39.refs_0_.message), channel_id=1, source_target_pairs={{28,0},{24,4},{20,8},{16,12},{12,16},{8,20},{4,24},{0,28},{29,1},{... | collective-permute-start | bytes 405512 | tf_op jit(solution)/shard_map/ppermute | solution.py:500
  6.3 0.4 collective-permute-start.3
  6.8 5.4 %shard_map.132 = (f32[512,256]{1,0:T(8,128)S(1)}, f32[512,256]{1,0:T(8,128)S(1)}, f32[16,256]{1,0:T(8,128)S(1)}, bf16[512,512]{1,0:T(8,128)(2,1)S(1)}, bf16[512,...) custom-call(s32[2]{0:T(128)S(1)} %pad_add_fusion.ids, ...), custom_call_target="tpu_custom_call" | custom-call | flops 5000000000 | bytes 1048576 | tf_op jit(solution)/shard_map/pallas_call | solution.py:472
  12.2 0.2 collective-permute-start.4
  12.4 1.3 %collective-permute-done.1.refs_2_.refs_1_ = f32[264,128]{1,0:T(8,128)S(1)} collective-permute-done((f32[264,128]{1,0:T(8,128)S(1)}, f32[264,128]{1,0:T(8,128)S(1)}, u32[]{:S(2)}, u32[]{:S(2)}) %collective-permute-start.1) | collective-permute-done | bytes 135200 | tf_op jit(solution)/shard_map/ppermute | solution.py:500
  13.8 0.2 collective-permute-start.5
  14.0 0.7 %shard_map.134 = (bf16[512,256]{1,0:T(8,128)(2,1)S(1)}, bf16[512,256]{1,0:T(8,128)(2,1)S(1)}) custom-call(f32[512,256]{1,0:T(8,128)S(1)} %get-tuple-element.36.gat, bf16[384,256]{1,0:T(8,128)(2,1)S(1)} %get-tuple-element.37.gh, bf16[384,256]{1,0:T(8,128)(2,1)S(1)} %get-tuple-element.38.gl, f32[264,128]{1,0:T(8,128)S(1)} %collective-permute-done.refs_1_.refs_0_, ...), custom_call_target="tpu_custom_call" | custom-call | flops 1000000000 | bytes 1048576 | tf_op jit(solution)/shard_map/pallas_call | solution.py:472
  14.7 0.4 collective-permute-done.5.refs_1_
  15.0 1.6 %collective-permute-start.6 = (f32[2,8,128]{2,1,0:T(8,128)S(1)}, f32[2,8,128]{2,1,0:T(8,128)S(1)}, u32[]{:S(2)}, u32[]{:S(2)}) collective-permute-start(f32[2,8,128]{2,1,0:T(8,128)S(1)} %shard_map.136.refs_0_), channel_id=1, source_target_pairs={{1,0},{0,1},{3,2},{2,3},{5,4},{4,5},{7,6},{6,7},{9,8},{8,9},{11,10... | collective-permute-start | bytes 24584 | tf_op jit(solution)/shard_map/ppermute | solution.py:504
  16.6 2.6 %collective-permute-start.7 = (f32[2,8,128]{2,1,0:T(8,128)S(1)}, f32[2,8,128]{2,1,0:T(8,128)S(1)}, u32[]{:S(2)}, u32[]{:S(2)}) collective-permute-start(f32[2,8,128]{2,1,0:T(8,128)S(1)} %shard_map.136.refs_0_), channel_id=1, source_target_pairs={{2,0},{3,1},{0,2},{1,3},{6,4},{7,5},{4,6},{5,7},{10,8},{11,9},{8,1... | collective-permute-start | bytes 24584 | tf_op jit(solution)/shard_map/ppermute | solution.py:504
  19.2 0.2 collective-permute-start.8
  19.4 0.6 %shard_map.135.part = f32[512,256]{1,0:T(8,128)S(1)} custom-call(f32[512,256]{1,0:T(8,128)S(1)} %get-tuple-element.33.loc, bf16[512,512]{1,0:T(8,128)(2,1)S(1)} %get-tuple-element.34.nh, bf16[512,512]{1,0:T(8,128)(2,1)S(1)} %get-tuple-element.35.nl, bf16[512,256]{1,0:T(8,128)(2,1)S(1)} %get-tuple-element.42.hi, bf16[512,256]{1,0:T(8,128)(2,1)S(1)} %get-tuple-element.43.lo.refs_2_), custom_call_target="tpu_custom_call" | custom-call | flops 1000000000 | bytes 1048576 | tf_op jit(solution)/shard_map/pallas_call | solution.py:472
  20.0 1.1 %collective-permute-done.7.refs_2_ = f32[2,8,128]{2,1,0:T(8,128)S(1)} collective-permute-done((f32[2,8,128]{2,1,0:T(8,128)S(1)}, f32[2,8,128]{2,1,0:T(8,128)S(1)}, u32[]{:S(2)}, u32[]{:S(2)}) %collective-permute-start.7) | collective-permute-done | bytes 8224 | tf_op jit(solution)/shard_map/ppermute | solution.py:504
  21.2 3.5 %collective-permute-done.8.refs_3_ = f32[2,8,128]{2,1,0:T(8,128)S(1)} collective-permute-done((f32[2,8,128]{2,1,0:T(8,128)S(1)}, f32[2,8,128]{2,1,0:T(8,128)S(1)}, u32[]{:S(2)}, u32[]{:S(2)}) %collective-permute-start.8) | collective-permute-done | bytes 8224 | tf_op jit(solution)/shard_map/ppermute | solution.py:504
  24.6 0.6 %shard_map.137 = (f32[512,256]{1,0:T(8,128)S(1)}, f32[264,128]{1,0:T(8,128)S(1)}) custom-call(f32[512,256]{1,0:T(8,128)S(1)} %shard_map.135.part, f32[192,1536]{1,0:T(8,128)S(1)} %get-tuple-element.44.far_op, s32[1,1,256]{2,1,0:T(1,128)S(1)} %get-tuple-element.45.cells, f32[168,128]{1,0:T(8,128)S(1)} %get-tuple-element.46.col, ...), custom_call_target="tpu_custom_call" | custom-call | flops 100000000 | bytes 1048576 | tf_op jit(solution)/shard_map/pallas_call | solution.py:472
  25.2 1.1 %collective-permute-start.9 = (f32[264,128]{1,0:T(8,128)S(1)}, f32[264,128]{1,0:T(8,128)S(1)}, u32[]{:S(2)}, u32[]{:S(2)}) collective-permute-start(f32[264,128]{1,0:T(8,128)S(1)} %get-tuple-element.54.refs_0_.message), channel_id=1, source_target_pairs={{4,0},{0,4},{12,8},{8,12},{20,16},{16,20},{28,24},{24,28},{5,1},{1... | collective-permute-start | bytes 405512 | tf_op jit(solution)/shard_map/ppermute | solution.py:500
  26.4 2.1 %collective-permute-start.11 = (f32[264,128]{1,0:T(8,128)S(1)}, f32[264,128]{1,0:T(8,128)S(1)}, u32[]{:S(2)}, u32[]{:S(2)}) collective-permute-start(f32[264,128]{1,0:T(8,128)S(1)} %get-tuple-element.54.refs_0_.message), channel_id=1, source_target_pairs={{28,0},{24,4},{20,8},{16,12},{12,16},{8,20},{4,24},{0,28},{29,1},{... | collective-permute-start | bytes 405512 | tf_op jit(solution)/shard_map/ppermute | solution.py:500
  28.5 1.1 %shard_map.138 = (f32[512,256]{1,0:T(8,128)S(1)}, f32[512,256]{1,0:T(8,128)S(1)}, f32[512,256]{1,0:T(8,128)S(1)}, f32[8,128]{1,0:T(8,128)S(1)}) custom-call(f32[512,256]{1,0:T(8,128)S(1)} %get-tuple-element.47.u_in, f32[512,256]{1,0:T(8,128)S(1)} %get-tuple-element.32.f_in, f32[16,256]{1,0:T(8,128)S(1)} %get-tuple-element.40.refs_4_.rot, ...), custom_call_target="tpu_custom_call" | custom-call | flops 1000000000 | bytes 1048576 | tf_op jit(solution)/shard_map/pallas_call | solution.py:472
  29.5 0.7 %collective-permute-done.9.refs_1_.refs_0_ = f32[264,128]{1,0:T(8,128)S(1)} collective-permute-done((f32[264,128]{1,0:T(8,128)S(1)}, f32[264,128]{1,0:T(8,128)S(1)}, u32[]{:S(2)}, u32[]{:S(2)}) %collective-permute-start.9) | collective-permute-done | bytes 135200 | tf_op jit(solution)/shard_map/ppermute | solution.py:500
  30.3 4.8 %collective-permute-done.10.refs_2_.refs_1_ = f32[264,128]{1,0:T(8,128)S(1)} collective-permute-done((f32[264,128]{1,0:T(8,128)S(1)}, f32[264,128]{1,0:T(8,128)S(1)}, u32[]{:S(2)}, u32[]{:S(2)}) %collective-permute-start.10) | collective-permute-done | bytes 135200 | tf_op jit(solution)/shard_map/ppermute | solution.py:500
  35.3 0.7 %shard_map.140 = (bf16[512,256]{1,0:T(8,128)(2,1)S(1)}, bf16[512,256]{1,0:T(8,128)(2,1)S(1)}) custom-call(f32[512,256]{1,0:T(8,128)S(1)} %get-tuple-element.53.gat, bf16[384,256]{1,0:T(8,128)(2,1)S(1)} %get-tuple-element.37.gh, bf16[384,256]{1,0:T(8,128)(2,1)S(1)} %get-tuple-element.38.gl, f32[264,128]{1,0:T(8,128)S(1)} %collective-permute-done.9.refs_1_.refs_0_, ...), custom_call_target="tpu_custom_call" | custom-call | flops 1000000000 | bytes 1048576 | tf_op jit(solution)/shard_map/pallas_call | solution.py:472
  36.0 0.4 collective-permute-done.14.refs_1_
  36.3 0.8 %collective-permute-start.16 = (f32[2,8,128]{2,1,0:T(8,128)S(1)}, f32[2,8,128]{2,1,0:T(8,128)S(1)}, u32[]{:S(2)}, u32[]{:S(2)}) collective-permute-start(f32[2,8,128]{2,1,0:T(8,128)S(1)} %shard_map.142.refs_0_), channel_id=1, source_target_pairs={{2,0},{3,1},{0,2},{1,3},{6,4},{7,5},{4,6},{5,7},{10,8},{11,9},{8,1... | collective-permute-start | bytes 24584 | tf_op jit(solution)/shard_map/ppermute | solution.py:504
  37.1 3.6 %collective-permute-start.17 = (f32[2,8,128]{2,1,0:T(8,128)S(1)}, f32[2,8,128]{2,1,0:T(8,128)S(1)}, u32[]{:S(2)}, u32[]{:S(2)}) collective-permute-start(f32[2,8,128]{2,1,0:T(8,128)S(1)} %shard_map.142.refs_0_), channel_id=1, source_target_pairs={{3,0},{2,1},{1,2},{0,3},{7,4},{6,5},{5,6},{4,7},{11,8},{10,9},{9,1... | collective-permute-start | bytes 24584 | tf_op jit(solution)/shard_map/ppermute | solution.py:504
  40.7 0.6 %shard_map.141.part = f32[512,256]{1,0:T(8,128)S(1)} custom-call(f32[512,256]{1,0:T(8,128)S(1)} %get-tuple-element.52.loc, bf16[512,512]{1,0:T(8,128)(2,1)S(1)} %get-tuple-element.34.nh, bf16[512,512]{1,0:T(8,128)(2,1)S(1)} %get-tuple-element.35.nl, bf16[512,256]{1,0:T(8,128)(2,1)S(1)} %get-tuple-element.57.hi, bf16[512,256]{1,0:T(8,128)(2,1)S(1)} %get-tuple-element.58.lo.refs_2_), custom_call_target="tpu_custom_call" | custom-call | flops 1000000000 | bytes 1048576 | tf_op jit(solution)/shard_map/pallas_call | solution.py:472
  41.3 1.2 %collective-permute-done.17.refs_3_ = f32[2,8,128]{2,1,0:T(8,128)S(1)} collective-permute-done((f32[2,8,128]{2,1,0:T(8,128)S(1)}, f32[2,8,128]{2,1,0:T(8,128)S(1)}, u32[]{:S(2)}, u32[]{:S(2)}) %collective-permute-start.17) | collective-permute-done | bytes 8224 | tf_op jit(solution)/shard_map/ppermute | solution.py:504
  42.6 0.9 %shard_map.143 = f32[32,1,128]{2,1,0:T(1,128)S(1)} custom-call(f32[512,256]{1,0:T(8,128)S(1)} %shard_map.141.part, f32[192,1536]{1,0:T(8,128)S(1)} %get-tuple-element.44.far_op, s32[1,1,256]{2,1,0:T(1,128)S(1)} %get-tuple-element.45.cells, f32[168,128]{1,0:T(8,128)S(1)} %get-tuple-element.46.col, f32[512,256]{1,0:T(8,128)S(1)} %get-tuple-element.32.f_in, ...), custom_call_target="tpu_custom_call" | custom-call | flops 100000000 | bytes 1048576 | tf_op jit(solution)/shard_map/pallas_call | solution.py:472
  43.5 11.3 %all_to_all.5.stats = f32[32,1,128]{2,1,0:T(1,128)S(1)} all-to-all(f32[32,1,128]{2,1,0:T(1,128)S(1)} %shard_map.143), channel_id=1, replica_groups=mesh['gx'=4,'gy'=2,'gz'=4] {'gx','gy','gz'}, dimensions={0} | all-to-all | bytes 32768 | tf_op jit(solution)/shard_map/all_to_all | solution.py:600
  54.8 2.1 %shard_map.144 = (f32[486,1,256]{2,1,0:T(1,128)}, f32[1,1]{1,0:T(1,128)}) custom-call(f32[512,256]{1,0:T(8,128)S(1)} %get-tuple-element.32.f_in, f32[512,256]{1,0:T(8,128)S(1)} %get-tuple-element.47.u_in, f32[32,1,128]{2,1,0:T(1,128)S(1)} %all_to_all.5.stats), custom_call_target="tpu_custom_call" | custom-call | flops 10000000 | bytes 1048576 | tf_op jit(solution)/shard_map/pallas_call | solution.py:472
  (20 shorter events, 0.3 us)
Async XLA Ops:
  2.1 10.2 %collective-permute-start = (f32[264,128]{1,0:T(8,128)S(1)}, f32[264,128]{1,0:T(8,128)S(1)}, u32[]{:S(2)}, u32[]{:S(2)}) collective-permute-start(f32[264,128]{1,0:T(8,128)S(1)} %get-tuple-element.39.refs_0_.message), channel_id=1, source_target_pairs={{4,0},{0,4},{12,8},{8,12},{20,16},{16,20},{28,24},{24,28},{5,1},{1... | collective-permute-start | bytes 405512 | tf_op jit(solution)/shard_map/ppermute | solution.py:500
  5.1 8.7 %collective-permute-start.1 = (f32[264,128]{1,0:T(8,128)S(1)}, f32[264,128]{1,0:T(8,128)S(1)}, u32[]{:S(2)}, u32[]{:S(2)}) collective-permute-start(f32[264,128]{1,0:T(8,128)S(1)} %get-tuple-element.39.refs_0_.message), channel_id=1, source_target_pairs={{24,0},{28,4},{16,8},{20,12},{8,16},{12,20},{0,24},{4,28},{25,1},{... | collective-permute-start | bytes 405512 | tf_op jit(solution)/shard_map/ppermute | solution.py:500
  5.7 8.0 %collective-permute-start.2 = (f32[264,128]{1,0:T(8,128)S(1)}, f32[264,128]{1,0:T(8,128)S(1)}, u32[]{:S(2)}, u32[]{:S(2)}) collective-permute-start(f32[264,128]{1,0:T(8,128)S(1)} %get-tuple-element.39.refs_0_.message), channel_id=1, source_target_pairs={{28,0},{24,4},{20,8},{16,12},{12,16},{8,20},{4,24},{0,28},{29,1},{... | collective-permute-start | bytes 405512 | tf_op jit(solution)/shard_map/ppermute | solution.py:500
  6.3 7.6 %collective-permute-start.3 = (f32[264,128]{1,0:T(8,128)S(1)}, f32[264,128]{1,0:T(8,128)S(1)}, u32[]{:S(2)}, u32[]{:S(2)}) collective-permute-start(f32[264,128]{1,0:T(8,128)S(1)} %get-tuple-element.39.refs_0_.message), channel_id=1, source_target_pairs={{8,0},{12,4},{0,8},{4,12},{24,16},{28,20},{16,24},{20,28},{9,1},{1... | collective-permute-start | bytes 405512 | tf_op jit(solution)/shard_map/ppermute | solution.py:500
  12.2 1.7 %collective-permute-start.4 = (f32[264,128]{1,0:T(8,128)S(1)}, f32[264,128]{1,0:T(8,128)S(1)}, u32[]{:S(2)}, u32[]{:S(2)}) collective-permute-start(f32[264,128]{1,0:T(8,128)S(1)} %collective-permute-done.refs_1_.refs_0_), channel_id=1, source_target_pairs={{8,0},{12,4},{0,8},{4,12},{24,16},{28,20},{16,24},{20,28},{9,1},{1... | collective-permute-start | bytes 405512 | tf_op jit(solution)/shard_map/ppermute | solution.py:500
  13.8 1.2 %collective-permute-start.5 = (f32[8,128]{1,0:T(8,128)S(1)}, f32[8,128]{1,0:T(8,128)S(1)}, u32[]{:S(2)}, u32[]{:S(2)}) collective-permute-start(f32[8,128]{1,0:T(8,128)S(1)} %shard_map.133.refs_5_.refs_0_), channel_id=1, source_target_pairs={{8,0},{12,4},{0,8},{4,12},{24,16},{28,20},{16,24},{20,28},{9,1},{1... | collective-permute-start | bytes 12296 | tf_op jit(solution)/shard_map/ppermute | solution.py:500
  15.0 5.0 %collective-permute-start.6 = (f32[2,8,128]{2,1,0:T(8,128)S(1)}, f32[2,8,128]{2,1,0:T(8,128)S(1)}, u32[]{:S(2)}, u32[]{:S(2)}) collective-permute-start(f32[2,8,128]{2,1,0:T(8,128)S(1)} %shard_map.136.refs_0_), channel_id=1, source_target_pairs={{1,0},{0,1},{3,2},{2,3},{5,4},{4,5},{7,6},{6,7},{9,8},{8,9},{11,10... | collective-permute-start | bytes 24584 | tf_op jit(solution)/shard_map/ppermute | solution.py:504
  16.6 4.5 %collective-permute-start.7 = (f32[2,8,128]{2,1,0:T(8,128)S(1)}, f32[2,8,128]{2,1,0:T(8,128)S(1)}, u32[]{:S(2)}, u32[]{:S(2)}) collective-permute-start(f32[2,8,128]{2,1,0:T(8,128)S(1)} %shard_map.136.refs_0_), channel_id=1, source_target_pairs={{2,0},{3,1},{0,2},{1,3},{6,4},{7,5},{4,6},{5,7},{10,8},{11,9},{8,1... | collective-permute-start | bytes 24584 | tf_op jit(solution)/shard_map/ppermute | solution.py:504
  19.2 5.4 %collective-permute-start.8 = (f32[2,8,128]{2,1,0:T(8,128)S(1)}, f32[2,8,128]{2,1,0:T(8,128)S(1)}, u32[]{:S(2)}, u32[]{:S(2)}) collective-permute-start(f32[2,8,128]{2,1,0:T(8,128)S(1)} %shard_map.136.refs_0_), channel_id=1, source_target_pairs={{3,0},{2,1},{1,2},{0,3},{7,4},{6,5},{5,6},{4,7},{11,8},{10,9},{9,1... | collective-permute-start | bytes 24584 | tf_op jit(solution)/shard_map/ppermute | solution.py:504
  25.2 5.0 %collective-permute-start.9 = (f32[264,128]{1,0:T(8,128)S(1)}, f32[264,128]{1,0:T(8,128)S(1)}, u32[]{:S(2)}, u32[]{:S(2)}) collective-permute-start(f32[264,128]{1,0:T(8,128)S(1)} %get-tuple-element.54.refs_0_.message), channel_id=1, source_target_pairs={{4,0},{0,4},{12,8},{8,12},{20,16},{16,20},{28,24},{24,28},{5,1},{1... | collective-permute-start | bytes 405512 | tf_op jit(solution)/shard_map/ppermute | solution.py:500
  26.4 8.7 %collective-permute-start.10 = (f32[264,128]{1,0:T(8,128)S(1)}, f32[264,128]{1,0:T(8,128)S(1)}, u32[]{:S(2)}, u32[]{:S(2)}) collective-permute-start(f32[264,128]{1,0:T(8,128)S(1)} %get-tuple-element.54.refs_0_.message), channel_id=1, source_target_pairs={{24,0},{28,4},{16,8},{20,12},{8,16},{12,20},{0,24},{4,28},{25,1},{... | collective-permute-start | bytes 405512 | tf_op jit(solution)/shard_map/ppermute | solution.py:500
  26.4 8.7 %collective-permute-start.11 = (f32[264,128]{1,0:T(8,128)S(1)}, f32[264,128]{1,0:T(8,128)S(1)}, u32[]{:S(2)}, u32[]{:S(2)}) collective-permute-start(f32[264,128]{1,0:T(8,128)S(1)} %get-tuple-element.54.refs_0_.message), channel_id=1, source_target_pairs={{28,0},{24,4},{20,8},{16,12},{12,16},{8,20},{4,24},{0,28},{29,1},{... | collective-permute-start | bytes 405512 | tf_op jit(solution)/shard_map/ppermute | solution.py:500
  28.5 6.8 %collective-permute-start.12 = (f32[264,128]{1,0:T(8,128)S(1)}, f32[264,128]{1,0:T(8,128)S(1)}, u32[]{:S(2)}, u32[]{:S(2)}) collective-permute-start(f32[264,128]{1,0:T(8,128)S(1)} %get-tuple-element.54.refs_0_.message), channel_id=1, source_target_pairs={{8,0},{12,4},{0,8},{4,12},{24,16},{28,20},{16,24},{20,28},{9,1},{1... | collective-permute-start | bytes 405512 | tf_op jit(solution)/shard_map/ppermute | solution.py:500
  30.3 5.0 %collective-permute-start.13 = (f32[264,128]{1,0:T(8,128)S(1)}, f32[264,128]{1,0:T(8,128)S(1)}, u32[]{:S(2)}, u32[]{:S(2)}) collective-permute-start(f32[264,128]{1,0:T(8,128)S(1)} %collective-permute-done.9.refs_1_.refs_0_), channel_id=1, source_target_pairs={{8,0},{12,4},{0,8},{4,12},{24,16},{28,20},{16,24},{20,28},{9,1},{1... | collective-permute-start | bytes 405512 | tf_op jit(solution)/shard_map/ppermute | solution.py:500
  35.1 1.2 %collective-permute-start.14 = (f32[8,128]{1,0:T(8,128)S(1)}, f32[8,128]{1,0:T(8,128)S(1)}, u32[]{:S(2)}, u32[]{:S(2)}) collective-permute-start(f32[8,128]{1,0:T(8,128)S(1)} %shard_map.139.refs_5_.refs_0_), channel_id=1, source_target_pairs={{8,0},{12,4},{0,8},{4,12},{24,16},{28,20},{16,24},{20,28},{9,1},{1... | collective-permute-start | bytes 12296 | tf_op jit(solution)/shard_map/ppermute | solution.py:500
  36.3 5.0 %collective-permute-start.15 = (f32[2,8,128]{2,1,0:T(8,128)S(1)}, f32[2,8,128]{2,1,0:T(8,128)S(1)}, u32[]{:S(2)}, u32[]{:S(2)}) collective-permute-start(f32[2,8,128]{2,1,0:T(8,128)S(1)} %shard_map.142.refs_0_), channel_id=1, source_target_pairs={{1,0},{0,1},{3,2},{2,3},{5,4},{4,5},{7,6},{6,7},{9,8},{8,9},{11,10... | collective-permute-start | bytes 24584 | tf_op jit(solution)/shard_map/ppermute | solution.py:504
  36.3 5.0 %collective-permute-start.16 = (f32[2,8,128]{2,1,0:T(8,128)S(1)}, f32[2,8,128]{2,1,0:T(8,128)S(1)}, u32[]{:S(2)}, u32[]{:S(2)}) collective-permute-start(f32[2,8,128]{2,1,0:T(8,128)S(1)} %shard_map.142.refs_0_), channel_id=1, source_target_pairs={{2,0},{3,1},{0,2},{1,3},{6,4},{7,5},{4,6},{5,7},{10,8},{11,9},{8,1... | collective-permute-start | bytes 24584 | tf_op jit(solution)/shard_map/ppermute | solution.py:504
  37.1 5.4 %collective-permute-start.17 = (f32[2,8,128]{2,1,0:T(8,128)S(1)}, f32[2,8,128]{2,1,0:T(8,128)S(1)}, u32[]{:S(2)}, u32[]{:S(2)}) collective-permute-start(f32[2,8,128]{2,1,0:T(8,128)S(1)} %shard_map.142.refs_0_), channel_id=1, source_target_pairs={{3,0},{2,1},{1,2},{0,3},{7,4},{6,5},{5,6},{4,7},{11,8},{10,9},{9,1... | collective-permute-start | bytes 24584 | tf_op jit(solution)/shard_map/ppermute | solution.py:504

commit v7 on v6

--- a/solution.py
+++ b/solution.py
@@ -205,20 +205,17 @@
     return out
 
 
-def setup_kernel(
-    s, ids, f_in, *refs
-):
-    count = 9
-    sources, refs = refs[:count], refs[count:]
-    copies, refs = refs[-1 - count :], refs[: -1 - count]
-    copies, sems = copies[:-1], copies[-1]
-    setup(s, ids, f_in, begin(sources, copies, sems), *copies, *refs)
+def setup_kernel(s, ids, f_in, *refs):
+    sources, tree, outs, (padded, *copies, sems) = refs[:9], refs[9:13], refs[13:24], refs[24:]
+    moves = begin(sources, (*copies, *tree), sems)
+    setup(s, ids, f_in, moves[:5], *copies, *outs, padded)
+    for move in moves[5:]:
+        move.wait()
 
 
 def setup(
-    s, ids, f_in, moves, angles, near_weight, neighbours, self_mob, near_mat, perm, interp, sibling, root,
-    loc_out, gat_out, rot_out, sh_out, sl_out, nh_out, nl_out, oh_out, ol_out, gh_out, gl_out,
-    far_out, padded, ups_ref,
+    s, ids, f_in, moves, angles, near_weight, neighbours, self_mob, near_mat,
+    loc_out, gat_out, rot_out, sh_out, sl_out, nh_out, nl_out, oh_out, ol_out, gh_out, gl_out, padded,
 ):
     f = f_in[...]
     for move in moves[:3]:
@@ -265,6 +262,8 @@
     loc_out[...] = loc
     gat_out[...] = gat
 
+
+def far_kernel(s, ids, perm, interp, sibling, root, _, far_out, ups_ref):
     n = s.skel
     z = ids[1]
     halves = []
@@ -310,9 +309,9 @@
 
 def half_kernel(s, *refs):
     *messages, _, out = refs
-    acc = messages[0][s.half :, :]
+    acc = messages[0][-8:, :]
     for message in messages[1:]:
-        acc = acc + message[s.half :, :]
+        acc = acc + message[-8:, :]
     out[...] = acc
 
 
@@ -321,7 +320,7 @@
     acc = sums[0][...]
     for part in sums[1:]:
         acc = acc + part[...]
-    out[0] = message[s.half :, :]
+    out[0] = message[-8:, :]
     out[1] = acc
 
 
@@ -378,11 +377,12 @@
 
 
 def first_kernel(s, part, far_op, cells, col, *refs):
-    *layers, u_out, message_out = refs
+    *layers, u_out, rim_out, charges_out = refs
     weight_col = col[:, :1]
     u = with_far(s, part, layers, far_op, cells, weight_col)
     u_out[...] = u
-    message_out[...] = pack_message(u, weight_col, cells[0], s)
+    rim_out[...] = pack_rim(u, s)
+    charges_out[...] = pack_charges(pieces(u, s), weight_col, occupancy(cells[0], s), s)
 
 
 def safe_inverse(x):
@@ -504,40 +504,40 @@
             lax.ppermute(x, "gz", [(z ^ k, z) for z in range(s.nz)]) for k in range(1, s.nz)
         ]
 
-    def fetch_messages(message):
+    def fetch_rims(rim):
         got = {}
         for dy in s.shifts:
-            got["same", dy] = fetch(message, "same", dy)
+            got["same", dy] = fetch(rim, "same", dy)
         for dy in s.shifts:
-            got["other", dy] = fetch(message, "other", dy)
-        got["other", 0] = fetch(message, "other", 0)
-        got["partner", 0] = fetch(message, "partner", 0)
+            got["other", dy] = fetch(rim, "other", dy)
+        got["other", 0] = fetch(rim, "other", 0)
+        got["partner", 0] = fetch(rim, "partner", 0)
         return got
 
-    def forward_messages(got, after):
+    def forward_rims(got, after):
         for dy in s.shifts:
             ready, _ = lax.optimization_barrier((got["same", dy], after))
             got["partner", dy] = fetch(ready, "partner", 0)
 
-    def share(message, got, gat, after):
-        forward_messages(got, after)
-        if s.direct:
-            quarter = [message] + [got[key] for key in s.sources if key[0] != "partner"]
-            (half,) = call(functools.partial(half_kernel, s), [(tile, f32)], quarter + [after])
-            sums = [half, fetch(half, "partner", 0)]
-        else:
-            half = lax.psum(message[s.half :], ("gx", "gy"))
-            sums = [half]
-        gathered = call(
+    def half_sum(own, got, after):
+        if not s.direct:
+            return [lax.psum(own[-8:], ("gx", "gy"))]
+        parts = [own] + [got[key] for key in s.sources if key[0] != "partner" and key in got]
+        (half,) = call(functools.partial(half_kernel, s), [(tile, f32)], parts + [after])
+        return [half, fetch(half, "partner", 0)]
+
+    def gather(gat, got, after):
+        return call(
             functools.partial(gather_kernel, s),
             [(full, bf16), (full, bf16)],
-            [gat, gh, gl] + [got[key] for key in s.sources] + [half],
+            [gat, gh, gl] + [got[key] for key in s.sources] + [after],
             flops=10**9,
         )
-        (pair,) = call(
-            functools.partial(layer_kernel, s), [((2,) + tile, f32)], [message] + sums + [gathered[1]]
-        )
-        return gathered, fetch_layers(pair)
+
+    def layer_pair(own, sums, after):
+        return call(
+            functools.partial(layer_kernel, s), [((2,) + tile, f32)], [own] + sums + [after]
+        )[0]
 
     def near_part(loc, gathered):
         return call(
@@ -554,42 +554,62 @@
         scratch=[pltpu.VMEM(flat, f32), pltpu.VMEM(small, f32), pltpu.SemaphoreType.DMA((3,))],
         flops=10**7,
     )
-    got = fetch_messages(message)
-    operators = [
-        angles.reshape(3, 1, s.bodies), near_weight, neighbours, self_mob, near_mat, skel_perm, interp,
-        sibling_ops, root_op,
-    ]
-    loc, gat, rot, sh, sl, nh, nl, oh, ol, gh, gl, far_op = call(
+    got = fetch_rims(message)
+    tree = [skel_perm, interp, sibling_ops, root_op]
+    operators = [angles.reshape(3, 1, s.bodies), near_weight, neighbours, self_mob, near_mat]
+    *tree, loc, gat, rot, sh, sl, nh, nl, oh, ol, gh, gl = call(
         functools.partial(setup_kernel, s),
-        [(full, f32), (full, f32), ((16, s.bodies), f32)]
+        [(x.shape, x.dtype) for x in tree]
+        + [(full, f32), (full, f32), ((16, s.bodies), f32)]
         + [(square, bf16)] * 4
         + [((s.bodies, s.bodies), bf16)] * 2
-        + [((s.ghosts, s.bodies), bf16)] * 2
-        + [(far_shape, f32)],
-        [ids, f] + operators,
+        + [((s.ghosts, s.bodies), bf16)] * 2,
+        [ids, f] + operators + tree,
         scalars=1,
-        far_args=len(operators),
-        scratch=[pltpu.VMEM(square, f32), pltpu.VMEM((s.levels, 2 * s.skel, s.skel), f32)]
+        far_args=9,
+        scratch=[pltpu.VMEM(square, f32)]
         + [pltpu.VMEM(x.shape, x.dtype) for x in operators]
-        + [pltpu.SemaphoreType.DMA((len(operators),))],
-        flops=5 * 10**9,
-    )
-    gathered, layers = share(message, got, gat, rot)
+        + [pltpu.SemaphoreType.DMA((9,))],
+        flops=4 * 10**9,
+    )
+    sums = half_sum(message, got, rot)
+    forward_rims(got, rot)
+    gathered = gather(gat, got, sums[0])
+    pair = layer_pair(message, sums, gathered[1])
+    layers = fetch_layers(pair)
     part = near_part(loc, gathered)
-    u, message = call(
+    (far_op,) = call(
+        functools.partial(far_kernel, s),
+        [(far_shape, f32)],
+        [ids, *tree, pair],
+        scalars=1,
+        scratch=[pltpu.VMEM((s.levels, 2 * s.skel, s.skel), f32)],
+        flops=2 * 10**9,
+    )
+    u, rim, charges = call(
         functools.partial(first_kernel, s),
-        [(full, f32), ((s.message, LANES), f32)],
+        [(full, f32), ((s.half, LANES), f32), (tile, f32)],
         [part, far_op, cells, col, *layers],
         flops=10**8,
     )
-    got = fetch_messages(message)
+    got = {}
+    if s.direct:
+        for key in s.sources:
+            if key[0] != "partner":
+                got[key] = fetch(charges, *key)
     loc, gat, ortho, stat = call(
         functools.partial(middle_kernel, s),
         [(full, f32), (full, f32), (full, f32), (tile, f32)],
         [u, f, rot, sh, sl, oh, ol],
         flops=10**9,
     )
-    gathered, layers = share(message, got, gat, stat)
+    sums = half_sum(charges, got, stat)
+    rim, _ = lax.optimization_barrier((rim, sums[0]))
+    got = fetch_rims(rim)
+    pair = layer_pair(charges, sums, stat)
+    layers = fetch_layers(pair)
+    forward_rims(got, pair)
+    gathered = gather(gat, got, pair)
     part = near_part(loc, gathered)
     (stats,) = call(
         functools.partial(second_kernel, s),

time: 57.1 us -> 58.2 us (1.019)
  blocking collectives: 11.3 us -> 9.45 us
  waiting for transfers between devices: 13.5 us -> 15.3 us
  starting transfers between devices: 17.2 us -> 17.9 us
    ppermute x12 -> x15, starting transfers between devices: 8.42 us -> 12 us  [fetch(): return lax.ppermute(x, ('gx', 'gy'), pairs)]
    ppermute x12 -> x15, waiting for transfers between devices: 7.65 us -> 10.5 us  [fetch(): return lax.ppermute(x, ('gx', 'gy'), pairs)]
    ppermute x6, starting transfers between devices: 8.77 us -> 5.93 us  [fetch_layers(): lax.ppermute(x, 'gz', [(z ^ k, z) for z in range(s.nz)])]
    all_to_all x1, blocking collectives: 11.3 us -> 9.45 us  [body(): stats = lax.all_to_all(stats, ('gx', 'gy', 'gz'), 0, 0)]
    ppermute x6, waiting for transfers between devices: 5.89 us -> 4.78 us  [fetch_layers(): lax.ppermute(x, 'gz', [(z ^ k, z) for z in range(s.nz)])]
    pallas_call x14 -> x15, Pallas kernels: 14 us -> 14.5 us  [call(): pl.pallas_call(kernel, out_shape=[jax.ShapeDtypeStruct(shape, kind) for s...]
  transfers between devices with their start and end apart: 18 -> 21, of which waited for: 8 -> 9; matrix products, arithmetic and copies ran while one was open for 0% -> 0% of each run, Pallas kernels for 16% -> 16%
where the time goes in v7:
time: 58.2 us; the launch traced here: 58 us
  starting transfers between devices  17.9 us (31%)
  waiting for transfers between devices  15.3 us (26%)
  Pallas kernels  14.5 us (25%)
  blocking collectives  9.45 us (16%)
  between operations  0.77 us (1%)
    pallas_call x15, Pallas kernels, call(): pl.pallas_call(kernel, out_shape=[jax.ShapeDtypeStruct(shape, kind) for s...  14.5 us
    ppermute x15, starting transfers between devices, fetch(): return lax.ppermute(x, ('gx', 'gy'), pairs)  12 us
    ppermute x15, waiting for transfers between devices, fetch(): return lax.ppermute(x, ('gx', 'gy'), pairs)  10.5 us
    all_to_all x1, blocking collectives, body(): stats = lax.all_to_all(stats, ('gx', 'gy', 'gz'), 0, 0)  9.45 us
    ppermute x6, starting transfers between devices, fetch_layers(): lax.ppermute(x, 'gz', [(z ^ k, z) for z in range(s.nz)])  5.93 us
    ppermute x6, waiting for transfers between devices, fetch_layers(): lax.ppermute(x, 'gz', [(z ^ k, z) for z in range(s.nz)])  4.78 us
  transfers between devices with their start and end apart: 21, of which 9 were waited for; matrix products, arithmetic and copies ran while one was open for 0% of the time, Pallas kernels for 16%

profile of v7, /device:TPU:0, one launch (start us, length us, event | category | flops | bytes accessed | tf_op | source)
XLA Modules:
  0.0 58.0 jit_solution(15407233686964055915)
XLA Ops:
  0.6 1.4 %shard_map.131 = (f32[264,128]{1,0:T(8,128)S(1)}, f32[168,128]{1,0:T(8,128)S(1)}, s32[1,1,256]{2,1,0:T(1,128)S(1)}, f32[512,256]{1,0:T(8,128)S(1)}) custom-call(f32[486,1,256]{2,1,0:T(1,128)} %bitcast.9, s32[1,1,256]{2,1,0:T(1,128)} %cells.1, f32[1,162]{1,0:T(1,128)} %bitcast.10), custom_call_target="tpu_custom_call" | custom-call | flops 10000000 | bytes 1048576 | tf_op jit(solution)/shard_map/pallas_call | solution.py:472
  2.1 3.0 %collective-permute-start = (f32[264,128]{1,0:T(8,128)S(1)}, f32[264,128]{1,0:T(8,128)S(1)}, u32[]{:S(2)}, u32[]{:S(2)}) collective-permute-start(f32[264,128]{1,0:T(8,128)S(1)} %get-tuple-element.44.refs_0_.message), channel_id=1, source_target_pairs={{4,0},{0,4},{12,8},{8,12},{20,16},{16,20},{28,24},{24,28},{5,1},{1... | collective-permute-start | bytes 405512 | tf_op jit(solution)/shard_map/ppermute | solution.py:500
  5.1 0.7 %collective-permute-start.1 = (f32[264,128]{1,0:T(8,128)S(1)}, f32[264,128]{1,0:T(8,128)S(1)}, u32[]{:S(2)}, u32[]{:S(2)}) collective-permute-start(f32[264,128]{1,0:T(8,128)S(1)} %get-tuple-element.44.refs_0_.message), channel_id=1, source_target_pairs={{24,0},{28,4},{16,8},{20,12},{8,16},{12,20},{0,24},{4,28},{25,1},{... | collective-permute-start | bytes 405512 | tf_op jit(solution)/shard_map/ppermute | solution.py:500
  5.7 0.6 %collective-permute-start.2 = (f32[264,128]{1,0:T(8,128)S(1)}, f32[264,128]{1,0:T(8,128)S(1)}, u32[]{:S(2)}, u32[]{:S(2)}) collective-permute-start(f32[264,128]{1,0:T(8,128)S(1)} %get-tuple-element.44.refs_0_.message), channel_id=1, source_target_pairs={{28,0},{24,4},{20,8},{16,12},{12,16},{8,20},{4,24},{0,28},{29,1},{... | collective-permute-start | bytes 405512 | tf_op jit(solution)/shard_map/ppermute | solution.py:500
  6.3 0.4 collective-permute-start.3
  6.8 3.5 %shard_map.132 = (s32[2,384]{1,0:T(2,128)S(1)}, f32[2,192,192]{2,1,0:T(8,128)S(1)}, f32[2,192,192]{2,1,0:T(8,128)S(1)}, f32[192,192]{1,0:T(8,128)S(1)}, f32[512,...) custom-call(s32[2]{0:T(128)S(1)} %pad_add_fusion.ids, ...), custom_call_target="tpu_custom_call" | custom-call | flops 4000000000 | bytes 1048576 | tf_op jit(solution)/shard_map/pallas_call | solution.py:472
  10.5 3.3 %collective-permute-done.1.refs_2_.refs_1_ = f32[264,128]{1,0:T(8,128)S(1)} collective-permute-done((f32[264,128]{1,0:T(8,128)S(1)}, f32[264,128]{1,0:T(8,128)S(1)}, u32[]{:S(2)}, u32[]{:S(2)}) %collective-permute-start.1) | collective-permute-done | bytes 135200 | tf_op jit(solution)/shard_map/ppermute | solution.py:500
  14.0 0.7 %shard_map.134 = (bf16[512,256]{1,0:T(8,128)(2,1)S(1)}, bf16[512,256]{1,0:T(8,128)(2,1)S(1)}) custom-call(f32[512,256]{1,0:T(8,128)S(1)} %get-tuple-element.41.gat, bf16[384,256]{1,0:T(8,128)(2,1)S(1)} %get-tuple-element.42.gh, bf16[384,256]{1,0:T(8,128)(2,1)S(1)} %get-tuple-element.43.gl, f32[264,128]{1,0:T(8,128)S(1)} %collective-permute-done.refs_1_.refs_0_, ...), custom_call_target="tpu_custom_call" | custom-call | flops 1000000000 | bytes 1048576 | tf_op jit(solution)/shard_map/pallas_call | solution.py:472
  14.7 0.4 collective-permute-done.5.refs_1_
  15.0 1.6 %collective-permute-start.6 = (f32[2,8,128]{2,1,0:T(8,128)S(1)}, f32[2,8,128]{2,1,0:T(8,128)S(1)}, u32[]{:S(2)}, u32[]{:S(2)}) collective-permute-start(f32[2,8,128]{2,1,0:T(8,128)S(1)} %shard_map.136._.refs_0_), channel_id=1, source_target_pairs={{1,0},{0,1},{3,2},{2,3},{5,4},{4,5},{7,6},{6,7},{9,8},{8,9},{11,10... | collective-permute-start | bytes 24584 | tf_op jit(solution)/shard_map/ppermute | solution.py:504
  16.6 2.6 %collective-permute-start.7 = (f32[2,8,128]{2,1,0:T(8,128)S(1)}, f32[2,8,128]{2,1,0:T(8,128)S(1)}, u32[]{:S(2)}, u32[]{:S(2)}) collective-permute-start(f32[2,8,128]{2,1,0:T(8,128)S(1)} %shard_map.136._.refs_0_), channel_id=1, source_target_pairs={{2,0},{3,1},{0,2},{1,3},{6,4},{7,5},{4,6},{5,7},{10,8},{11,9},{8,1... | collective-permute-start | bytes 24584 | tf_op jit(solution)/shard_map/ppermute | solution.py:504
  19.4 2.5 %shard_map.137.far_op = f32[192,1536]{1,0:T(8,128)S(1)} custom-call(s32[2]{0:T(128)S(1)} %pad_add_fusion.ids, s32[2,384]{1,0:T(2,128)S(1)} %get-tuple-element.49.perm, f32[2,192,192]{2,1,0:T(8,128)S(1)} %get-tuple-element.50.interp, f32[2,192,192]{2,1,0:T(8,128)S(1)} %get-tuple-element.51.sibling, f32[192,192]{1,0:T(8,128)S(1)} %get-tuple-element.52.root, ...), custom_call_target="tpu_custom_call" | custom-call | flops 2000000000 | bytes 1048576 | tf_op jit(solution)/shard_map/pallas_call | solution.py:472
  21.9 0.6 shard_map.135.part
  22.5 2.1 %collective-permute-done.8.refs_3_ = f32[2,8,128]{2,1,0:T(8,128)S(1)} collective-permute-done((f32[2,8,128]{2,1,0:T(8,128)S(1)}, f32[2,8,128]{2,1,0:T(8,128)S(1)}, u32[]{:S(2)}, u32[]{:S(2)}) %collective-permute-start.8) | collective-permute-done | bytes 8224 | tf_op jit(solution)/shard_map/ppermute | solution.py:504
  24.6 0.6 %shard_map.138 = (f32[512,256]{1,0:T(8,128)S(1)}, f32[256,128]{1,0:T(8,128)S(1)}, f32[8,128]{1,0:T(8,128)S(1)}) custom-call(f32[512,256]{1,0:T(8,128)S(1)} %shard_map.135.part, f32[192,1536]{1,0:T(8,128)S(1)} %shard_map.137.far_op, s32[1,1,256]{2,1,0:T(1,128)S(1)} %get-tuple-element.53.cells, f32[168,128]{1,0:T(8,128)S(1)} %get-tuple-element.54.col, ...), custom_call_target="tpu_custom_call" | custom-call | flops 100000000 | bytes 1048576 | tf_op jit(solution)/shard_map/pallas_call | solution.py:472
  25.2 1.3 %collective-permute-start.11 = (f32[8,128]{1,0:T(8,128)S(1)}, f32[8,128]{1,0:T(8,128)S(1)}, u32[]{:S(2)}, u32[]{:S(2)}) collective-permute-start(f32[8,128]{1,0:T(8,128)S(1)} %get-tuple-element.63.refs_0_.message), channel_id=1, source_target_pairs={{28,0},{24,4},{20,8},{16,12},{12,16},{8,20},{4,24},{0,28},{29,1},{... | collective-permute-start | bytes 12296 | tf_op jit(solution)/shard_map/ppermute | solution.py:500
  26.5 1.9 %collective-permute-start.9 = (f32[8,128]{1,0:T(8,128)S(1)}, f32[8,128]{1,0:T(8,128)S(1)}, u32[]{:S(2)}, u32[]{:S(2)}) collective-permute-start(f32[8,128]{1,0:T(8,128)S(1)} %get-tuple-element.63.refs_0_.message), channel_id=1, source_target_pairs={{4,0},{0,4},{12,8},{8,12},{20,16},{16,20},{28,24},{24,28},{5,1},{1... | collective-permute-start | bytes 12296 | tf_op jit(solution)/shard_map/ppermute | solution.py:500
  28.5 1.1 %shard_map.139 = (f32[512,256]{1,0:T(8,128)S(1)}, f32[512,256]{1,0:T(8,128)S(1)}, f32[512,256]{1,0:T(8,128)S(1)}, f32[8,128]{1,0:T(8,128)S(1)}) custom-call(f32[512,256]{1,0:T(8,128)S(1)} %get-tuple-element.55.u_in, f32[512,256]{1,0:T(8,128)S(1)} %get-tuple-element.37.f_in, f32[16,256]{1,0:T(8,128)S(1)} %get-tuple-element.45.refs_4_.rot, ...), custom_call_target="tpu_custom_call" | custom-call | flops 1000000000 | bytes 1048576 | tf_op jit(solution)/shard_map/pallas_call | solution.py:472
  29.5 0.6 collective-permute-done.9.refs_1_
  30.1 1.9 %collective-permute-start.12 = (f32[256,128]{1,0:T(8,128)S(1)}, f32[256,128]{1,0:T(8,128)S(1)}, u32[]{:S(2)}, u32[]{:S(2)}) collective-permute-start(f32[256,128]{1,0:T(8,128)S(1)} %get-tuple-element.65), channel_id=1, source_target_pairs={{4,0},{0,4},{12,8},{8,12},{20,16},{16,20},{28,24},{24,28},{5,1},{1... | collective-permute-start | bytes 393224 | tf_op jit(solution)/shard_map/ppermute | solution.py:500
  32.1 1.4 %collective-permute-start.13 = (f32[256,128]{1,0:T(8,128)S(1)}, f32[256,128]{1,0:T(8,128)S(1)}, u32[]{:S(2)}, u32[]{:S(2)}) collective-permute-start(f32[256,128]{1,0:T(8,128)S(1)} %get-tuple-element.65), channel_id=1, source_target_pairs={{24,0},{28,4},{16,8},{20,12},{8,16},{12,20},{0,24},{4,28},{25,1},{... | collective-permute-start | bytes 393224 | tf_op jit(solution)/shard_map/ppermute | solution.py:500
  33.9 2.2 %collective-permute-done.12.refs_0_ = f32[256,128]{1,0:T(8,128)S(1)} collective-permute-done((f32[256,128]{1,0:T(8,128)S(1)}, f32[256,128]{1,0:T(8,128)S(1)}, u32[]{:S(2)}, u32[]{:S(2)}) %collective-permute-start.12) | collective-permute-done | bytes 131104 | tf_op jit(solution)/shard_map/ppermute | solution.py:500
  36.1 3.4 %collective-permute-done.13.refs_1_ = f32[256,128]{1,0:T(8,128)S(1)} collective-permute-done((f32[256,128]{1,0:T(8,128)S(1)}, f32[256,128]{1,0:T(8,128)S(1)}, u32[]{:S(2)}, u32[]{:S(2)}) %collective-permute-start.13) | collective-permute-done | bytes 131104 | tf_op jit(solution)/shard_map/ppermute | solution.py:500
  39.5 0.6 %collective-permute-done.14.refs_2_ = f32[256,128]{1,0:T(8,128)S(1)} collective-permute-done((f32[256,128]{1,0:T(8,128)S(1)}, f32[256,128]{1,0:T(8,128)S(1)}, u32[]{:S(2)}, u32[]{:S(2)}) %collective-permute-start.14) | collective-permute-done | bytes 131104 | tf_op jit(solution)/shard_map/ppermute | solution.py:500
  40.1 1.5 %collective-permute-start.20 = (f32[2,8,128]{2,1,0:T(8,128)S(1)}, f32[2,8,128]{2,1,0:T(8,128)S(1)}, u32[]{:S(2)}, u32[]{:S(2)}) collective-permute-start(f32[2,8,128]{2,1,0:T(8,128)S(1)} %shard_map.141.refs_5_.refs_0_), channel_id=1, source_target_pairs={{3,0},{2,1},{1,2},{0,3},{7,4},{6,5},{5,6},{4,7},{11,8},{10,9},{9,1... | collective-permute-start | bytes 24584 | tf_op jit(solution)/shard_map/ppermute | solution.py:504
  41.7 0.7 %shard_map.142 = (bf16[512,256]{1,0:T(8,128)(2,1)S(1)}, bf16[512,256]{1,0:T(8,128)(2,1)S(1)}) custom-call(f32[512,256]{1,0:T(8,128)S(1)} %get-tuple-element.61.gat, bf16[384,256]{1,0:T(8,128)(2,1)S(1)} %get-tuple-element.42.gh, bf16[384,256]{1,0:T(8,128)(2,1)S(1)} %get-tuple-element.43.gl, f32[256,128]{1,0:T(8,128)S(1)} %collective-permute-done.12.refs_0_, ...), custom_call_target="tpu_custom_call" | custom-call | flops 1000000000 | bytes 1048576 | tf_op jit(solution)/shard_map/pallas_call | solution.py:472
  42.3 0.6 shard_map.143.part
  42.9 1.2 %collective-permute-done.19.refs_2_ = f32[2,8,128]{2,1,0:T(8,128)S(1)} collective-permute-done((f32[2,8,128]{2,1,0:T(8,128)S(1)}, f32[2,8,128]{2,1,0:T(8,128)S(1)}, u32[]{:S(2)}, u32[]{:S(2)}) %collective-permute-start.19) | collective-permute-done | bytes 8224 | tf_op jit(solution)/shard_map/ppermute | solution.py:504
  44.2 1.4 %collective-permute-done.20.refs_3_ = f32[2,8,128]{2,1,0:T(8,128)S(1)} collective-permute-done((f32[2,8,128]{2,1,0:T(8,128)S(1)}, f32[2,8,128]{2,1,0:T(8,128)S(1)}, u32[]{:S(2)}, u32[]{:S(2)}) %collective-permute-start.20) | collective-permute-done | bytes 8224 | tf_op jit(solution)/shard_map/ppermute | solution.py:504
  45.6 0.9 %shard_map.144 = f32[32,1,128]{2,1,0:T(1,128)S(1)} custom-call(f32[512,256]{1,0:T(8,128)S(1)} %shard_map.143.part, f32[192,1536]{1,0:T(8,128)S(1)} %shard_map.137.far_op, s32[1,1,256]{2,1,0:T(1,128)S(1)} %get-tuple-element.53.cells, f32[168,128]{1,0:T(8,128)S(1)} %get-tuple-element.54.col, f32[512,256]{1,0:T(8,128)S(1)} %get-tuple-element.37.f_in, ...), custom_call_target="tpu_custom_call" | custom-call | flops 100000000 | bytes 1048576 | tf_op jit(solution)/shard_map/pallas_call | solution.py:472
  46.5 9.5 %all_to_all.5.stats = f32[32,1,128]{2,1,0:T(1,128)S(1)} all-to-all(f32[32,1,128]{2,1,0:T(1,128)S(1)} %shard_map.144), channel_id=1, replica_groups=mesh['gx'=4,'gy'=2,'gz'=4] {'gx','gy','gz'}, dimensions={0} | all-to-all | bytes 32768 | tf_op jit(solution)/shard_map/all_to_all | solution.py:620
  55.9 2.1 %shard_map.145 = (f32[486,1,256]{2,1,0:T(1,128)}, f32[1,1]{1,0:T(1,128)}) custom-call(f32[512,256]{1,0:T(8,128)S(1)} %get-tuple-element.37.f_in, f32[512,256]{1,0:T(8,128)S(1)} %get-tuple-element.55.u_in, f32[32,1,128]{2,1,0:T(1,128)S(1)} %all_to_all.5.stats), custom_call_target="tpu_custom_call" | custom-call | flops 10000000 | bytes 1048576 | tf_op jit(solution)/shard_map/pallas_call | solution.py:472
  (27 shorter events, 1.1 us)
Async XLA Ops:
  2.1 8.2 %collective-permute-start = (f32[264,128]{1,0:T(8,128)S(1)}, f32[264,128]{1,0:T(8,128)S(1)}, u32[]{:S(2)}, u32[]{:S(2)}) collective-permute-start(f32[264,128]{1,0:T(8,128)S(1)} %get-tuple-element.44.refs_0_.message), channel_id=1, source_target_pairs={{4,0},{0,4},{12,8},{8,12},{20,16},{16,20},{28,24},{24,28},{5,1},{1... | collective-permute-start | bytes 405512 | tf_op jit(solution)/shard_map/ppermute | solution.py:500
  5.1 8.7 %collective-permute-start.1 = (f32[264,128]{1,0:T(8,128)S(1)}, f32[264,128]{1,0:T(8,128)S(1)}, u32[]{:S(2)}, u32[]{:S(2)}) collective-permute-start(f32[264,128]{1,0:T(8,128)S(1)} %get-tuple-element.44.refs_0_.message), channel_id=1, source_target_pairs={{24,0},{28,4},{16,8},{20,12},{8,16},{12,20},{0,24},{4,28},{25,1},{... | collective-permute-start | bytes 405512 | tf_op jit(solution)/shard_map/ppermute | solution.py:500
  5.7 8.0 %collective-permute-start.2 = (f32[264,128]{1,0:T(8,128)S(1)}, f32[264,128]{1,0:T(8,128)S(1)}, u32[]{:S(2)}, u32[]{:S(2)}) collective-permute-start(f32[264,128]{1,0:T(8,128)S(1)} %get-tuple-element.44.refs_0_.message), channel_id=1, source_target_pairs={{28,0},{24,4},{20,8},{16,12},{12,16},{8,20},{4,24},{0,28},{29,1},{... | collective-permute-start | bytes 405512 | tf_op jit(solution)/shard_map/ppermute | solution.py:500
  6.3 7.6 %collective-permute-start.3 = (f32[264,128]{1,0:T(8,128)S(1)}, f32[264,128]{1,0:T(8,128)S(1)}, u32[]{:S(2)}, u32[]{:S(2)}) collective-permute-start(f32[264,128]{1,0:T(8,128)S(1)} %get-tuple-element.44.refs_0_.message), channel_id=1, source_target_pairs={{8,0},{12,4},{0,8},{4,12},{24,16},{28,20},{16,24},{20,28},{9,1},{1... | collective-permute-start | bytes 405512 | tf_op jit(solution)/shard_map/ppermute | solution.py:500
  10.3 3.7 %collective-permute-start.4 = (f32[264,128]{1,0:T(8,128)S(1)}, f32[264,128]{1,0:T(8,128)S(1)}, u32[]{:S(2)}, u32[]{:S(2)}) collective-permute-start(f32[264,128]{1,0:T(8,128)S(1)} %collective-permute-done.refs_1_.refs_0_), channel_id=1, source_target_pairs={{8,0},{12,4},{0,8},{4,12},{24,16},{28,20},{16,24},{20,28},{9,1},{1... | collective-permute-start | bytes 405512 | tf_op jit(solution)/shard_map/ppermute | solution.py:500
  13.8 1.2 %collective-permute-start.5 = (f32[8,128]{1,0:T(8,128)S(1)}, f32[8,128]{1,0:T(8,128)S(1)}, u32[]{:S(2)}, u32[]{:S(2)}) collective-permute-start(f32[8,128]{1,0:T(8,128)S(1)} %shard_map.133.refs_5_.refs_0_), channel_id=1, source_target_pairs={{8,0},{12,4},{0,8},{4,12},{24,16},{28,20},{16,24},{20,28},{9,1},{1... | collective-permute-start | bytes 12296 | tf_op jit(solution)/shard_map/ppermute | solution.py:500
  15.0 7.5 %collective-permute-start.6 = (f32[2,8,128]{2,1,0:T(8,128)S(1)}, f32[2,8,128]{2,1,0:T(8,128)S(1)}, u32[]{:S(2)}, u32[]{:S(2)}) collective-permute-start(f32[2,8,128]{2,1,0:T(8,128)S(1)} %shard_map.136._.refs_0_), channel_id=1, source_target_pairs={{1,0},{0,1},{3,2},{2,3},{5,4},{4,5},{7,6},{6,7},{9,8},{8,9},{11,10... | collective-permute-start | bytes 24584 | tf_op jit(solution)/shard_map/ppermute | solution.py:504
  16.6 5.9 %collective-permute-start.7 = (f32[2,8,128]{2,1,0:T(8,128)S(1)}, f32[2,8,128]{2,1,0:T(8,128)S(1)}, u32[]{:S(2)}, u32[]{:S(2)}) collective-permute-start(f32[2,8,128]{2,1,0:T(8,128)S(1)} %shard_map.136._.refs_0_), channel_id=1, source_target_pairs={{2,0},{3,1},{0,2},{1,3},{6,4},{7,5},{4,6},{5,7},{10,8},{11,9},{8,1... | collective-permute-start | bytes 24584 | tf_op jit(solution)/shard_map/ppermute | solution.py:504
  19.2 5.4 %collective-permute-start.8 = (f32[2,8,128]{2,1,0:T(8,128)S(1)}, f32[2,8,128]{2,1,0:T(8,128)S(1)}, u32[]{:S(2)}, u32[]{:S(2)}) collective-permute-start(f32[2,8,128]{2,1,0:T(8,128)S(1)} %shard_map.136._.refs_0_), channel_id=1, source_target_pairs={{3,0},{2,1},{1,2},{0,3},{7,4},{6,5},{5,6},{4,7},{11,8},{10,9},{9,1... | collective-permute-start | bytes 24584 | tf_op jit(solution)/shard_map/ppermute | solution.py:504
  25.2 4.3 %collective-permute-start.10 = (f32[8,128]{1,0:T(8,128)S(1)}, f32[8,128]{1,0:T(8,128)S(1)}, u32[]{:S(2)}, u32[]{:S(2)}) collective-permute-start(f32[8,128]{1,0:T(8,128)S(1)} %get-tuple-element.63.refs_0_.message), channel_id=1, source_target_pairs={{24,0},{28,4},{16,8},{20,12},{8,16},{12,20},{0,24},{4,28},{25,1},{... | collective-permute-start | bytes 12296 | tf_op jit(solution)/shard_map/ppermute | solution.py:500
  25.2 4.3 %collective-permute-start.11 = (f32[8,128]{1,0:T(8,128)S(1)}, f32[8,128]{1,0:T(8,128)S(1)}, u32[]{:S(2)}, u32[]{:S(2)}) collective-permute-start(f32[8,128]{1,0:T(8,128)S(1)} %get-tuple-element.63.refs_0_.message), channel_id=1, source_target_pairs={{28,0},{24,4},{20,8},{16,12},{12,16},{8,20},{4,24},{0,28},{29,1},{... | collective-permute-start | bytes 12296 | tf_op jit(solution)/shard_map/ppermute | solution.py:500
  26.5 3.6 %collective-permute-start.9 = (f32[8,128]{1,0:T(8,128)S(1)}, f32[8,128]{1,0:T(8,128)S(1)}, u32[]{:S(2)}, u32[]{:S(2)}) collective-permute-start(f32[8,128]{1,0:T(8,128)S(1)} %get-tuple-element.63.refs_0_.message), channel_id=1, source_target_pairs={{4,0},{0,4},{12,8},{8,12},{20,16},{16,20},{28,24},{24,28},{5,1},{1... | collective-permute-start | bytes 12296 | tf_op jit(solution)/shard_map/ppermute | solution.py:500
  30.1 6.0 %collective-permute-start.12 = (f32[256,128]{1,0:T(8,128)S(1)}, f32[256,128]{1,0:T(8,128)S(1)}, u32[]{:S(2)}, u32[]{:S(2)}) collective-permute-start(f32[256,128]{1,0:T(8,128)S(1)} %get-tuple-element.65), channel_id=1, source_target_pairs={{4,0},{0,4},{12,8},{8,12},{20,16},{16,20},{28,24},{24,28},{5,1},{1... | collective-permute-start | bytes 393224 | tf_op jit(solution)/shard_map/ppermute | solution.py:500
  32.1 1.8 %collective-permute-start.16 = (f32[8,128]{1,0:T(8,128)S(1)}, f32[8,128]{1,0:T(8,128)S(1)}, u32[]{:S(2)}, u32[]{:S(2)}) collective-permute-start(f32[8,128]{1,0:T(8,128)S(1)} %shard_map.140.refs_0_), channel_id=1, source_target_pairs={{8,0},{12,4},{0,8},{4,12},{24,16},{28,20},{16,24},{20,28},{9,1},{1... | collective-permute-start | bytes 12296 | tf_op jit(solution)/shard_map/ppermute | solution.py:500
  32.1 7.5 %collective-permute-start.13 = (f32[256,128]{1,0:T(8,128)S(1)}, f32[256,128]{1,0:T(8,128)S(1)}, u32[]{:S(2)}, u32[]{:S(2)}) collective-permute-start(f32[256,128]{1,0:T(8,128)S(1)} %get-tuple-element.65), channel_id=1, source_target_pairs={{24,0},{28,4},{16,8},{20,12},{8,16},{12,20},{0,24},{4,28},{25,1},{... | collective-permute-start | bytes 393224 | tf_op jit(solution)/shard_map/ppermute | solution.py:500
  33.5 6.6 %collective-permute-start.14 = (f32[256,128]{1,0:T(8,128)S(1)}, f32[256,128]{1,0:T(8,128)S(1)}, u32[]{:S(2)}, u32[]{:S(2)}) collective-permute-start(f32[256,128]{1,0:T(8,128)S(1)} %get-tuple-element.65), channel_id=1, source_target_pairs={{28,0},{24,4},{20,8},{16,12},{12,16},{8,20},{4,24},{0,28},{29,1},{... | collective-permute-start | bytes 393224 | tf_op jit(solution)/shard_map/ppermute | solution.py:500
  33.6 8.0 %collective-permute-start.15 = (f32[256,128]{1,0:T(8,128)S(1)}, f32[256,128]{1,0:T(8,128)S(1)}, u32[]{:S(2)}, u32[]{:S(2)}) collective-permute-start(f32[256,128]{1,0:T(8,128)S(1)} %get-tuple-element.65), channel_id=1, source_target_pairs={{8,0},{12,4},{0,8},{4,12},{24,16},{28,20},{16,24},{20,28},{9,1},{1... | collective-permute-start | bytes 393224 | tf_op jit(solution)/shard_map/ppermute | solution.py:500
  36.1 5.6 %collective-permute-start.17 = (f32[256,128]{1,0:T(8,128)S(1)}, f32[256,128]{1,0:T(8,128)S(1)}, u32[]{:S(2)}, u32[]{:S(2)}) collective-permute-start(f32[256,128]{1,0:T(8,128)S(1)} %collective-permute-done.12.refs_0_), channel_id=1, source_target_pairs={{8,0},{12,4},{0,8},{4,12},{24,16},{28,20},{16,24},{20,28},{9,1},{1... | collective-permute-start | bytes 393224 | tf_op jit(solution)/shard_map/ppermute | solution.py:500
  36.1 6.8 %collective-permute-start.18 = (f32[2,8,128]{2,1,0:T(8,128)S(1)}, f32[2,8,128]{2,1,0:T(8,128)S(1)}, u32[]{:S(2)}, u32[]{:S(2)}) collective-permute-start(f32[2,8,128]{2,1,0:T(8,128)S(1)} %shard_map.141.refs_5_.refs_0_), channel_id=1, source_target_pairs={{1,0},{0,1},{3,2},{2,3},{5,4},{4,5},{7,6},{6,7},{9,8},{8,9},{11,10... | collective-permute-start | bytes 24584 | tf_op jit(solution)/shard_map/ppermute | solution.py:504
  39.5 4.6 %collective-permute-start.19 = (f32[2,8,128]{2,1,0:T(8,128)S(1)}, f32[2,8,128]{2,1,0:T(8,128)S(1)}, u32[]{:S(2)}, u32[]{:S(2)}) collective-permute-start(f32[2,8,128]{2,1,0:T(8,128)S(1)} %shard_map.141.refs_5_.refs_0_), channel_id=1, source_target_pairs={{2,0},{3,1},{0,2},{1,3},{6,4},{7,5},{4,6},{5,7},{10,8},{11,9},{8,1... | collective-permute-start | bytes 24584 | tf_op jit(solution)/shard_map/ppermute | solution.py:504
  40.1 5.5 %collective-permute-start.20 = (f32[2,8,128]{2,1,0:T(8,128)S(1)}, f32[2,8,128]{2,1,0:T(8,128)S(1)}, u32[]{:S(2)}, u32[]{:S(2)}) collective-permute-start(f32[2,8,128]{2,1,0:T(8,128)S(1)} %shard_map.141.refs_5_.refs_0_), channel_id=1, source_target_pairs={{3,0},{2,1},{1,2},{0,3},{7,4},{6,5},{5,6},{4,7},{11,8},{10,9},{9,1... | collective-permute-start | bytes 24584 | tf_op jit(solution)/shard_map/ppermute | solution.py:504

commit v8 on v6

--- a/solution.py
+++ b/solution.py
@@ -103,9 +103,10 @@
     return jnp.where(cells == row, 1.0, 0.0).astype(bf16)
 
 
-def pack_charges(parts, weight_col, occ, s):
+def pack_charges(parts, weight_col, occ, s, count=False):
     moments = [jnp.sum(part * weight_col, axis=0, keepdims=True) for part in parts]
-    moments = jnp.concatenate(moments + [jnp.zeros((5, s.bodies), f32)], axis=0)
+    moments.append(jnp.full((1, s.bodies), 1.0 if count else 0.0, f32))
+    moments = jnp.concatenate(moments + [jnp.zeros((4, s.bodies), f32)], axis=0)
     high, rest = split(moments)
     mid, low = split(moments - high.astype(f32))
     stack = jnp.concatenate([high.astype(f32), mid.astype(f32), low.astype(f32)], axis=0).astype(bf16)
@@ -218,7 +219,7 @@
 def setup(
     s, ids, f_in, moves, angles, near_weight, neighbours, self_mob, near_mat, perm, interp, sibling, root,
     loc_out, gat_out, rot_out, sh_out, sl_out, nh_out, nl_out, oh_out, ol_out, gh_out, gl_out,
-    far_out, padded, ups_ref,
+    far_out, uh_out, ul_out, bh_out, bl_out, rh_out, rl_out, padded, ups_ref,
 ):
     f = f_in[...]
     for move in moves[:3]:
@@ -273,7 +274,10 @@
         kept = jnp.where(perm[level : level + 1, :n] == spot, 1.0, 0.0)
         moved = jnp.where(perm[level : level + 1, n:] == spot, 1.0, 0.0).astype(bf16)
         hi, lo = split(interp[level])
-        ups_ref[level] = kept + (mm(moved, hi) + mm(moved, lo))
+        up = kept + (mm(moved, hi) + mm(moved, lo))
+        ups_ref[level] = up
+        uh_out[level], ul_out[level] = split(up)
+        bh_out[level], bl_out[level] = split(sibling[level])
         bit = (z >> level) & 1
         halves.append(
             [ups_ref[level, pl.ds(pl.multiple_of(side * n, 8), n), :] for side in (bit, 1 - bit)]
@@ -283,6 +287,7 @@
         return product(dot, split(halves[level][0]), split(block))
 
     spread = root[...]
+    rh_out[...], rl_out[...] = split(spread)
     beside = []
     for level in reversed(range(s.levels)):
         spread = down(spread, level, mt if level == s.levels - 1 else mm)
@@ -378,11 +383,12 @@
 
 
 def first_kernel(s, part, far_op, cells, col, *refs):
-    *layers, u_out, message_out = refs
+    *layers, u_out, rim_out, charges_out = refs
     weight_col = col[:, :1]
     u = with_far(s, part, layers, far_op, cells, weight_col)
     u_out[...] = u
-    message_out[...] = pack_message(u, weight_col, cells[0], s)
+    rim_out[...] = pack_rim(u, s)
+    charges_out[...] = pack_charges(pieces(u, s), weight_col, occupancy(cells[0], s), s)
 
 
 def safe_inverse(x):
@@ -404,30 +410,122 @@
     )
 
 
-def second_kernel(s, part, far_op, cells, col, f_in, ortho_in, stat, *refs):
-    *layers, stat_out = refs
-    t = with_far(s, part, layers, far_op, cells, col[:, :1])
+def second_kernel(
+    s, loc, nh, nl, hi, lo, cells, col, f_in, ortho_in, stat, charges_f, charges_u, packed_out
+):
+    part = loc[...] + product(mm, (nh[...], nl[...]), (hi[...], lo[...]))
     f, ortho = f_in[...], ortho_in[...]
     ff, fu, oo = (stat[i : i + 1, :1] for i in range(3))
-    ft = total(f * t) * safe_inverse(ff)
-    ot = total(ortho * t) * safe_inverse(oo)
-    rest_t = t - ft * f - ot * ortho
-    tt = total(rest_t * rest_t)
+    fa = total(f * part) * safe_inverse(ff)
+    oa = total(ortho * part) * safe_inverse(oo)
+    rest = part - fa * f - oa * ortho
+    aa = total(rest * rest)
     rf, ro = jnp.sqrt(ff), jnp.sqrt(oo)
-    lane = lax.broadcasted_iota(jnp.int32, (1, LANES), 1)
-    stats = jnp.zeros((1, LANES), f32)
-    for index, value in enumerate((rf, rf * fu, ro, rf * ft, ro * ot, jnp.sqrt(tt))):
-        stats = jnp.where(lane == index, value, stats)
-    stat_out[:, 0, :] = jnp.broadcast_to(stats, (s.devices, LANES))
-
-
-def finish_kernel(s, f_in, u_in, stats, x_out, lsq_out, raw, sem):
-    rows = stats[:, 0, :]
-    rest = round_up(s.devices, LANES) - s.devices
+    of_f = charges_f[-8:, :]
+    of_u = charges_u[...]
+    of_a = pack_charges(pieces(rest, s), col[:, :1], occupancy(cells[0], s), s, count=True)
+    row = lax.broadcasted_iota(jnp.int32, (8, LANES), 0)
+    lane = lax.broadcasted_iota(jnp.int32, (8, LANES), 1)
+    left = lane < RIM
+    first = jnp.where(left, of_u, pltpu.roll(of_a, RIM, 1))
+    first = jnp.where(row < 4, of_u, first)
+    first = jnp.where((row == 7) & left, pltpu.roll(of_f, 1, 0), first)
+    for index, value in enumerate((rf, rf * fu, ro, rf * fa, ro * oa, aa)):
+        first = jnp.where((row == 3) & (lane == index), value, first)
+    tails = jnp.where(left, pltpu.roll(of_f, 3, 0), pltpu.roll(pltpu.roll(of_f, 2, 0), RIM, 1))
+    second = jnp.where(row < 3, of_f, of_a)
+    second = jnp.where(row < 4, second, pltpu.roll(of_a, 4, 0))
+    second = jnp.where(row == 7, tails, second)
+    packed = jnp.concatenate([first, second], axis=0)
+    packed_out[...] = jnp.broadcast_to(packed[None], packed_out.shape)
+
+
+def tree(s, leaves, ups, siblings, root):
+    def apply(dot, blocks, factor):
+        rows = blocks[0].shape[0]
+        out = product(dot, split(jnp.concatenate(blocks, axis=0)), factor)
+        return [out[i * rows : (i + 1) * rows] for i in range(len(blocks))]
+
+    n = s.skel
+    halves = [[(hi[level, j * n : (j + 1) * n, :], lo[level, j * n : (j + 1) * n, :]) for j in range(2)]
+              for level, (hi, lo) in ((k, ups) for k in range(s.levels))]
+    charges = [leaves]
+    for level in range(s.levels):
+        low, high = (apply(mm, charges[-1][j::2], halves[level][j]) for j in range(2))
+        charges.append([a + b for a, b in zip(low, high)])
+    own = charges[-1][0]
+    whole = own[:8]
+    for column in range(1, s.nx * s.ny):
+        whole = whole + own[8 * column : 8 * column + 8]
+    others = jnp.concatenate([whole] * (s.nx * s.ny), axis=0) - own
+    potential = apply(mm, [others], root)
+    for level in reversed(range(s.levels)):
+        beside = apply(mm, charges[level], (siblings[0][level], siblings[1][level]))
+        down = [apply(mt, potential, halves[level][j]) for j in range(2)]
+        potential = [
+            down[z % 2][z // 2] + beside[z ^ 1] for z in range(len(charges[level]))
+        ]
+    return potential
+
+
+def box_numbers(s, boxes, ups, siblings, root):
+    columns = s.nx * s.ny
+    row = lax.broadcasted_iota(jnp.int32, (8, LANES), 0)
+    lane = lax.broadcasted_iota(jnp.int32, (8, LANES), 1)
+    left, valid = lane < RIM, row < 3
+    leaves = []
+    for z in range(s.nz):
+        wide = []
+        for column in range(columns):
+            tile = boxes[column * s.nz + z, :8, :]
+            wide.append(jnp.concatenate([tile, pltpu.roll(tile, 4, 0)], axis=1)[:, : s.skel])
+        leaves.append(jnp.concatenate(wide, axis=0))
+    potential = tree(s, leaves, ups, siblings, root)
+    out = []
+    for start in range(0, s.devices, 8):
+        sums = [jnp.zeros((8, LANES), f32) for _ in range(5)]
+        for box in range(start, min(s.devices, start + 8)):
+            column, z = box // s.nz, box % s.nz
+            phi = potential[z][8 * column : 8 * column + 8]
+            main, tail = phi[:, :LANES], phi[:, LANES:]
+            tail = jnp.concatenate([tail, tail], axis=1)
+            first, second = boxes[box, :8, :], boxes[box, 8:, :]
+            both = pltpu.roll(first, 4, 0) * tail
+            of_f = jnp.where(row == 0, pltpu.roll(second, 1, 0), jnp.where(row == 1, pltpu.roll(second, 2, 0), pltpu.roll(first, 3, 0)))
+            of_f = jnp.where(left == (row != 1), of_f * tail, 0.0)
+            count = jnp.broadcast_to(second[3:4], (8, LANES))
+            count_tail = jnp.where(left, 0.0, jnp.broadcast_to(first[7:8], (8, LANES)))
+            terms = (
+                second * main + of_f,
+                first * main + jnp.where(left, both, 0.0),
+                pltpu.roll(second, 4, 0) * main + jnp.where(left, 0.0, both),
+                count * (main * main) + count_tail * (tail * tail),
+            )
+            here = row == box - start
+            for index, term in enumerate(terms):
+                value = jnp.sum(jnp.where(valid, term, 0.0), axis=0, keepdims=True)
+                sums[index] = jnp.where(here, value, sums[index])
+            sums[4] = jnp.where(here, first[3:4], sums[4])
+        numbers = sums[4]
+        for index in range(4):
+            numbers = jnp.where(lane == 6 + index, jnp.sum(sums[index], axis=1, keepdims=True), numbers)
+        out.append(numbers)
+    rest = round_up(s.devices, LANES) - 8 * len(out)
     if rest:
-        rows = jnp.concatenate([rows, jnp.zeros((rest, LANES), f32)], axis=0)
-    rows = rows.T
-    f1, u1, u2, t1, t2, t3 = (rows[i : i + 1] for i in range(6))
+        out.append(jnp.zeros((rest, LANES), f32))
+    return jnp.concatenate(out, axis=0)
+
+
+def finish_kernel(s, f_in, u_in, boxes, col, uh, ul, bh, bl, rh, rl, x_out, lsq_out, raw, sem):
+    rows = box_numbers(s, boxes, (uh, ul), (bh, bl), (rh[...], rl[...])).T
+    f1, u1, u2, t1, t2, aa, far_f, far_u, far_a, far_far = (rows[i : i + 1] for i in range(10))
+    by_f = safe_inverse(f1)
+    by_o = jnp.where(u2 * u2 > 1e-10 * (u1 * u1), safe_inverse(u2), 0.0)
+    on_one = far_f * by_f
+    on_two = (far_u - u1 * by_f * far_f) * by_o
+    weight = jnp.sum(col[:, :1] * col[:, :1], axis=0, keepdims=True)
+    t3 = aa + 2.0 * far_a + weight * far_far - on_one * on_one - on_two * on_two
+    t1, t2, t3 = t1 + on_one, t2 + on_two, jnp.sqrt(jnp.maximum(t3, 0.0))
 
     def along(x):
         return jnp.sum(x, axis=1, keepdims=True)
@@ -504,23 +602,31 @@
             lax.ppermute(x, "gz", [(z ^ k, z) for z in range(s.nz)]) for k in range(1, s.nz)
         ]
 
-    def fetch_messages(message):
+    def fetch_rims(rim):
         got = {}
         for dy in s.shifts:
-            got["same", dy] = fetch(message, "same", dy)
+            got["same", dy] = fetch(rim, "same", dy)
         for dy in s.shifts:
-            got["other", dy] = fetch(message, "other", dy)
-        got["other", 0] = fetch(message, "other", 0)
-        got["partner", 0] = fetch(message, "partner", 0)
+            got["other", dy] = fetch(rim, "other", dy)
+        got["other", 0] = fetch(rim, "other", 0)
+        got["partner", 0] = fetch(rim, "partner", 0)
         return got
 
-    def forward_messages(got, after):
+    def forward_rims(got, after):
         for dy in s.shifts:
             ready, _ = lax.optimization_barrier((got["same", dy], after))
             got["partner", dy] = fetch(ready, "partner", 0)
 
+    def gather(gat, got, after):
+        return call(
+            functools.partial(gather_kernel, s),
+            [(full, bf16), (full, bf16)],
+            [gat, gh, gl] + [got[key] for key in s.sources] + [after],
+            flops=10**9,
+        )
+
     def share(message, got, gat, after):
-        forward_messages(got, after)
+        forward_rims(got, after)
         if s.direct:
             quarter = [message] + [got[key] for key in s.sources if key[0] != "partner"]
             (half,) = call(functools.partial(half_kernel, s), [(tile, f32)], quarter + [after])
@@ -528,12 +634,7 @@
         else:
             half = lax.psum(message[s.half :], ("gx", "gy"))
             sums = [half]
-        gathered = call(
-            functools.partial(gather_kernel, s),
-            [(full, bf16), (full, bf16)],
-            [gat, gh, gl] + [got[key] for key in s.sources] + [half],
-            flops=10**9,
-        )
+        gathered = gather(gat, got, half)
         (pair,) = call(
             functools.partial(layer_kernel, s), [((2,) + tile, f32)], [message] + sums + [gathered[1]]
         )
@@ -554,18 +655,21 @@
         scratch=[pltpu.VMEM(flat, f32), pltpu.VMEM(small, f32), pltpu.SemaphoreType.DMA((3,))],
         flops=10**7,
     )
-    got = fetch_messages(message)
+    got = fetch_rims(message)
     operators = [
         angles.reshape(3, 1, s.bodies), near_weight, neighbours, self_mob, near_mat, skel_perm, interp,
         sibling_ops, root_op,
     ]
-    loc, gat, rot, sh, sl, nh, nl, oh, ol, gh, gl, far_op = call(
+    loc, gat, rot, sh, sl, nh, nl, oh, ol, gh, gl, far_op, *operators_out = call(
         functools.partial(setup_kernel, s),
         [(full, f32), (full, f32), ((16, s.bodies), f32)]
         + [(square, bf16)] * 4
         + [((s.bodies, s.bodies), bf16)] * 2
         + [((s.ghosts, s.bodies), bf16)] * 2
-        + [(far_shape, f32)],
+        + [(far_shape, f32)]
+        + [((s.levels, 2 * s.skel, s.skel), bf16)] * 2
+        + [((s.levels, s.skel, s.skel), bf16)] * 2
+        + [((s.skel, s.skel), bf16)] * 2,
         [ids, f] + operators,
         scalars=1,
         far_args=len(operators),
@@ -576,32 +680,32 @@
     )
     gathered, layers = share(message, got, gat, rot)
     part = near_part(loc, gathered)
-    u, message = call(
+    u, rim, charges = call(
         functools.partial(first_kernel, s),
-        [(full, f32), ((s.message, LANES), f32)],
+        [(full, f32), ((s.half, LANES), f32), (tile, f32)],
         [part, far_op, cells, col, *layers],
         flops=10**8,
     )
-    got = fetch_messages(message)
+    got = fetch_rims(rim)
     loc, gat, ortho, stat = call(
         functools.partial(middle_kernel, s),
         [(full, f32), (full, f32), (full, f32), (tile, f32)],
         [u, f, rot, sh, sl, oh, ol],
         flops=10**9,
     )
-    gathered, layers = share(message, got, gat, stat)
-    part = near_part(loc, gathered)
-    (stats,) = call(
+    forward_rims(got, stat)
+    gathered = gather(gat, got, stat)
+    (packed,) = call(
         functools.partial(second_kernel, s),
-        [((s.devices, 1, LANES), f32)],
-        [part, far_op, cells, col, f, ortho, stat, *layers],
-        flops=10**8,
-    )
-    stats = lax.all_to_all(stats, ("gx", "gy", "gz"), 0, 0)
+        [((s.devices, 16, LANES), f32)],
+        [loc, nh, nl, *gathered, cells, col, f, ortho, stat, message, charges],
+        flops=10**9,
+    )
+    boxes = lax.all_to_all(packed, ("gx", "gy", "gz"), 0, 0)
     result, lsq = call(
         functools.partial(finish_kernel, s),
         [(flat, f32), ((1, 1), f32)],
-        [f, u, stats],
+        [f, u, boxes, col, *operators_out],
         far_outs=1,
         scratch=[pltpu.VMEM(flat, f32), pltpu.SemaphoreType.DMA],
         flops=10**7,

time: 57.1 us -> 53.6 us (0.939)
  starting transfers between devices: 17.2 us -> 12.6 us
  Pallas kernels: 14 us -> 15.7 us
  waiting for transfers between devices: 13.5 us -> 11.8 us
  blocking collectives: 11.3 us -> 12.5 us
    ppermute x6 -> x3, starting transfers between devices: 8.77 us -> 4.39 us  [fetch_layers(): lax.ppermute(x, 'gz', [(z ^ k, z) for z in range(s.nz)])]
    pallas_call x14 -> x11, Pallas kernels: 14 us -> 15.7 us  [call(): pl.pallas_call(kernel, out_shape=[jax.ShapeDtypeStruct(shape, kind) for s...]
    ppermute x6 -> x3, waiting for transfers between devices: 5.89 us -> 4.64 us  [fetch_layers(): lax.ppermute(x, 'gz', [(z ^ k, z) for z in range(s.nz)])]
    all_to_all x1, blocking collectives: 11.3 us -> 12.5 us  [body(): boxes = lax.all_to_all(packed, ('gx', 'gy', 'gz'), 0, 0)]
    ppermute x12 -> x11, waiting for transfers between devices: 7.65 us -> 7.13 us  [fetch(): return lax.ppermute(x, ('gx', 'gy'), pairs)]
    ppermute x12 -> x11, starting transfers between devices: 8.42 us -> 8.25 us  [fetch(): return lax.ppermute(x, ('gx', 'gy'), pairs)]
  transfers between devices with their start and end apart: 18 -> 14, of which waited for: 8 -> 6; matrix products, arithmetic and copies ran while one was open for 0% -> 0% of each run, Pallas kernels for 16% -> 15%
where the time goes in v8:
time: 53.6 us; the launch traced here: 53.3 us
  Pallas kernels  15.7 us (29%)
  starting transfers between devices  12.6 us (24%)
  blocking collectives  12.5 us (23%)
  waiting for transfers between devices  11.8 us (22%)
  between operations  0.72 us (1%)
    pallas_call x11, Pallas kernels, call(): pl.pallas_call(kernel, out_shape=[jax.ShapeDtypeStruct(shape, kind) for s...  15.7 us
    all_to_all x1, blocking collectives, body(): boxes = lax.all_to_all(packed, ('gx', 'gy', 'gz'), 0, 0)  12.5 us
    ppermute x11, starting transfers between devices, fetch(): return lax.ppermute(x, ('gx', 'gy'), pairs)  8.25 us
    ppermute x11, waiting for transfers between devices, fetch(): return lax.ppermute(x, ('gx', 'gy'), pairs)  7.13 us
    ppermute x3, waiting for transfers between devices, fetch_layers(): lax.ppermute(x, 'gz', [(z ^ k, z) for z in range(s.nz)])  4.64 us
    ppermute x3, starting transfers between devices, fetch_layers(): lax.ppermute(x, 'gz', [(z ^ k, z) for z in range(s.nz)])  4.39 us
  transfers between devices with their start and end apart: 14, of which 6 were waited for; matrix products, arithmetic and copies ran while one was open for 0% of the time, Pallas kernels for 15%

profile of v8, /device:TPU:0, one launch (start us, length us, event | category | flops | bytes accessed | tf_op | source)
XLA Modules:
  0.0 53.3 jit_solution(5077834149572315637)
XLA Ops:
  0.6 1.4 %shard_map.131 = (f32[264,128]{1,0:T(8,128)S(1)}, f32[168,128]{1,0:T(8,128)S(1)}, s32[1,1,256]{2,1,0:T(1,128)S(1)}, f32[512,256]{1,0:T(8,128)S(1)}) custom-call(f32[486,1,256]{2,1,0:T(1,128)} %bitcast.9, s32[1,1,256]{2,1,0:T(1,128)} %cells.1, f32[1,162]{1,0:T(1,128)} %bitcast.10), custom_call_target="tpu_custom_call" | custom-call | flops 10000000 | bytes 1048576 | tf_op jit(solution)/shard_map/pallas_call | solution.py:570
  2.1 3.0 %collective-permute-start = (f32[264,128]{1,0:T(8,128)S(1)}, f32[264,128]{1,0:T(8,128)S(1)}, u32[]{:S(2)}, u32[]{:S(2)}) collective-permute-start(f32[264,128]{1,0:T(8,128)S(1)} %get-tuple-element.46.refs_0_.message.charges_f), channel_id=1, source_target_pairs={{4,0},{0,4},{12,8},{8,12},{20,16},{16,20},{28,24},{24,28},{5,1},{1... | collective-permute-start | bytes 405512 | tf_op jit(solution)/shard_map/ppermute | solution.py:598
  5.1 0.7 %collective-permute-start.1 = (f32[264,128]{1,0:T(8,128)S(1)}, f32[264,128]{1,0:T(8,128)S(1)}, u32[]{:S(2)}, u32[]{:S(2)}) collective-permute-start(f32[264,128]{1,0:T(8,128)S(1)} %get-tuple-element.46.refs_0_.message.charges_f), channel_id=1, source_target_pairs={{24,0},{28,4},{16,8},{20,12},{8,16},{12,20},{0,24},{4,28},{25,1},{... | collective-permute-start | bytes 405512 | tf_op jit(solution)/shard_map/ppermute | solution.py:598
  5.7 0.6 %collective-permute-start.2 = (f32[264,128]{1,0:T(8,128)S(1)}, f32[264,128]{1,0:T(8,128)S(1)}, u32[]{:S(2)}, u32[]{:S(2)}) collective-permute-start(f32[264,128]{1,0:T(8,128)S(1)} %get-tuple-element.46.refs_0_.message.charges_f), channel_id=1, source_target_pairs={{28,0},{24,4},{20,8},{16,12},{12,16},{8,20},{4,24},{0,28},{29,1},{... | collective-permute-start | bytes 405512 | tf_op jit(solution)/shard_map/ppermute | solution.py:598
  6.3 0.4 collective-permute-start.3
  6.7 0.1 pad_add_fusion.ids
  6.8 5.6 %shard_map.132 = (f32[512,256]{1,0:T(8,128)S(1)}, f32[512,256]{1,0:T(8,128)S(1)}, f32[16,256]{1,0:T(8,128)S(1)}, bf16[512,512]{1,0:T(8,128)(2,1)S(1)}, bf16[512,...) custom-call(s32[2]{0:T(128)S(1)} %pad_add_fusion.ids, ...), custom_call_target="tpu_custom_call" | custom-call | flops 5000000000 | bytes 1048576 | tf_op jit(solution)/shard_map/pallas_call | solution.py:570
  12.4 0.2 collective-permute-start.4
  12.6 1.2 %collective-permute-done.1.refs_2_.refs_1_ = f32[264,128]{1,0:T(8,128)S(1)} collective-permute-done((f32[264,128]{1,0:T(8,128)S(1)}, f32[264,128]{1,0:T(8,128)S(1)}, u32[]{:S(2)}, u32[]{:S(2)}) %collective-permute-start.1) | collective-permute-done | bytes 135200 | tf_op jit(solution)/shard_map/ppermute | solution.py:598
  13.8 0.0 collective-permute-done.2.refs_3_.refs_2_
  13.8 0.2 collective-permute-start.5
  14.0 0.7 %shard_map.134 = (bf16[512,256]{1,0:T(8,128)(2,1)S(1)}, bf16[512,256]{1,0:T(8,128)(2,1)S(1)}) custom-call(f32[512,256]{1,0:T(8,128)S(1)} %get-tuple-element.43.gat, bf16[384,256]{1,0:T(8,128)(2,1)S(1)} %get-tuple-element.44.gh, bf16[384,256]{1,0:T(8,128)(2,1)S(1)} %get-tuple-element.45.gl, f32[264,128]{1,0:T(8,128)S(1)} %collective-permute-done.refs_1_.refs_0_, ...), custom_call_target="tpu_custom_call" | custom-call | flops 1000000000 | bytes 1048576 | tf_op jit(solution)/shard_map/pallas_call | solution.py:570
  14.7 0.4 collective-permute-done.5.refs_1_
  15.0 1.6 %collective-permute-start.6 = (f32[2,8,128]{2,1,0:T(8,128)S(1)}, f32[2,8,128]{2,1,0:T(8,128)S(1)}, u32[]{:S(2)}, u32[]{:S(2)}) collective-permute-start(f32[2,8,128]{2,1,0:T(8,128)S(1)} %shard_map.136.refs_0_), channel_id=1, source_target_pairs={{1,0},{0,1},{3,2},{2,3},{5,4},{4,5},{7,6},{6,7},{9,8},{8,9},{11,10... | collective-permute-start | bytes 24584 | tf_op jit(solution)/shard_map/ppermute | solution.py:602
  16.6 2.6 %collective-permute-start.7 = (f32[2,8,128]{2,1,0:T(8,128)S(1)}, f32[2,8,128]{2,1,0:T(8,128)S(1)}, u32[]{:S(2)}, u32[]{:S(2)}) collective-permute-start(f32[2,8,128]{2,1,0:T(8,128)S(1)} %shard_map.136.refs_0_), channel_id=1, source_target_pairs={{2,0},{3,1},{0,2},{1,3},{6,4},{7,5},{4,6},{5,7},{10,8},{11,9},{8,1... | collective-permute-start | bytes 24584 | tf_op jit(solution)/shard_map/ppermute | solution.py:602
  19.2 0.2 collective-permute-start.8
  19.4 0.6 %shard_map.135.part = f32[512,256]{1,0:T(8,128)S(1)} custom-call(f32[512,256]{1,0:T(8,128)S(1)} %get-tuple-element.40.loc, bf16[512,512]{1,0:T(8,128)(2,1)S(1)} %get-tuple-element.41.nh, bf16[512,512]{1,0:T(8,128)(2,1)S(1)} %get-tuple-element.42.nl, bf16[512,256]{1,0:T(8,128)(2,1)S(1)} %get-tuple-element.49.hi, bf16[512,256]{1,0:T(8,128)(2,1)S(1)} %get-tuple-element.50.lo.refs_2_), custom_call_target="tpu_custom_call" | custom-call | flops 1000000000 | bytes 1048576 | tf_op jit(solution)/shard_map/pallas_call | solution.py:570
  20.0 0.0 collective-permute-done.6.refs_1_
  20.0 1.1 %collective-permute-done.7.refs_2_ = f32[2,8,128]{2,1,0:T(8,128)S(1)} collective-permute-done((f32[2,8,128]{2,1,0:T(8,128)S(1)}, f32[2,8,128]{2,1,0:T(8,128)S(1)}, u32[]{:S(2)}, u32[]{:S(2)}) %collective-permute-start.7) | collective-permute-done | bytes 8224 | tf_op jit(solution)/shard_map/ppermute | solution.py:602
  21.2 3.5 %collective-permute-done.8.refs_3_ = f32[2,8,128]{2,1,0:T(8,128)S(1)} collective-permute-done((f32[2,8,128]{2,1,0:T(8,128)S(1)}, f32[2,8,128]{2,1,0:T(8,128)S(1)}, u32[]{:S(2)}, u32[]{:S(2)}) %collective-permute-start.8) | collective-permute-done | bytes 8224 | tf_op jit(solution)/shard_map/ppermute | solution.py:602
  24.6 0.6 %shard_map.137 = (f32[512,256]{1,0:T(8,128)S(1)}, f32[256,128]{1,0:T(8,128)S(1)}, f32[8,128]{1,0:T(8,128)S(1)}) custom-call(f32[512,256]{1,0:T(8,128)S(1)} %shard_map.135.part, f32[192,1536]{1,0:T(8,128)S(1)} %get-tuple-element.51.far_op, s32[1,1,256]{2,1,0:T(1,128)S(1)} %get-tuple-element.52.cells, f32[168,128]{1,0:T(8,128)S(1)} %get-tuple-element.53.col, ...), custom_call_target="tpu_custom_call" | custom-call | flops 100000000 | bytes 1048576 | tf_op jit(solution)/shard_map/pallas_call | solution.py:570
  25.2 1.3 %collective-permute-start.9 = (f32[256,128]{1,0:T(8,128)S(1)}, f32[256,128]{1,0:T(8,128)S(1)}, u32[]{:S(2)}, u32[]{:S(2)}) collective-permute-start(f32[256,128]{1,0:T(8,128)S(1)} %get-tuple-element.61), channel_id=1, source_target_pairs={{4,0},{0,4},{12,8},{8,12},{20,16},{16,20},{28,24},{24,28},{5,1},{1... | collective-permute-start | bytes 393224 | tf_op jit(solution)/shard_map/ppermute | solution.py:598
  26.5 0.0 collective-permute-start.10
  26.5 1.9 %collective-permute-start.11 = (f32[256,128]{1,0:T(8,128)S(1)}, f32[256,128]{1,0:T(8,128)S(1)}, u32[]{:S(2)}, u32[]{:S(2)}) collective-permute-start(f32[256,128]{1,0:T(8,128)S(1)} %get-tuple-element.61), channel_id=1, source_target_pairs={{28,0},{24,4},{20,8},{16,12},{12,16},{8,20},{4,24},{0,28},{29,1},{... | collective-permute-start | bytes 393224 | tf_op jit(solution)/shard_map/ppermute | solution.py:598
  28.4 0.0 collective-permute-start.12
  28.5 1.0 %shard_map.138 = (f32[512,256]{1,0:T(8,128)S(1)}, f32[512,256]{1,0:T(8,128)S(1)}, f32[512,256]{1,0:T(8,128)S(1)}, f32[8,128]{1,0:T(8,128)S(1)}) custom-call(f32[512,256]{1,0:T(8,128)S(1)} %get-tuple-element.54.u_in, f32[512,256]{1,0:T(8,128)S(1)} %get-tuple-element.39.f_in, f32[16,256]{1,0:T(8,128)S(1)} %get-tuple-element.47.refs_4_.rot, ...), custom_call_target="tpu_custom_call" | custom-call | flops 1000000000 | bytes 1048576 | tf_op jit(solution)/shard_map/pallas_call | solution.py:570
  29.5 0.7 %collective-permute-done.9.refs_0_ = f32[256,128]{1,0:T(8,128)S(1)} collective-permute-done((f32[256,128]{1,0:T(8,128)S(1)}, f32[256,128]{1,0:T(8,128)S(1)}, u32[]{:S(2)}, u32[]{:S(2)}) %collective-permute-start.9) | collective-permute-done | bytes 131104 | tf_op jit(solution)/shard_map/ppermute | solution.py:598
  30.2 4.8 %collective-permute-done.10.refs_1_ = f32[256,128]{1,0:T(8,128)S(1)} collective-permute-done((f32[256,128]{1,0:T(8,128)S(1)}, f32[256,128]{1,0:T(8,128)S(1)}, u32[]{:S(2)}, u32[]{:S(2)}) %collective-permute-start.10) | collective-permute-done | bytes 131104 | tf_op jit(solution)/shard_map/ppermute | solution.py:598
  35.1 0.7 %shard_map.139 = (bf16[512,256]{1,0:T(8,128)(2,1)S(1)}, bf16[512,256]{1,0:T(8,128)(2,1)S(1)}) custom-call(f32[512,256]{1,0:T(8,128)S(1)} %get-tuple-element.60.gat, bf16[384,256]{1,0:T(8,128)(2,1)S(1)} %get-tuple-element.44.gh, bf16[384,256]{1,0:T(8,128)(2,1)S(1)} %get-tuple-element.45.gl, f32[256,128]{1,0:T(8,128)S(1)} %collective-permute-done.9.refs_0_, ...), custom_call_target="tpu_custom_call" | custom-call | flops 1000000000 | bytes 1048576 | tf_op jit(solution)/shard_map/pallas_call | solution.py:570
  35.7 1.3 %shard_map.140 = f32[32,16,128]{2,1,0:T(8,128)S(1)} custom-call(f32[512,256]{1,0:T(8,128)S(1)} %get-tuple-element.59.loc, bf16[512,512]{1,0:T(8,128)(2,1)S(1)} %get-tuple-element.41.nh, bf16[512,512]{1,0:T(8,128)(2,1)S(1)} %get-tuple-element.42.nl, bf16[512,256]{1,0:T(8,128)(2,1)S(1)} %get-tuple-element.64.hi, bf16[512,256]{1,0:T(8,128)(2,1)S(1)} %get-tuple-element.65.lo, ...), custom_call_target="tpu_custom_call" | custom-call | flops 1000000000 | bytes 1048576 | tf_op jit(solution)/shard_map/pallas_call | solution.py:570
  37.0 12.5 %all_to_all.5.boxes = f32[32,16,128]{2,1,0:T(8,128)S(1)} all-to-all(f32[32,16,128]{2,1,0:T(8,128)S(1)} %shard_map.140), channel_id=1, replica_groups=mesh['gx'=4,'gy'=2,'gz'=4] {'gx','gy','gz'}, dimensions={0} | all-to-all | bytes 524288 | tf_op jit(solution)/shard_map/all_to_all | solution.py:704
  49.5 3.8 %shard_map.141 = (f32[486,1,256]{2,1,0:T(1,128)}, f32[1,1]{1,0:T(1,128)}) custom-call(f32[512,256]{1,0:T(8,128)S(1)} %get-tuple-element.39.f_in, f32[512,256]{1,0:T(8,128)S(1)} %get-tuple-element.54.u_in, f32[32,16,128]{2,1,0:T(8,128)S(1)} %all_to_all.5.boxes, f32[168,128]{1,0:T(8,128)S(1)} %get-tuple-element.53.col, ...), custom_call_target="tpu_custom_call" | custom-call | flops 10000000 | bytes 1048576 | tf_op jit(solution)/shard_map/pallas_call | solution.py:570
  (9 shorter events, 0.0 us)
Async XLA Ops:
  2.1 10.3 %collective-permute-start = (f32[264,128]{1,0:T(8,128)S(1)}, f32[264,128]{1,0:T(8,128)S(1)}, u32[]{:S(2)}, u32[]{:S(2)}) collective-permute-start(f32[264,128]{1,0:T(8,128)S(1)} %get-tuple-element.46.refs_0_.message.charges_f), channel_id=1, source_target_pairs={{4,0},{0,4},{12,8},{8,12},{20,16},{16,20},{28,24},{24,28},{5,1},{1... | collective-permute-start | bytes 405512 | tf_op jit(solution)/shard_map/ppermute | solution.py:598
  5.1 8.7 %collective-permute-start.1 = (f32[264,128]{1,0:T(8,128)S(1)}, f32[264,128]{1,0:T(8,128)S(1)}, u32[]{:S(2)}, u32[]{:S(2)}) collective-permute-start(f32[264,128]{1,0:T(8,128)S(1)} %get-tuple-element.46.refs_0_.message.charges_f), channel_id=1, source_target_pairs={{24,0},{28,4},{16,8},{20,12},{8,16},{12,20},{0,24},{4,28},{25,1},{... | collective-permute-start | bytes 405512 | tf_op jit(solution)/shard_map/ppermute | solution.py:598
  5.7 8.0 %collective-permute-start.2 = (f32[264,128]{1,0:T(8,128)S(1)}, f32[264,128]{1,0:T(8,128)S(1)}, u32[]{:S(2)}, u32[]{:S(2)}) collective-permute-start(f32[264,128]{1,0:T(8,128)S(1)} %get-tuple-element.46.refs_0_.message.charges_f), channel_id=1, source_target_pairs={{28,0},{24,4},{20,8},{16,12},{12,16},{8,20},{4,24},{0,28},{29,1},{... | collective-permute-start | bytes 405512 | tf_op jit(solution)/shard_map/ppermute | solution.py:598
  6.3 7.6 %collective-permute-start.3 = (f32[264,128]{1,0:T(8,128)S(1)}, f32[264,128]{1,0:T(8,128)S(1)}, u32[]{:S(2)}, u32[]{:S(2)}) collective-permute-start(f32[264,128]{1,0:T(8,128)S(1)} %get-tuple-element.46.refs_0_.message.charges_f), channel_id=1, source_target_pairs={{8,0},{12,4},{0,8},{4,12},{24,16},{28,20},{16,24},{20,28},{9,1},{1... | collective-permute-start | bytes 405512 | tf_op jit(solution)/shard_map/ppermute | solution.py:598
  12.4 1.6 %collective-permute-start.4 = (f32[264,128]{1,0:T(8,128)S(1)}, f32[264,128]{1,0:T(8,128)S(1)}, u32[]{:S(2)}, u32[]{:S(2)}) collective-permute-start(f32[264,128]{1,0:T(8,128)S(1)} %collective-permute-done.refs_1_.refs_0_), channel_id=1, source_target_pairs={{8,0},{12,4},{0,8},{4,12},{24,16},{28,20},{16,24},{20,28},{9,1},{1... | collective-permute-start | bytes 405512 | tf_op jit(solution)/shard_map/ppermute | solution.py:598
  13.8 1.2 %collective-permute-start.5 = (f32[8,128]{1,0:T(8,128)S(1)}, f32[8,128]{1,0:T(8,128)S(1)}, u32[]{:S(2)}, u32[]{:S(2)}) collective-permute-start(f32[8,128]{1,0:T(8,128)S(1)} %shard_map.133.refs_5_.refs_0_), channel_id=1, source_target_pairs={{8,0},{12,4},{0,8},{4,12},{24,16},{28,20},{16,24},{20,28},{9,1},{1... | collective-permute-start | bytes 12296 | tf_op jit(solution)/shard_map/ppermute | solution.py:598
  15.0 5.0 %collective-permute-start.6 = (f32[2,8,128]{2,1,0:T(8,128)S(1)}, f32[2,8,128]{2,1,0:T(8,128)S(1)}, u32[]{:S(2)}, u32[]{:S(2)}) collective-permute-start(f32[2,8,128]{2,1,0:T(8,128)S(1)} %shard_map.136.refs_0_), channel_id=1, source_target_pairs={{1,0},{0,1},{3,2},{2,3},{5,4},{4,5},{7,6},{6,7},{9,8},{8,9},{11,10... | collective-permute-start | bytes 24584 | tf_op jit(solution)/shard_map/ppermute | solution.py:602
  16.6 4.5 %collective-permute-start.7 = (f32[2,8,128]{2,1,0:T(8,128)S(1)}, f32[2,8,128]{2,1,0:T(8,128)S(1)}, u32[]{:S(2)}, u32[]{:S(2)}) collective-permute-start(f32[2,8,128]{2,1,0:T(8,128)S(1)} %shard_map.136.refs_0_), channel_id=1, source_target_pairs={{2,0},{3,1},{0,2},{1,3},{6,4},{7,5},{4,6},{5,7},{10,8},{11,9},{8,1... | collective-permute-start | bytes 24584 | tf_op jit(solution)/shard_map/ppermute | solution.py:602
  19.2 5.4 %collective-permute-start.8 = (f32[2,8,128]{2,1,0:T(8,128)S(1)}, f32[2,8,128]{2,1,0:T(8,128)S(1)}, u32[]{:S(2)}, u32[]{:S(2)}) collective-permute-start(f32[2,8,128]{2,1,0:T(8,128)S(1)} %shard_map.136.refs_0_), channel_id=1, source_target_pairs={{3,0},{2,1},{1,2},{0,3},{7,4},{6,5},{5,6},{4,7},{11,8},{10,9},{9,1... | collective-permute-start | bytes 24584 | tf_op jit(solution)/shard_map/ppermute | solution.py:602
  25.2 5.0 %collective-permute-start.9 = (f32[256,128]{1,0:T(8,128)S(1)}, f32[256,128]{1,0:T(8,128)S(1)}, u32[]{:S(2)}, u32[]{:S(2)}) collective-permute-start(f32[256,128]{1,0:T(8,128)S(1)} %get-tuple-element.61), channel_id=1, source_target_pairs={{4,0},{0,4},{12,8},{8,12},{20,16},{16,20},{28,24},{24,28},{5,1},{1... | collective-permute-start | bytes 393224 | tf_op jit(solution)/shard_map/ppermute | solution.py:598
  26.5 8.5 %collective-permute-start.10 = (f32[256,128]{1,0:T(8,128)S(1)}, f32[256,128]{1,0:T(8,128)S(1)}, u32[]{:S(2)}, u32[]{:S(2)}) collective-permute-start(f32[256,128]{1,0:T(8,128)S(1)} %get-tuple-element.61), channel_id=1, source_target_pairs={{24,0},{28,4},{16,8},{20,12},{8,16},{12,20},{0,24},{4,28},{25,1},{... | collective-permute-start | bytes 393224 | tf_op jit(solution)/shard_map/ppermute | solution.py:598
  26.5 8.5 %collective-permute-start.11 = (f32[256,128]{1,0:T(8,128)S(1)}, f32[256,128]{1,0:T(8,128)S(1)}, u32[]{:S(2)}, u32[]{:S(2)}) collective-permute-start(f32[256,128]{1,0:T(8,128)S(1)} %get-tuple-element.61), channel_id=1, source_target_pairs={{28,0},{24,4},{20,8},{16,12},{12,16},{8,20},{4,24},{0,28},{29,1},{... | collective-permute-start | bytes 393224 | tf_op jit(solution)/shard_map/ppermute | solution.py:598
  28.4 6.6 %collective-permute-start.12 = (f32[256,128]{1,0:T(8,128)S(1)}, f32[256,128]{1,0:T(8,128)S(1)}, u32[]{:S(2)}, u32[]{:S(2)}) collective-permute-start(f32[256,128]{1,0:T(8,128)S(1)} %get-tuple-element.61), channel_id=1, source_target_pairs={{8,0},{12,4},{0,8},{4,12},{24,16},{28,20},{16,24},{20,28},{9,1},{1... | collective-permute-start | bytes 393224 | tf_op jit(solution)/shard_map/ppermute | solution.py:598
  30.2 4.9 %collective-permute-start.13 = (f32[256,128]{1,0:T(8,128)S(1)}, f32[256,128]{1,0:T(8,128)S(1)}, u32[]{:S(2)}, u32[]{:S(2)}) collective-permute-start(f32[256,128]{1,0:T(8,128)S(1)} %collective-permute-done.9.refs_0_), channel_id=1, source_target_pairs={{8,0},{12,4},{0,8},{4,12},{24,16},{28,20},{16,24},{20,28},{9,1},{1... | collective-permute-start | bytes 393224 | tf_op jit(solution)/shard_map/ppermute | solution.py:598

commit v9 on v8

--- a/solution.py
+++ b/solution.py
@@ -66,6 +66,9 @@
         if (kind, dy) == ("same", 0):
             return 0
         return self.bodies + RIM * self.sources.index((kind, dy))
+
+    def odd(self, device):
+        return (device // (self.ny * self.nz)) % 2
 
     def beside(self, kind, x):
         if kind == "same":
@@ -436,8 +439,8 @@
     second = jnp.where(row < 3, of_f, of_a)
     second = jnp.where(row < 4, second, pltpu.roll(of_a, 4, 0))
     second = jnp.where(row == 7, tails, second)
-    packed = jnp.concatenate([first, second], axis=0)
-    packed_out[...] = jnp.broadcast_to(packed[None], packed_out.shape)
+    for device in range(s.devices):
+        packed_out[device] = second if s.odd(device) else first
 
 
 def tree(s, leaves, ups, siblings, root):
@@ -468,7 +471,7 @@
     return potential
 
 
-def box_numbers(s, boxes, ups, siblings, root):
+def box_numbers(s, firsts, seconds, ups, siblings, root):
     columns = s.nx * s.ny
     row = lax.broadcasted_iota(jnp.int32, (8, LANES), 0)
     lane = lax.broadcasted_iota(jnp.int32, (8, LANES), 1)
@@ -477,7 +480,7 @@
     for z in range(s.nz):
         wide = []
         for column in range(columns):
-            tile = boxes[column * s.nz + z, :8, :]
+            tile = firsts[column * s.nz + z]
             wide.append(jnp.concatenate([tile, pltpu.roll(tile, 4, 0)], axis=1)[:, : s.skel])
         leaves.append(jnp.concatenate(wide, axis=0))
     potential = tree(s, leaves, ups, siblings, root)
@@ -489,7 +492,7 @@
             phi = potential[z][8 * column : 8 * column + 8]
             main, tail = phi[:, :LANES], phi[:, LANES:]
             tail = jnp.concatenate([tail, tail], axis=1)
-            first, second = boxes[box, :8, :], boxes[box, 8:, :]
+            first, second = firsts[box], seconds[box]
             both = pltpu.roll(first, 4, 0) * tail
             of_f = jnp.where(row == 0, pltpu.roll(second, 1, 0), jnp.where(row == 1, pltpu.roll(second, 2, 0), pltpu.roll(first, 3, 0)))
             of_f = jnp.where(left == (row != 1), of_f * tail, 0.0)
@@ -516,8 +519,11 @@
     return jnp.concatenate(out, axis=0)
 
 
-def finish_kernel(s, f_in, u_in, boxes, col, uh, ul, bh, bl, rh, rl, x_out, lsq_out, raw, sem):
-    rows = box_numbers(s, boxes, (uh, ul), (bh, bl), (rh[...], rl[...])).T
+def finish_kernel(s, ids, f_in, u_in, mine, other, col, uh, ul, bh, bl, rh, rl, x_out, lsq_out, raw, sem):
+    odd = (ids[0] // s.ny) % 2 == 1
+    firsts = [jnp.where(odd, other[box], mine[box]) for box in range(s.devices)]
+    seconds = [jnp.where(odd, mine[box], other[box]) for box in range(s.devices)]
+    rows = box_numbers(s, firsts, seconds, (uh, ul), (bh, bl), (rh[...], rl[...])).T
     f1, u1, u2, t1, t2, aa, far_f, far_u, far_a, far_far = (rows[i : i + 1] for i in range(10))
     by_f = safe_inverse(f1)
     by_o = jnp.where(u2 * u2 > 1e-10 * (u1 * u1), safe_inverse(u2), 0.0)
@@ -605,9 +611,9 @@
     def fetch_rims(rim):
         got = {}
         for dy in s.shifts:
+            got["other", dy] = fetch(rim, "other", dy)
+        for dy in s.shifts:
             got["same", dy] = fetch(rim, "same", dy)
-        for dy in s.shifts:
-            got["other", dy] = fetch(rim, "other", dy)
         got["other", 0] = fetch(rim, "other", 0)
         got["partner", 0] = fetch(rim, "partner", 0)
         return got
@@ -697,7 +703,7 @@
     gathered = gather(gat, got, stat)
     (packed,) = call(
         functools.partial(second_kernel, s),
-        [((s.devices, 16, LANES), f32)],
+        [((s.devices, 8, LANES), f32)],
         [loc, nh, nl, *gathered, cells, col, f, ortho, stat, message, charges],
         flops=10**9,
     )
@@ -705,7 +711,8 @@
     result, lsq = call(
         functools.partial(finish_kernel, s),
         [(flat, f32), ((1, 1), f32)],
-        [f, u, boxes, col, *operators_out],
+        [ids, f, u, boxes, fetch(boxes, "partner", 0), col, *operators_out],
+        scalars=1,
         far_outs=1,
         scratch=[pltpu.VMEM(flat, f32), pltpu.SemaphoreType.DMA],
         flops=10**7,

time: 53.6 us -> 52.4 us (0.978)
  blocking collectives: 12.5 us -> 9.45 us
  waiting for transfers between devices: 11.8 us -> 13 us
    all_to_all x1, blocking collectives: 12.5 us -> 9.45 us  [body(): boxes = lax.all_to_all(packed, ('gx', 'gy', 'gz'), 0, 0)]
    ppermute x11 -> x12, waiting for transfers between devices: 7.13 us -> 8.39 us  [fetch(): return lax.ppermute(x, ('gx', 'gy'), pairs)]
    pallas_call x11, Pallas kernels: 15.7 us -> 16.2 us  [call(): pl.pallas_call(kernel, out_shape=[jax.ShapeDtypeStruct(shape, kind) for s...]
    ppermute x11 -> x12, starting transfers between devices: 8.25 us -> 8.35 us  [fetch(): return lax.ppermute(x, ('gx', 'gy'), pairs)]
  transfers between devices with their start and end apart: 14 -> 15, of which waited for: 6 -> 7; matrix products, arithmetic and copies ran while one was open for 0% -> 0% of each run, Pallas kernels for 15% -> 15%
where the time goes in v9:
time: 52.4 us; the launch traced here: 52.2 us
  Pallas kernels  16.2 us (31%)
  waiting for transfers between devices  13 us (25%)
  starting transfers between devices  12.7 us (24%)
  blocking collectives  9.45 us (18%)
  between operations  0.72 us (1%)
    pallas_call x11, Pallas kernels, call(): pl.pallas_call(kernel, out_shape=[jax.ShapeDtypeStruct(shape, kind) for s...  16.2 us
    all_to_all x1, blocking collectives, body(): boxes = lax.all_to_all(packed, ('gx', 'gy', 'gz'), 0, 0)  9.45 us
    ppermute x12, waiting for transfers between devices, fetch(): return lax.ppermute(x, ('gx', 'gy'), pairs)  8.39 us
    ppermute x12, starting transfers between devices, fetch(): return lax.ppermute(x, ('gx', 'gy'), pairs)  8.35 us
    ppermute x3, waiting for transfers between devices, fetch_layers(): lax.ppermute(x, 'gz', [(z ^ k, z) for z in range(s.nz)])  4.64 us
    ppermute x3, starting transfers between devices, fetch_layers(): lax.ppermute(x, 'gz', [(z ^ k, z) for z in range(s.nz)])  4.39 us
  transfers between devices with their start and end apart: 15, of which 7 were waited for; matrix products, arithmetic and copies ran while one was open for 0% of the time, Pallas kernels for 15%

profile of v9, /device:TPU:0, one launch (start us, length us, event | category | flops | bytes accessed | tf_op | source)
XLA Modules:
  0.0 52.2 jit_solution(5119757444414558672)
XLA Ops:
  0.6 1.4 %shard_map.131 = (f32[264,128]{1,0:T(8,128)S(1)}, f32[168,128]{1,0:T(8,128)S(1)}, s32[1,1,256]{2,1,0:T(1,128)S(1)}, f32[512,256]{1,0:T(8,128)S(1)}) custom-call(f32[486,1,256]{2,1,0:T(1,128)} %bitcast.9, s32[1,1,256]{2,1,0:T(1,128)} %cells.1, f32[1,162]{1,0:T(1,128)} %bitcast.10), custom_call_target="tpu_custom_call" | custom-call | flops 10000000 | bytes 1048576 | tf_op jit(solution)/shard_map/pallas_call | solution.py:576
  2.1 3.0 %collective-permute-start = (f32[264,128]{1,0:T(8,128)S(1)}, f32[264,128]{1,0:T(8,128)S(1)}, u32[]{:S(2)}, u32[]{:S(2)}) collective-permute-start(f32[264,128]{1,0:T(8,128)S(1)} %get-tuple-element.46.refs_0_.message.charges_f), channel_id=1, source_target_pairs={{4,0},{0,4},{12,8},{8,12},{20,16},{16,20},{28,24},{24,28},{5,1},{1... | collective-permute-start | bytes 405512 | tf_op jit(solution)/shard_map/ppermute | solution.py:604
  5.1 0.7 %collective-permute-start.1 = (f32[264,128]{1,0:T(8,128)S(1)}, f32[264,128]{1,0:T(8,128)S(1)}, u32[]{:S(2)}, u32[]{:S(2)}) collective-permute-start(f32[264,128]{1,0:T(8,128)S(1)} %get-tuple-element.46.refs_0_.message.charges_f), channel_id=1, source_target_pairs={{24,0},{28,4},{16,8},{20,12},{8,16},{12,20},{0,24},{4,28},{25,1},{... | collective-permute-start | bytes 405512 | tf_op jit(solution)/shard_map/ppermute | solution.py:604
  5.7 0.6 %collective-permute-start.2 = (f32[264,128]{1,0:T(8,128)S(1)}, f32[264,128]{1,0:T(8,128)S(1)}, u32[]{:S(2)}, u32[]{:S(2)}) collective-permute-start(f32[264,128]{1,0:T(8,128)S(1)} %get-tuple-element.46.refs_0_.message.charges_f), channel_id=1, source_target_pairs={{28,0},{24,4},{20,8},{16,12},{12,16},{8,20},{4,24},{0,28},{29,1},{... | collective-permute-start | bytes 405512 | tf_op jit(solution)/shard_map/ppermute | solution.py:604
  6.3 0.4 collective-permute-start.3
  6.7 0.1 pad_add_fusion.ids
  6.8 5.6 %shard_map.132 = (f32[512,256]{1,0:T(8,128)S(1)}, f32[512,256]{1,0:T(8,128)S(1)}, f32[16,256]{1,0:T(8,128)S(1)}, bf16[512,512]{1,0:T(8,128)(2,1)S(1)}, bf16[512,...) custom-call(s32[2]{0:T(128)S(1)} %pad_add_fusion.ids, ...), custom_call_target="tpu_custom_call" | custom-call | flops 5000000000 | bytes 1048576 | tf_op jit(solution)/shard_map/pallas_call | solution.py:576
  12.4 0.0 collective-permute-done.refs_1_.refs_0_
  12.4 0.2 collective-permute-start.4
  12.6 1.2 %collective-permute-done.1.refs_2_.refs_1_ = f32[264,128]{1,0:T(8,128)S(1)} collective-permute-done((f32[264,128]{1,0:T(8,128)S(1)}, f32[264,128]{1,0:T(8,128)S(1)}, u32[]{:S(2)}, u32[]{:S(2)}) %collective-permute-start.1) | collective-permute-done | bytes 135200 | tf_op jit(solution)/shard_map/ppermute | solution.py:604
  13.8 0.2 collective-permute-start.5
  14.0 0.0 collective-permute-done.4.refs_4_
  14.0 0.7 %shard_map.134 = (bf16[512,256]{1,0:T(8,128)(2,1)S(1)}, bf16[512,256]{1,0:T(8,128)(2,1)S(1)}) custom-call(f32[512,256]{1,0:T(8,128)S(1)} %get-tuple-element.43.gat, bf16[384,256]{1,0:T(8,128)(2,1)S(1)} %get-tuple-element.44.gh, bf16[384,256]{1,0:T(8,128)(2,1)S(1)} %get-tuple-element.45.gl, f32[264,128]{1,0:T(8,128)S(1)} %collective-permute-done.refs_1_.refs_0_, ...), custom_call_target="tpu_custom_call" | custom-call | flops 1000000000 | bytes 1048576 | tf_op jit(solution)/shard_map/pallas_call | solution.py:576
  14.7 0.4 collective-permute-done.5.refs_1_
  15.0 1.6 %collective-permute-start.6 = (f32[2,8,128]{2,1,0:T(8,128)S(1)}, f32[2,8,128]{2,1,0:T(8,128)S(1)}, u32[]{:S(2)}, u32[]{:S(2)}) collective-permute-start(f32[2,8,128]{2,1,0:T(8,128)S(1)} %shard_map.136.refs_0_), channel_id=1, source_target_pairs={{1,0},{0,1},{3,2},{2,3},{5,4},{4,5},{7,6},{6,7},{9,8},{8,9},{11,10... | collective-permute-start | bytes 24584 | tf_op jit(solution)/shard_map/ppermute | solution.py:608
  16.6 2.6 %collective-permute-start.7 = (f32[2,8,128]{2,1,0:T(8,128)S(1)}, f32[2,8,128]{2,1,0:T(8,128)S(1)}, u32[]{:S(2)}, u32[]{:S(2)}) collective-permute-start(f32[2,8,128]{2,1,0:T(8,128)S(1)} %shard_map.136.refs_0_), channel_id=1, source_target_pairs={{2,0},{3,1},{0,2},{1,3},{6,4},{7,5},{4,6},{5,7},{10,8},{11,9},{8,1... | collective-permute-start | bytes 24584 | tf_op jit(solution)/shard_map/ppermute | solution.py:608
  19.2 0.2 collective-permute-start.8
  19.4 0.6 %shard_map.135.part = f32[512,256]{1,0:T(8,128)S(1)} custom-call(f32[512,256]{1,0:T(8,128)S(1)} %get-tuple-element.40.loc, bf16[512,512]{1,0:T(8,128)(2,1)S(1)} %get-tuple-element.41.nh, bf16[512,512]{1,0:T(8,128)(2,1)S(1)} %get-tuple-element.42.nl, bf16[512,256]{1,0:T(8,128)(2,1)S(1)} %get-tuple-element.49.hi, bf16[512,256]{1,0:T(8,128)(2,1)S(1)} %get-tuple-element.50.lo.refs_2_), custom_call_target="tpu_custom_call" | custom-call | flops 1000000000 | bytes 1048576 | tf_op jit(solution)/shard_map/pallas_call | solution.py:576
  20.0 1.1 %collective-permute-done.7.refs_2_ = f32[2,8,128]{2,1,0:T(8,128)S(1)} collective-permute-done((f32[2,8,128]{2,1,0:T(8,128)S(1)}, f32[2,8,128]{2,1,0:T(8,128)S(1)}, u32[]{:S(2)}, u32[]{:S(2)}) %collective-permute-start.7) | collective-permute-done | bytes 8224 | tf_op jit(solution)/shard_map/ppermute | solution.py:608
  21.2 3.5 %collective-permute-done.8.refs_3_ = f32[2,8,128]{2,1,0:T(8,128)S(1)} collective-permute-done((f32[2,8,128]{2,1,0:T(8,128)S(1)}, f32[2,8,128]{2,1,0:T(8,128)S(1)}, u32[]{:S(2)}, u32[]{:S(2)}) %collective-permute-start.8) | collective-permute-done | bytes 8224 | tf_op jit(solution)/shard_map/ppermute | solution.py:608
  24.6 0.6 %shard_map.137 = (f32[512,256]{1,0:T(8,128)S(1)}, f32[256,128]{1,0:T(8,128)S(1)}, f32[8,128]{1,0:T(8,128)S(1)}) custom-call(f32[512,256]{1,0:T(8,128)S(1)} %shard_map.135.part, f32[192,1536]{1,0:T(8,128)S(1)} %get-tuple-element.51.far_op, s32[1,1,256]{2,1,0:T(1,128)S(1)} %get-tuple-element.52.cells, f32[168,128]{1,0:T(8,128)S(1)} %get-tuple-element.53.col, ...), custom_call_target="tpu_custom_call" | custom-call | flops 100000000 | bytes 1048576 | tf_op jit(solution)/shard_map/pallas_call | solution.py:576
  25.2 1.3 %collective-permute-start.9 = (f32[256,128]{1,0:T(8,128)S(1)}, f32[256,128]{1,0:T(8,128)S(1)}, u32[]{:S(2)}, u32[]{:S(2)}) collective-permute-start(f32[256,128]{1,0:T(8,128)S(1)} %get-tuple-element.61), channel_id=1, source_target_pairs={{4,0},{0,4},{12,8},{8,12},{20,16},{16,20},{28,24},{24,28},{5,1},{1... | collective-permute-start | bytes 393224 | tf_op jit(solution)/shard_map/ppermute | solution.py:604
  26.5 1.9 %collective-permute-start.11 = (f32[256,128]{1,0:T(8,128)S(1)}, f32[256,128]{1,0:T(8,128)S(1)}, u32[]{:S(2)}, u32[]{:S(2)}) collective-permute-start(f32[256,128]{1,0:T(8,128)S(1)} %get-tuple-element.61), channel_id=1, source_target_pairs={{28,0},{24,4},{20,8},{16,12},{12,16},{8,20},{4,24},{0,28},{29,1},{... | collective-permute-start | bytes 393224 | tf_op jit(solution)/shard_map/ppermute | solution.py:604
  28.5 1.0 %shard_map.138 = (f32[512,256]{1,0:T(8,128)S(1)}, f32[512,256]{1,0:T(8,128)S(1)}, f32[512,256]{1,0:T(8,128)S(1)}, f32[8,128]{1,0:T(8,128)S(1)}) custom-call(f32[512,256]{1,0:T(8,128)S(1)} %get-tuple-element.54.u_in, f32[512,256]{1,0:T(8,128)S(1)} %get-tuple-element.39.f_in, f32[16,256]{1,0:T(8,128)S(1)} %get-tuple-element.47.refs_4_.rot, ...), custom_call_target="tpu_custom_call" | custom-call | flops 1000000000 | bytes 1048576 | tf_op jit(solution)/shard_map/pallas_call | solution.py:576
  29.5 0.7 %collective-permute-done.9.refs_0_ = f32[256,128]{1,0:T(8,128)S(1)} collective-permute-done((f32[256,128]{1,0:T(8,128)S(1)}, f32[256,128]{1,0:T(8,128)S(1)}, u32[]{:S(2)}, u32[]{:S(2)}) %collective-permute-start.9) | collective-permute-done | bytes 131104 | tf_op jit(solution)/shard_map/ppermute | solution.py:604
  30.2 4.9 %collective-permute-done.10.refs_1_ = f32[256,128]{1,0:T(8,128)S(1)} collective-permute-done((f32[256,128]{1,0:T(8,128)S(1)}, f32[256,128]{1,0:T(8,128)S(1)}, u32[]{:S(2)}, u32[]{:S(2)}) %collective-permute-start.10) | collective-permute-done | bytes 131104 | tf_op jit(solution)/shard_map/ppermute | solution.py:604
  35.1 0.7 %shard_map.139 = (bf16[512,256]{1,0:T(8,128)(2,1)S(1)}, bf16[512,256]{1,0:T(8,128)(2,1)S(1)}) custom-call(f32[512,256]{1,0:T(8,128)S(1)} %get-tuple-element.60.gat, bf16[384,256]{1,0:T(8,128)(2,1)S(1)} %get-tuple-element.44.gh, bf16[384,256]{1,0:T(8,128)(2,1)S(1)} %get-tuple-element.45.gl, f32[256,128]{1,0:T(8,128)S(1)} %collective-permute-done.9.refs_0_, ...), custom_call_target="tpu_custom_call" | custom-call | flops 1000000000 | bytes 1048576 | tf_op jit(solution)/shard_map/pallas_call | solution.py:576
  35.8 1.3 %shard_map.140 = f32[32,8,128]{2,1,0:T(8,128)S(1)} custom-call(f32[512,256]{1,0:T(8,128)S(1)} %get-tuple-element.59.loc, bf16[512,512]{1,0:T(8,128)(2,1)S(1)} %get-tuple-element.41.nh, bf16[512,512]{1,0:T(8,128)(2,1)S(1)} %get-tuple-element.42.nl, bf16[512,256]{1,0:T(8,128)(2,1)S(1)} %get-tuple-element.64.hi, bf16[512,256]{1,0:T(8,128)(2,1)S(1)} %get-tuple-element.65.lo, ...), custom_call_target="tpu_custom_call" | custom-call | flops 1000000000 | bytes 1048576 | tf_op jit(solution)/shard_map/pallas_call | solution.py:576
  37.0 9.5 %all_to_all.5.mine = f32[32,8,128]{2,1,0:T(8,128)S(1)} all-to-all(f32[32,8,128]{2,1,0:T(8,128)S(1)} %shard_map.140), channel_id=1, replica_groups=mesh['gx'=4,'gy'=2,'gz'=4] {'gx','gy','gz'}, dimensions={0} | all-to-all | bytes 262144 | tf_op jit(solution)/shard_map/all_to_all | solution.py:710
  46.5 0.1 collective-permute-start.14
  46.6 1.2 %collective-permute-done.14.other = f32[32,8,128]{2,1,0:T(8,128)S(1)} collective-permute-done((f32[32,8,128]{2,1,0:T(8,128)S(1)}, f32[32,8,128]{2,1,0:T(8,128)S(1)}, u32[]{:S(2)}, u32[]{:S(2)}) %collective-permute-start.14) | collective-permute-done | bytes 131104 | tf_op jit(solution)/shard_map/ppermute | solution.py:604
  47.8 4.4 %shard_map.141 = (f32[486,1,256]{2,1,0:T(1,128)}, f32[1,1]{1,0:T(1,128)}) custom-call(s32[2]{0:T(128)S(1)} %pad_add_fusion.ids, f32[512,256]{1,0:T(8,128)S(1)} %get-tuple-element.39.f_in, f32[512,256]{1,0:T(8,128)S(1)} %get-tuple-element.54.u_in, f32[32,8,128]{2,1,0:T(8,128)S(1)} %all_to_all.5.mine, f32[32,8,128]{2,1,0:T(8,128)S(1)} %collective-permute-done.14.other, ...), custom_call_target="tpu_custom_call" | custom-call | flops 10000000 | bytes 1048576 | tf_op jit(solution)/shard_map/pallas_call | solution.py:576
  (11 shorter events, 0.0 us)
Async XLA Ops:
  2.1 10.3 %collective-permute-start = (f32[264,128]{1,0:T(8,128)S(1)}, f32[264,128]{1,0:T(8,128)S(1)}, u32[]{:S(2)}, u32[]{:S(2)}) collective-permute-start(f32[264,128]{1,0:T(8,128)S(1)} %get-tuple-element.46.refs_0_.message.charges_f), channel_id=1, source_target_pairs={{4,0},{0,4},{12,8},{8,12},{20,16},{16,20},{28,24},{24,28},{5,1},{1... | collective-permute-start | bytes 405512 | tf_op jit(solution)/shard_map/ppermute | solution.py:604
  5.1 8.7 %collective-permute-start.1 = (f32[264,128]{1,0:T(8,128)S(1)}, f32[264,128]{1,0:T(8,128)S(1)}, u32[]{:S(2)}, u32[]{:S(2)}) collective-permute-start(f32[264,128]{1,0:T(8,128)S(1)} %get-tuple-element.46.refs_0_.message.charges_f), channel_id=1, source_target_pairs={{24,0},{28,4},{16,8},{20,12},{8,16},{12,20},{0,24},{4,28},{25,1},{... | collective-permute-start | bytes 405512 | tf_op jit(solution)/shard_map/ppermute | solution.py:604
  5.7 8.0 %collective-permute-start.2 = (f32[264,128]{1,0:T(8,128)S(1)}, f32[264,128]{1,0:T(8,128)S(1)}, u32[]{:S(2)}, u32[]{:S(2)}) collective-permute-start(f32[264,128]{1,0:T(8,128)S(1)} %get-tuple-element.46.refs_0_.message.charges_f), channel_id=1, source_target_pairs={{28,0},{24,4},{20,8},{16,12},{12,16},{8,20},{4,24},{0,28},{29,1},{... | collective-permute-start | bytes 405512 | tf_op jit(solution)/shard_map/ppermute | solution.py:604
  6.3 7.6 %collective-permute-start.3 = (f32[264,128]{1,0:T(8,128)S(1)}, f32[264,128]{1,0:T(8,128)S(1)}, u32[]{:S(2)}, u32[]{:S(2)}) collective-permute-start(f32[264,128]{1,0:T(8,128)S(1)} %get-tuple-element.46.refs_0_.message.charges_f), channel_id=1, source_target_pairs={{8,0},{12,4},{0,8},{4,12},{24,16},{28,20},{16,24},{20,28},{9,1},{1... | collective-permute-start | bytes 405512 | tf_op jit(solution)/shard_map/ppermute | solution.py:604
  12.4 1.6 %collective-permute-start.4 = (f32[264,128]{1,0:T(8,128)S(1)}, f32[264,128]{1,0:T(8,128)S(1)}, u32[]{:S(2)}, u32[]{:S(2)}) collective-permute-start(f32[264,128]{1,0:T(8,128)S(1)} %collective-permute-done.refs_1_.refs_0_), channel_id=1, source_target_pairs={{8,0},{12,4},{0,8},{4,12},{24,16},{28,20},{16,24},{20,28},{9,1},{1... | collective-permute-start | bytes 405512 | tf_op jit(solution)/shard_map/ppermute | solution.py:604
  13.8 1.2 %collective-permute-start.5 = (f32[8,128]{1,0:T(8,128)S(1)}, f32[8,128]{1,0:T(8,128)S(1)}, u32[]{:S(2)}, u32[]{:S(2)}) collective-permute-start(f32[8,128]{1,0:T(8,128)S(1)} %shard_map.133.refs_5_.refs_0_), channel_id=1, source_target_pairs={{8,0},{12,4},{0,8},{4,12},{24,16},{28,20},{16,24},{20,28},{9,1},{1... | collective-permute-start | bytes 12296 | tf_op jit(solution)/shard_map/ppermute | solution.py:604
  15.0 5.0 %collective-permute-start.6 = (f32[2,8,128]{2,1,0:T(8,128)S(1)}, f32[2,8,128]{2,1,0:T(8,128)S(1)}, u32[]{:S(2)}, u32[]{:S(2)}) collective-permute-start(f32[2,8,128]{2,1,0:T(8,128)S(1)} %shard_map.136.refs_0_), channel_id=1, source_target_pairs={{1,0},{0,1},{3,2},{2,3},{5,4},{4,5},{7,6},{6,7},{9,8},{8,9},{11,10... | collective-permute-start | bytes 24584 | tf_op jit(solution)/shard_map/ppermute | solution.py:608
  16.6 4.5 %collective-permute-start.7 = (f32[2,8,128]{2,1,0:T(8,128)S(1)}, f32[2,8,128]{2,1,0:T(8,128)S(1)}, u32[]{:S(2)}, u32[]{:S(2)}) collective-permute-start(f32[2,8,128]{2,1,0:T(8,128)S(1)} %shard_map.136.refs_0_), channel_id=1, source_target_pairs={{2,0},{3,1},{0,2},{1,3},{6,4},{7,5},{4,6},{5,7},{10,8},{11,9},{8,1... | collective-permute-start | bytes 24584 | tf_op jit(solution)/shard_map/ppermute | solution.py:608
  19.2 5.4 %collective-permute-start.8 = (f32[2,8,128]{2,1,0:T(8,128)S(1)}, f32[2,8,128]{2,1,0:T(8,128)S(1)}, u32[]{:S(2)}, u32[]{:S(2)}) collective-permute-start(f32[2,8,128]{2,1,0:T(8,128)S(1)} %shard_map.136.refs_0_), channel_id=1, source_target_pairs={{3,0},{2,1},{1,2},{0,3},{7,4},{6,5},{5,6},{4,7},{11,8},{10,9},{9,1... | collective-permute-start | bytes 24584 | tf_op jit(solution)/shard_map/ppermute | solution.py:608
  25.2 5.0 %collective-permute-start.9 = (f32[256,128]{1,0:T(8,128)S(1)}, f32[256,128]{1,0:T(8,128)S(1)}, u32[]{:S(2)}, u32[]{:S(2)}) collective-permute-start(f32[256,128]{1,0:T(8,128)S(1)} %get-tuple-element.61), channel_id=1, source_target_pairs={{4,0},{0,4},{12,8},{8,12},{20,16},{16,20},{28,24},{24,28},{5,1},{1... | collective-permute-start | bytes 393224 | tf_op jit(solution)/shard_map/ppermute | solution.py:604
  26.5 8.5 %collective-permute-start.10 = (f32[256,128]{1,0:T(8,128)S(1)}, f32[256,128]{1,0:T(8,128)S(1)}, u32[]{:S(2)}, u32[]{:S(2)}) collective-permute-start(f32[256,128]{1,0:T(8,128)S(1)} %get-tuple-element.61), channel_id=1, source_target_pairs={{24,0},{28,4},{16,8},{20,12},{8,16},{12,20},{0,24},{4,28},{25,1},{... | collective-permute-start | bytes 393224 | tf_op jit(solution)/shard_map/ppermute | solution.py:604
  26.5 8.5 %collective-permute-start.11 = (f32[256,128]{1,0:T(8,128)S(1)}, f32[256,128]{1,0:T(8,128)S(1)}, u32[]{:S(2)}, u32[]{:S(2)}) collective-permute-start(f32[256,128]{1,0:T(8,128)S(1)} %get-tuple-element.61), channel_id=1, source_target_pairs={{28,0},{24,4},{20,8},{16,12},{12,16},{8,20},{4,24},{0,28},{29,1},{... | collective-permute-start | bytes 393224 | tf_op jit(solution)/shard_map/ppermute | solution.py:604
  28.4 6.6 %collective-permute-start.12 = (f32[256,128]{1,0:T(8,128)S(1)}, f32[256,128]{1,0:T(8,128)S(1)}, u32[]{:S(2)}, u32[]{:S(2)}) collective-permute-start(f32[256,128]{1,0:T(8,128)S(1)} %get-tuple-element.61), channel_id=1, source_target_pairs={{8,0},{12,4},{0,8},{4,12},{24,16},{28,20},{16,24},{20,28},{9,1},{1... | collective-permute-start | bytes 393224 | tf_op jit(solution)/shard_map/ppermute | solution.py:604
  30.2 4.9 %collective-permute-start.13 = (f32[256,128]{1,0:T(8,128)S(1)}, f32[256,128]{1,0:T(8,128)S(1)}, u32[]{:S(2)}, u32[]{:S(2)}) collective-permute-start(f32[256,128]{1,0:T(8,128)S(1)} %collective-permute-done.9.refs_0_), channel_id=1, source_target_pairs={{8,0},{12,4},{0,8},{4,12},{24,16},{28,20},{16,24},{20,28},{9,1},{1... | collective-permute-start | bytes 393224 | tf_op jit(solution)/shard_map/ppermute | solution.py:604
  46.5 1.3 %collective-permute-start.14 = (f32[32,8,128]{2,1,0:T(8,128)S(1)}, f32[32,8,128]{2,1,0:T(8,128)S(1)}, u32[]{:S(2)}, u32[]{:S(2)}) collective-permute-start(f32[32,8,128]{2,1,0:T(8,128)S(1)} %all_to_all.5.mine), channel_id=1, source_target_pairs={{8,0},{12,4},{0,8},{4,12},{24,16},{28,20},{16,24},{20,28},{9,1},{1... | collective-permute-start | bytes 393224 | tf_op jit(solution)/shard_map/ppermute | solution.py:604

commit v10 on v9

--- a/solution.py
+++ b/solution.py
@@ -209,20 +209,17 @@
     return out
 
 
-def setup_kernel(
-    s, ids, f_in, *refs
-):
-    count = 9
-    sources, refs = refs[:count], refs[count:]
-    copies, refs = refs[-1 - count :], refs[: -1 - count]
-    copies, sems = copies[:-1], copies[-1]
-    setup(s, ids, f_in, begin(sources, copies, sems), *copies, *refs)
+def setup_kernel(s, ids, f_in, *refs):
+    sources, tree, outs, (padded, *copies, sems) = refs[:9], refs[9:13], refs[13:24], refs[24:]
+    moves = begin(sources, (*copies, *tree), sems)
+    setup(s, ids, f_in, moves[:5], *copies, *outs, padded)
+    for move in moves[5:]:
+        move.wait()
 
 
 def setup(
-    s, ids, f_in, moves, angles, near_weight, neighbours, self_mob, near_mat, perm, interp, sibling, root,
-    loc_out, gat_out, rot_out, sh_out, sl_out, nh_out, nl_out, oh_out, ol_out, gh_out, gl_out,
-    far_out, uh_out, ul_out, bh_out, bl_out, rh_out, rl_out, padded, ups_ref,
+    s, ids, f_in, moves, angles, near_weight, neighbours, self_mob, near_mat,
+    loc_out, gat_out, rot_out, sh_out, sl_out, nh_out, nl_out, oh_out, ol_out, gh_out, gl_out, padded,
 ):
     f = f_in[...]
     for move in moves[:3]:
@@ -269,6 +266,10 @@
     loc_out[...] = loc
     gat_out[...] = gat
 
+
+def far_kernel(
+    s, ids, perm, interp, sibling, root, _, far_out, uh_out, ul_out, bh_out, bl_out, rh_out, rl_out, ups_ref
+):
     n = s.skel
     z = ids[1]
     halves = []
@@ -325,7 +326,7 @@
 
 
 def layer_kernel(s, message, *refs):
-    *sums, _, out = refs
+    *sums, out = refs
     acc = sums[0][...]
     for part in sums[1:]:
         acc = acc + part[...]
@@ -333,10 +334,19 @@
     out[1] = acc
 
 
+def join_kernel(x, y, _, out):
+    out[: x.shape[0]] = x[...]
+    out[x.shape[0] :] = y[...]
+
+
+def order_kernel(x, *refs):
+    refs[-1][...] = x[...]
+
+
 def far_potential(s, charges, far_op):
     rows = []
     for group in range(2):
-        tiles = [layer[group] for layer in charges]
+        tiles = [layer[2 * k + group] for layer in charges for k in range(layer.shape[0] // 2)]
         rows += tiles
         for leaf in range(0, s.nz, 2):
             pair = tiles[leaf]
@@ -603,11 +613,6 @@
                 pairs.append((s.beside(kind, gx) * s.ny + (gy + dy) % s.ny, gx * s.ny + gy))
         return lax.ppermute(x, ("gx", "gy"), pairs)
 
-    def fetch_layers(x):
-        return [x] + [
-            lax.ppermute(x, "gz", [(z ^ k, z) for z in range(s.nz)]) for k in range(1, s.nz)
-        ]
-
     def fetch_rims(rim):
         got = {}
         for dy in s.shifts:
@@ -620,8 +625,9 @@
 
     def forward_rims(got, after):
         for dy in s.shifts:
-            ready, _ = lax.optimization_barrier((got["same", dy], after))
-            got["partner", dy] = fetch(ready, "partner", 0)
+            held = got["same", dy]
+            (held,) = call(order_kernel, [(held.shape, f32)], [held, got["other", dy], after])
+            got["partner", dy] = fetch(held, "partner", 0)
 
     def gather(gat, got, after):
         return call(
@@ -631,20 +637,21 @@
             flops=10**9,
         )
 
-    def share(message, got, gat, after):
-        forward_rims(got, after)
+    def plane_pair(message, got, after):
         if s.direct:
             quarter = [message] + [got[key] for key in s.sources if key[0] != "partner"]
             (half,) = call(functools.partial(half_kernel, s), [(tile, f32)], quarter + [after])
             sums = [half, fetch(half, "partner", 0)]
         else:
-            half = lax.psum(message[s.half :], ("gx", "gy"))
-            sums = [half]
-        gathered = gather(gat, got, half)
-        (pair,) = call(
-            functools.partial(layer_kernel, s), [((2,) + tile, f32)], [message] + sums + [gathered[1]]
-        )
-        return gathered, fetch_layers(pair)
+            sums = [lax.psum(message[s.half :], ("gx", "gy"))]
+        return call(functools.partial(layer_kernel, s), [((2,) + tile, f32)], [message] + sums)[0]
+
+    def swap_layers(x, k):
+        return lax.ppermute(x, "gz", [(z ^ k, z) for z in range(s.nz)])
+
+    def join(x, y, after):
+        shape = (2 * x.shape[0],) + tile
+        return call(join_kernel, [(shape, f32)], [x, y, after])[0]
 
     def near_part(loc, gathered):
         return call(
@@ -662,29 +669,42 @@
         flops=10**7,
     )
     got = fetch_rims(message)
-    operators = [
-        angles.reshape(3, 1, s.bodies), near_weight, neighbours, self_mob, near_mat, skel_perm, interp,
-        sibling_ops, root_op,
-    ]
-    loc, gat, rot, sh, sl, nh, nl, oh, ol, gh, gl, far_op, *operators_out = call(
+    tree_in = [skel_perm, interp, sibling_ops, root_op]
+    operators = [angles.reshape(3, 1, s.bodies), near_weight, neighbours, self_mob, near_mat]
+    *tree_in, loc, gat, rot, sh, sl, nh, nl, oh, ol, gh, gl = call(
         functools.partial(setup_kernel, s),
-        [(full, f32), (full, f32), ((16, s.bodies), f32)]
+        [(x.shape, x.dtype) for x in tree_in]
+        + [(full, f32), (full, f32), ((16, s.bodies), f32)]
         + [(square, bf16)] * 4
         + [((s.bodies, s.bodies), bf16)] * 2
-        + [((s.ghosts, s.bodies), bf16)] * 2
-        + [(far_shape, f32)]
+        + [((s.ghosts, s.bodies), bf16)] * 2,
+        [ids, f] + operators + tree_in,
+        scalars=1,
+        far_args=9,
+        scratch=[pltpu.VMEM(square, f32)]
+        + [pltpu.VMEM(x.shape, x.dtype) for x in operators]
+        + [pltpu.SemaphoreType.DMA((9,))],
+        flops=4 * 10**9,
+    )
+    forward_rims(got, rot)
+    layers = [plane_pair(message, got, rot)]
+    held = layers[0]
+    layers.append(swap_layers(held, 1))
+    far_op, *operators_out = call(
+        functools.partial(far_kernel, s),
+        [(far_shape, f32)]
         + [((s.levels, 2 * s.skel, s.skel), bf16)] * 2
         + [((s.levels, s.skel, s.skel), bf16)] * 2
         + [((s.skel, s.skel), bf16)] * 2,
-        [ids, f] + operators,
+        [ids, *tree_in, held],
         scalars=1,
-        far_args=len(operators),
-        scratch=[pltpu.VMEM(square, f32), pltpu.VMEM((s.levels, 2 * s.skel, s.skel), f32)]
-        + [pltpu.VMEM(x.shape, x.dtype) for x in operators]
-        + [pltpu.SemaphoreType.DMA((len(operators),))],
-        flops=5 * 10**9,
-    )
-    gathered, layers = share(message, got, gat, rot)
+        scratch=[pltpu.VMEM((s.levels, 2 * s.skel, s.skel), f32)],
+        flops=2 * 10**9,
+    )
+    for level in range(1, s.levels):
+        held = join(held, layers[-1], far_op)
+        layers.append(swap_layers(held, 1 << level))
+    gathered = gather(gat, got, held)
     part = near_part(loc, gathered)
     u, rim, charges = call(
         functools.partial(first_kernel, s),

time: 52.4 us -> 53.7 us (1.025)
  blocking collectives: 9.45 us -> 11.4 us
  waiting for transfers between devices: 13 us -> 11.6 us
    ppermute x3 -> x2, waiting for transfers between devices: 4.64 us -> 0.78 us  [swap_layers(): return lax.ppermute(x, 'gz', [(z ^ k, z) for z in range(s.nz)])]
    ppermute x12, waiting for transfers between devices: 8.39 us -> 10.8 us  [fetch(): return lax.ppermute(x, ('gx', 'gy'), pairs)]
    all_to_all x1, blocking collectives: 9.45 us -> 11.4 us  [body(): boxes = lax.all_to_all(packed, ('gx', 'gy', 'gz'), 0, 0)]
    pallas_call x11 -> x15, Pallas kernels: 16.2 us -> 16.6 us  [call(): pl.pallas_call(kernel, out_shape=[jax.ShapeDtypeStruct(shape, kind) for s...]
    ppermute x3 -> x2, starting transfers between devices: 4.39 us -> 4.23 us  [swap_layers(): return lax.ppermute(x, 'gz', [(z ^ k, z) for z in range(s.nz)])]
  transfers between devices with their start and end apart: 15 -> 14, of which waited for: 7 -> 9; matrix products, arithmetic and copies ran while one was open for 0% -> 0% of each run, Pallas kernels for 15% -> 16%
where the time goes in v10:
time: 53.7 us; the launch traced here: 53.5 us
  Pallas kernels  16.6 us (31%)
  starting transfers between devices  13.1 us (24%)
  waiting for transfers between devices  11.6 us (22%)
  blocking collectives  11.4 us (21%)
  between operations  0.73 us (1%)
    pallas_call x15, Pallas kernels, call(): pl.pallas_call(kernel, out_shape=[jax.ShapeDtypeStruct(shape, kind) for s...  16.6 us
    all_to_all x1, blocking collectives, body(): boxes = lax.all_to_all(packed, ('gx', 'gy', 'gz'), 0, 0)  11.4 us
    ppermute x12, waiting for transfers between devices, fetch(): return lax.ppermute(x, ('gx', 'gy'), pairs)  10.8 us
    ppermute x12, starting transfers between devices, fetch(): return lax.ppermute(x, ('gx', 'gy'), pairs)  8.85 us
    ppermute x2, starting transfers between devices, swap_layers(): return lax.ppermute(x, 'gz', [(z ^ k, z) for z in range(s.nz)])  4.23 us
  transfers between devices with their start and end apart: 14, of which 9 were waited for; matrix products, arithmetic and copies ran while one was open for 0% of the time, Pallas kernels for 16%

profile of v10, /device:TPU:0, one launch (start us, length us, event | category | flops | bytes accessed | tf_op | source)
XLA Modules:
  0.0 53.5 jit_solution(13190736662915677819)
XLA Ops:
  0.6 1.4 %shard_map.131 = (f32[264,128]{1,0:T(8,128)S(1)}, f32[168,128]{1,0:T(8,128)S(1)}, s32[1,1,256]{2,1,0:T(1,128)S(1)}, f32[512,256]{1,0:T(8,128)S(1)}) custom-call(f32[486,1,256]{2,1,0:T(1,128)} %bitcast.9, s32[1,1,256]{2,1,0:T(1,128)} %cells.1, f32[1,162]{1,0:T(1,128)} %bitcast.10), custom_call_target="tpu_custom_call" | custom-call | flops 10000000 | bytes 1048576 | tf_op jit(solution)/shard_map/pallas_call | solution.py:586
  2.1 3.0 %collective-permute-start = (f32[264,128]{1,0:T(8,128)S(1)}, f32[264,128]{1,0:T(8,128)S(1)}, u32[]{:S(2)}, u32[]{:S(2)}) collective-permute-start(f32[264,128]{1,0:T(8,128)S(1)} %get-tuple-element.48.refs_0_.message.charges_f), channel_id=1, source_target_pairs={{4,0},{0,4},{12,8},{8,12},{20,16},{16,20},{28,24},{24,28},{5,1},{1... | collective-permute-start | bytes 405512 | tf_op jit(solution)/shard_map/ppermute | solution.py:614
  5.1 0.7 %collective-permute-start.2 = (f32[264,128]{1,0:T(8,128)S(1)}, f32[264,128]{1,0:T(8,128)S(1)}, u32[]{:S(2)}, u32[]{:S(2)}) collective-permute-start(f32[264,128]{1,0:T(8,128)S(1)} %get-tuple-element.48.refs_0_.message.charges_f), channel_id=1, source_target_pairs={{28,0},{24,4},{20,8},{16,12},{12,16},{8,20},{4,24},{0,28},{29,1},{... | collective-permute-start | bytes 405512 | tf_op jit(solution)/shard_map/ppermute | solution.py:614
  5.7 0.6 %collective-permute-start.1 = (f32[264,128]{1,0:T(8,128)S(1)}, f32[264,128]{1,0:T(8,128)S(1)}, u32[]{:S(2)}, u32[]{:S(2)}) collective-permute-start(f32[264,128]{1,0:T(8,128)S(1)} %get-tuple-element.48.refs_0_.message.charges_f), channel_id=1, source_target_pairs={{24,0},{28,4},{16,8},{20,12},{8,16},{12,20},{0,24},{4,28},{25,1},{... | collective-permute-start | bytes 405512 | tf_op jit(solution)/shard_map/ppermute | solution.py:614
  6.4 3.4 %shard_map.132 = (s32[2,384]{1,0:T(2,128)S(1)}, f32[2,192,192]{2,1,0:T(8,128)S(1)}, f32[2,192,192]{2,1,0:T(8,128)S(1)}, f32[192,192]{1,0:T(8,128)S(1)}, f32[512,...) custom-call(s32[2]{0:T(128)S(1)} %pad_add_fusion.ids, ...), custom_call_target="tpu_custom_call" | custom-call | flops 4000000000 | bytes 1048576 | tf_op jit(solution)/shard_map/pallas_call | solution.py:586
  9.9 2.0 %collective-permute-done.2.refs_0_.refs_3_.refs_2_ = f32[264,128]{1,0:T(8,128)S(1)} collective-permute-done((f32[264,128]{1,0:T(8,128)S(1)}, f32[264,128]{1,0:T(8,128)S(1)}, u32[]{:S(2)}, u32[]{:S(2)}) %collective-permute-start.2) | collective-permute-done | bytes 135200 | tf_op jit(solution)/shard_map/ppermute | solution.py:614
  11.9 1.9 %collective-permute-done.1.refs_2_.refs_1_ = f32[264,128]{1,0:T(8,128)S(1)} collective-permute-done((f32[264,128]{1,0:T(8,128)S(1)}, f32[264,128]{1,0:T(8,128)S(1)}, u32[]{:S(2)}, u32[]{:S(2)}) %collective-permute-start.1) | collective-permute-done | bytes 135200 | tf_op jit(solution)/shard_map/ppermute | solution.py:614
  13.8 0.5 collective-permute-start.5
  14.4 0.5 collective-permute-start.4
  14.9 0.2 collective-permute-done.5.refs_1_
  15.2 1.6 %collective-permute-start.6 = (f32[2,8,128]{2,1,0:T(8,128)S(1)}, f32[2,8,128]{2,1,0:T(8,128)S(1)}, u32[]{:S(2)}, u32[]{:S(2)}) collective-permute-start(f32[2,8,128]{2,1,0:T(8,128)S(1)} %shard_map.135._.x.refs_0_), channel_id=1, source_target_pairs={{1,0},{0,1},{3,2},{2,3},{5,4},{4,5},{7,6},{6,7},{9,8},{8,9},{11,10... | collective-permute-start | bytes 24584 | tf_op jit(solution)/shard_map/ppermute | solution.py:650
  16.7 2.6 %shard_map.136 = (f32[192,1536]{1,0:T(8,128)S(1)}, bf16[2,384,192]{2,1,0:T(8,128)(2,1)S(1)}, bf16[2,384,192]{2,1,0:T(8,128)(2,1)S(1)}, bf16[2,192,192]{2,1,0:T(8...) custom-call(s32[2]{0:T(128)S(1)} %pad_add_fusion.ids, ...), custom_call_target="tpu_custom_call" | custom-call | flops 2000000000 | bytes 1048576 | tf_op jit(solution)/shard_map/pallas_call | solution.py:586
  19.3 2.7 %collective-permute-start.7 = (f32[4,8,128]{2,1,0:T(8,128)S(1)}, f32[4,8,128]{2,1,0:T(8,128)S(1)}, u32[]{:S(2)}, u32[]{:S(2)}) collective-permute-start(f32[4,8,128]{2,1,0:T(8,128)S(1)} %shard_map.137.refs_5_), channel_id=1, source_target_pairs={{2,0},{3,1},{0,2},{1,3},{6,4},{7,5},{4,6},{5,7},{10,8},{11,9},{8,1... | collective-permute-start | bytes 49160 | tf_op jit(solution)/shard_map/ppermute | solution.py:650
  22.0 0.7 %shard_map.138 = (bf16[512,256]{1,0:T(8,128)(2,1)S(1)}, bf16[512,256]{1,0:T(8,128)(2,1)S(1)}) custom-call(f32[512,256]{1,0:T(8,128)S(1)} %get-tuple-element.45.gat, bf16[384,256]{1,0:T(8,128)(2,1)S(1)} %get-tuple-element.46.gh, bf16[384,256]{1,0:T(8,128)(2,1)S(1)} %get-tuple-element.47.gl, f32[264,128]{1,0:T(8,128)S(1)} %collective-permute-done.x.refs_1_.refs_0_, ...), custom_call_target="tpu_custom_call" | custom-call | flops 1000000000 | bytes 1048576 | tf_op jit(solution)/shard_map/pallas_call | solution.py:586
  22.7 0.6 %shard_map.139.part = f32[512,256]{1,0:T(8,128)S(1)} custom-call(f32[512,256]{1,0:T(8,128)S(1)} %get-tuple-element.42.loc, bf16[512,512]{1,0:T(8,128)(2,1)S(1)} %get-tuple-element.43.nh, bf16[512,512]{1,0:T(8,128)(2,1)S(1)} %get-tuple-element.44.nl, bf16[512,256]{1,0:T(8,128)(2,1)S(1)} %get-tuple-element.55.hi, bf16[512,256]{1,0:T(8,128)(2,1)S(1)} %get-tuple-element.56.lo), custom_call_target="tpu_custom_call" | custom-call | flops 1000000000 | bytes 1048576 | tf_op jit(solution)/shard_map/pallas_call | solution.py:586
  23.2 0.8 %collective-permute-done.7.refs_2_ = f32[4,8,128]{2,1,0:T(8,128)S(1)} collective-permute-done((f32[4,8,128]{2,1,0:T(8,128)S(1)}, f32[4,8,128]{2,1,0:T(8,128)S(1)}, u32[]{:S(2)}, u32[]{:S(2)}) %collective-permute-start.7) | collective-permute-done | bytes 16416 | tf_op jit(solution)/shard_map/ppermute | solution.py:650
  24.0 0.6 %shard_map.140 = (f32[512,256]{1,0:T(8,128)S(1)}, f32[256,128]{1,0:T(8,128)S(1)}, f32[8,128]{1,0:T(8,128)S(1)}) custom-call(f32[512,256]{1,0:T(8,128)S(1)} %shard_map.139.part, f32[192,1536]{1,0:T(8,128)S(1)} %get-tuple-element.54._.far_op, s32[1,1,256]{2,1,0:T(1,128)S(1)} %get-tuple-element.57.cells, f32[168,128]{1,0:T(8,128)S(1)} %get-tuple-element.58.col, ...), custom_call_target="tpu_custom_call" | custom-call | flops 100000000 | bytes 1048576 | tf_op jit(solution)/shard_map/pallas_call | solution.py:586
  24.6 0.4 collective-permute-start.10
  25.0 1.2 %collective-permute-start.8 = (f32[256,128]{1,0:T(8,128)S(1)}, f32[256,128]{1,0:T(8,128)S(1)}, u32[]{:S(2)}, u32[]{:S(2)}) collective-permute-start(f32[256,128]{1,0:T(8,128)S(1)} %get-tuple-element.66), channel_id=1, source_target_pairs={{4,0},{0,4},{12,8},{8,12},{20,16},{16,20},{28,24},{24,28},{5,1},{1... | collective-permute-start | bytes 393224 | tf_op jit(solution)/shard_map/ppermute | solution.py:614
  26.2 0.6 %collective-permute-start.11 = (f32[256,128]{1,0:T(8,128)S(1)}, f32[256,128]{1,0:T(8,128)S(1)}, u32[]{:S(2)}, u32[]{:S(2)}) collective-permute-start(f32[256,128]{1,0:T(8,128)S(1)} %get-tuple-element.66), channel_id=1, source_target_pairs={{8,0},{12,4},{0,8},{4,12},{24,16},{28,20},{16,24},{20,28},{9,1},{1... | collective-permute-start | bytes 393224 | tf_op jit(solution)/shard_map/ppermute | solution.py:614
  26.8 0.8 %collective-permute-start.9 = (f32[256,128]{1,0:T(8,128)S(1)}, f32[256,128]{1,0:T(8,128)S(1)}, u32[]{:S(2)}, u32[]{:S(2)}) collective-permute-start(f32[256,128]{1,0:T(8,128)S(1)} %get-tuple-element.66), channel_id=1, source_target_pairs={{24,0},{28,4},{16,8},{20,12},{8,16},{12,20},{0,24},{4,28},{25,1},{... | collective-permute-start | bytes 393224 | tf_op jit(solution)/shard_map/ppermute | solution.py:614
  27.5 1.0 %shard_map.141 = (f32[512,256]{1,0:T(8,128)S(1)}, f32[512,256]{1,0:T(8,128)S(1)}, f32[512,256]{1,0:T(8,128)S(1)}, f32[8,128]{1,0:T(8,128)S(1)}) custom-call(f32[512,256]{1,0:T(8,128)S(1)} %get-tuple-element.59.u_in, f32[512,256]{1,0:T(8,128)S(1)} %get-tuple-element.41.f_in, f32[16,256]{1,0:T(8,128)S(1)} %get-tuple-element.49.refs_1_.refs_4_.rot, ...), custom_call_target="tpu_custom_call" | custom-call | flops 1000000000 | bytes 1048576 | tf_op jit(solution)/shard_map/pallas_call | solution.py:586
  28.6 2.6 %collective-permute-done.10.refs_0_.refs_2_ = f32[256,128]{1,0:T(8,128)S(1)} collective-permute-done((f32[256,128]{1,0:T(8,128)S(1)}, f32[256,128]{1,0:T(8,128)S(1)}, u32[]{:S(2)}, u32[]{:S(2)}) %collective-permute-start.10) | collective-permute-done | bytes 131104 | tf_op jit(solution)/shard_map/ppermute | solution.py:614
  31.2 1.8 %collective-permute-done.8.x.refs_0_ = f32[256,128]{1,0:T(8,128)S(1)} collective-permute-done((f32[256,128]{1,0:T(8,128)S(1)}, f32[256,128]{1,0:T(8,128)S(1)}, u32[]{:S(2)}, u32[]{:S(2)}) %collective-permute-start.8) | collective-permute-done | bytes 131104 | tf_op jit(solution)/shard_map/ppermute | solution.py:614
  33.0 0.4 collective-permute-start.12
  33.5 0.2 collective-permute-done.9.refs_1_
  33.6 0.8 %collective-permute-done.12.refs_4_ = f32[256,128]{1,0:T(8,128)S(1)} collective-permute-done((f32[256,128]{1,0:T(8,128)S(1)}, f32[256,128]{1,0:T(8,128)S(1)}, u32[]{:S(2)}, u32[]{:S(2)}) %collective-permute-start.12) | collective-permute-done | bytes 131104 | tf_op jit(solution)/shard_map/ppermute | solution.py:614
  34.4 0.7 %shard_map.143 = (bf16[512,256]{1,0:T(8,128)(2,1)S(1)}, bf16[512,256]{1,0:T(8,128)(2,1)S(1)}) custom-call(f32[512,256]{1,0:T(8,128)S(1)} %get-tuple-element.65.gat, bf16[384,256]{1,0:T(8,128)(2,1)S(1)} %get-tuple-element.46.gh, bf16[384,256]{1,0:T(8,128)(2,1)S(1)} %get-tuple-element.47.gl, f32[256,128]{1,0:T(8,128)S(1)} %collective-permute-done.8.x.refs_0_, ...), custom_call_target="tpu_custom_call" | custom-call | flops 1000000000 | bytes 1048576 | tf_op jit(solution)/shard_map/pallas_call | solution.py:586
  35.1 1.3 %shard_map.144 = f32[32,8,128]{2,1,0:T(8,128)S(1)} custom-call(f32[512,256]{1,0:T(8,128)S(1)} %get-tuple-element.64.loc, bf16[512,512]{1,0:T(8,128)(2,1)S(1)} %get-tuple-element.43.nh, bf16[512,512]{1,0:T(8,128)(2,1)S(1)} %get-tuple-element.44.nl, bf16[512,256]{1,0:T(8,128)(2,1)S(1)} %get-tuple-element.68.hi, bf16[512,256]{1,0:T(8,128)(2,1)S(1)} %get-tuple-element.69.lo, ...), custom_call_target="tpu_custom_call" | custom-call | flops 1000000000 | bytes 1048576 | tf_op jit(solution)/shard_map/pallas_call | solution.py:586
  36.4 11.4 %all_to_all.5.mine = f32[32,8,128]{2,1,0:T(8,128)S(1)} all-to-all(f32[32,8,128]{2,1,0:T(8,128)S(1)} %shard_map.144), channel_id=1, replica_groups=mesh['gx'=4,'gy'=2,'gz'=4] {'gx','gy','gz'}, dimensions={0} | all-to-all | bytes 262144 | tf_op jit(solution)/shard_map/all_to_all | solution.py:730
  47.9 1.2 %collective-permute-done.13.other = f32[32,8,128]{2,1,0:T(8,128)S(1)} collective-permute-done((f32[32,8,128]{2,1,0:T(8,128)S(1)}, f32[32,8,128]{2,1,0:T(8,128)S(1)}, u32[]{:S(2)}, u32[]{:S(2)}) %collective-permute-start.13) | collective-permute-done | bytes 131104 | tf_op jit(solution)/shard_map/ppermute | solution.py:614
  49.1 4.4 %shard_map.145 = (f32[486,1,256]{2,1,0:T(1,128)}, f32[1,1]{1,0:T(1,128)}) custom-call(s32[2]{0:T(128)S(1)} %pad_add_fusion.ids, f32[512,256]{1,0:T(8,128)S(1)} %get-tuple-element.41.f_in, f32[512,256]{1,0:T(8,128)S(1)} %get-tuple-element.59.u_in, f32[32,8,128]{2,1,0:T(8,128)S(1)} %all_to_all.5.mine, f32[32,8,128]{2,1,0:T(8,128)S(1)} %collective-permute-done.13.other, ...), custom_call_target="tpu_custom_call" | custom-call | flops 10000000 | bytes 1048576 | tf_op jit(solution)/shard_map/pallas_call | solution.py:586
  (13 shorter events, 0.3 us)
Async XLA Ops:
  2.1 7.8 %collective-permute-start = (f32[264,128]{1,0:T(8,128)S(1)}, f32[264,128]{1,0:T(8,128)S(1)}, u32[]{:S(2)}, u32[]{:S(2)}) collective-permute-start(f32[264,128]{1,0:T(8,128)S(1)} %get-tuple-element.48.refs_0_.message.charges_f), channel_id=1, source_target_pairs={{4,0},{0,4},{12,8},{8,12},{20,16},{16,20},{28,24},{24,28},{5,1},{1... | collective-permute-start | bytes 405512 | tf_op jit(solution)/shard_map/ppermute | solution.py:614
  5.1 6.8 %collective-permute-start.2 = (f32[264,128]{1,0:T(8,128)S(1)}, f32[264,128]{1,0:T(8,128)S(1)}, u32[]{:S(2)}, u32[]{:S(2)}) collective-permute-start(f32[264,128]{1,0:T(8,128)S(1)} %get-tuple-element.48.refs_0_.message.charges_f), channel_id=1, source_target_pairs={{28,0},{24,4},{20,8},{16,12},{12,16},{8,20},{4,24},{0,28},{29,1},{... | collective-permute-start | bytes 405512 | tf_op jit(solution)/shard_map/ppermute | solution.py:614
  5.7 8.1 %collective-permute-start.1 = (f32[264,128]{1,0:T(8,128)S(1)}, f32[264,128]{1,0:T(8,128)S(1)}, u32[]{:S(2)}, u32[]{:S(2)}) collective-permute-start(f32[264,128]{1,0:T(8,128)S(1)} %get-tuple-element.48.refs_0_.message.charges_f), channel_id=1, source_target_pairs={{24,0},{28,4},{16,8},{20,12},{8,16},{12,20},{0,24},{4,28},{25,1},{... | collective-permute-start | bytes 405512 | tf_op jit(solution)/shard_map/ppermute | solution.py:614
  13.8 1.3 %collective-permute-start.5 = (f32[8,128]{1,0:T(8,128)S(1)}, f32[8,128]{1,0:T(8,128)S(1)}, u32[]{:S(2)}, u32[]{:S(2)}) collective-permute-start(f32[8,128]{1,0:T(8,128)S(1)} %shard_map.134.refs_0_), channel_id=1, source_target_pairs={{8,0},{12,4},{0,8},{4,12},{24,16},{28,20},{16,24},{20,28},{9,1},{1... | collective-permute-start | bytes 12296 | tf_op jit(solution)/shard_map/ppermute | solution.py:614
  14.3 7.6 %collective-permute-start.3 = (f32[264,128]{1,0:T(8,128)S(1)}, f32[264,128]{1,0:T(8,128)S(1)}, u32[]{:S(2)}, u32[]{:S(2)}) collective-permute-start(f32[264,128]{1,0:T(8,128)S(1)} %get-tuple-element.48.refs_0_.message.charges_f), channel_id=1, source_target_pairs={{8,0},{12,4},{0,8},{4,12},{24,16},{28,20},{16,24},{20,28},{9,1},{1... | collective-permute-start | bytes 405512 | tf_op jit(solution)/shard_map/ppermute | solution.py:614
  14.4 7.6 %collective-permute-start.4 = (f32[264,128]{1,0:T(8,128)S(1)}, f32[264,128]{1,0:T(8,128)S(1)}, u32[]{:S(2)}, u32[]{:S(2)}) collective-permute-start(f32[264,128]{1,0:T(8,128)S(1)} %shard_map.133), channel_id=1, source_target_pairs={{8,0},{12,4},{0,8},{4,12},{24,16},{28,20},{16,24},{20,28},{9,1},{1... | collective-permute-start | bytes 405512 | tf_op jit(solution)/shard_map/ppermute | solution.py:614
  15.2 4.1 %collective-permute-start.6 = (f32[2,8,128]{2,1,0:T(8,128)S(1)}, f32[2,8,128]{2,1,0:T(8,128)S(1)}, u32[]{:S(2)}, u32[]{:S(2)}) collective-permute-start(f32[2,8,128]{2,1,0:T(8,128)S(1)} %shard_map.135._.x.refs_0_), channel_id=1, source_target_pairs={{1,0},{0,1},{3,2},{2,3},{5,4},{4,5},{7,6},{6,7},{9,8},{8,9},{11,10... | collective-permute-start | bytes 24584 | tf_op jit(solution)/shard_map/ppermute | solution.py:650
  19.3 4.7 %collective-permute-start.7 = (f32[4,8,128]{2,1,0:T(8,128)S(1)}, f32[4,8,128]{2,1,0:T(8,128)S(1)}, u32[]{:S(2)}, u32[]{:S(2)}) collective-permute-start(f32[4,8,128]{2,1,0:T(8,128)S(1)} %shard_map.137.refs_5_), channel_id=1, source_target_pairs={{2,0},{3,1},{0,2},{1,3},{6,4},{7,5},{4,6},{5,7},{10,8},{11,9},{8,1... | collective-permute-start | bytes 49160 | tf_op jit(solution)/shard_map/ppermute | solution.py:650
  24.6 6.6 %collective-permute-start.10 = (f32[256,128]{1,0:T(8,128)S(1)}, f32[256,128]{1,0:T(8,128)S(1)}, u32[]{:S(2)}, u32[]{:S(2)}) collective-permute-start(f32[256,128]{1,0:T(8,128)S(1)} %get-tuple-element.66), channel_id=1, source_target_pairs={{28,0},{24,4},{20,8},{16,12},{12,16},{8,20},{4,24},{0,28},{29,1},{... | collective-permute-start | bytes 393224 | tf_op jit(solution)/shard_map/ppermute | solution.py:614
  25.0 8.0 %collective-permute-start.8 = (f32[256,128]{1,0:T(8,128)S(1)}, f32[256,128]{1,0:T(8,128)S(1)}, u32[]{:S(2)}, u32[]{:S(2)}) collective-permute-start(f32[256,128]{1,0:T(8,128)S(1)} %get-tuple-element.66), channel_id=1, source_target_pairs={{4,0},{0,4},{12,8},{8,12},{20,16},{16,20},{28,24},{24,28},{5,1},{1... | collective-permute-start | bytes 393224 | tf_op jit(solution)/shard_map/ppermute | solution.py:614
  26.2 7.3 %collective-permute-start.11 = (f32[256,128]{1,0:T(8,128)S(1)}, f32[256,128]{1,0:T(8,128)S(1)}, u32[]{:S(2)}, u32[]{:S(2)}) collective-permute-start(f32[256,128]{1,0:T(8,128)S(1)} %get-tuple-element.66), channel_id=1, source_target_pairs={{8,0},{12,4},{0,8},{4,12},{24,16},{28,20},{16,24},{20,28},{9,1},{1... | collective-permute-start | bytes 393224 | tf_op jit(solution)/shard_map/ppermute | solution.py:614
  26.8 6.9 %collective-permute-start.9 = (f32[256,128]{1,0:T(8,128)S(1)}, f32[256,128]{1,0:T(8,128)S(1)}, u32[]{:S(2)}, u32[]{:S(2)}) collective-permute-start(f32[256,128]{1,0:T(8,128)S(1)} %get-tuple-element.66), channel_id=1, source_target_pairs={{24,0},{28,4},{16,8},{20,12},{8,16},{12,20},{0,24},{4,28},{25,1},{... | collective-permute-start | bytes 393224 | tf_op jit(solution)/shard_map/ppermute | solution.py:614
  33.0 1.4 %collective-permute-start.12 = (f32[256,128]{1,0:T(8,128)S(1)}, f32[256,128]{1,0:T(8,128)S(1)}, u32[]{:S(2)}, u32[]{:S(2)}) collective-permute-start(f32[256,128]{1,0:T(8,128)S(1)} %shard_map.142), channel_id=1, source_target_pairs={{8,0},{12,4},{0,8},{4,12},{24,16},{28,20},{16,24},{20,28},{9,1},{1... | collective-permute-start | bytes 393224 | tf_op jit(solution)/shard_map/ppermute | solution.py:614
  47.8 1.3 %collective-permute-start.13 = (f32[32,8,128]{2,1,0:T(8,128)S(1)}, f32[32,8,128]{2,1,0:T(8,128)S(1)}, u32[]{:S(2)}, u32[]{:S(2)}) collective-permute-start(f32[32,8,128]{2,1,0:T(8,128)S(1)} %all_to_all.5.mine), channel_id=1, source_target_pairs={{8,0},{12,4},{0,8},{4,12},{24,16},{28,20},{16,24},{20,28},{9,1},{1... | collective-permute-start | bytes 393224 | tf_op jit(solution)/shard_map/ppermute | solution.py:614

commit v11 on v9

--- a/solution.py
+++ b/solution.py
@@ -97,7 +97,7 @@
 def stacked(parts, s):
     rest = s.rows - 3 * s.step
     if rest:
-        parts = list(parts) + [jnp.zeros((rest, s.bodies), f32)]
+        parts = list(parts) + [jnp.zeros((rest, parts[0].shape[1]), f32)]
     return jnp.concatenate(parts, axis=0)
 
 
@@ -141,6 +141,8 @@
 
 def pack_message(x, weight_col, cells, s):
     charges = pack_charges(pieces(x, s), weight_col, occupancy(cells, s), s)
+    row = lax.broadcasted_iota(jnp.int32, (8, LANES), 0)
+    charges = jnp.where(row == 3, cells[:, :LANES].astype(f32), charges)
     return jnp.concatenate([pack_rim(x, s), charges], axis=0)
 
 
@@ -222,7 +224,7 @@
 def setup(
     s, ids, f_in, moves, angles, near_weight, neighbours, self_mob, near_mat, perm, interp, sibling, root,
     loc_out, gat_out, rot_out, sh_out, sl_out, nh_out, nl_out, oh_out, ol_out, gh_out, gl_out,
-    far_out, uh_out, ul_out, bh_out, bl_out, rh_out, rl_out, padded, ups_ref,
+    fh_out, fl_out, uh_out, ul_out, bh_out, bl_out, rh_out, rl_out, padded, ups_ref, far_ref,
 ):
     f = f_in[...]
     for move in moves[:3]:
@@ -306,14 +308,15 @@
     for blocks in reversed(sub):
         near_leaves += blocks
     tail = n - LANES
-    far_out[...] = jnp.zeros_like(far_out)
+    far_ref[...] = jnp.zeros_like(far_ref)
     own = [a - b for a, b in zip(near_leaves, far_leaves)]
     for group, blocks in enumerate((own, far_leaves)):
         for leaf, block in enumerate(blocks):
             at = (group * s.far_tiles + leaf) * LANES
-            far_out[:, at : at + LANES] = block[:, :LANES]
+            far_ref[:, at : at + LANES] = block[:, :LANES]
             at = (group * s.far_tiles + s.nz + leaf // 2) * LANES + leaf % 2 * RIM
-            far_out[:, at : at + tail] = block[:, LANES:]
+            far_ref[:, at : at + tail] = block[:, LANES:]
+    fh_out[...], fl_out[...] = split(far_ref[...])
 
 
 def half_kernel(s, *refs):
@@ -324,74 +327,100 @@
     out[...] = acc
 
 
-def layer_kernel(s, message, *refs):
-    *sums, _, out = refs
+def layer_kernel(s, count, message, *refs):
+    sums, around, out = refs[:count], refs[count:-1], refs[-1]
     acc = sums[0][...]
     for part in sums[1:]:
         acc = acc + part[...]
     out[0] = message[s.half :, :]
     out[1] = acc
-
-
-def far_potential(s, charges, far_op):
-    rows = []
-    for group in range(2):
-        tiles = [layer[group] for layer in charges]
-        rows += tiles
-        for leaf in range(0, s.nz, 2):
-            pair = tiles[leaf]
-            if leaf + 1 < s.nz:
-                lane = lax.broadcasted_iota(jnp.int32, (8, LANES), 1)
-                pair = jnp.where(lane < RIM, pair, pltpu.roll(tiles[leaf + 1], RIM, 1))
-            rows.append(pltpu.roll(pair, 4, 0))
-    columns = [[], [], []]
-    for r in range(0, s.skel, 64):
-        acc = [None] * 3
-        for index, row in enumerate(rows):
-            block = far_op[r : r + 64, index * LANES : (index + 1) * LANES]
-            for c in range(3):
-                term = block * row[c : c + 1]
-                acc[c] = term if acc[c] is None else acc[c] + term
-        for c in range(3):
-            columns[c].append(jnp.sum(acc[c], axis=1, keepdims=True))
-    return columns
-
-
-def far_values(s, charges, far_op, cells):
-    columns = far_potential(s, charges, far_op)
+    for index, other in enumerate(around):
+        out[2 + index] = other[s.half :, :]
+
+
+def layer_row(s, tiles):
+    row = list(tiles)
+    lane = lax.broadcasted_iota(jnp.int32, (8, LANES), 1)
+    for leaf in range(0, s.nz, 2):
+        pair = tiles[leaf]
+        if leaf + 1 < s.nz:
+            pair = jnp.where(lane < RIM, pair, pltpu.roll(tiles[leaf + 1], RIM, 1))
+        row.append(pltpu.roll(pair, 4, 0))
+    return jnp.concatenate(row, axis=1)
+
+
+def far_potentials(s, layers, far_op):
+    own = [layer_row(s, [layer[k] for layer in layers]) for k in range(layers[0].shape[0])]
+    wide = own[0].shape[1]
+    hi, lo = far_op
+    whole = product(mt, split(own.pop(1)), (hi[:, wide:], lo[:, wide:]))
+    boxes = product(mt, split(jnp.concatenate(own, axis=0)), (hi[:, :wide], lo[:, :wide]))
+    return [boxes[8 * k : 8 * k + 8] + whole for k in range(len(own))]
+
+
+def pick(potential, onehot):
+    high, _ = split(potential)
+    mid, low = split(potential - high.astype(f32))
+    parts = [x.astype(f32) for x in (high, mid, low)]
+    picked = mm(jnp.concatenate(parts, axis=0).astype(bf16), onehot)
+    n = potential.shape[0]
+    return picked[:n] + (picked[n : 2 * n] + picked[2 * n :])
+
+
+def rim_values(s, layers, potentials):
+    lane = lax.broadcasted_iota(jnp.int32, (8, LANES), 1)
+    place = lax.broadcasted_iota(jnp.int32, (s.skel, LANES), 0).astype(f32)
+    count = len(potentials) - 1
     out = []
-    for c in range(3):
-        acc = jnp.zeros((1, s.bodies), f32)
-        for index, r in enumerate(range(0, s.skel, 64)):
-            row = lax.broadcasted_iota(jnp.int32, (64, s.bodies), 0) + r
-            acc = acc + jnp.sum(jnp.where(cells == row, columns[c][index], 0.0), axis=0, keepdims=True)
-        out.append(acc)
+    for i in range(0, count, 2):
+        last = min(i + 1, count - 1)
+        cells = jnp.where(lane < RIM, layers[0][2 + i], pltpu.roll(layers[0][2 + last], RIM, 1))
+        onehot = jnp.where(cells[3:4] == place, 1.0, 0.0).astype(bf16)
+        both = pick(jnp.concatenate([potentials[1 + i], potentials[1 + last]], axis=0), onehot)
+        out.append(jnp.where(lane < RIM, both[:8], both[8:]))
     return out
 
 
 def gather_kernel(s, gat, gh, gl, *refs):
     *messages, _, hi_out, lo_out = refs
-    rims = [message[: s.half, :] for message in messages]
-    gathered = gat[...] + product(mm, split(unpack_rims(rims, s)), (gh[...], gl[...]))
+    rims = unpack_rims([message[: s.half, :] for message in messages], s)
+    gathered = gat[...] + product(mm, split(rims), (gh[...], gl[...]))
     hi_out[...], lo_out[...] = split(gathered)
 
 
-def near_kernel(s, loc, nh, nl, hi, lo, out):
-    out[...] = loc[...] + product(mm, (nh[...], nl[...]), (hi[...], lo[...]))
-
-
-def with_far(s, part, layers, far_op, cells, col):
-    values = far_values(s, layers, far_op, cells[0])
-    return part[...] + stacked([col * value for value in values], s)
-
-
-def first_kernel(s, part, far_op, cells, col, *refs):
-    *layers, u_out, rim_out, charges_out = refs
+def gather_far_kernel(s, gat, gh, gl, col, values, *refs):
+    *messages, hi_out, lo_out = refs
+    rims = unpack_rims([message[...] for message in messages], s)
+    far = []
+    for c in range(3):
+        value = jnp.concatenate([values[i, c : c + 1, :] for i in range(values.shape[0])], axis=1)
+        far.append(col[:, :1] * value)
+    rims = rims + stacked(far, s)
+    gathered = gat[...] + product(mm, split(rims), (gh[...], gl[...]))
+    hi_out[...], lo_out[...] = split(gathered)
+
+
+def near_kernel(s, loc, nh, nl, hi, lo, out, rim_out):
+    part = loc[...] + product(mm, (nh[...], nl[...]), (hi[...], lo[...]))
+    out[...] = part
+    rim_out[...] = pack_rim(part, s)
+
+
+def first_kernel(s, part, fh, fl, cells, col, *refs):
+    *layers, u_out, charges_out, values_out = refs
     weight_col = col[:, :1]
-    u = with_far(s, part, layers, far_op, cells, weight_col)
+    occ = occupancy(cells[0], s)
+    potentials = far_potentials(s, layers, (fh[...], fl[...]))
+    values = pick(potentials[0], occ)
+    u = part[...] + stacked([weight_col * values[c : c + 1] for c in range(3)], s)
     u_out[...] = u
-    rim_out[...] = pack_rim(u, s)
-    charges_out[...] = pack_charges(pieces(u, s), weight_col, occupancy(cells[0], s), s)
+    charges_out[...] = pack_charges(pieces(u, s), weight_col, occ, s)
+    for index, value in enumerate(rim_values(s, layers, potentials)):
+        values_out[index] = value
+
+
+def order_kernel(x, _, out):
+    out[...] = x[...]
 
 
 def safe_inverse(x):
@@ -620,36 +649,16 @@
 
     def forward_rims(got, after):
         for dy in s.shifts:
-            ready, _ = lax.optimization_barrier((got["same", dy], after))
-            got["partner", dy] = fetch(ready, "partner", 0)
-
-    def gather(gat, got, after):
-        return call(
-            functools.partial(gather_kernel, s),
-            [(full, bf16), (full, bf16)],
-            [gat, gh, gl] + [got[key] for key in s.sources] + [after],
-            flops=10**9,
-        )
-
-    def share(message, got, gat, after):
-        forward_rims(got, after)
-        if s.direct:
-            quarter = [message] + [got[key] for key in s.sources if key[0] != "partner"]
-            (half,) = call(functools.partial(half_kernel, s), [(tile, f32)], quarter + [after])
-            sums = [half, fetch(half, "partner", 0)]
-        else:
-            half = lax.psum(message[s.half :], ("gx", "gy"))
-            sums = [half]
-        gathered = gather(gat, got, half)
-        (pair,) = call(
-            functools.partial(layer_kernel, s), [((2,) + tile, f32)], [message] + sums + [gathered[1]]
-        )
-        return gathered, fetch_layers(pair)
-
-    def near_part(loc, gathered):
-        return call(
-            functools.partial(near_kernel, s), [(full, f32)], [loc, nh, nl, *gathered], flops=10**9
-        )[0]
+            held = got["same", dy]
+            (held,) = call(order_kernel, [(held.shape, f32)], [held, after])
+            got["partner", dy] = fetch(held, "partner", 0)
+
+    def plane_sum(message, got, after):
+        if not s.direct:
+            return [lax.psum(message[s.half :], ("gx", "gy"))]
+        quarter = [message] + [got[key] for key in s.sources if key[0] != "partner"]
+        (half,) = call(functools.partial(half_kernel, s), [(tile, f32)], quarter + [after])
+        return [half, fetch(half, "partner", 0)]
 
     flat = (3 * s.blobs, 1, s.bodies)
     small = (1, s.blobs)
@@ -666,33 +675,54 @@
         angles.reshape(3, 1, s.bodies), near_weight, neighbours, self_mob, near_mat, skel_perm, interp,
         sibling_ops, root_op,
     ]
-    loc, gat, rot, sh, sl, nh, nl, oh, ol, gh, gl, far_op, *operators_out = call(
+    loc, gat, rot, sh, sl, nh, nl, oh, ol, gh, gl, fh, fl, *operators_out = call(
         functools.partial(setup_kernel, s),
         [(full, f32), (full, f32), ((16, s.bodies), f32)]
         + [(square, bf16)] * 4
         + [((s.bodies, s.bodies), bf16)] * 2
         + [((s.ghosts, s.bodies), bf16)] * 2
-        + [(far_shape, f32)]
+        + [(far_shape, bf16)] * 2
         + [((s.levels, 2 * s.skel, s.skel), bf16)] * 2
         + [((s.levels, s.skel, s.skel), bf16)] * 2
         + [((s.skel, s.skel), bf16)] * 2,
         [ids, f] + operators,
         scalars=1,
         far_args=len(operators),
-        scratch=[pltpu.VMEM(square, f32), pltpu.VMEM((s.levels, 2 * s.skel, s.skel), f32)]
+        scratch=[
+            pltpu.VMEM(square, f32), pltpu.VMEM((s.levels, 2 * s.skel, s.skel), f32), pltpu.VMEM(far_shape, f32)
+        ]
         + [pltpu.VMEM(x.shape, x.dtype) for x in operators]
         + [pltpu.SemaphoreType.DMA((len(operators),))],
         flops=5 * 10**9,
     )
-    gathered, layers = share(message, got, gat, rot)
-    part = near_part(loc, gathered)
-    u, rim, charges = call(
+    forward_rims(got, rot)
+    sums = plane_sum(message, got, rot)
+    around = [got[key] for key in s.sources]
+    (tiles,) = call(
+        functools.partial(layer_kernel, s, len(sums)),
+        [((2 + len(around),) + tile, f32)],
+        [message] + sums + around,
+    )
+    layers = fetch_layers(tiles)
+    gathered = call(
+        functools.partial(gather_kernel, s),
+        [(full, bf16), (full, bf16)],
+        [gat, gh, gl] + around + [tiles],
+        flops=10**9,
+    )
+    part, rim = call(
+        functools.partial(near_kernel, s),
+        [(full, f32), ((s.half, LANES), f32)],
+        [loc, nh, nl, *gathered],
+        flops=10**9,
+    )
+    got = fetch_rims(rim)
+    u, charges, values = call(
         functools.partial(first_kernel, s),
-        [(full, f32), ((s.half, LANES), f32), (tile, f32)],
-        [part, far_op, cells, col, *layers],
+        [(full, f32), (tile, f32), ((s.ghosts // LANES,) + tile, f32)],
+        [part, fh, fl, cells, col, *layers],
         flops=10**8,
     )
-    got = fetch_rims(rim)
     loc, gat, ortho, stat = call(
         functools.partial(middle_kernel, s),
         [(full, f32), (full, f32), (full, f32), (tile, f32)],
@@ -700,7 +730,12 @@
         flops=10**9,
     )
     forward_rims(got, stat)
-    gathered = gather(gat, got, stat)
+    gathered = call(
+        functools.partial(gather_far_kernel, s),
+        [(full, bf16), (full, bf16)],
+        [gat, gh, gl, col, values] + [got[key] for key in s.sources],
+        flops=10**9,
+    )
     (packed,) = call(
         functools.partial(second_kernel, s),
         [((s.devices, 8, LANES), f32)],

time: 52.4 us -> 52.1 us (level)
  waiting for transfers between devices: 13 us -> 8.29 us
  blocking collectives: 9.45 us -> 12.3 us
  starting transfers between devices: 12.7 us -> 13.6 us
  Pallas kernels: 16.2 us -> 16.8 us
    ppermute x3, waiting for transfers between devices: 4.64 us -> 0.01 us  [fetch_layers(): lax.ppermute(x, 'gz', [(z ^ k, z) for z in range(s.nz)])]
    all_to_all x1, blocking collectives: 9.45 us -> 12.3 us  [body(): boxes = lax.all_to_all(packed, ('gx', 'gy', 'gz'), 0, 0)]
    ppermute x12, starting transfers between devices: 8.35 us -> 9.18 us  [fetch(): return lax.ppermute(x, ('gx', 'gy'), pairs)]
    pallas_call x11 -> x13, Pallas kernels: 16.2 us -> 16.8 us  [call(): pl.pallas_call(kernel, out_shape=[jax.ShapeDtypeStruct(shape, kind) for s...]
  transfers between devices with their start and end apart: 15 -> 15, of which waited for: 7 -> 6; matrix products, arithmetic and copies ran while one was open for 0% -> 0% of each run, Pallas kernels for 15% -> 17%
where the time goes in v11:
time: 52.1 us; the launch traced here: 51.9 us
  Pallas kernels  16.8 us (32%)
  starting transfers between devices  13.6 us (26%)
  blocking collectives  12.3 us (24%)
  waiting for transfers between devices  8.29 us (16%)
  between operations  0.74 us (1%)
    pallas_call x13, Pallas kernels, call(): pl.pallas_call(kernel, out_shape=[jax.ShapeDtypeStruct(shape, kind) for s...  16.8 us
    all_to_all x1, blocking collectives, body(): boxes = lax.all_to_all(packed, ('gx', 'gy', 'gz'), 0, 0)  12.3 us
    ppermute x12, starting transfers between devices, fetch(): return lax.ppermute(x, ('gx', 'gy'), pairs)  9.18 us
    ppermute x12, waiting for transfers between devices, fetch(): return lax.ppermute(x, ('gx', 'gy'), pairs)  8.28 us
    ppermute x3, starting transfers between devices, fetch_layers(): lax.ppermute(x, 'gz', [(z ^ k, z) for z in range(s.nz)])  4.45 us
  transfers between devices with their start and end apart: 15, of which 6 were waited for; matrix products, arithmetic and copies ran while one was open for 0% of the time, Pallas kernels for 17%

profile of v11, /device:TPU:0, one launch (start us, length us, event | category | flops | bytes accessed | tf_op | source)
XLA Modules:
  0.0 51.9 jit_solution(6931477291582166718)
XLA Ops:
  0.6 1.4 %shard_map.131 = (f32[264,128]{1,0:T(8,128)S(1)}, f32[168,128]{1,0:T(8,128)S(1)}, s32[1,1,256]{2,1,0:T(1,128)S(1)}, f32[512,256]{1,0:T(8,128)S(1)}) custom-call(f32[486,1,256]{2,1,0:T(1,128)} %bitcast.9, s32[1,1,256]{2,1,0:T(1,128)} %cells.1, f32[1,162]{1,0:T(1,128)} %bitcast.10), custom_call_target="tpu_custom_call" | custom-call | flops 10000000 | bytes 1048576 | tf_op jit(solution)/shard_map/pallas_call | solution.py:605
  2.1 0.5 collective-permute-start.3
  2.6 3.6 %collective-permute-start.2 = (f32[264,128]{1,0:T(8,128)S(1)}, f32[264,128]{1,0:T(8,128)S(1)}, u32[]{:S(2)}, u32[]{:S(2)}) collective-permute-start(f32[264,128]{1,0:T(8,128)S(1)} %get-tuple-element.47.refs_0_.message.charges_f), channel_id=1, source_target_pairs={{28,0},{24,4},{20,8},{16,12},{12,16},{8,20},{4,24},{0,28},{29,1},{... | collective-permute-start | bytes 405512 | tf_op jit(solution)/shard_map/ppermute | solution.py:633
  6.2 0.2 collective-permute-start.1
  6.3 0.4 collective-permute-start
  6.7 0.1 pad_add_fusion.ids
  6.8 5.6 %shard_map.132 = (f32[512,256]{1,0:T(8,128)S(1)}, f32[512,256]{1,0:T(8,128)S(1)}, f32[16,256]{1,0:T(8,128)S(1)}, bf16[512,512]{1,0:T(8,128)(2,1)S(1)}, bf16[512,...) custom-call(s32[2]{0:T(128)S(1)} %pad_add_fusion.ids, ...), custom_call_target="tpu_custom_call" | custom-call | flops 5000000000 | bytes 1048576 | tf_op jit(solution)/shard_map/pallas_call | solution.py:605
  12.4 1.0 %collective-permute-done.x.refs_1_.refs_2_.refs_0_ = f32[264,128]{1,0:T(8,128)S(1)} collective-permute-done((f32[264,128]{1,0:T(8,128)S(1)}, f32[264,128]{1,0:T(8,128)S(1)}, u32[]{:S(2)}, u32[]{:S(2)}) %collective-permute-start) | collective-permute-done | bytes 135200 | tf_op jit(solution)/shard_map/ppermute | solution.py:633
  13.4 0.1 collective-permute-start.4
  13.5 0.0 collective-permute-done.2.refs_3_.refs_4_.refs_2_
  13.5 0.5 %collective-permute-start.5 = (f32[8,128]{1,0:T(8,128)S(1)}, f32[8,128]{1,0:T(8,128)S(1)}, u32[]{:S(2)}, u32[]{:S(2)}) collective-permute-start(f32[8,128]{1,0:T(8,128)S(1)} %shard_map.134.refs_0_), channel_id=1, source_target_pairs={{8,0},{12,4},{0,8},{4,12},{24,16},{28,20},{16,24},{20,28},{9,1},{1... | collective-permute-start | bytes 12296 | tf_op jit(solution)/shard_map/ppermute | solution.py:633
  14.1 0.8 %collective-permute-done.5.refs_1_ = f32[8,128]{1,0:T(8,128)S(1)} collective-permute-done((f32[8,128]{1,0:T(8,128)S(1)}, f32[8,128]{1,0:T(8,128)S(1)}, u32[]{:S(2)}, u32[]{:S(2)}) %collective-permute-start.5) | collective-permute-done | bytes 4128 | tf_op jit(solution)/shard_map/ppermute | solution.py:633
  14.9 3.7 %collective-permute-start.8 = (f32[7,8,128]{2,1,0:T(8,128)S(1)}, f32[7,8,128]{2,1,0:T(8,128)S(1)}, u32[]{:S(2)}, u32[]{:S(2)}) collective-permute-start(f32[7,8,128]{2,1,0:T(8,128)S(1)} %shard_map.135.refs_5_.refs_0_), channel_id=1, source_target_pairs={{3,0},{2,1},{1,2},{0,3},{7,4},{6,5},{5,6},{4,7},{11,8},{10,9},{9,1... | collective-permute-start | bytes 86024 | tf_op jit(solution)/shard_map/ppermute | solution.py:637
  18.6 0.0 collective-permute-start.7
  18.6 0.8 %collective-permute-start.6 = (f32[7,8,128]{2,1,0:T(8,128)S(1)}, f32[7,8,128]{2,1,0:T(8,128)S(1)}, u32[]{:S(2)}, u32[]{:S(2)}) collective-permute-start(f32[7,8,128]{2,1,0:T(8,128)S(1)} %shard_map.135.refs_5_.refs_0_), channel_id=1, source_target_pairs={{1,0},{0,1},{3,2},{2,3},{5,4},{4,5},{7,6},{6,7},{9,8},{8,9},{11,10... | collective-permute-start | bytes 86024 | tf_op jit(solution)/shard_map/ppermute | solution.py:637
  19.4 0.7 %shard_map.136 = (bf16[512,256]{1,0:T(8,128)(2,1)S(1)}, bf16[512,256]{1,0:T(8,128)(2,1)S(1)}) custom-call(f32[512,256]{1,0:T(8,128)S(1)} %get-tuple-element.44.gat, bf16[384,256]{1,0:T(8,128)(2,1)S(1)} %get-tuple-element.45.gh, bf16[384,256]{1,0:T(8,128)(2,1)S(1)} %get-tuple-element.46.gl, f32[264,128]{1,0:T(8,128)S(1)} %collective-permute-done.x.refs_1_.refs_2_.refs_0_, ...), custom_call_target="tpu_custom_call" | custom-call | flops 1000000000 | bytes 1048576 | tf_op jit(solution)/shard_map/pallas_call | solution.py:605
  20.1 0.6 %shard_map.137 = (f32[512,256]{1,0:T(8,128)S(1)}, f32[256,128]{1,0:T(8,128)S(1)}) custom-call(f32[512,256]{1,0:T(8,128)S(1)} %get-tuple-element.41.loc, bf16[512,512]{1,0:T(8,128)(2,1)S(1)} %get-tuple-element.42.nh, bf16[512,512]{1,0:T(8,128)(2,1)S(1)} %get-tuple-element.43.nl, bf16[512,256]{1,0:T(8,128)(2,1)S(1)} %get-tuple-element.49.hi, ...), custom_call_target="tpu_custom_call" | custom-call | flops 1000000000 | bytes 1048576 | tf_op jit(solution)/shard_map/pallas_call | solution.py:605
  20.7 1.6 %collective-permute-start.9 = (f32[256,128]{1,0:T(8,128)S(1)}, f32[256,128]{1,0:T(8,128)S(1)}, u32[]{:S(2)}, u32[]{:S(2)}) collective-permute-start(f32[256,128]{1,0:T(8,128)S(1)} %get-tuple-element.64), channel_id=1, source_target_pairs={{4,0},{0,4},{12,8},{8,12},{20,16},{16,20},{28,24},{24,28},{5,1},{1... | collective-permute-start | bytes 393224 | tf_op jit(solution)/shard_map/ppermute | solution.py:633
  22.3 1.2 %collective-permute-start.11 = (f32[256,128]{1,0:T(8,128)S(1)}, f32[256,128]{1,0:T(8,128)S(1)}, u32[]{:S(2)}, u32[]{:S(2)}) collective-permute-start(f32[256,128]{1,0:T(8,128)S(1)} %get-tuple-element.64), channel_id=1, source_target_pairs={{28,0},{24,4},{20,8},{16,12},{12,16},{8,20},{4,24},{0,28},{29,1},{... | collective-permute-start | bytes 393224 | tf_op jit(solution)/shard_map/ppermute | solution.py:633
  23.4 0.5 %collective-permute-start.10 = (f32[256,128]{1,0:T(8,128)S(1)}, f32[256,128]{1,0:T(8,128)S(1)}, u32[]{:S(2)}, u32[]{:S(2)}) collective-permute-start(f32[256,128]{1,0:T(8,128)S(1)} %get-tuple-element.64), channel_id=1, source_target_pairs={{24,0},{28,4},{16,8},{20,12},{8,16},{12,20},{0,24},{4,28},{25,1},{... | collective-permute-start | bytes 393224 | tf_op jit(solution)/shard_map/ppermute | solution.py:633
  24.0 1.0 %shard_map.138 = (f32[512,256]{1,0:T(8,128)S(1)}, f32[8,128]{1,0:T(8,128)S(1)}, f32[3,8,128]{2,1,0:T(8,128)S(1)}) custom-call(f32[512,256]{1,0:T(8,128)S(1)} %get-tuple-element.51.part, bf16[192,1536]{1,0:T(8,128)(2,1)S(1)} %get-tuple-element.52.fh, bf16[192,1536]{1,0:T(8,128)(2,1)S(1)} %get-tuple-element.53.fl, s32[1,1,256]{2,1,0:T(1,128)S(1)} %get-tuple-element.54.cells, ...), custom_call_target="tpu_custom_call" | custom-call | flops 100000000 | bytes 1048576 | tf_op jit(solution)/shard_map/pallas_call | solution.py:605
  25.0 1.1 %shard_map.139 = (f32[512,256]{1,0:T(8,128)S(1)}, f32[512,256]{1,0:T(8,128)S(1)}, f32[512,256]{1,0:T(8,128)S(1)}, f32[8,128]{1,0:T(8,128)S(1)}) custom-call(f32[512,256]{1,0:T(8,128)S(1)} %get-tuple-element.56.u_in, f32[512,256]{1,0:T(8,128)S(1)} %get-tuple-element.40.f_in, f32[16,256]{1,0:T(8,128)S(1)} %get-tuple-element.48._.refs_4_.rot, ...), custom_call_target="tpu_custom_call" | custom-call | flops 1000000000 | bytes 1048576 | tf_op jit(solution)/shard_map/pallas_call | solution.py:605
  26.1 0.1 collective-permute-done.9.x.refs_0_
  26.2 0.5 %collective-permute-start.13 = (f32[256,128]{1,0:T(8,128)S(1)}, f32[256,128]{1,0:T(8,128)S(1)}, u32[]{:S(2)}, u32[]{:S(2)}) collective-permute-start(f32[256,128]{1,0:T(8,128)S(1)} %shard_map.140), channel_id=1, source_target_pairs={{8,0},{12,4},{0,8},{4,12},{24,16},{28,20},{16,24},{20,28},{9,1},{1... | collective-permute-start | bytes 393224 | tf_op jit(solution)/shard_map/ppermute | solution.py:633
  26.8 1.8 %collective-permute-done.11.refs_2_ = f32[256,128]{1,0:T(8,128)S(1)} collective-permute-done((f32[256,128]{1,0:T(8,128)S(1)}, f32[256,128]{1,0:T(8,128)S(1)}, u32[]{:S(2)}, u32[]{:S(2)}) %collective-permute-start.11) | collective-permute-done | bytes 131104 | tf_op jit(solution)/shard_map/ppermute | solution.py:633
  28.6 3.2 %collective-permute-done.10.refs_1_ = f32[256,128]{1,0:T(8,128)S(1)} collective-permute-done((f32[256,128]{1,0:T(8,128)S(1)}, f32[256,128]{1,0:T(8,128)S(1)}, u32[]{:S(2)}, u32[]{:S(2)}) %collective-permute-start.10) | collective-permute-done | bytes 131104 | tf_op jit(solution)/shard_map/ppermute | solution.py:633
  31.9 0.7 %shard_map.141 = (bf16[512,256]{1,0:T(8,128)(2,1)S(1)}, bf16[512,256]{1,0:T(8,128)(2,1)S(1)}) custom-call(f32[512,256]{1,0:T(8,128)S(1)} %get-tuple-element.62.gat, bf16[384,256]{1,0:T(8,128)(2,1)S(1)} %get-tuple-element.45.gh, bf16[384,256]{1,0:T(8,128)(2,1)S(1)} %get-tuple-element.46.gl, f32[168,128]{1,0:T(8,128)S(1)} %get-tuple-element.55.col, ...), custom_call_target="tpu_custom_call" | custom-call | flops 1000000000 | bytes 1048576 | tf_op jit(solution)/shard_map/pallas_call | solution.py:605
  32.6 1.2 %shard_map.142 = f32[32,8,128]{2,1,0:T(8,128)S(1)} custom-call(f32[512,256]{1,0:T(8,128)S(1)} %get-tuple-element.61.loc, bf16[512,512]{1,0:T(8,128)(2,1)S(1)} %get-tuple-element.42.nh, bf16[512,512]{1,0:T(8,128)(2,1)S(1)} %get-tuple-element.43.nl, bf16[512,256]{1,0:T(8,128)(2,1)S(1)} %get-tuple-element.66.hi, bf16[512,256]{1,0:T(8,128)(2,1)S(1)} %get-tuple-element.67.lo, ...), custom_call_target="tpu_custom_call" | custom-call | flops 1000000000 | bytes 1048576 | tf_op jit(solution)/shard_map/pallas_call | solution.py:605
  33.8 12.3 %all_to_all.5.mine = f32[32,8,128]{2,1,0:T(8,128)S(1)} all-to-all(f32[32,8,128]{2,1,0:T(8,128)S(1)} %shard_map.142), channel_id=1, replica_groups=mesh['gx'=4,'gy'=2,'gz'=4] {'gx','gy','gz'}, dimensions={0} | all-to-all | bytes 262144 | tf_op jit(solution)/shard_map/all_to_all | solution.py:745
  46.1 0.1 collective-permute-start.14
  46.2 1.2 %collective-permute-done.14.other = f32[32,8,128]{2,1,0:T(8,128)S(1)} collective-permute-done((f32[32,8,128]{2,1,0:T(8,128)S(1)}, f32[32,8,128]{2,1,0:T(8,128)S(1)}, u32[]{:S(2)}, u32[]{:S(2)}) %collective-permute-start.14) | collective-permute-done | bytes 131104 | tf_op jit(solution)/shard_map/ppermute | solution.py:633
  47.5 4.4 %shard_map.143 = (f32[486,1,256]{2,1,0:T(1,128)}, f32[1,1]{1,0:T(1,128)}) custom-call(s32[2]{0:T(128)S(1)} %pad_add_fusion.ids, f32[512,256]{1,0:T(8,128)S(1)} %get-tuple-element.40.f_in, f32[512,256]{1,0:T(8,128)S(1)} %get-tuple-element.56.u_in, f32[32,8,128]{2,1,0:T(8,128)S(1)} %all_to_all.5.mine, f32[32,8,128]{2,1,0:T(8,128)S(1)} %collective-permute-done.14.other, ...), custom_call_target="tpu_custom_call" | custom-call | flops 10000000 | bytes 1048576 | tf_op jit(solution)/shard_map/pallas_call | solution.py:605
  (13 shorter events, 0.1 us)
Async XLA Ops:
  2.1 12.0 %collective-permute-start.3 = (f32[264,128]{1,0:T(8,128)S(1)}, f32[264,128]{1,0:T(8,128)S(1)}, u32[]{:S(2)}, u32[]{:S(2)}) collective-permute-start(f32[264,128]{1,0:T(8,128)S(1)} %get-tuple-element.47.refs_0_.message.charges_f), channel_id=1, source_target_pairs={{8,0},{12,4},{0,8},{4,12},{24,16},{28,20},{16,24},{20,28},{9,1},{1... | collective-permute-start | bytes 405512 | tf_op jit(solution)/shard_map/ppermute | solution.py:633
  2.6 10.9 %collective-permute-start.2 = (f32[264,128]{1,0:T(8,128)S(1)}, f32[264,128]{1,0:T(8,128)S(1)}, u32[]{:S(2)}, u32[]{:S(2)}) collective-permute-start(f32[264,128]{1,0:T(8,128)S(1)} %get-tuple-element.47.refs_0_.message.charges_f), channel_id=1, source_target_pairs={{28,0},{24,4},{20,8},{16,12},{12,16},{8,20},{4,24},{0,28},{29,1},{... | collective-permute-start | bytes 405512 | tf_op jit(solution)/shard_map/ppermute | solution.py:633
  6.2 7.4 %collective-permute-start.1 = (f32[264,128]{1,0:T(8,128)S(1)}, f32[264,128]{1,0:T(8,128)S(1)}, u32[]{:S(2)}, u32[]{:S(2)}) collective-permute-start(f32[264,128]{1,0:T(8,128)S(1)} %get-tuple-element.47.refs_0_.message.charges_f), channel_id=1, source_target_pairs={{24,0},{28,4},{16,8},{20,12},{8,16},{12,20},{0,24},{4,28},{25,1},{... | collective-permute-start | bytes 405512 | tf_op jit(solution)/shard_map/ppermute | solution.py:633
  6.3 7.1 %collective-permute-start = (f32[264,128]{1,0:T(8,128)S(1)}, f32[264,128]{1,0:T(8,128)S(1)}, u32[]{:S(2)}, u32[]{:S(2)}) collective-permute-start(f32[264,128]{1,0:T(8,128)S(1)} %get-tuple-element.47.refs_0_.message.charges_f), channel_id=1, source_target_pairs={{4,0},{0,4},{12,8},{8,12},{20,16},{16,20},{28,24},{24,28},{5,1},{1... | collective-permute-start | bytes 405512 | tf_op jit(solution)/shard_map/ppermute | solution.py:633
  13.4 1.5 %collective-permute-start.4 = (f32[264,128]{1,0:T(8,128)S(1)}, f32[264,128]{1,0:T(8,128)S(1)}, u32[]{:S(2)}, u32[]{:S(2)}) collective-permute-start(f32[264,128]{1,0:T(8,128)S(1)} %shard_map.133), channel_id=1, source_target_pairs={{8,0},{12,4},{0,8},{4,12},{24,16},{28,20},{16,24},{20,28},{9,1},{1... | collective-permute-start | bytes 405512 | tf_op jit(solution)/shard_map/ppermute | solution.py:633
  13.5 1.4 %collective-permute-start.5 = (f32[8,128]{1,0:T(8,128)S(1)}, f32[8,128]{1,0:T(8,128)S(1)}, u32[]{:S(2)}, u32[]{:S(2)}) collective-permute-start(f32[8,128]{1,0:T(8,128)S(1)} %shard_map.134.refs_0_), channel_id=1, source_target_pairs={{8,0},{12,4},{0,8},{4,12},{24,16},{28,20},{16,24},{20,28},{9,1},{1... | collective-permute-start | bytes 12296 | tf_op jit(solution)/shard_map/ppermute | solution.py:633
  14.9 7.4 %collective-permute-start.8 = (f32[7,8,128]{2,1,0:T(8,128)S(1)}, f32[7,8,128]{2,1,0:T(8,128)S(1)}, u32[]{:S(2)}, u32[]{:S(2)}) collective-permute-start(f32[7,8,128]{2,1,0:T(8,128)S(1)} %shard_map.135.refs_5_.refs_0_), channel_id=1, source_target_pairs={{3,0},{2,1},{1,2},{0,3},{7,4},{6,5},{5,6},{4,7},{11,8},{10,9},{9,1... | collective-permute-start | bytes 86024 | tf_op jit(solution)/shard_map/ppermute | solution.py:637
  18.6 4.9 %collective-permute-start.7 = (f32[7,8,128]{2,1,0:T(8,128)S(1)}, f32[7,8,128]{2,1,0:T(8,128)S(1)}, u32[]{:S(2)}, u32[]{:S(2)}) collective-permute-start(f32[7,8,128]{2,1,0:T(8,128)S(1)} %shard_map.135.refs_5_.refs_0_), channel_id=1, source_target_pairs={{2,0},{3,1},{0,2},{1,3},{6,4},{7,5},{4,6},{5,7},{10,8},{11,9},{8,1... | collective-permute-start | bytes 86024 | tf_op jit(solution)/shard_map/ppermute | solution.py:637
  18.6 5.4 %collective-permute-start.6 = (f32[7,8,128]{2,1,0:T(8,128)S(1)}, f32[7,8,128]{2,1,0:T(8,128)S(1)}, u32[]{:S(2)}, u32[]{:S(2)}) collective-permute-start(f32[7,8,128]{2,1,0:T(8,128)S(1)} %shard_map.135.refs_5_.refs_0_), channel_id=1, source_target_pairs={{1,0},{0,1},{3,2},{2,3},{5,4},{4,5},{7,6},{6,7},{9,8},{8,9},{11,10... | collective-permute-start | bytes 86024 | tf_op jit(solution)/shard_map/ppermute | solution.py:637
  20.7 5.5 %collective-permute-start.9 = (f32[256,128]{1,0:T(8,128)S(1)}, f32[256,128]{1,0:T(8,128)S(1)}, u32[]{:S(2)}, u32[]{:S(2)}) collective-permute-start(f32[256,128]{1,0:T(8,128)S(1)} %get-tuple-element.64), channel_id=1, source_target_pairs={{4,0},{0,4},{12,8},{8,12},{20,16},{16,20},{28,24},{24,28},{5,1},{1... | collective-permute-start | bytes 393224 | tf_op jit(solution)/shard_map/ppermute | solution.py:633
  22.3 4.5 %collective-permute-start.12 = (f32[256,128]{1,0:T(8,128)S(1)}, f32[256,128]{1,0:T(8,128)S(1)}, u32[]{:S(2)}, u32[]{:S(2)}) collective-permute-start(f32[256,128]{1,0:T(8,128)S(1)} %get-tuple-element.64), channel_id=1, source_target_pairs={{8,0},{12,4},{0,8},{4,12},{24,16},{28,20},{16,24},{20,28},{9,1},{1... | collective-permute-start | bytes 393224 | tf_op jit(solution)/shard_map/ppermute | solution.py:633
  22.3 6.3 %collective-permute-start.11 = (f32[256,128]{1,0:T(8,128)S(1)}, f32[256,128]{1,0:T(8,128)S(1)}, u32[]{:S(2)}, u32[]{:S(2)}) collective-permute-start(f32[256,128]{1,0:T(8,128)S(1)} %get-tuple-element.64), channel_id=1, source_target_pairs={{28,0},{24,4},{20,8},{16,12},{12,16},{8,20},{4,24},{0,28},{29,1},{... | collective-permute-start | bytes 393224 | tf_op jit(solution)/shard_map/ppermute | solution.py:633
  23.4 8.4 %collective-permute-start.10 = (f32[256,128]{1,0:T(8,128)S(1)}, f32[256,128]{1,0:T(8,128)S(1)}, u32[]{:S(2)}, u32[]{:S(2)}) collective-permute-start(f32[256,128]{1,0:T(8,128)S(1)} %get-tuple-element.64), channel_id=1, source_target_pairs={{24,0},{28,4},{16,8},{20,12},{8,16},{12,20},{0,24},{4,28},{25,1},{... | collective-permute-start | bytes 393224 | tf_op jit(solution)/shard_map/ppermute | solution.py:633
  26.2 5.6 %collective-permute-start.13 = (f32[256,128]{1,0:T(8,128)S(1)}, f32[256,128]{1,0:T(8,128)S(1)}, u32[]{:S(2)}, u32[]{:S(2)}) collective-permute-start(f32[256,128]{1,0:T(8,128)S(1)} %shard_map.140), channel_id=1, source_target_pairs={{8,0},{12,4},{0,8},{4,12},{24,16},{28,20},{16,24},{20,28},{9,1},{1... | collective-permute-start | bytes 393224 | tf_op jit(solution)/shard_map/ppermute | solution.py:633
  46.1 1.3 %collective-permute-start.14 = (f32[32,8,128]{2,1,0:T(8,128)S(1)}, f32[32,8,128]{2,1,0:T(8,128)S(1)}, u32[]{:S(2)}, u32[]{:S(2)}) collective-permute-start(f32[32,8,128]{2,1,0:T(8,128)S(1)} %all_to_all.5.mine), channel_id=1, source_target_pairs={{8,0},{12,4},{0,8},{4,12},{24,16},{28,20},{16,24},{20,28},{9,1},{1... | collective-permute-start | bytes 393224 | tf_op jit(solution)/shard_map/ppermute | solution.py:633

commit v12 on v11

--- a/solution.py
+++ b/solution.py
@@ -408,6 +408,7 @@
 
 def first_kernel(s, part, fh, fl, cells, col, *refs):
     *layers, u_out, charges_out, values_out = refs
+    layers = layers[: s.nz]
     weight_col = col[:, :1]
     occ = occupancy(cells[0], s)
     potentials = far_potentials(s, layers, (fh[...], fl[...]))
@@ -720,7 +721,7 @@
     u, charges, values = call(
         functools.partial(first_kernel, s),
         [(full, f32), (tile, f32), ((s.ghosts // LANES,) + tile, f32)],
-        [part, fh, fl, cells, col, *layers],
+        [part, fh, fl, cells, col, *layers] + [got[kind, dy] for kind in ("other", "same") for dy in s.shifts],
         flops=10**8,
     )
     loc, gat, ortho, stat = call(
@@ -729,7 +730,7 @@
         [u, f, rot, sh, sl, oh, ol],
         flops=10**9,
     )
-    forward_rims(got, stat)
+    forward_rims(got, charges)
     gathered = call(
         functools.partial(gather_far_kernel, s),
         [(full, bf16), (full, bf16)],

time: 52.1 us -> 50.4 us (0.967)
  blocking collectives: 12.3 us -> 10.3 us
  waiting for transfers between devices: 8.29 us -> 9.09 us
    ppermute x3, waiting for transfers between devices: 0.01 us -> 3.98 us  [fetch_layers(): lax.ppermute(x, 'gz', [(z ^ k, z) for z in range(s.nz)])]
    ppermute x12, waiting for transfers between devices: 8.28 us -> 5.11 us  [fetch(): return lax.ppermute(x, ('gx', 'gy'), pairs)]
    all_to_all x1, blocking collectives: 12.3 us -> 10.3 us  [body(): boxes = lax.all_to_all(packed, ('gx', 'gy', 'gz'), 0, 0)]
  transfers between devices with their start and end apart: 15 -> 15, of which waited for: 6 -> 6; matrix products, arithmetic and copies ran while one was open for 0% -> 0% of each run, Pallas kernels for 17% -> 15%
where the time goes in v12:
time: 50.4 us; the launch traced here: 50.2 us
  Pallas kernels  16.8 us (33%)
  starting transfers between devices  13.1 us (26%)
  blocking collectives  10.3 us (20%)
  waiting for transfers between devices  9.09 us (18%)
  between operations  0.76 us (2%)
    pallas_call x13, Pallas kernels, call(): pl.pallas_call(kernel, out_shape=[jax.ShapeDtypeStruct(shape, kind) for s...  16.8 us
    all_to_all x1, blocking collectives, body(): boxes = lax.all_to_all(packed, ('gx', 'gy', 'gz'), 0, 0)  10.3 us
    ppermute x12, starting transfers between devices, fetch(): return lax.ppermute(x, ('gx', 'gy'), pairs)  8.76 us
    ppermute x12, waiting for transfers between devices, fetch(): return lax.ppermute(x, ('gx', 'gy'), pairs)  5.11 us
    ppermute x3, starting transfers between devices, fetch_layers(): lax.ppermute(x, 'gz', [(z ^ k, z) for z in range(s.nz)])  4.39 us
    ppermute x3, waiting for transfers between devices, fetch_layers(): lax.ppermute(x, 'gz', [(z ^ k, z) for z in range(s.nz)])  3.98 us
  transfers between devices with their start and end apart: 15, of which 6 were waited for; matrix products, arithmetic and copies ran while one was open for 0% of the time, Pallas kernels for 15%

profile of v12, /device:TPU:0, one launch (start us, length us, event | category | flops | bytes accessed | tf_op | source)
XLA Modules:
  0.0 50.2 jit_solution(5793121432660144589)
XLA Ops:
  0.6 1.4 %shard_map.131 = (f32[264,128]{1,0:T(8,128)S(1)}, f32[168,128]{1,0:T(8,128)S(1)}, s32[1,1,256]{2,1,0:T(1,128)S(1)}, f32[512,256]{1,0:T(8,128)S(1)}) custom-call(f32[486,1,256]{2,1,0:T(1,128)} %bitcast.9, s32[1,1,256]{2,1,0:T(1,128)} %cells.1, f32[1,162]{1,0:T(1,128)} %bitcast.10), custom_call_target="tpu_custom_call" | custom-call | flops 10000000 | bytes 1048576 | tf_op jit(solution)/shard_map/pallas_call | solution.py:606
  2.1 0.5 %collective-permute-start.3 = (f32[264,128]{1,0:T(8,128)S(1)}, f32[264,128]{1,0:T(8,128)S(1)}, u32[]{:S(2)}, u32[]{:S(2)}) collective-permute-start(f32[264,128]{1,0:T(8,128)S(1)} %get-tuple-element.47.refs_0_.message.charges_f), channel_id=1, source_target_pairs={{8,0},{12,4},{0,8},{4,12},{24,16},{28,20},{16,24},{20,28},{9,1},{1... | collective-permute-start | bytes 405512 | tf_op jit(solution)/shard_map/ppermute | solution.py:634
  2.6 3.6 %collective-permute-start.2 = (f32[264,128]{1,0:T(8,128)S(1)}, f32[264,128]{1,0:T(8,128)S(1)}, u32[]{:S(2)}, u32[]{:S(2)}) collective-permute-start(f32[264,128]{1,0:T(8,128)S(1)} %get-tuple-element.47.refs_0_.message.charges_f), channel_id=1, source_target_pairs={{28,0},{24,4},{20,8},{16,12},{12,16},{8,20},{4,24},{0,28},{29,1},{... | collective-permute-start | bytes 405512 | tf_op jit(solution)/shard_map/ppermute | solution.py:634
  6.2 0.2 collective-permute-start.1
  6.3 0.4 collective-permute-start
  6.7 0.1 pad_add_fusion.ids
  6.8 5.6 %shard_map.132 = (f32[512,256]{1,0:T(8,128)S(1)}, f32[512,256]{1,0:T(8,128)S(1)}, f32[16,256]{1,0:T(8,128)S(1)}, bf16[512,512]{1,0:T(8,128)(2,1)S(1)}, bf16[512,...) custom-call(s32[2]{0:T(128)S(1)} %pad_add_fusion.ids, ...), custom_call_target="tpu_custom_call" | custom-call | flops 5000000000 | bytes 1048576 | tf_op jit(solution)/shard_map/pallas_call | solution.py:606
  12.4 1.0 %collective-permute-done.x.refs_1_.refs_2_.refs_0_ = f32[264,128]{1,0:T(8,128)S(1)} collective-permute-done((f32[264,128]{1,0:T(8,128)S(1)}, f32[264,128]{1,0:T(8,128)S(1)}, u32[]{:S(2)}, u32[]{:S(2)}) %collective-permute-start) | collective-permute-done | bytes 135200 | tf_op jit(solution)/shard_map/ppermute | solution.py:634
  13.4 0.1 collective-permute-start.4
  13.5 0.0 collective-permute-done.2.refs_3_.refs_4_.refs_2_
  13.5 0.5 %collective-permute-start.5 = (f32[8,128]{1,0:T(8,128)S(1)}, f32[8,128]{1,0:T(8,128)S(1)}, u32[]{:S(2)}, u32[]{:S(2)}) collective-permute-start(f32[8,128]{1,0:T(8,128)S(1)} %shard_map.134.refs_0_), channel_id=1, source_target_pairs={{8,0},{12,4},{0,8},{4,12},{24,16},{28,20},{16,24},{20,28},{9,1},{1... | collective-permute-start | bytes 12296 | tf_op jit(solution)/shard_map/ppermute | solution.py:634
  14.1 0.0 collective-permute-done.3.refs_5_.refs_3_
  14.1 0.8 %collective-permute-done.5.refs_1_ = f32[8,128]{1,0:T(8,128)S(1)} collective-permute-done((f32[8,128]{1,0:T(8,128)S(1)}, f32[8,128]{1,0:T(8,128)S(1)}, u32[]{:S(2)}, u32[]{:S(2)}) %collective-permute-start.5) | collective-permute-done | bytes 4128 | tf_op jit(solution)/shard_map/ppermute | solution.py:634
  14.9 0.7 %shard_map.136 = (bf16[512,256]{1,0:T(8,128)(2,1)S(1)}, bf16[512,256]{1,0:T(8,128)(2,1)S(1)}) custom-call(f32[512,256]{1,0:T(8,128)S(1)} %get-tuple-element.44.gat, bf16[384,256]{1,0:T(8,128)(2,1)S(1)} %get-tuple-element.45.gh, bf16[384,256]{1,0:T(8,128)(2,1)S(1)} %get-tuple-element.46.gl, f32[264,128]{1,0:T(8,128)S(1)} %collective-permute-done.x.refs_1_.refs_2_.refs_0_, ...), custom_call_target="tpu_custom_call" | custom-call | flops 1000000000 | bytes 1048576 | tf_op jit(solution)/shard_map/pallas_call | solution.py:606
  15.6 0.6 %shard_map.137 = (f32[512,256]{1,0:T(8,128)S(1)}, f32[256,128]{1,0:T(8,128)S(1)}) custom-call(f32[512,256]{1,0:T(8,128)S(1)} %get-tuple-element.41.loc, bf16[512,512]{1,0:T(8,128)(2,1)S(1)} %get-tuple-element.42.nh, bf16[512,512]{1,0:T(8,128)(2,1)S(1)} %get-tuple-element.43.nl, bf16[512,256]{1,0:T(8,128)(2,1)S(1)} %get-tuple-element.49.hi, ...), custom_call_target="tpu_custom_call" | custom-call | flops 1000000000 | bytes 1048576 | tf_op jit(solution)/shard_map/pallas_call | solution.py:606
  16.3 1.6 %collective-permute-start.10 = (f32[256,128]{1,0:T(8,128)S(1)}, f32[256,128]{1,0:T(8,128)S(1)}, u32[]{:S(2)}, u32[]{:S(2)}) collective-permute-start(f32[256,128]{1,0:T(8,128)S(1)} %get-tuple-element.56), channel_id=1, source_target_pairs={{4,0},{0,4},{12,8},{8,12},{20,16},{16,20},{28,24},{24,28},{5,1},{1... | collective-permute-start | bytes 393224 | tf_op jit(solution)/shard_map/ppermute | solution.py:634
  17.8 0.5 %collective-permute-start.9 = (f32[256,128]{1,0:T(8,128)S(1)}, f32[256,128]{1,0:T(8,128)S(1)}, u32[]{:S(2)}, u32[]{:S(2)}) collective-permute-start(f32[256,128]{1,0:T(8,128)S(1)} %get-tuple-element.56), channel_id=1, source_target_pairs={{28,0},{24,4},{20,8},{16,12},{12,16},{8,20},{4,24},{0,28},{29,1},{... | collective-permute-start | bytes 393224 | tf_op jit(solution)/shard_map/ppermute | solution.py:634
  18.4 3.6 %collective-permute-start.8 = (f32[7,8,128]{2,1,0:T(8,128)S(1)}, f32[7,8,128]{2,1,0:T(8,128)S(1)}, u32[]{:S(2)}, u32[]{:S(2)}) collective-permute-start(f32[7,8,128]{2,1,0:T(8,128)S(1)} %shard_map.135.refs_5_.refs_0_), channel_id=1, source_target_pairs={{3,0},{2,1},{1,2},{0,3},{7,4},{6,5},{5,6},{4,7},{11,8},{10,9},{9,1... | collective-permute-start | bytes 86024 | tf_op jit(solution)/shard_map/ppermute | solution.py:638
  22.0 0.0 collective-permute-start.7
  22.0 0.8 %collective-permute-start.6 = (f32[7,8,128]{2,1,0:T(8,128)S(1)}, f32[7,8,128]{2,1,0:T(8,128)S(1)}, u32[]{:S(2)}, u32[]{:S(2)}) collective-permute-start(f32[7,8,128]{2,1,0:T(8,128)S(1)} %shard_map.135.refs_5_.refs_0_), channel_id=1, source_target_pairs={{1,0},{0,1},{3,2},{2,3},{5,4},{4,5},{7,6},{6,7},{9,8},{8,9},{11,10... | collective-permute-start | bytes 86024 | tf_op jit(solution)/shard_map/ppermute | solution.py:638
  22.8 1.3 %collective-permute-done.8.refs_3_ = f32[7,8,128]{2,1,0:T(8,128)S(1)} collective-permute-done((f32[7,8,128]{2,1,0:T(8,128)S(1)}, f32[7,8,128]{2,1,0:T(8,128)S(1)}, u32[]{:S(2)}, u32[]{:S(2)}) %collective-permute-start.8) | collective-permute-done | bytes 28704 | tf_op jit(solution)/shard_map/ppermute | solution.py:638
  24.1 2.7 %collective-permute-done.7.refs_2_ = f32[7,8,128]{2,1,0:T(8,128)S(1)} collective-permute-done((f32[7,8,128]{2,1,0:T(8,128)S(1)}, f32[7,8,128]{2,1,0:T(8,128)S(1)}, u32[]{:S(2)}, u32[]{:S(2)}) %collective-permute-start.7) | collective-permute-done | bytes 28704 | tf_op jit(solution)/shard_map/ppermute | solution.py:638
  26.8 1.0 %shard_map.138 = (f32[512,256]{1,0:T(8,128)S(1)}, f32[8,128]{1,0:T(8,128)S(1)}, f32[3,8,128]{2,1,0:T(8,128)S(1)}) custom-call(f32[512,256]{1,0:T(8,128)S(1)} %get-tuple-element.51.part, bf16[192,1536]{1,0:T(8,128)(2,1)S(1)} %get-tuple-element.52.fh, bf16[192,1536]{1,0:T(8,128)(2,1)S(1)} %get-tuple-element.53.fl, s32[1,1,256]{2,1,0:T(1,128)S(1)} %get-tuple-element.54.cells, ...), custom_call_target="tpu_custom_call" | custom-call | flops 100000000 | bytes 1048576 | tf_op jit(solution)/shard_map/pallas_call | solution.py:606
  27.8 1.3 %collective-permute-start.13 = (f32[256,128]{1,0:T(8,128)S(1)}, f32[256,128]{1,0:T(8,128)S(1)}, u32[]{:S(2)}, u32[]{:S(2)}) collective-permute-start(f32[256,128]{1,0:T(8,128)S(1)} %shard_map.140), channel_id=1, source_target_pairs={{8,0},{12,4},{0,8},{4,12},{24,16},{28,20},{16,24},{20,28},{9,1},{1... | collective-permute-start | bytes 393224 | tf_op jit(solution)/shard_map/ppermute | solution.py:634
  29.1 1.0 %shard_map.139 = (f32[512,256]{1,0:T(8,128)S(1)}, f32[512,256]{1,0:T(8,128)S(1)}, f32[512,256]{1,0:T(8,128)S(1)}, f32[8,128]{1,0:T(8,128)S(1)}) custom-call(f32[512,256]{1,0:T(8,128)S(1)} %get-tuple-element.57.u_in, f32[512,256]{1,0:T(8,128)S(1)} %get-tuple-element.40.f_in, f32[16,256]{1,0:T(8,128)S(1)} %get-tuple-element.48._.refs_4_.rot, ...), custom_call_target="tpu_custom_call" | custom-call | flops 1000000000 | bytes 1048576 | tf_op jit(solution)/shard_map/pallas_call | solution.py:606
  30.2 2.0 %collective-permute-done.11.refs_1_ = f32[256,128]{1,0:T(8,128)S(1)} collective-permute-done((f32[256,128]{1,0:T(8,128)S(1)}, f32[256,128]{1,0:T(8,128)S(1)}, u32[]{:S(2)}, u32[]{:S(2)}) %collective-permute-start.11) | collective-permute-done | bytes 131104 | tf_op jit(solution)/shard_map/ppermute | solution.py:634
  32.2 0.7 %shard_map.141 = (bf16[512,256]{1,0:T(8,128)(2,1)S(1)}, bf16[512,256]{1,0:T(8,128)(2,1)S(1)}) custom-call(f32[512,256]{1,0:T(8,128)S(1)} %get-tuple-element.63.gat, bf16[384,256]{1,0:T(8,128)(2,1)S(1)} %get-tuple-element.45.gh, bf16[384,256]{1,0:T(8,128)(2,1)S(1)} %get-tuple-element.46.gl, f32[168,128]{1,0:T(8,128)S(1)} %get-tuple-element.55.col, ...), custom_call_target="tpu_custom_call" | custom-call | flops 1000000000 | bytes 1048576 | tf_op jit(solution)/shard_map/pallas_call | solution.py:606
  32.9 1.3 %shard_map.142 = f32[32,8,128]{2,1,0:T(8,128)S(1)} custom-call(f32[512,256]{1,0:T(8,128)S(1)} %get-tuple-element.62.loc, bf16[512,512]{1,0:T(8,128)(2,1)S(1)} %get-tuple-element.42.nh, bf16[512,512]{1,0:T(8,128)(2,1)S(1)} %get-tuple-element.43.nl, bf16[512,256]{1,0:T(8,128)(2,1)S(1)} %get-tuple-element.66.hi, bf16[512,256]{1,0:T(8,128)(2,1)S(1)} %get-tuple-element.67.lo, ...), custom_call_target="tpu_custom_call" | custom-call | flops 1000000000 | bytes 1048576 | tf_op jit(solution)/shard_map/pallas_call | solution.py:606
  34.2 10.3 %all_to_all.5.mine = f32[32,8,128]{2,1,0:T(8,128)S(1)} all-to-all(f32[32,8,128]{2,1,0:T(8,128)S(1)} %shard_map.142), channel_id=1, replica_groups=mesh['gx'=4,'gy'=2,'gz'=4] {'gx','gy','gz'}, dimensions={0} | all-to-all | bytes 262144 | tf_op jit(solution)/shard_map/all_to_all | solution.py:746
  44.5 0.1 collective-permute-start.14
  44.6 1.2 %collective-permute-done.14.other = f32[32,8,128]{2,1,0:T(8,128)S(1)} collective-permute-done((f32[32,8,128]{2,1,0:T(8,128)S(1)}, f32[32,8,128]{2,1,0:T(8,128)S(1)}, u32[]{:S(2)}, u32[]{:S(2)}) %collective-permute-start.14) | collective-permute-done | bytes 131104 | tf_op jit(solution)/shard_map/ppermute | solution.py:634
  45.8 4.4 %shard_map.143 = (f32[486,1,256]{2,1,0:T(1,128)}, f32[1,1]{1,0:T(1,128)}) custom-call(s32[2]{0:T(128)S(1)} %pad_add_fusion.ids, f32[512,256]{1,0:T(8,128)S(1)} %get-tuple-element.40.f_in, f32[512,256]{1,0:T(8,128)S(1)} %get-tuple-element.57.u_in, f32[32,8,128]{2,1,0:T(8,128)S(1)} %all_to_all.5.mine, f32[32,8,128]{2,1,0:T(8,128)S(1)} %collective-permute-done.14.other, ...), custom_call_target="tpu_custom_call" | custom-call | flops 10000000 | bytes 1048576 | tf_op jit(solution)/shard_map/pallas_call | solution.py:606
  (13 shorter events, 0.1 us)
Async XLA Ops:
  2.1 12.0 %collective-permute-start.3 = (f32[264,128]{1,0:T(8,128)S(1)}, f32[264,128]{1,0:T(8,128)S(1)}, u32[]{:S(2)}, u32[]{:S(2)}) collective-permute-start(f32[264,128]{1,0:T(8,128)S(1)} %get-tuple-element.47.refs_0_.message.charges_f), channel_id=1, source_target_pairs={{8,0},{12,4},{0,8},{4,12},{24,16},{28,20},{16,24},{20,28},{9,1},{1... | collective-permute-start | bytes 405512 | tf_op jit(solution)/shard_map/ppermute | solution.py:634
  2.6 10.9 %collective-permute-start.2 = (f32[264,128]{1,0:T(8,128)S(1)}, f32[264,128]{1,0:T(8,128)S(1)}, u32[]{:S(2)}, u32[]{:S(2)}) collective-permute-start(f32[264,128]{1,0:T(8,128)S(1)} %get-tuple-element.47.refs_0_.message.charges_f), channel_id=1, source_target_pairs={{28,0},{24,4},{20,8},{16,12},{12,16},{8,20},{4,24},{0,28},{29,1},{... | collective-permute-start | bytes 405512 | tf_op jit(solution)/shard_map/ppermute | solution.py:634
  6.2 7.4 %collective-permute-start.1 = (f32[264,128]{1,0:T(8,128)S(1)}, f32[264,128]{1,0:T(8,128)S(1)}, u32[]{:S(2)}, u32[]{:S(2)}) collective-permute-start(f32[264,128]{1,0:T(8,128)S(1)} %get-tuple-element.47.refs_0_.message.charges_f), channel_id=1, source_target_pairs={{24,0},{28,4},{16,8},{20,12},{8,16},{12,20},{0,24},{4,28},{25,1},{... | collective-permute-start | bytes 405512 | tf_op jit(solution)/shard_map/ppermute | solution.py:634
  6.3 7.1 %collective-permute-start = (f32[264,128]{1,0:T(8,128)S(1)}, f32[264,128]{1,0:T(8,128)S(1)}, u32[]{:S(2)}, u32[]{:S(2)}) collective-permute-start(f32[264,128]{1,0:T(8,128)S(1)} %get-tuple-element.47.refs_0_.message.charges_f), channel_id=1, source_target_pairs={{4,0},{0,4},{12,8},{8,12},{20,16},{16,20},{28,24},{24,28},{5,1},{1... | collective-permute-start | bytes 405512 | tf_op jit(solution)/shard_map/ppermute | solution.py:634
  13.4 1.5 %collective-permute-start.4 = (f32[264,128]{1,0:T(8,128)S(1)}, f32[264,128]{1,0:T(8,128)S(1)}, u32[]{:S(2)}, u32[]{:S(2)}) collective-permute-start(f32[264,128]{1,0:T(8,128)S(1)} %shard_map.133), channel_id=1, source_target_pairs={{8,0},{12,4},{0,8},{4,12},{24,16},{28,20},{16,24},{20,28},{9,1},{1... | collective-permute-start | bytes 405512 | tf_op jit(solution)/shard_map/ppermute | solution.py:634
  13.5 1.4 %collective-permute-start.5 = (f32[8,128]{1,0:T(8,128)S(1)}, f32[8,128]{1,0:T(8,128)S(1)}, u32[]{:S(2)}, u32[]{:S(2)}) collective-permute-start(f32[8,128]{1,0:T(8,128)S(1)} %shard_map.134.refs_0_), channel_id=1, source_target_pairs={{8,0},{12,4},{0,8},{4,12},{24,16},{28,20},{16,24},{20,28},{9,1},{1... | collective-permute-start | bytes 12296 | tf_op jit(solution)/shard_map/ppermute | solution.py:634
  16.3 10.5 %collective-permute-start.10 = (f32[256,128]{1,0:T(8,128)S(1)}, f32[256,128]{1,0:T(8,128)S(1)}, u32[]{:S(2)}, u32[]{:S(2)}) collective-permute-start(f32[256,128]{1,0:T(8,128)S(1)} %get-tuple-element.56), channel_id=1, source_target_pairs={{4,0},{0,4},{12,8},{8,12},{20,16},{16,20},{28,24},{24,28},{5,1},{1... | collective-permute-start | bytes 393224 | tf_op jit(solution)/shard_map/ppermute | solution.py:634
  17.8 8.9 %collective-permute-start.9 = (f32[256,128]{1,0:T(8,128)S(1)}, f32[256,128]{1,0:T(8,128)S(1)}, u32[]{:S(2)}, u32[]{:S(2)}) collective-permute-start(f32[256,128]{1,0:T(8,128)S(1)} %get-tuple-element.56), channel_id=1, source_target_pairs={{28,0},{24,4},{20,8},{16,12},{12,16},{8,20},{4,24},{0,28},{29,1},{... | collective-permute-start | bytes 393224 | tf_op jit(solution)/shard_map/ppermute | solution.py:634
  18.4 5.7 %collective-permute-start.8 = (f32[7,8,128]{2,1,0:T(8,128)S(1)}, f32[7,8,128]{2,1,0:T(8,128)S(1)}, u32[]{:S(2)}, u32[]{:S(2)}) collective-permute-start(f32[7,8,128]{2,1,0:T(8,128)S(1)} %shard_map.135.refs_5_.refs_0_), channel_id=1, source_target_pairs={{3,0},{2,1},{1,2},{0,3},{7,4},{6,5},{5,6},{4,7},{11,8},{10,9},{9,1... | collective-permute-start | bytes 86024 | tf_op jit(solution)/shard_map/ppermute | solution.py:638
  22.0 4.8 %collective-permute-start.7 = (f32[7,8,128]{2,1,0:T(8,128)S(1)}, f32[7,8,128]{2,1,0:T(8,128)S(1)}, u32[]{:S(2)}, u32[]{:S(2)}) collective-permute-start(f32[7,8,128]{2,1,0:T(8,128)S(1)} %shard_map.135.refs_5_.refs_0_), channel_id=1, source_target_pairs={{2,0},{3,1},{0,2},{1,3},{6,4},{7,5},{4,6},{5,7},{10,8},{11,9},{8,1... | collective-permute-start | bytes 86024 | tf_op jit(solution)/shard_map/ppermute | solution.py:638
  22.0 4.8 %collective-permute-start.6 = (f32[7,8,128]{2,1,0:T(8,128)S(1)}, f32[7,8,128]{2,1,0:T(8,128)S(1)}, u32[]{:S(2)}, u32[]{:S(2)}) collective-permute-start(f32[7,8,128]{2,1,0:T(8,128)S(1)} %shard_map.135.refs_5_.refs_0_), channel_id=1, source_target_pairs={{1,0},{0,1},{3,2},{2,3},{5,4},{4,5},{7,6},{6,7},{9,8},{8,9},{11,10... | collective-permute-start | bytes 86024 | tf_op jit(solution)/shard_map/ppermute | solution.py:638
  24.1 6.1 %collective-permute-start.12 = (f32[256,128]{1,0:T(8,128)S(1)}, f32[256,128]{1,0:T(8,128)S(1)}, u32[]{:S(2)}, u32[]{:S(2)}) collective-permute-start(f32[256,128]{1,0:T(8,128)S(1)} %get-tuple-element.56), channel_id=1, source_target_pairs={{8,0},{12,4},{0,8},{4,12},{24,16},{28,20},{16,24},{20,28},{9,1},{1... | collective-permute-start | bytes 393224 | tf_op jit(solution)/shard_map/ppermute | solution.py:634
  26.7 5.5 %collective-permute-start.11 = (f32[256,128]{1,0:T(8,128)S(1)}, f32[256,128]{1,0:T(8,128)S(1)}, u32[]{:S(2)}, u32[]{:S(2)}) collective-permute-start(f32[256,128]{1,0:T(8,128)S(1)} %get-tuple-element.56), channel_id=1, source_target_pairs={{24,0},{28,4},{16,8},{20,12},{8,16},{12,20},{0,24},{4,28},{25,1},{... | collective-permute-start | bytes 393224 | tf_op jit(solution)/shard_map/ppermute | solution.py:634
  27.8 4.4 %collective-permute-start.13 = (f32[256,128]{1,0:T(8,128)S(1)}, f32[256,128]{1,0:T(8,128)S(1)}, u32[]{:S(2)}, u32[]{:S(2)}) collective-permute-start(f32[256,128]{1,0:T(8,128)S(1)} %shard_map.140), channel_id=1, source_target_pairs={{8,0},{12,4},{0,8},{4,12},{24,16},{28,20},{16,24},{20,28},{9,1},{1... | collective-permute-start | bytes 393224 | tf_op jit(solution)/shard_map/ppermute | solution.py:634
  44.5 1.3 %collective-permute-start.14 = (f32[32,8,128]{2,1,0:T(8,128)S(1)}, f32[32,8,128]{2,1,0:T(8,128)S(1)}, u32[]{:S(2)}, u32[]{:S(2)}) collective-permute-start(f32[32,8,128]{2,1,0:T(8,128)S(1)} %all_to_all.5.mine), channel_id=1, source_target_pairs={{8,0},{12,4},{0,8},{4,12},{24,16},{28,20},{16,24},{20,28},{9,1},{1... | collective-permute-start | bytes 393224 | tf_op jit(solution)/shard_map/ppermute | solution.py:634

commit v13 on v12

--- a/solution.py
+++ b/solution.py
@@ -718,10 +718,11 @@
         flops=10**9,
     )
     got = fetch_rims(rim)
+    ahead = [got["other", 0]] + [got[kind, dy] for kind in ("other", "same") for dy in s.shifts]
     u, charges, values = call(
         functools.partial(first_kernel, s),
         [(full, f32), (tile, f32), ((s.ghosts // LANES,) + tile, f32)],
-        [part, fh, fl, cells, col, *layers] + [got[kind, dy] for kind in ("other", "same") for dy in s.shifts],
+        [part, fh, fl, cells, col, *layers] + ahead,
         flops=10**8,
     )
     loc, gat, ortho, stat = call(

time: 50.4 us -> 52.1 us (1.034)
  blocking collectives: 10.3 us -> 12.6 us
  starting transfers between devices: 13.1 us -> 12.3 us
    all_to_all x1, blocking collectives: 10.3 us -> 12.6 us  [body(): boxes = lax.all_to_all(packed, ('gx', 'gy', 'gz'), 0, 0)]
    ppermute x3, waiting for transfers between devices: 3.98 us -> 5.91 us  [fetch_layers(): lax.ppermute(x, 'gz', [(z ^ k, z) for z in range(s.nz)])]
    ppermute x12, waiting for transfers between devices: 5.11 us -> 3.31 us  [fetch(): return lax.ppermute(x, ('gx', 'gy'), pairs)]
    ppermute x3, starting transfers between devices: 4.39 us -> 3.62 us  [fetch_layers(): lax.ppermute(x, 'gz', [(z ^ k, z) for z in range(s.nz)])]
  transfers between devices with their start and end apart: 15 -> 15, of which waited for: 6 -> 7; matrix products, arithmetic and copies ran while one was open for 0% -> 0% of each run, Pallas kernels for 15% -> 15%
where the time goes in v13:
time: 52.1 us; the launch traced here: 51.8 us
  Pallas kernels  16.9 us (32%)
  blocking collectives  12.6 us (24%)
  starting transfers between devices  12.3 us (24%)
  waiting for transfers between devices  9.23 us (18%)
  between operations  0.76 us (1%)
    pallas_call x13, Pallas kernels, call(): pl.pallas_call(kernel, out_shape=[jax.ShapeDtypeStruct(shape, kind) for s...  16.9 us
    all_to_all x1, blocking collectives, body(): boxes = lax.all_to_all(packed, ('gx', 'gy', 'gz'), 0, 0)  12.6 us
    ppermute x12, starting transfers between devices, fetch(): return lax.ppermute(x, ('gx', 'gy'), pairs)  8.7 us
    ppermute x3, waiting for transfers between devices, fetch_layers(): lax.ppermute(x, 'gz', [(z ^ k, z) for z in range(s.nz)])  5.91 us
    ppermute x3, starting transfers between devices, fetch_layers(): lax.ppermute(x, 'gz', [(z ^ k, z) for z in range(s.nz)])  3.62 us
    ppermute x12, waiting for transfers between devices, fetch(): return lax.ppermute(x, ('gx', 'gy'), pairs)  3.31 us
  transfers between devices with their start and end apart: 15, of which 7 were waited for; matrix products, arithmetic and copies ran while one was open for 0% of the time, Pallas kernels for 15%

profile of v13, /device:TPU:0, one launch (start us, length us, event | category | flops | bytes accessed | tf_op | source)
XLA Modules:
  0.0 51.8 jit_solution(11305647628670247245)
XLA Ops:
  0.6 1.4 %shard_map.131 = (f32[264,128]{1,0:T(8,128)S(1)}, f32[168,128]{1,0:T(8,128)S(1)}, s32[1,1,256]{2,1,0:T(1,128)S(1)}, f32[512,256]{1,0:T(8,128)S(1)}) custom-call(f32[486,1,256]{2,1,0:T(1,128)} %bitcast.9, s32[1,1,256]{2,1,0:T(1,128)} %cells.1, f32[1,162]{1,0:T(1,128)} %bitcast.10), custom_call_target="tpu_custom_call" | custom-call | flops 10000000 | bytes 1048576 | tf_op jit(solution)/shard_map/pallas_call | solution.py:606
  2.1 0.5 collective-permute-start.3
  2.6 3.6 %collective-permute-start.2 = (f32[264,128]{1,0:T(8,128)S(1)}, f32[264,128]{1,0:T(8,128)S(1)}, u32[]{:S(2)}, u32[]{:S(2)}) collective-permute-start(f32[264,128]{1,0:T(8,128)S(1)} %get-tuple-element.47.refs_0_.message.charges_f), channel_id=1, source_target_pairs={{28,0},{24,4},{20,8},{16,12},{12,16},{8,20},{4,24},{0,28},{29,1},{... | collective-permute-start | bytes 405512 | tf_op jit(solution)/shard_map/ppermute | solution.py:634
  6.2 0.2 collective-permute-start.1
  6.3 0.4 collective-permute-start
  6.7 0.1 pad_add_fusion.ids
  6.8 5.7 %shard_map.132 = (f32[512,256]{1,0:T(8,128)S(1)}, f32[512,256]{1,0:T(8,128)S(1)}, f32[16,256]{1,0:T(8,128)S(1)}, bf16[512,512]{1,0:T(8,128)(2,1)S(1)}, bf16[512,...) custom-call(s32[2]{0:T(128)S(1)} %pad_add_fusion.ids, ...), custom_call_target="tpu_custom_call" | custom-call | flops 5000000000 | bytes 1048576 | tf_op jit(solution)/shard_map/pallas_call | solution.py:606
  12.4 1.0 %collective-permute-done.x.refs_1_.refs_2_.refs_0_ = f32[264,128]{1,0:T(8,128)S(1)} collective-permute-done((f32[264,128]{1,0:T(8,128)S(1)}, f32[264,128]{1,0:T(8,128)S(1)}, u32[]{:S(2)}, u32[]{:S(2)}) %collective-permute-start) | collective-permute-done | bytes 135200 | tf_op jit(solution)/shard_map/ppermute | solution.py:634
  13.4 0.1 collective-permute-start.4
  13.5 0.0 collective-permute-done.2.refs_3_.refs_4_.refs_2_
  13.5 0.5 %collective-permute-start.5 = (f32[8,128]{1,0:T(8,128)S(1)}, f32[8,128]{1,0:T(8,128)S(1)}, u32[]{:S(2)}, u32[]{:S(2)}) collective-permute-start(f32[8,128]{1,0:T(8,128)S(1)} %shard_map.134.refs_0_), channel_id=1, source_target_pairs={{8,0},{12,4},{0,8},{4,12},{24,16},{28,20},{16,24},{20,28},{9,1},{1... | collective-permute-start | bytes 12296 | tf_op jit(solution)/shard_map/ppermute | solution.py:634
  14.1 0.8 %collective-permute-done.5.refs_1_ = f32[8,128]{1,0:T(8,128)S(1)} collective-permute-done((f32[8,128]{1,0:T(8,128)S(1)}, f32[8,128]{1,0:T(8,128)S(1)}, u32[]{:S(2)}, u32[]{:S(2)}) %collective-permute-start.5) | collective-permute-done | bytes 4128 | tf_op jit(solution)/shard_map/ppermute | solution.py:634
  14.9 0.7 %shard_map.136 = (bf16[512,256]{1,0:T(8,128)(2,1)S(1)}, bf16[512,256]{1,0:T(8,128)(2,1)S(1)}) custom-call(f32[512,256]{1,0:T(8,128)S(1)} %get-tuple-element.44.gat, bf16[384,256]{1,0:T(8,128)(2,1)S(1)} %get-tuple-element.45.gh, bf16[384,256]{1,0:T(8,128)(2,1)S(1)} %get-tuple-element.46.gl, f32[264,128]{1,0:T(8,128)S(1)} %collective-permute-done.x.refs_1_.refs_2_.refs_0_, ...), custom_call_target="tpu_custom_call" | custom-call | flops 1000000000 | bytes 1048576 | tf_op jit(solution)/shard_map/pallas_call | solution.py:606
  15.6 0.6 %shard_map.137 = (f32[512,256]{1,0:T(8,128)S(1)}, f32[256,128]{1,0:T(8,128)S(1)}) custom-call(f32[512,256]{1,0:T(8,128)S(1)} %get-tuple-element.41.loc, bf16[512,512]{1,0:T(8,128)(2,1)S(1)} %get-tuple-element.42.nh, bf16[512,512]{1,0:T(8,128)(2,1)S(1)} %get-tuple-element.43.nl, bf16[512,256]{1,0:T(8,128)(2,1)S(1)} %get-tuple-element.49.hi, ...), custom_call_target="tpu_custom_call" | custom-call | flops 1000000000 | bytes 1048576 | tf_op jit(solution)/shard_map/pallas_call | solution.py:606
  16.3 1.6 %collective-permute-start.11 = (f32[256,128]{1,0:T(8,128)S(1)}, f32[256,128]{1,0:T(8,128)S(1)}, u32[]{:S(2)}, u32[]{:S(2)}) collective-permute-start(f32[256,128]{1,0:T(8,128)S(1)} %get-tuple-element.56), channel_id=1, source_target_pairs={{4,0},{0,4},{12,8},{8,12},{20,16},{16,20},{28,24},{24,28},{5,1},{1... | collective-permute-start | bytes 393224 | tf_op jit(solution)/shard_map/ppermute | solution.py:634
  17.8 0.5 %collective-permute-start.10 = (f32[256,128]{1,0:T(8,128)S(1)}, f32[256,128]{1,0:T(8,128)S(1)}, u32[]{:S(2)}, u32[]{:S(2)}) collective-permute-start(f32[256,128]{1,0:T(8,128)S(1)} %get-tuple-element.56), channel_id=1, source_target_pairs={{28,0},{24,4},{20,8},{16,12},{12,16},{8,20},{4,24},{0,28},{29,1},{... | collective-permute-start | bytes 393224 | tf_op jit(solution)/shard_map/ppermute | solution.py:634
  18.4 1.2 %collective-permute-start.9 = (f32[256,128]{1,0:T(8,128)S(1)}, f32[256,128]{1,0:T(8,128)S(1)}, u32[]{:S(2)}, u32[]{:S(2)}) collective-permute-start(f32[256,128]{1,0:T(8,128)S(1)} %get-tuple-element.56), channel_id=1, source_target_pairs={{24,0},{28,4},{16,8},{20,12},{8,16},{12,20},{0,24},{4,28},{25,1},{... | collective-permute-start | bytes 393224 | tf_op jit(solution)/shard_map/ppermute | solution.py:634
  19.5 3.6 %collective-permute-start.8 = (f32[7,8,128]{2,1,0:T(8,128)S(1)}, f32[7,8,128]{2,1,0:T(8,128)S(1)}, u32[]{:S(2)}, u32[]{:S(2)}) collective-permute-start(f32[7,8,128]{2,1,0:T(8,128)S(1)} %shard_map.135.refs_5_.refs_0_), channel_id=1, source_target_pairs={{3,0},{2,1},{1,2},{0,3},{7,4},{6,5},{5,6},{4,7},{11,8},{10,9},{9,1... | collective-permute-start | bytes 86024 | tf_op jit(solution)/shard_map/ppermute | solution.py:638
  23.1 2.1 %collective-permute-done.8.refs_3_ = f32[7,8,128]{2,1,0:T(8,128)S(1)} collective-permute-done((f32[7,8,128]{2,1,0:T(8,128)S(1)}, f32[7,8,128]{2,1,0:T(8,128)S(1)}, u32[]{:S(2)}, u32[]{:S(2)}) %collective-permute-start.8) | collective-permute-done | bytes 28704 | tf_op jit(solution)/shard_map/ppermute | solution.py:638
  25.2 0.0 collective-permute-start.6
  25.2 2.7 %collective-permute-done.7.refs_2_ = f32[7,8,128]{2,1,0:T(8,128)S(1)} collective-permute-done((f32[7,8,128]{2,1,0:T(8,128)S(1)}, f32[7,8,128]{2,1,0:T(8,128)S(1)}, u32[]{:S(2)}, u32[]{:S(2)}) %collective-permute-start.7) | collective-permute-done | bytes 28704 | tf_op jit(solution)/shard_map/ppermute | solution.py:638
  27.9 1.2 %collective-permute-done.6.refs_1_ = f32[7,8,128]{2,1,0:T(8,128)S(1)} collective-permute-done((f32[7,8,128]{2,1,0:T(8,128)S(1)}, f32[7,8,128]{2,1,0:T(8,128)S(1)}, u32[]{:S(2)}, u32[]{:S(2)}) %collective-permute-start.6) | collective-permute-done | bytes 28704 | tf_op jit(solution)/shard_map/ppermute | solution.py:638
  29.1 1.0 %shard_map.138 = (f32[512,256]{1,0:T(8,128)S(1)}, f32[8,128]{1,0:T(8,128)S(1)}, f32[3,8,128]{2,1,0:T(8,128)S(1)}) custom-call(f32[512,256]{1,0:T(8,128)S(1)} %get-tuple-element.51.part, bf16[192,1536]{1,0:T(8,128)(2,1)S(1)} %get-tuple-element.52.fh, bf16[192,1536]{1,0:T(8,128)(2,1)S(1)} %get-tuple-element.53.fl, s32[1,1,256]{2,1,0:T(1,128)S(1)} %get-tuple-element.54.cells, ...), custom_call_target="tpu_custom_call" | custom-call | flops 100000000 | bytes 1048576 | tf_op jit(solution)/shard_map/pallas_call | solution.py:606
  30.1 0.1 collective-permute-start.13
  30.2 1.1 %shard_map.139 = (f32[512,256]{1,0:T(8,128)S(1)}, f32[512,256]{1,0:T(8,128)S(1)}, f32[512,256]{1,0:T(8,128)S(1)}, f32[8,128]{1,0:T(8,128)S(1)}) custom-call(f32[512,256]{1,0:T(8,128)S(1)} %get-tuple-element.57.u_in, f32[512,256]{1,0:T(8,128)S(1)} %get-tuple-element.40.f_in, f32[16,256]{1,0:T(8,128)S(1)} %get-tuple-element.48._.refs_4_.rot, ...), custom_call_target="tpu_custom_call" | custom-call | flops 1000000000 | bytes 1048576 | tf_op jit(solution)/shard_map/pallas_call | solution.py:606
  31.3 0.3 collective-permute-done.13.refs_4_
  31.6 0.7 %shard_map.141 = (bf16[512,256]{1,0:T(8,128)(2,1)S(1)}, bf16[512,256]{1,0:T(8,128)(2,1)S(1)}) custom-call(f32[512,256]{1,0:T(8,128)S(1)} %get-tuple-element.63.gat, bf16[384,256]{1,0:T(8,128)(2,1)S(1)} %get-tuple-element.45.gh, bf16[384,256]{1,0:T(8,128)(2,1)S(1)} %get-tuple-element.46.gl, f32[168,128]{1,0:T(8,128)S(1)} %get-tuple-element.55.col, ...), custom_call_target="tpu_custom_call" | custom-call | flops 1000000000 | bytes 1048576 | tf_op jit(solution)/shard_map/pallas_call | solution.py:606
  32.2 1.3 %shard_map.142 = f32[32,8,128]{2,1,0:T(8,128)S(1)} custom-call(f32[512,256]{1,0:T(8,128)S(1)} %get-tuple-element.62.loc, bf16[512,512]{1,0:T(8,128)(2,1)S(1)} %get-tuple-element.42.nh, bf16[512,512]{1,0:T(8,128)(2,1)S(1)} %get-tuple-element.43.nl, bf16[512,256]{1,0:T(8,128)(2,1)S(1)} %get-tuple-element.66.hi, bf16[512,256]{1,0:T(8,128)(2,1)S(1)} %get-tuple-element.67.lo, ...), custom_call_target="tpu_custom_call" | custom-call | flops 1000000000 | bytes 1048576 | tf_op jit(solution)/shard_map/pallas_call | solution.py:606
  33.5 12.6 %all_to_all.5.mine = f32[32,8,128]{2,1,0:T(8,128)S(1)} all-to-all(f32[32,8,128]{2,1,0:T(8,128)S(1)} %shard_map.142), channel_id=1, replica_groups=mesh['gx'=4,'gy'=2,'gz'=4] {'gx','gy','gz'}, dimensions={0} | all-to-all | bytes 262144 | tf_op jit(solution)/shard_map/all_to_all | solution.py:747
  46.1 0.1 collective-permute-start.14
  46.2 1.2 %collective-permute-done.14.other = f32[32,8,128]{2,1,0:T(8,128)S(1)} collective-permute-done((f32[32,8,128]{2,1,0:T(8,128)S(1)}, f32[32,8,128]{2,1,0:T(8,128)S(1)}, u32[]{:S(2)}, u32[]{:S(2)}) %collective-permute-start.14) | collective-permute-done | bytes 131104 | tf_op jit(solution)/shard_map/ppermute | solution.py:634
  47.4 4.4 %shard_map.143 = (f32[486,1,256]{2,1,0:T(1,128)}, f32[1,1]{1,0:T(1,128)}) custom-call(s32[2]{0:T(128)S(1)} %pad_add_fusion.ids, f32[512,256]{1,0:T(8,128)S(1)} %get-tuple-element.40.f_in, f32[512,256]{1,0:T(8,128)S(1)} %get-tuple-element.57.u_in, f32[32,8,128]{2,1,0:T(8,128)S(1)} %all_to_all.5.mine, f32[32,8,128]{2,1,0:T(8,128)S(1)} %collective-permute-done.14.other, ...), custom_call_target="tpu_custom_call" | custom-call | flops 10000000 | bytes 1048576 | tf_op jit(solution)/shard_map/pallas_call | solution.py:606
  (13 shorter events, 0.1 us)
Async XLA Ops:
  2.1 12.0 %collective-permute-start.3 = (f32[264,128]{1,0:T(8,128)S(1)}, f32[264,128]{1,0:T(8,128)S(1)}, u32[]{:S(2)}, u32[]{:S(2)}) collective-permute-start(f32[264,128]{1,0:T(8,128)S(1)} %get-tuple-element.47.refs_0_.message.charges_f), channel_id=1, source_target_pairs={{8,0},{12,4},{0,8},{4,12},{24,16},{28,20},{16,24},{20,28},{9,1},{1... | collective-permute-start | bytes 405512 | tf_op jit(solution)/shard_map/ppermute | solution.py:634
  2.6 10.9 %collective-permute-start.2 = (f32[264,128]{1,0:T(8,128)S(1)}, f32[264,128]{1,0:T(8,128)S(1)}, u32[]{:S(2)}, u32[]{:S(2)}) collective-permute-start(f32[264,128]{1,0:T(8,128)S(1)} %get-tuple-element.47.refs_0_.message.charges_f), channel_id=1, source_target_pairs={{28,0},{24,4},{20,8},{16,12},{12,16},{8,20},{4,24},{0,28},{29,1},{... | collective-permute-start | bytes 405512 | tf_op jit(solution)/shard_map/ppermute | solution.py:634
  6.2 7.4 %collective-permute-start.1 = (f32[264,128]{1,0:T(8,128)S(1)}, f32[264,128]{1,0:T(8,128)S(1)}, u32[]{:S(2)}, u32[]{:S(2)}) collective-permute-start(f32[264,128]{1,0:T(8,128)S(1)} %get-tuple-element.47.refs_0_.message.charges_f), channel_id=1, source_target_pairs={{24,0},{28,4},{16,8},{20,12},{8,16},{12,20},{0,24},{4,28},{25,1},{... | collective-permute-start | bytes 405512 | tf_op jit(solution)/shard_map/ppermute | solution.py:634
  6.3 7.1 %collective-permute-start = (f32[264,128]{1,0:T(8,128)S(1)}, f32[264,128]{1,0:T(8,128)S(1)}, u32[]{:S(2)}, u32[]{:S(2)}) collective-permute-start(f32[264,128]{1,0:T(8,128)S(1)} %get-tuple-element.47.refs_0_.message.charges_f), channel_id=1, source_target_pairs={{4,0},{0,4},{12,8},{8,12},{20,16},{16,20},{28,24},{24,28},{5,1},{1... | collective-permute-start | bytes 405512 | tf_op jit(solution)/shard_map/ppermute | solution.py:634
  13.4 1.5 %collective-permute-start.4 = (f32[264,128]{1,0:T(8,128)S(1)}, f32[264,128]{1,0:T(8,128)S(1)}, u32[]{:S(2)}, u32[]{:S(2)}) collective-permute-start(f32[264,128]{1,0:T(8,128)S(1)} %shard_map.133), channel_id=1, source_target_pairs={{8,0},{12,4},{0,8},{4,12},{24,16},{28,20},{16,24},{20,28},{9,1},{1... | collective-permute-start | bytes 405512 | tf_op jit(solution)/shard_map/ppermute | solution.py:634
  13.5 1.4 %collective-permute-start.5 = (f32[8,128]{1,0:T(8,128)S(1)}, f32[8,128]{1,0:T(8,128)S(1)}, u32[]{:S(2)}, u32[]{:S(2)}) collective-permute-start(f32[8,128]{1,0:T(8,128)S(1)} %shard_map.134.refs_0_), channel_id=1, source_target_pairs={{8,0},{12,4},{0,8},{4,12},{24,16},{28,20},{16,24},{20,28},{9,1},{1... | collective-permute-start | bytes 12296 | tf_op jit(solution)/shard_map/ppermute | solution.py:634
  16.3 12.8 %collective-permute-start.11 = (f32[256,128]{1,0:T(8,128)S(1)}, f32[256,128]{1,0:T(8,128)S(1)}, u32[]{:S(2)}, u32[]{:S(2)}) collective-permute-start(f32[256,128]{1,0:T(8,128)S(1)} %get-tuple-element.56), channel_id=1, source_target_pairs={{4,0},{0,4},{12,8},{8,12},{20,16},{16,20},{28,24},{24,28},{5,1},{1... | collective-permute-start | bytes 393224 | tf_op jit(solution)/shard_map/ppermute | solution.py:634
  17.8 11.2 %collective-permute-start.10 = (f32[256,128]{1,0:T(8,128)S(1)}, f32[256,128]{1,0:T(8,128)S(1)}, u32[]{:S(2)}, u32[]{:S(2)}) collective-permute-start(f32[256,128]{1,0:T(8,128)S(1)} %get-tuple-element.56), channel_id=1, source_target_pairs={{28,0},{24,4},{20,8},{16,12},{12,16},{8,20},{4,24},{0,28},{29,1},{... | collective-permute-start | bytes 393224 | tf_op jit(solution)/shard_map/ppermute | solution.py:634
  18.4 10.7 %collective-permute-start.9 = (f32[256,128]{1,0:T(8,128)S(1)}, f32[256,128]{1,0:T(8,128)S(1)}, u32[]{:S(2)}, u32[]{:S(2)}) collective-permute-start(f32[256,128]{1,0:T(8,128)S(1)} %get-tuple-element.56), channel_id=1, source_target_pairs={{24,0},{28,4},{16,8},{20,12},{8,16},{12,20},{0,24},{4,28},{25,1},{... | collective-permute-start | bytes 393224 | tf_op jit(solution)/shard_map/ppermute | solution.py:634
  19.5 5.7 %collective-permute-start.8 = (f32[7,8,128]{2,1,0:T(8,128)S(1)}, f32[7,8,128]{2,1,0:T(8,128)S(1)}, u32[]{:S(2)}, u32[]{:S(2)}) collective-permute-start(f32[7,8,128]{2,1,0:T(8,128)S(1)} %shard_map.135.refs_5_.refs_0_), channel_id=1, source_target_pairs={{3,0},{2,1},{1,2},{0,3},{7,4},{6,5},{5,6},{4,7},{11,8},{10,9},{9,1... | collective-permute-start | bytes 86024 | tf_op jit(solution)/shard_map/ppermute | solution.py:638
  23.1 4.8 %collective-permute-start.7 = (f32[7,8,128]{2,1,0:T(8,128)S(1)}, f32[7,8,128]{2,1,0:T(8,128)S(1)}, u32[]{:S(2)}, u32[]{:S(2)}) collective-permute-start(f32[7,8,128]{2,1,0:T(8,128)S(1)} %shard_map.135.refs_5_.refs_0_), channel_id=1, source_target_pairs={{2,0},{3,1},{0,2},{1,3},{6,4},{7,5},{4,6},{5,7},{10,8},{11,9},{8,1... | collective-permute-start | bytes 86024 | tf_op jit(solution)/shard_map/ppermute | solution.py:638
  25.2 3.9 %collective-permute-start.6 = (f32[7,8,128]{2,1,0:T(8,128)S(1)}, f32[7,8,128]{2,1,0:T(8,128)S(1)}, u32[]{:S(2)}, u32[]{:S(2)}) collective-permute-start(f32[7,8,128]{2,1,0:T(8,128)S(1)} %shard_map.135.refs_5_.refs_0_), channel_id=1, source_target_pairs={{1,0},{0,1},{3,2},{2,3},{5,4},{4,5},{7,6},{6,7},{9,8},{8,9},{11,10... | collective-permute-start | bytes 86024 | tf_op jit(solution)/shard_map/ppermute | solution.py:638
  27.9 3.4 %collective-permute-start.12 = (f32[256,128]{1,0:T(8,128)S(1)}, f32[256,128]{1,0:T(8,128)S(1)}, u32[]{:S(2)}, u32[]{:S(2)}) collective-permute-start(f32[256,128]{1,0:T(8,128)S(1)} %get-tuple-element.56), channel_id=1, source_target_pairs={{8,0},{12,4},{0,8},{4,12},{24,16},{28,20},{16,24},{20,28},{9,1},{1... | collective-permute-start | bytes 393224 | tf_op jit(solution)/shard_map/ppermute | solution.py:634
  30.1 1.4 %collective-permute-start.13 = (f32[256,128]{1,0:T(8,128)S(1)}, f32[256,128]{1,0:T(8,128)S(1)}, u32[]{:S(2)}, u32[]{:S(2)}) collective-permute-start(f32[256,128]{1,0:T(8,128)S(1)} %shard_map.140), channel_id=1, source_target_pairs={{8,0},{12,4},{0,8},{4,12},{24,16},{28,20},{16,24},{20,28},{9,1},{1... | collective-permute-start | bytes 393224 | tf_op jit(solution)/shard_map/ppermute | solution.py:634
  46.1 1.3 %collective-permute-start.14 = (f32[32,8,128]{2,1,0:T(8,128)S(1)}, f32[32,8,128]{2,1,0:T(8,128)S(1)}, u32[]{:S(2)}, u32[]{:S(2)}) collective-permute-start(f32[32,8,128]{2,1,0:T(8,128)S(1)} %all_to_all.5.mine), channel_id=1, source_target_pairs={{8,0},{12,4},{0,8},{4,12},{24,16},{28,20},{16,24},{20,28},{9,1},{1... | collective-permute-start | bytes 393224 | tf_op jit(solution)/shard_map/ppermute | solution.py:634

commit v14 on v13

--- a/solution.py
+++ b/solution.py
@@ -328,7 +328,7 @@
 
 
 def layer_kernel(s, count, message, *refs):
-    sums, around, out = refs[:count], refs[count:-1], refs[-1]
+    sums, around, out = refs[:count], refs[count:-2], refs[-1]
     acc = sums[0][...]
     for part in sums[1:]:
         acc = acc + part[...]
@@ -336,6 +336,11 @@
     out[1] = acc
     for index, other in enumerate(around):
         out[2 + index] = other[s.half :, :]
+
+
+def join_kernel(x, y, out):
+    out[: x.shape[0]] = x[...]
+    out[x.shape[0] :] = y[...]
 
 
 def layer_row(s, tiles):
@@ -350,7 +355,7 @@
 
 
 def far_potentials(s, layers, far_op):
-    own = [layer_row(s, [layer[k] for layer in layers]) for k in range(layers[0].shape[0])]
+    own = [layer_row(s, [layer[k] for layer in layers]) for k in range(len(layers[0]))]
     wide = own[0].shape[1]
     hi, lo = far_op
     whole = product(mt, split(own.pop(1)), (hi[:, wide:], lo[:, wide:]))
@@ -367,16 +372,24 @@
     return picked[:n] + (picked[n : 2 * n] + picked[2 * n :])
 
 
-def rim_values(s, layers, potentials):
+def place_kernel(s, cells, tiles, own_out, rims_out):
+    own_out[...] = occupancy(cells[0], s)
     lane = lax.broadcasted_iota(jnp.int32, (8, LANES), 1)
     place = lax.broadcasted_iota(jnp.int32, (s.skel, LANES), 0).astype(f32)
+    count = len(s.sources)
+    for i in range(0, count, 2):
+        last = min(i + 1, count - 1)
+        pair = jnp.where(lane < RIM, tiles[2 + i], pltpu.roll(tiles[2 + last], RIM, 1))
+        rims_out[i // 2] = jnp.where(pair[3:4] == place, 1.0, 0.0).astype(bf16)
+
+
+def rim_values(s, potentials, onehots):
+    lane = lax.broadcasted_iota(jnp.int32, (8, LANES), 1)
     count = len(potentials) - 1
     out = []
     for i in range(0, count, 2):
         last = min(i + 1, count - 1)
-        cells = jnp.where(lane < RIM, layers[0][2 + i], pltpu.roll(layers[0][2 + last], RIM, 1))
-        onehot = jnp.where(cells[3:4] == place, 1.0, 0.0).astype(bf16)
-        both = pick(jnp.concatenate([potentials[1 + i], potentials[1 + last]], axis=0), onehot)
+        both = pick(jnp.concatenate([potentials[1 + i], potentials[1 + last]], axis=0), onehots[i // 2])
         out.append(jnp.where(lane < RIM, both[:8], both[8:]))
     return out
 
@@ -406,17 +419,19 @@
     rim_out[...] = pack_rim(part, s)
 
 
-def first_kernel(s, part, fh, fl, cells, col, *refs):
+def first_kernel(s, part, fh, fl, own, rims, col, *refs):
     *layers, u_out, charges_out, values_out = refs
-    layers = layers[: s.nz]
+    count = 2 + len(s.sources)
+    parts = layers[: s.levels + 1]
+    layers = [[part[at + k] for k in range(count)] for part in parts for at in range(0, part.shape[0], count)]
     weight_col = col[:, :1]
-    occ = occupancy(cells[0], s)
+    occ = own[...]
     potentials = far_potentials(s, layers, (fh[...], fl[...]))
     values = pick(potentials[0], occ)
     u = part[...] + stacked([weight_col * values[c : c + 1] for c in range(3)], s)
     u_out[...] = u
     charges_out[...] = pack_charges(pieces(u, s), weight_col, occ, s)
-    for index, value in enumerate(rim_values(s, layers, potentials)):
+    for index, value in enumerate(rim_values(s, potentials, rims)):
         values_out[index] = value
 
 
@@ -634,9 +649,13 @@
         return lax.ppermute(x, ("gx", "gy"), pairs)
 
     def fetch_layers(x):
-        return [x] + [
-            lax.ppermute(x, "gz", [(z ^ k, z) for z in range(s.nz)]) for k in range(1, s.nz)
-        ]
+        parts = [x]
+        for level in range(s.levels):
+            pairs = [(z ^ (1 << level), z) for z in range(s.nz)]
+            parts.append(lax.ppermute(x, "gz", pairs))
+            if level + 1 < s.levels:
+                (x,) = call(join_kernel, [((2 * x.shape[0],) + tile, f32)], [x, parts[-1]])
+        return parts
 
     def fetch_rims(rim):
         got = {}
@@ -699,16 +718,10 @@
     forward_rims(got, rot)
     sums = plane_sum(message, got, rot)
     around = [got[key] for key in s.sources]
-    (tiles,) = call(
-        functools.partial(layer_kernel, s, len(sums)),
-        [((2 + len(around),) + tile, f32)],
-        [message] + sums + around,
-    )
-    layers = fetch_layers(tiles)
     gathered = call(
         functools.partial(gather_kernel, s),
         [(full, bf16), (full, bf16)],
-        [gat, gh, gl] + around + [tiles],
+        [gat, gh, gl] + around + [sums[0]],
         flops=10**9,
     )
     part, rim = call(
@@ -717,12 +730,24 @@
         [loc, nh, nl, *gathered],
         flops=10**9,
     )
+    (tiles,) = call(
+        functools.partial(layer_kernel, s, len(sums)),
+        [((2 + len(around),) + tile, f32)],
+        [message] + sums + around + [gathered[1]],
+    )
+    layers = fetch_layers(tiles)
     got = fetch_rims(rim)
+    places = call(
+        functools.partial(place_kernel, s),
+        [((s.skel, s.bodies), bf16), ((s.ghosts // LANES, s.skel, LANES), bf16)],
+        [cells, tiles],
+        flops=2 * 10**10,
+    )
     ahead = [got["other", 0]] + [got[kind, dy] for kind in ("other", "same") for dy in s.shifts]
     u, charges, values = call(
         functools.partial(first_kernel, s),
         [(full, f32), (tile, f32), ((s.ghosts // LANES,) + tile, f32)],
-        [part, fh, fl, cells, col, *layers] + ahead,
+        [part, fh, fl, *places, col, *layers] + ahead,
         flops=10**8,
     )
     loc, gat, ortho, stat = call(

time: 52.1 us -> 49.6 us (0.952)
  waiting for transfers between devices: 9.23 us -> 6.79 us
  blocking collectives: 12.6 us -> 12 us
    ppermute x3 -> x2, waiting for transfers between devices: 5.91 us -> 3.65 us  [fetch_layers(): parts.append(lax.ppermute(x, 'gz', pairs))]
    ppermute x3 -> x2, starting transfers between devices: 3.62 us -> 4.23 us  [fetch_layers(): parts.append(lax.ppermute(x, 'gz', pairs))]
    all_to_all x1, blocking collectives: 12.6 us -> 12 us  [body(): boxes = lax.all_to_all(packed, ('gx', 'gy', 'gz'), 0, 0)]
    pallas_call x13 -> x15, Pallas kernels: 16.9 us -> 16.9 us  [call(): pl.pallas_call(kernel, out_shape=[jax.ShapeDtypeStruct(shape, kind) for s...]
  transfers between devices with their start and end apart: 15 -> 14, of which waited for: 7 -> 6; matrix products, arithmetic and copies ran while one was open for 0% -> 0% of each run, Pallas kernels for 15% -> 19%
where the time goes in v14:
time: 49.6 us; the launch traced here: 49.4 us
  Pallas kernels  16.9 us (34%)
  starting transfers between devices  12.8 us (26%)
  blocking collectives  12 us (24%)
  waiting for transfers between devices  6.79 us (14%)
  between operations  0.74 us (1%)
    pallas_call x15, Pallas kernels, call(): pl.pallas_call(kernel, out_shape=[jax.ShapeDtypeStruct(shape, kind) for s...  16.9 us
    all_to_all x1, blocking collectives, body(): boxes = lax.all_to_all(packed, ('gx', 'gy', 'gz'), 0, 0)  12 us
    ppermute x12, starting transfers between devices, fetch(): return lax.ppermute(x, ('gx', 'gy'), pairs)  8.59 us
    ppermute x2, starting transfers between devices, fetch_layers(): parts.append(lax.ppermute(x, 'gz', pairs))  4.23 us
    ppermute x2, waiting for transfers between devices, fetch_layers(): parts.append(lax.ppermute(x, 'gz', pairs))  3.65 us
    ppermute x12, waiting for transfers between devices, fetch(): return lax.ppermute(x, ('gx', 'gy'), pairs)  3.14 us
  transfers between devices with their start and end apart: 14, of which 6 were waited for; matrix products, arithmetic and copies ran while one was open for 0% of the time, Pallas kernels for 19%

profile of v14, /device:TPU:0, one launch (start us, length us, event | category | flops | bytes accessed | tf_op | source)
XLA Modules:
  0.0 49.4 jit_solution(5781426281224246432)
XLA Ops:
  0.6 1.4 %shard_map.131 = (f32[264,128]{1,0:T(8,128)S(1)}, f32[168,128]{1,0:T(8,128)S(1)}, s32[1,1,256]{2,1,0:T(1,128)S(1)}, f32[512,256]{1,0:T(8,128)S(1)}) custom-call(f32[486,1,256]{2,1,0:T(1,128)} %bitcast.9, s32[1,1,256]{2,1,0:T(1,128)} %cells.1, f32[1,162]{1,0:T(1,128)} %bitcast.10), custom_call_target="tpu_custom_call" | custom-call | flops 10000000 | bytes 1048576 | tf_op jit(solution)/shard_map/pallas_call | solution.py:621
  2.1 3.0 %collective-permute-start = (f32[264,128]{1,0:T(8,128)S(1)}, f32[264,128]{1,0:T(8,128)S(1)}, u32[]{:S(2)}, u32[]{:S(2)}) collective-permute-start(f32[264,128]{1,0:T(8,128)S(1)} %get-tuple-element.49.refs_0_.message.charges_f), channel_id=1, source_target_pairs={{4,0},{0,4},{12,8},{8,12},{20,16},{16,20},{28,24},{24,28},{5,1},{1... | collective-permute-start | bytes 405512 | tf_op jit(solution)/shard_map/ppermute | solution.py:649
  5.1 0.7 %collective-permute-start.1 = (f32[264,128]{1,0:T(8,128)S(1)}, f32[264,128]{1,0:T(8,128)S(1)}, u32[]{:S(2)}, u32[]{:S(2)}) collective-permute-start(f32[264,128]{1,0:T(8,128)S(1)} %get-tuple-element.49.refs_0_.message.charges_f), channel_id=1, source_target_pairs={{24,0},{28,4},{16,8},{20,12},{8,16},{12,20},{0,24},{4,28},{25,1},{... | collective-permute-start | bytes 405512 | tf_op jit(solution)/shard_map/ppermute | solution.py:649
  5.7 0.6 %collective-permute-start.2 = (f32[264,128]{1,0:T(8,128)S(1)}, f32[264,128]{1,0:T(8,128)S(1)}, u32[]{:S(2)}, u32[]{:S(2)}) collective-permute-start(f32[264,128]{1,0:T(8,128)S(1)} %get-tuple-element.49.refs_0_.message.charges_f), channel_id=1, source_target_pairs={{28,0},{24,4},{20,8},{16,12},{12,16},{8,20},{4,24},{0,28},{29,1},{... | collective-permute-start | bytes 405512 | tf_op jit(solution)/shard_map/ppermute | solution.py:649
  6.3 0.4 collective-permute-start.3
  6.7 0.1 pad_add_fusion.ids
  6.8 5.6 %shard_map.132 = (f32[512,256]{1,0:T(8,128)S(1)}, f32[512,256]{1,0:T(8,128)S(1)}, f32[16,256]{1,0:T(8,128)S(1)}, bf16[512,512]{1,0:T(8,128)(2,1)S(1)}, bf16[512,...) custom-call(s32[2]{0:T(128)S(1)} %pad_add_fusion.ids, ...), custom_call_target="tpu_custom_call" | custom-call | flops 5000000000 | bytes 1048576 | tf_op jit(solution)/shard_map/pallas_call | solution.py:621
  12.4 0.2 collective-permute-start.4
  12.7 1.1 %collective-permute-done.1.refs_2_.refs_1_.refs_3_ = f32[264,128]{1,0:T(8,128)S(1)} collective-permute-done((f32[264,128]{1,0:T(8,128)S(1)}, f32[264,128]{1,0:T(8,128)S(1)}, u32[]{:S(2)}, u32[]{:S(2)}) %collective-permute-start.1) | collective-permute-done | bytes 135200 | tf_op jit(solution)/shard_map/ppermute | solution.py:649
  13.8 0.0 collective-permute-done.2.refs_3_.refs_2_.refs_4_
  13.8 0.2 collective-permute-start.5
  14.0 0.7 %shard_map.135 = (bf16[512,256]{1,0:T(8,128)(2,1)S(1)}, bf16[512,256]{1,0:T(8,128)(2,1)S(1)}) custom-call(f32[512,256]{1,0:T(8,128)S(1)} %get-tuple-element.46.gat, bf16[384,256]{1,0:T(8,128)(2,1)S(1)} %get-tuple-element.47.gh, bf16[384,256]{1,0:T(8,128)(2,1)S(1)} %get-tuple-element.48.gl, f32[264,128]{1,0:T(8,128)S(1)} %collective-permute-done.x.refs_1_.refs_0_.refs_2_, ...), custom_call_target="tpu_custom_call" | custom-call | flops 1000000000 | bytes 1048576 | tf_op jit(solution)/shard_map/pallas_call | solution.py:621
  14.7 0.4 collective-permute-done.5.refs_1_
  15.0 1.6 %collective-permute-start.6 = (f32[7,8,128]{2,1,0:T(8,128)S(1)}, f32[7,8,128]{2,1,0:T(8,128)S(1)}, u32[]{:S(2)}, u32[]{:S(2)}) collective-permute-start(f32[7,8,128]{2,1,0:T(8,128)S(1)} %shard_map.137.tiles.x.refs_0_), channel_id=1, source_target_pairs={{1,0},{0,1},{3,2},{2,3},{5,4},{4,5},{7,6},{6,7},{9,8},{8,9},{11,10... | collective-permute-start | bytes 86024 | tf_op jit(solution)/shard_map/ppermute | solution.py:655
  16.6 0.6 %shard_map.136 = (f32[512,256]{1,0:T(8,128)S(1)}, f32[256,128]{1,0:T(8,128)S(1)}) custom-call(f32[512,256]{1,0:T(8,128)S(1)} %get-tuple-element.43.loc, bf16[512,512]{1,0:T(8,128)(2,1)S(1)} %get-tuple-element.44.nh, bf16[512,512]{1,0:T(8,128)(2,1)S(1)} %get-tuple-element.45.nl, bf16[512,256]{1,0:T(8,128)(2,1)S(1)} %get-tuple-element.51.hi, ...), custom_call_target="tpu_custom_call" | custom-call | flops 1000000000 | bytes 1048576 | tf_op jit(solution)/shard_map/pallas_call | solution.py:621
  17.2 1.4 %collective-permute-start.10 = (f32[256,128]{1,0:T(8,128)S(1)}, f32[256,128]{1,0:T(8,128)S(1)}, u32[]{:S(2)}, u32[]{:S(2)}) collective-permute-start(f32[256,128]{1,0:T(8,128)S(1)} %get-tuple-element.60), channel_id=1, source_target_pairs={{4,0},{0,4},{12,8},{8,12},{20,16},{16,20},{28,24},{24,28},{5,1},{1... | collective-permute-start | bytes 393224 | tf_op jit(solution)/shard_map/ppermute | solution.py:649
  18.7 0.9 %collective-permute-start.8 = (f32[256,128]{1,0:T(8,128)S(1)}, f32[256,128]{1,0:T(8,128)S(1)}, u32[]{:S(2)}, u32[]{:S(2)}) collective-permute-start(f32[256,128]{1,0:T(8,128)S(1)} %get-tuple-element.60), channel_id=1, source_target_pairs={{24,0},{28,4},{16,8},{20,12},{8,16},{12,20},{0,24},{4,28},{25,1},{... | collective-permute-start | bytes 393224 | tf_op jit(solution)/shard_map/ppermute | solution.py:649
  19.6 0.9 %collective-permute-start.9 = (f32[256,128]{1,0:T(8,128)S(1)}, f32[256,128]{1,0:T(8,128)S(1)}, u32[]{:S(2)}, u32[]{:S(2)}) collective-permute-start(f32[256,128]{1,0:T(8,128)S(1)} %get-tuple-element.60), channel_id=1, source_target_pairs={{28,0},{24,4},{20,8},{16,12},{12,16},{8,20},{4,24},{0,28},{29,1},{... | collective-permute-start | bytes 393224 | tf_op jit(solution)/shard_map/ppermute | solution.py:649
  20.5 2.7 %collective-permute-start.7 = (f32[14,8,128]{2,1,0:T(8,128)S(1)}, f32[14,8,128]{2,1,0:T(8,128)S(1)}, u32[]{:S(2)}, u32[]{:S(2)}) collective-permute-start(f32[14,8,128]{2,1,0:T(8,128)S(1)} %shard_map.139), channel_id=1, source_target_pairs={{2,0},{3,1},{0,2},{1,3},{6,4},{7,5},{4,6},{5,7},{10,8},{11,9},{8,1... | collective-permute-start | bytes 172040 | tf_op jit(solution)/shard_map/ppermute | solution.py:655
  23.2 0.1 shard_map.138
  23.3 3.7 %collective-permute-done.7.refs_2_ = f32[14,8,128]{2,1,0:T(8,128)S(1)} collective-permute-done((f32[14,8,128]{2,1,0:T(8,128)S(1)}, f32[14,8,128]{2,1,0:T(8,128)S(1)}, u32[]{:S(2)}, u32[]{:S(2)}) %collective-permute-start.7) | collective-permute-done | bytes 57376 | tf_op jit(solution)/shard_map/ppermute | solution.py:655
  26.9 0.2 collective-permute-done.8.refs_3_.refs_1_
  27.2 1.0 %shard_map.140 = (f32[512,256]{1,0:T(8,128)S(1)}, f32[8,128]{1,0:T(8,128)S(1)}, f32[3,8,128]{2,1,0:T(8,128)S(1)}) custom-call(f32[512,256]{1,0:T(8,128)S(1)} %get-tuple-element.53.part, bf16[192,1536]{1,0:T(8,128)(2,1)S(1)} %get-tuple-element.54.fh, bf16[192,1536]{1,0:T(8,128)(2,1)S(1)} %get-tuple-element.55.fl, bf16[192,256]{1,0:T(8,128)(2,1)S(1)} %get-tuple-element.57.own, ...), custom_call_target="tpu_custom_call" | custom-call | flops 100000000 | bytes 1048576 | tf_op jit(solution)/shard_map/pallas_call | solution.py:621
  28.2 0.2 collective-permute-start.12
  28.4 1.0 %shard_map.141 = (f32[512,256]{1,0:T(8,128)S(1)}, f32[512,256]{1,0:T(8,128)S(1)}, f32[512,256]{1,0:T(8,128)S(1)}, f32[8,128]{1,0:T(8,128)S(1)}) custom-call(f32[512,256]{1,0:T(8,128)S(1)} %get-tuple-element.61.u_in, f32[512,256]{1,0:T(8,128)S(1)} %get-tuple-element.42.f_in, f32[16,256]{1,0:T(8,128)S(1)} %get-tuple-element.50._.refs_4_.rot, ...), custom_call_target="tpu_custom_call" | custom-call | flops 1000000000 | bytes 1048576 | tf_op jit(solution)/shard_map/pallas_call | solution.py:621
  29.5 0.2 collective-permute-done.12.refs_4_
  29.6 0.7 %shard_map.143 = (bf16[512,256]{1,0:T(8,128)(2,1)S(1)}, bf16[512,256]{1,0:T(8,128)(2,1)S(1)}) custom-call(f32[512,256]{1,0:T(8,128)S(1)} %get-tuple-element.67.gat, bf16[384,256]{1,0:T(8,128)(2,1)S(1)} %get-tuple-element.47.gh, bf16[384,256]{1,0:T(8,128)(2,1)S(1)} %get-tuple-element.48.gl, f32[168,128]{1,0:T(8,128)S(1)} %get-tuple-element.59.col, ...), custom_call_target="tpu_custom_call" | custom-call | flops 1000000000 | bytes 1048576 | tf_op jit(solution)/shard_map/pallas_call | solution.py:621
  30.3 1.3 %shard_map.144 = f32[32,8,128]{2,1,0:T(8,128)S(1)} custom-call(f32[512,256]{1,0:T(8,128)S(1)} %get-tuple-element.66.loc, bf16[512,512]{1,0:T(8,128)(2,1)S(1)} %get-tuple-element.44.nh, bf16[512,512]{1,0:T(8,128)(2,1)S(1)} %get-tuple-element.45.nl, bf16[512,256]{1,0:T(8,128)(2,1)S(1)} %get-tuple-element.70.hi, bf16[512,256]{1,0:T(8,128)(2,1)S(1)} %get-tuple-element.71.lo, ...), custom_call_target="tpu_custom_call" | custom-call | flops 1000000000 | bytes 1048576 | tf_op jit(solution)/shard_map/pallas_call | solution.py:621
  31.6 12.0 %all_to_all.5.mine = f32[32,8,128]{2,1,0:T(8,128)S(1)} all-to-all(f32[32,8,128]{2,1,0:T(8,128)S(1)} %shard_map.144), channel_id=1, replica_groups=mesh['gx'=4,'gy'=2,'gz'=4] {'gx','gy','gz'}, dimensions={0} | all-to-all | bytes 262144 | tf_op jit(solution)/shard_map/all_to_all | solution.py:772
  43.6 0.1 collective-permute-start.13
  43.7 1.2 %collective-permute-done.13.other = f32[32,8,128]{2,1,0:T(8,128)S(1)} collective-permute-done((f32[32,8,128]{2,1,0:T(8,128)S(1)}, f32[32,8,128]{2,1,0:T(8,128)S(1)}, u32[]{:S(2)}, u32[]{:S(2)}) %collective-permute-start.13) | collective-permute-done | bytes 131104 | tf_op jit(solution)/shard_map/ppermute | solution.py:649
  45.0 4.4 %shard_map.145 = (f32[486,1,256]{2,1,0:T(1,128)}, f32[1,1]{1,0:T(1,128)}) custom-call(s32[2]{0:T(128)S(1)} %pad_add_fusion.ids, f32[512,256]{1,0:T(8,128)S(1)} %get-tuple-element.42.f_in, f32[512,256]{1,0:T(8,128)S(1)} %get-tuple-element.61.u_in, f32[32,8,128]{2,1,0:T(8,128)S(1)} %all_to_all.5.mine, f32[32,8,128]{2,1,0:T(8,128)S(1)} %collective-permute-done.13.other, ...), custom_call_target="tpu_custom_call" | custom-call | flops 10000000 | bytes 1048576 | tf_op jit(solution)/shard_map/pallas_call | solution.py:621
  (13 shorter events, 0.1 us)
Async XLA Ops:
  2.1 10.4 %collective-permute-start = (f32[264,128]{1,0:T(8,128)S(1)}, f32[264,128]{1,0:T(8,128)S(1)}, u32[]{:S(2)}, u32[]{:S(2)}) collective-permute-start(f32[264,128]{1,0:T(8,128)S(1)} %get-tuple-element.49.refs_0_.message.charges_f), channel_id=1, source_target_pairs={{4,0},{0,4},{12,8},{8,12},{20,16},{16,20},{28,24},{24,28},{5,1},{1... | collective-permute-start | bytes 405512 | tf_op jit(solution)/shard_map/ppermute | solution.py:649
  5.1 8.7 %collective-permute-start.1 = (f32[264,128]{1,0:T(8,128)S(1)}, f32[264,128]{1,0:T(8,128)S(1)}, u32[]{:S(2)}, u32[]{:S(2)}) collective-permute-start(f32[264,128]{1,0:T(8,128)S(1)} %get-tuple-element.49.refs_0_.message.charges_f), channel_id=1, source_target_pairs={{24,0},{28,4},{16,8},{20,12},{8,16},{12,20},{0,24},{4,28},{25,1},{... | collective-permute-start | bytes 405512 | tf_op jit(solution)/shard_map/ppermute | solution.py:649
  5.7 8.0 %collective-permute-start.2 = (f32[264,128]{1,0:T(8,128)S(1)}, f32[264,128]{1,0:T(8,128)S(1)}, u32[]{:S(2)}, u32[]{:S(2)}) collective-permute-start(f32[264,128]{1,0:T(8,128)S(1)} %get-tuple-element.49.refs_0_.message.charges_f), channel_id=1, source_target_pairs={{28,0},{24,4},{20,8},{16,12},{12,16},{8,20},{4,24},{0,28},{29,1},{... | collective-permute-start | bytes 405512 | tf_op jit(solution)/shard_map/ppermute | solution.py:649
  6.3 7.6 %collective-permute-start.3 = (f32[264,128]{1,0:T(8,128)S(1)}, f32[264,128]{1,0:T(8,128)S(1)}, u32[]{:S(2)}, u32[]{:S(2)}) collective-permute-start(f32[264,128]{1,0:T(8,128)S(1)} %get-tuple-element.49.refs_0_.message.charges_f), channel_id=1, source_target_pairs={{8,0},{12,4},{0,8},{4,12},{24,16},{28,20},{16,24},{20,28},{9,1},{1... | collective-permute-start | bytes 405512 | tf_op jit(solution)/shard_map/ppermute | solution.py:649
  12.4 1.5 %collective-permute-start.4 = (f32[264,128]{1,0:T(8,128)S(1)}, f32[264,128]{1,0:T(8,128)S(1)}, u32[]{:S(2)}, u32[]{:S(2)}) collective-permute-start(f32[264,128]{1,0:T(8,128)S(1)} %shard_map.133), channel_id=1, source_target_pairs={{8,0},{12,4},{0,8},{4,12},{24,16},{28,20},{16,24},{20,28},{9,1},{1... | collective-permute-start | bytes 405512 | tf_op jit(solution)/shard_map/ppermute | solution.py:649
  13.8 1.2 %collective-permute-start.5 = (f32[8,128]{1,0:T(8,128)S(1)}, f32[8,128]{1,0:T(8,128)S(1)}, u32[]{:S(2)}, u32[]{:S(2)}) collective-permute-start(f32[8,128]{1,0:T(8,128)S(1)} %shard_map.134.refs_5_.refs_0_), channel_id=1, source_target_pairs={{8,0},{12,4},{0,8},{4,12},{24,16},{28,20},{16,24},{20,28},{9,1},{1... | collective-permute-start | bytes 12296 | tf_op jit(solution)/shard_map/ppermute | solution.py:649
  15.0 5.5 %collective-permute-start.6 = (f32[7,8,128]{2,1,0:T(8,128)S(1)}, f32[7,8,128]{2,1,0:T(8,128)S(1)}, u32[]{:S(2)}, u32[]{:S(2)}) collective-permute-start(f32[7,8,128]{2,1,0:T(8,128)S(1)} %shard_map.137.tiles.x.refs_0_), channel_id=1, source_target_pairs={{1,0},{0,1},{3,2},{2,3},{5,4},{4,5},{7,6},{6,7},{9,8},{8,9},{11,10... | collective-permute-start | bytes 86024 | tf_op jit(solution)/shard_map/ppermute | solution.py:655
  17.2 9.7 %collective-permute-start.10 = (f32[256,128]{1,0:T(8,128)S(1)}, f32[256,128]{1,0:T(8,128)S(1)}, u32[]{:S(2)}, u32[]{:S(2)}) collective-permute-start(f32[256,128]{1,0:T(8,128)S(1)} %get-tuple-element.60), channel_id=1, source_target_pairs={{4,0},{0,4},{12,8},{8,12},{20,16},{16,20},{28,24},{24,28},{5,1},{1... | collective-permute-start | bytes 393224 | tf_op jit(solution)/shard_map/ppermute | solution.py:649
  18.7 8.5 %collective-permute-start.8 = (f32[256,128]{1,0:T(8,128)S(1)}, f32[256,128]{1,0:T(8,128)S(1)}, u32[]{:S(2)}, u32[]{:S(2)}) collective-permute-start(f32[256,128]{1,0:T(8,128)S(1)} %get-tuple-element.60), channel_id=1, source_target_pairs={{24,0},{28,4},{16,8},{20,12},{8,16},{12,20},{0,24},{4,28},{25,1},{... | collective-permute-start | bytes 393224 | tf_op jit(solution)/shard_map/ppermute | solution.py:649
  19.6 7.6 %collective-permute-start.9 = (f32[256,128]{1,0:T(8,128)S(1)}, f32[256,128]{1,0:T(8,128)S(1)}, u32[]{:S(2)}, u32[]{:S(2)}) collective-permute-start(f32[256,128]{1,0:T(8,128)S(1)} %get-tuple-element.60), channel_id=1, source_target_pairs={{28,0},{24,4},{20,8},{16,12},{12,16},{8,20},{4,24},{0,28},{29,1},{... | collective-permute-start | bytes 393224 | tf_op jit(solution)/shard_map/ppermute | solution.py:649
  20.5 8.9 %collective-permute-start.11 = (f32[256,128]{1,0:T(8,128)S(1)}, f32[256,128]{1,0:T(8,128)S(1)}, u32[]{:S(2)}, u32[]{:S(2)}) collective-permute-start(f32[256,128]{1,0:T(8,128)S(1)} %get-tuple-element.60), channel_id=1, source_target_pairs={{8,0},{12,4},{0,8},{4,12},{24,16},{28,20},{16,24},{20,28},{9,1},{1... | collective-permute-start | bytes 393224 | tf_op jit(solution)/shard_map/ppermute | solution.py:649
  20.5 6.4 %collective-permute-start.7 = (f32[14,8,128]{2,1,0:T(8,128)S(1)}, f32[14,8,128]{2,1,0:T(8,128)S(1)}, u32[]{:S(2)}, u32[]{:S(2)}) collective-permute-start(f32[14,8,128]{2,1,0:T(8,128)S(1)} %shard_map.139), channel_id=1, source_target_pairs={{2,0},{3,1},{0,2},{1,3},{6,4},{7,5},{4,6},{5,7},{10,8},{11,9},{8,1... | collective-permute-start | bytes 172040 | tf_op jit(solution)/shard_map/ppermute | solution.py:655
  28.2 1.4 %collective-permute-start.12 = (f32[256,128]{1,0:T(8,128)S(1)}, f32[256,128]{1,0:T(8,128)S(1)}, u32[]{:S(2)}, u32[]{:S(2)}) collective-permute-start(f32[256,128]{1,0:T(8,128)S(1)} %shard_map.142), channel_id=1, source_target_pairs={{8,0},{12,4},{0,8},{4,12},{24,16},{28,20},{16,24},{20,28},{9,1},{1... | collective-permute-start | bytes 393224 | tf_op jit(solution)/shard_map/ppermute | solution.py:649
  43.6 1.3 %collective-permute-start.13 = (f32[32,8,128]{2,1,0:T(8,128)S(1)}, f32[32,8,128]{2,1,0:T(8,128)S(1)}, u32[]{:S(2)}, u32[]{:S(2)}) collective-permute-start(f32[32,8,128]{2,1,0:T(8,128)S(1)} %all_to_all.5.mine), channel_id=1, source_target_pairs={{8,0},{12,4},{0,8},{4,12},{24,16},{28,20},{16,24},{20,28},{9,1},{1... | collective-permute-start | bytes 393224 | tf_op jit(solution)/shard_map/ppermute | solution.py:649

commit v15 on v14

--- a/solution.py
+++ b/solution.py
@@ -422,8 +422,7 @@
 def first_kernel(s, part, fh, fl, own, rims, col, *refs):
     *layers, u_out, charges_out, values_out = refs
     count = 2 + len(s.sources)
-    parts = layers[: s.levels + 1]
-    layers = [[part[at + k] for k in range(count)] for part in parts for at in range(0, part.shape[0], count)]
+    layers = [[part[at + k] for k in range(count)] for part in layers for at in range(0, part.shape[0], count)]
     weight_col = col[:, :1]
     occ = own[...]
     potentials = far_potentials(s, layers, (fh[...], fl[...]))
@@ -649,20 +648,23 @@
         return lax.ppermute(x, ("gx", "gy"), pairs)
 
     def fetch_layers(x):
-        parts = [x]
+        parts, sent = [x], [x]
         for level in range(s.levels):
             pairs = [(z ^ (1 << level), z) for z in range(s.nz)]
-            parts.append(lax.ppermute(x, "gz", pairs))
+            parts.append(lax.ppermute(sent[-1], "gz", pairs))
             if level + 1 < s.levels:
-                (x,) = call(join_kernel, [((2 * x.shape[0],) + tile, f32)], [x, parts[-1]])
-        return parts
-
-    def fetch_rims(rim):
+                shape = (2 * sent[-1].shape[0],) + tile
+                sent += call(join_kernel, [(shape, f32)], [sent[-1], parts[-1]])
+        return parts, sent[-1]
+
+    def fetch_rims(rim, after=None):
         got = {}
         for dy in s.shifts:
             got["other", dy] = fetch(rim, "other", dy)
         for dy in s.shifts:
             got["same", dy] = fetch(rim, "same", dy)
+        if after is not None:
+            (rim,) = call(order_kernel, [(rim.shape, f32)], [rim, after])
         got["other", 0] = fetch(rim, "other", 0)
         got["partner", 0] = fetch(rim, "partner", 0)
         return got
@@ -735,19 +737,18 @@
         [((2 + len(around),) + tile, f32)],
         [message] + sums + around + [gathered[1]],
     )
-    layers = fetch_layers(tiles)
-    got = fetch_rims(rim)
+    layers, joined = fetch_layers(tiles)
+    got = fetch_rims(rim, joined)
     places = call(
         functools.partial(place_kernel, s),
         [((s.skel, s.bodies), bf16), ((s.ghosts // LANES, s.skel, LANES), bf16)],
         [cells, tiles],
         flops=2 * 10**10,
     )
-    ahead = [got["other", 0]] + [got[kind, dy] for kind in ("other", "same") for dy in s.shifts]
     u, charges, values = call(
         functools.partial(first_kernel, s),
         [(full, f32), (tile, f32), ((s.ghosts // LANES,) + tile, f32)],
-        [part, fh, fl, *places, col, *layers] + ahead,
+        [part, fh, fl, *places, col, *layers],
         flops=10**8,
     )
     loc, gat, ortho, stat = call(

time: 49.6 us -> 48.3 us (0.974)
  blocking collectives: 12 us -> 11.2 us
    all_to_all x1, blocking collectives: 12 us -> 11.2 us  [body(): boxes = lax.all_to_all(packed, ('gx', 'gy', 'gz'), 0, 0)]
    ppermute x2, waiting for transfers between devices: 3.65 us -> 2.99 us  [fetch_layers(): parts.append(lax.ppermute(sent[-1], 'gz', pairs))]
    pallas_call x15 -> x16, Pallas kernels: 16.9 us -> 16.9 us  [call(): pl.pallas_call(kernel, out_shape=[jax.ShapeDtypeStruct(shape, kind) for s...]
  transfers between devices with their start and end apart: 14 -> 14, of which waited for: 6 -> 5; matrix products, arithmetic and copies ran while one was open for 0% -> 0% of each run, Pallas kernels for 19% -> 19%
where the time goes in v15:
time: 48.3 us; the launch traced here: 48.1 us
  Pallas kernels  16.9 us (35%)
  starting transfers between devices  12.7 us (26%)
  blocking collectives  11.2 us (23%)
  waiting for transfers between devices  6.46 us (13%)
  between operations  0.76 us (2%)
    pallas_call x16, Pallas kernels, call(): pl.pallas_call(kernel, out_shape=[jax.ShapeDtypeStruct(shape, kind) for s...  16.9 us
    all_to_all x1, blocking collectives, body(): boxes = lax.all_to_all(packed, ('gx', 'gy', 'gz'), 0, 0)  11.2 us
    ppermute x12, starting transfers between devices, fetch(): return lax.ppermute(x, ('gx', 'gy'), pairs)  8.45 us
    ppermute x2, starting transfers between devices, fetch_layers(): parts.append(lax.ppermute(sent[-1], 'gz', pairs))  4.23 us
    ppermute x12, waiting for transfers between devices, fetch(): return lax.ppermute(x, ('gx', 'gy'), pairs)  3.47 us
    ppermute x2, waiting for transfers between devices, fetch_layers(): parts.append(lax.ppermute(sent[-1], 'gz', pairs))  2.99 us
  transfers between devices with their start and end apart: 14, of which 5 were waited for; matrix products, arithmetic and copies ran while one was open for 0% of the time, Pallas kernels for 19%

profile of v15, /device:TPU:0, one launch (start us, length us, event | category | flops | bytes accessed | tf_op | source)
XLA Modules:
  0.0 48.1 jit_solution(2976465983028793395)
XLA Ops:
  0.6 1.4 %shard_map.131 = (f32[264,128]{1,0:T(8,128)S(1)}, f32[168,128]{1,0:T(8,128)S(1)}, s32[1,1,256]{2,1,0:T(1,128)S(1)}, f32[512,256]{1,0:T(8,128)S(1)}) custom-call(f32[486,1,256]{2,1,0:T(1,128)} %bitcast.9, s32[1,1,256]{2,1,0:T(1,128)} %cells.1, f32[1,162]{1,0:T(1,128)} %bitcast.10), custom_call_target="tpu_custom_call" | custom-call | flops 10000000 | bytes 1048576 | tf_op jit(solution)/shard_map/pallas_call | solution.py:620
  2.1 3.0 %collective-permute-start = (f32[264,128]{1,0:T(8,128)S(1)}, f32[264,128]{1,0:T(8,128)S(1)}, u32[]{:S(2)}, u32[]{:S(2)}) collective-permute-start(f32[264,128]{1,0:T(8,128)S(1)} %get-tuple-element.49.refs_0_.message.charges_f), channel_id=1, source_target_pairs={{4,0},{0,4},{12,8},{8,12},{20,16},{16,20},{28,24},{24,28},{5,1},{1... | collective-permute-start | bytes 405512 | tf_op jit(solution)/shard_map/ppermute | solution.py:648
  5.1 0.7 %collective-permute-start.1 = (f32[264,128]{1,0:T(8,128)S(1)}, f32[264,128]{1,0:T(8,128)S(1)}, u32[]{:S(2)}, u32[]{:S(2)}) collective-permute-start(f32[264,128]{1,0:T(8,128)S(1)} %get-tuple-element.49.refs_0_.message.charges_f), channel_id=1, source_target_pairs={{24,0},{28,4},{16,8},{20,12},{8,16},{12,20},{0,24},{4,28},{25,1},{... | collective-permute-start | bytes 405512 | tf_op jit(solution)/shard_map/ppermute | solution.py:648
  5.7 0.6 %collective-permute-start.2 = (f32[264,128]{1,0:T(8,128)S(1)}, f32[264,128]{1,0:T(8,128)S(1)}, u32[]{:S(2)}, u32[]{:S(2)}) collective-permute-start(f32[264,128]{1,0:T(8,128)S(1)} %get-tuple-element.49.refs_0_.message.charges_f), channel_id=1, source_target_pairs={{28,0},{24,4},{20,8},{16,12},{12,16},{8,20},{4,24},{0,28},{29,1},{... | collective-permute-start | bytes 405512 | tf_op jit(solution)/shard_map/ppermute | solution.py:648
  6.3 0.4 collective-permute-start.3
  6.7 0.1 pad_add_fusion.ids
  6.8 5.6 %shard_map.132 = (f32[512,256]{1,0:T(8,128)S(1)}, f32[512,256]{1,0:T(8,128)S(1)}, f32[16,256]{1,0:T(8,128)S(1)}, bf16[512,512]{1,0:T(8,128)(2,1)S(1)}, bf16[512,...) custom-call(s32[2]{0:T(128)S(1)} %pad_add_fusion.ids, ...), custom_call_target="tpu_custom_call" | custom-call | flops 5000000000 | bytes 1048576 | tf_op jit(solution)/shard_map/pallas_call | solution.py:620
  12.4 0.0 collective-permute-done.x.refs_1_.refs_0_.refs_2_
  12.5 0.2 collective-permute-start.4
  12.7 1.1 %collective-permute-done.1.refs_2_.refs_1_.refs_3_ = f32[264,128]{1,0:T(8,128)S(1)} collective-permute-done((f32[264,128]{1,0:T(8,128)S(1)}, f32[264,128]{1,0:T(8,128)S(1)}, u32[]{:S(2)}, u32[]{:S(2)}) %collective-permute-start.1) | collective-permute-done | bytes 135200 | tf_op jit(solution)/shard_map/ppermute | solution.py:648
  13.8 0.2 collective-permute-start.5
  14.0 0.7 %shard_map.135 = (bf16[512,256]{1,0:T(8,128)(2,1)S(1)}, bf16[512,256]{1,0:T(8,128)(2,1)S(1)}) custom-call(f32[512,256]{1,0:T(8,128)S(1)} %get-tuple-element.46.gat, bf16[384,256]{1,0:T(8,128)(2,1)S(1)} %get-tuple-element.47.gh, bf16[384,256]{1,0:T(8,128)(2,1)S(1)} %get-tuple-element.48.gl, f32[264,128]{1,0:T(8,128)S(1)} %collective-permute-done.x.refs_1_.refs_0_.refs_2_, ...), custom_call_target="tpu_custom_call" | custom-call | flops 1000000000 | bytes 1048576 | tf_op jit(solution)/shard_map/pallas_call | solution.py:620
  14.7 0.4 collective-permute-done.5.refs_1_
  15.0 1.6 %collective-permute-start.6 = (f32[7,8,128]{2,1,0:T(8,128)S(1)}, f32[7,8,128]{2,1,0:T(8,128)S(1)}, u32[]{:S(2)}, u32[]{:S(2)}) collective-permute-start(f32[7,8,128]{2,1,0:T(8,128)S(1)} %shard_map.137.tiles.x.refs_0_), channel_id=1, source_target_pairs={{1,0},{0,1},{3,2},{2,3},{5,4},{4,5},{7,6},{6,7},{9,8},{8,9},{11,10... | collective-permute-start | bytes 86024 | tf_op jit(solution)/shard_map/ppermute | solution.py:654
  16.6 0.6 %shard_map.136 = (f32[512,256]{1,0:T(8,128)S(1)}, f32[256,128]{1,0:T(8,128)S(1)}) custom-call(f32[512,256]{1,0:T(8,128)S(1)} %get-tuple-element.43.loc, bf16[512,512]{1,0:T(8,128)(2,1)S(1)} %get-tuple-element.44.nh, bf16[512,512]{1,0:T(8,128)(2,1)S(1)} %get-tuple-element.45.nl, bf16[512,256]{1,0:T(8,128)(2,1)S(1)} %get-tuple-element.51.hi, ...), custom_call_target="tpu_custom_call" | custom-call | flops 1000000000 | bytes 1048576 | tf_op jit(solution)/shard_map/pallas_call | solution.py:620
  17.2 1.4 %collective-permute-start.8 = (f32[256,128]{1,0:T(8,128)S(1)}, f32[256,128]{1,0:T(8,128)S(1)}, u32[]{:S(2)}, u32[]{:S(2)}) collective-permute-start(f32[256,128]{1,0:T(8,128)S(1)} %get-tuple-element.68.x), channel_id=1, source_target_pairs={{4,0},{0,4},{12,8},{8,12},{20,16},{16,20},{28,24},{24,28},{5,1},{1... | collective-permute-start | bytes 393224 | tf_op jit(solution)/shard_map/ppermute | solution.py:648
  18.7 0.9 %collective-permute-start.10 = (f32[256,128]{1,0:T(8,128)S(1)}, f32[256,128]{1,0:T(8,128)S(1)}, u32[]{:S(2)}, u32[]{:S(2)}) collective-permute-start(f32[256,128]{1,0:T(8,128)S(1)} %get-tuple-element.68.x), channel_id=1, source_target_pairs={{28,0},{24,4},{20,8},{16,12},{12,16},{8,20},{4,24},{0,28},{29,1},{... | collective-permute-start | bytes 393224 | tf_op jit(solution)/shard_map/ppermute | solution.py:648
  19.6 2.7 %collective-permute-start.7 = (f32[14,8,128]{2,1,0:T(8,128)S(1)}, f32[14,8,128]{2,1,0:T(8,128)S(1)}, u32[]{:S(2)}, u32[]{:S(2)}) collective-permute-start(f32[14,8,128]{2,1,0:T(8,128)S(1)} %shard_map.139._), channel_id=1, source_target_pairs={{2,0},{3,1},{0,2},{1,3},{6,4},{7,5},{4,6},{5,7},{10,8},{11,9},{8,1... | collective-permute-start | bytes 172040 | tf_op jit(solution)/shard_map/ppermute | solution.py:654
  22.2 0.1 shard_map.138
  22.3 0.5 %collective-permute-start.11 = (f32[256,128]{1,0:T(8,128)S(1)}, f32[256,128]{1,0:T(8,128)S(1)}, u32[]{:S(2)}, u32[]{:S(2)}) collective-permute-start(f32[256,128]{1,0:T(8,128)S(1)} %shard_map.142), channel_id=1, source_target_pairs={{8,0},{12,4},{0,8},{4,12},{24,16},{28,20},{16,24},{20,28},{9,1},{1... | collective-permute-start | bytes 393224 | tf_op jit(solution)/shard_map/ppermute | solution.py:648
  22.9 0.3 collective-permute-start.9
  23.2 3.0 %collective-permute-done.7.refs_2_ = f32[14,8,128]{2,1,0:T(8,128)S(1)} collective-permute-done((f32[14,8,128]{2,1,0:T(8,128)S(1)}, f32[14,8,128]{2,1,0:T(8,128)S(1)}, u32[]{:S(2)}, u32[]{:S(2)}) %collective-permute-start.7) | collective-permute-done | bytes 57376 | tf_op jit(solution)/shard_map/ppermute | solution.py:654
  26.2 1.0 %shard_map.140 = (f32[512,256]{1,0:T(8,128)S(1)}, f32[8,128]{1,0:T(8,128)S(1)}, f32[3,8,128]{2,1,0:T(8,128)S(1)}) custom-call(f32[512,256]{1,0:T(8,128)S(1)} %get-tuple-element.53.part, bf16[192,1536]{1,0:T(8,128)(2,1)S(1)} %get-tuple-element.54.fh, bf16[192,1536]{1,0:T(8,128)(2,1)S(1)} %get-tuple-element.55.fl, bf16[192,256]{1,0:T(8,128)(2,1)S(1)} %get-tuple-element.57.own, ...), custom_call_target="tpu_custom_call" | custom-call | flops 100000000 | bytes 1048576 | tf_op jit(solution)/shard_map/pallas_call | solution.py:620
  27.2 0.2 collective-permute-start.12
  27.4 1.0 %shard_map.141 = (f32[512,256]{1,0:T(8,128)S(1)}, f32[512,256]{1,0:T(8,128)S(1)}, f32[512,256]{1,0:T(8,128)S(1)}, f32[8,128]{1,0:T(8,128)S(1)}) custom-call(f32[512,256]{1,0:T(8,128)S(1)} %get-tuple-element.60.u_in, f32[512,256]{1,0:T(8,128)S(1)} %get-tuple-element.42.f_in, f32[16,256]{1,0:T(8,128)S(1)} %get-tuple-element.50._.refs_4_.rot, ...), custom_call_target="tpu_custom_call" | custom-call | flops 1000000000 | bytes 1048576 | tf_op jit(solution)/shard_map/pallas_call | solution.py:620
  28.5 0.7 %collective-permute-done.9.refs_1_ = f32[256,128]{1,0:T(8,128)S(1)} collective-permute-done((f32[256,128]{1,0:T(8,128)S(1)}, f32[256,128]{1,0:T(8,128)S(1)}, u32[]{:S(2)}, u32[]{:S(2)}) %collective-permute-start.9) | collective-permute-done | bytes 131104 | tf_op jit(solution)/shard_map/ppermute | solution.py:648
  29.2 0.7 %shard_map.144 = (bf16[512,256]{1,0:T(8,128)(2,1)S(1)}, bf16[512,256]{1,0:T(8,128)(2,1)S(1)}) custom-call(f32[512,256]{1,0:T(8,128)S(1)} %get-tuple-element.66.gat, bf16[384,256]{1,0:T(8,128)(2,1)S(1)} %get-tuple-element.47.gh, bf16[384,256]{1,0:T(8,128)(2,1)S(1)} %get-tuple-element.48.gl, f32[168,128]{1,0:T(8,128)S(1)} %get-tuple-element.59.col, ...), custom_call_target="tpu_custom_call" | custom-call | flops 1000000000 | bytes 1048576 | tf_op jit(solution)/shard_map/pallas_call | solution.py:620
  29.9 1.3 %shard_map.145 = f32[32,8,128]{2,1,0:T(8,128)S(1)} custom-call(f32[512,256]{1,0:T(8,128)S(1)} %get-tuple-element.65.loc, bf16[512,512]{1,0:T(8,128)(2,1)S(1)} %get-tuple-element.44.nh, bf16[512,512]{1,0:T(8,128)(2,1)S(1)} %get-tuple-element.45.nl, bf16[512,256]{1,0:T(8,128)(2,1)S(1)} %get-tuple-element.70.hi, bf16[512,256]{1,0:T(8,128)(2,1)S(1)} %get-tuple-element.71.lo, ...), custom_call_target="tpu_custom_call" | custom-call | flops 1000000000 | bytes 1048576 | tf_op jit(solution)/shard_map/pallas_call | solution.py:620
  31.2 11.2 %all_to_all.5.mine = f32[32,8,128]{2,1,0:T(8,128)S(1)} all-to-all(f32[32,8,128]{2,1,0:T(8,128)S(1)} %shard_map.145), channel_id=1, replica_groups=mesh['gx'=4,'gy'=2,'gz'=4] {'gx','gy','gz'}, dimensions={0} | all-to-all | bytes 262144 | tf_op jit(solution)/shard_map/all_to_all | solution.py:773
  42.4 0.1 collective-permute-start.13
  42.5 1.2 %collective-permute-done.13.other = f32[32,8,128]{2,1,0:T(8,128)S(1)} collective-permute-done((f32[32,8,128]{2,1,0:T(8,128)S(1)}, f32[32,8,128]{2,1,0:T(8,128)S(1)}, u32[]{:S(2)}, u32[]{:S(2)}) %collective-permute-start.13) | collective-permute-done | bytes 131104 | tf_op jit(solution)/shard_map/ppermute | solution.py:648
  43.8 4.4 %shard_map.146 = (f32[486,1,256]{2,1,0:T(1,128)}, f32[1,1]{1,0:T(1,128)}) custom-call(s32[2]{0:T(128)S(1)} %pad_add_fusion.ids, f32[512,256]{1,0:T(8,128)S(1)} %get-tuple-element.42.f_in, f32[512,256]{1,0:T(8,128)S(1)} %get-tuple-element.60.u_in, f32[32,8,128]{2,1,0:T(8,128)S(1)} %all_to_all.5.mine, f32[32,8,128]{2,1,0:T(8,128)S(1)} %collective-permute-done.13.other, ...), custom_call_target="tpu_custom_call" | custom-call | flops 10000000 | bytes 1048576 | tf_op jit(solution)/shard_map/pallas_call | solution.py:620
  (14 shorter events, 0.1 us)
Async XLA Ops:
  2.1 10.4 %collective-permute-start = (f32[264,128]{1,0:T(8,128)S(1)}, f32[264,128]{1,0:T(8,128)S(1)}, u32[]{:S(2)}, u32[]{:S(2)}) collective-permute-start(f32[264,128]{1,0:T(8,128)S(1)} %get-tuple-element.49.refs_0_.message.charges_f), channel_id=1, source_target_pairs={{4,0},{0,4},{12,8},{8,12},{20,16},{16,20},{28,24},{24,28},{5,1},{1... | collective-permute-start | bytes 405512 | tf_op jit(solution)/shard_map/ppermute | solution.py:648
  5.1 8.7 %collective-permute-start.1 = (f32[264,128]{1,0:T(8,128)S(1)}, f32[264,128]{1,0:T(8,128)S(1)}, u32[]{:S(2)}, u32[]{:S(2)}) collective-permute-start(f32[264,128]{1,0:T(8,128)S(1)} %get-tuple-element.49.refs_0_.message.charges_f), channel_id=1, source_target_pairs={{24,0},{28,4},{16,8},{20,12},{8,16},{12,20},{0,24},{4,28},{25,1},{... | collective-permute-start | bytes 405512 | tf_op jit(solution)/shard_map/ppermute | solution.py:648
  5.7 8.0 %collective-permute-start.2 = (f32[264,128]{1,0:T(8,128)S(1)}, f32[264,128]{1,0:T(8,128)S(1)}, u32[]{:S(2)}, u32[]{:S(2)}) collective-permute-start(f32[264,128]{1,0:T(8,128)S(1)} %get-tuple-element.49.refs_0_.message.charges_f), channel_id=1, source_target_pairs={{28,0},{24,4},{20,8},{16,12},{12,16},{8,20},{4,24},{0,28},{29,1},{... | collective-permute-start | bytes 405512 | tf_op jit(solution)/shard_map/ppermute | solution.py:648
  6.3 7.6 %collective-permute-start.3 = (f32[264,128]{1,0:T(8,128)S(1)}, f32[264,128]{1,0:T(8,128)S(1)}, u32[]{:S(2)}, u32[]{:S(2)}) collective-permute-start(f32[264,128]{1,0:T(8,128)S(1)} %get-tuple-element.49.refs_0_.message.charges_f), channel_id=1, source_target_pairs={{8,0},{12,4},{0,8},{4,12},{24,16},{28,20},{16,24},{20,28},{9,1},{1... | collective-permute-start | bytes 405512 | tf_op jit(solution)/shard_map/ppermute | solution.py:648
  12.5 1.5 %collective-permute-start.4 = (f32[264,128]{1,0:T(8,128)S(1)}, f32[264,128]{1,0:T(8,128)S(1)}, u32[]{:S(2)}, u32[]{:S(2)}) collective-permute-start(f32[264,128]{1,0:T(8,128)S(1)} %shard_map.133), channel_id=1, source_target_pairs={{8,0},{12,4},{0,8},{4,12},{24,16},{28,20},{16,24},{20,28},{9,1},{1... | collective-permute-start | bytes 405512 | tf_op jit(solution)/shard_map/ppermute | solution.py:648
  13.8 1.2 %collective-permute-start.5 = (f32[8,128]{1,0:T(8,128)S(1)}, f32[8,128]{1,0:T(8,128)S(1)}, u32[]{:S(2)}, u32[]{:S(2)}) collective-permute-start(f32[8,128]{1,0:T(8,128)S(1)} %shard_map.134.refs_5_.refs_0_), channel_id=1, source_target_pairs={{8,0},{12,4},{0,8},{4,12},{24,16},{28,20},{16,24},{20,28},{9,1},{1... | collective-permute-start | bytes 12296 | tf_op jit(solution)/shard_map/ppermute | solution.py:648
  15.0 4.5 %collective-permute-start.6 = (f32[7,8,128]{2,1,0:T(8,128)S(1)}, f32[7,8,128]{2,1,0:T(8,128)S(1)}, u32[]{:S(2)}, u32[]{:S(2)}) collective-permute-start(f32[7,8,128]{2,1,0:T(8,128)S(1)} %shard_map.137.tiles.x.refs_0_), channel_id=1, source_target_pairs={{1,0},{0,1},{3,2},{2,3},{5,4},{4,5},{7,6},{6,7},{9,8},{8,9},{11,10... | collective-permute-start | bytes 86024 | tf_op jit(solution)/shard_map/ppermute | solution.py:654
  17.2 10.0 %collective-permute-start.8 = (f32[256,128]{1,0:T(8,128)S(1)}, f32[256,128]{1,0:T(8,128)S(1)}, u32[]{:S(2)}, u32[]{:S(2)}) collective-permute-start(f32[256,128]{1,0:T(8,128)S(1)} %get-tuple-element.68.x), channel_id=1, source_target_pairs={{4,0},{0,4},{12,8},{8,12},{20,16},{16,20},{28,24},{24,28},{5,1},{1... | collective-permute-start | bytes 393224 | tf_op jit(solution)/shard_map/ppermute | solution.py:648
  18.7 9.8 %collective-permute-start.10 = (f32[256,128]{1,0:T(8,128)S(1)}, f32[256,128]{1,0:T(8,128)S(1)}, u32[]{:S(2)}, u32[]{:S(2)}) collective-permute-start(f32[256,128]{1,0:T(8,128)S(1)} %get-tuple-element.68.x), channel_id=1, source_target_pairs={{28,0},{24,4},{20,8},{16,12},{12,16},{8,20},{4,24},{0,28},{29,1},{... | collective-permute-start | bytes 393224 | tf_op jit(solution)/shard_map/ppermute | solution.py:648
  19.6 6.6 %collective-permute-start.7 = (f32[14,8,128]{2,1,0:T(8,128)S(1)}, f32[14,8,128]{2,1,0:T(8,128)S(1)}, u32[]{:S(2)}, u32[]{:S(2)}) collective-permute-start(f32[14,8,128]{2,1,0:T(8,128)S(1)} %shard_map.139._), channel_id=1, source_target_pairs={{2,0},{3,1},{0,2},{1,3},{6,4},{7,5},{4,6},{5,7},{10,8},{11,9},{8,1... | collective-permute-start | bytes 172040 | tf_op jit(solution)/shard_map/ppermute | solution.py:654
  22.3 6.1 %collective-permute-start.11 = (f32[256,128]{1,0:T(8,128)S(1)}, f32[256,128]{1,0:T(8,128)S(1)}, u32[]{:S(2)}, u32[]{:S(2)}) collective-permute-start(f32[256,128]{1,0:T(8,128)S(1)} %shard_map.142), channel_id=1, source_target_pairs={{8,0},{12,4},{0,8},{4,12},{24,16},{28,20},{16,24},{20,28},{9,1},{1... | collective-permute-start | bytes 393224 | tf_op jit(solution)/shard_map/ppermute | solution.py:648
  22.9 6.3 %collective-permute-start.9 = (f32[256,128]{1,0:T(8,128)S(1)}, f32[256,128]{1,0:T(8,128)S(1)}, u32[]{:S(2)}, u32[]{:S(2)}) collective-permute-start(f32[256,128]{1,0:T(8,128)S(1)} %shard_map.142), channel_id=1, source_target_pairs={{24,0},{28,4},{16,8},{20,12},{8,16},{12,20},{0,24},{4,28},{25,1},{... | collective-permute-start | bytes 393224 | tf_op jit(solution)/shard_map/ppermute | solution.py:648
  27.2 2.0 %collective-permute-start.12 = (f32[256,128]{1,0:T(8,128)S(1)}, f32[256,128]{1,0:T(8,128)S(1)}, u32[]{:S(2)}, u32[]{:S(2)}) collective-permute-start(f32[256,128]{1,0:T(8,128)S(1)} %shard_map.143), channel_id=1, source_target_pairs={{8,0},{12,4},{0,8},{4,12},{24,16},{28,20},{16,24},{20,28},{9,1},{1... | collective-permute-start | bytes 393224 | tf_op jit(solution)/shard_map/ppermute | solution.py:648
  42.4 1.3 %collective-permute-start.13 = (f32[32,8,128]{2,1,0:T(8,128)S(1)}, f32[32,8,128]{2,1,0:T(8,128)S(1)}, u32[]{:S(2)}, u32[]{:S(2)}) collective-permute-start(f32[32,8,128]{2,1,0:T(8,128)S(1)} %all_to_all.5.mine), channel_id=1, source_target_pairs={{8,0},{12,4},{0,8},{4,12},{24,16},{28,20},{16,24},{20,28},{9,1},{1... | collective-permute-start | bytes 393224 | tf_op jit(solution)/shard_map/ppermute | solution.py:648

commit v16 on v15

--- a/solution.py
+++ b/solution.py
@@ -659,13 +659,12 @@
 
     def fetch_rims(rim, after=None):
         got = {}
-        for dy in s.shifts:
+        for dy in [0] + s.shifts:
             got["other", dy] = fetch(rim, "other", dy)
+        if after is not None:
+            (rim,) = call(order_kernel, [(rim.shape, f32)], [rim, after])
         for dy in s.shifts:
             got["same", dy] = fetch(rim, "same", dy)
-        if after is not None:
-            (rim,) = call(order_kernel, [(rim.shape, f32)], [rim, after])
-        got["other", 0] = fetch(rim, "other", 0)
         got["partner", 0] = fetch(rim, "partner", 0)
         return got
 
@@ -692,7 +691,7 @@
         scratch=[pltpu.VMEM(flat, f32), pltpu.VMEM(small, f32), pltpu.SemaphoreType.DMA((3,))],
         flops=10**7,
     )
-    got = fetch_rims(message)
+    got = fetch_rims(message, message)
     operators = [
         angles.reshape(3, 1, s.bodies), near_weight, neighbours, self_mob, near_mat, skel_perm, interp,
         sibling_ops, root_op,

time: 48.3 us -> 48.9 us (1.012)
    ppermute x12, waiting for transfers between devices: 3.47 us -> 4.3 us  [fetch(): return lax.ppermute(x, ('gx', 'gy'), pairs)]
    ppermute x2, waiting for transfers between devices: 2.99 us -> 2.4 us  [fetch_layers(): parts.append(lax.ppermute(sent[-1], 'gz', pairs))]
    pallas_call x16 -> x17, Pallas kernels: 16.9 us -> 16.9 us  [call(): pl.pallas_call(kernel, out_shape=[jax.ShapeDtypeStruct(shape, kind) for s...]
  transfers between devices with their start and end apart: 14 -> 14, of which waited for: 5 -> 6; matrix products, arithmetic and copies ran while one was open for 0% -> 0% of each run, Pallas kernels for 19% -> 19%
where the time goes in v16:
time: 48.9 us; the launch traced here: 48.7 us
  Pallas kernels  16.9 us (35%)
  starting transfers between devices  12.9 us (26%)
  blocking collectives  11.3 us (23%)
  waiting for transfers between devices  6.7 us (14%)
  between operations  0.78 us (2%)
    pallas_call x17, Pallas kernels, call(): pl.pallas_call(kernel, out_shape=[jax.ShapeDtypeStruct(shape, kind) for s...  16.9 us
    all_to_all x1, blocking collectives, body(): boxes = lax.all_to_all(packed, ('gx', 'gy', 'gz'), 0, 0)  11.3 us
    ppermute x12, starting transfers between devices, fetch(): return lax.ppermute(x, ('gx', 'gy'), pairs)  8.63 us
    ppermute x12, waiting for transfers between devices, fetch(): return lax.ppermute(x, ('gx', 'gy'), pairs)  4.3 us
    ppermute x2, starting transfers between devices, fetch_layers(): parts.append(lax.ppermute(sent[-1], 'gz', pairs))  4.3 us
    ppermute x2, waiting for transfers between devices, fetch_layers(): parts.append(lax.ppermute(sent[-1], 'gz', pairs))  2.4 us
  transfers between devices with their start and end apart: 14, of which 6 were waited for; matrix products, arithmetic and copies ran while one was open for 0% of the time, Pallas kernels for 19%

profile of v16, /device:TPU:0, one launch (start us, length us, event | category | flops | bytes accessed | tf_op | source)
XLA Modules:
  0.0 48.7 jit_solution(8600491393705129246)
XLA Ops:
  0.6 1.4 %shard_map.131 = (f32[264,128]{1,0:T(8,128)S(1)}, f32[168,128]{1,0:T(8,128)S(1)}, s32[1,1,256]{2,1,0:T(1,128)S(1)}, f32[512,256]{1,0:T(8,128)S(1)}) custom-call(f32[486,1,256]{2,1,0:T(1,128)} %bitcast.9, s32[1,1,256]{2,1,0:T(1,128)} %cells.1, f32[1,162]{1,0:T(1,128)} %bitcast.10), custom_call_target="tpu_custom_call" | custom-call | flops 10000000 | bytes 1048576 | tf_op jit(solution)/shard_map/pallas_call | solution.py:620
  2.1 2.5 %collective-permute-start.1 = (f32[264,128]{1,0:T(8,128)S(1)}, f32[264,128]{1,0:T(8,128)S(1)}, u32[]{:S(2)}, u32[]{:S(2)}) collective-permute-start(f32[264,128]{1,0:T(8,128)S(1)} %get-tuple-element.49.x._.refs_0_.message.charges_f), channel_id=1, source_target_pairs={{24,0},{28,4},{16,8},{20,12},{8,16},{12,20},{0,24},{4,28},{25,1},{... | collective-permute-start | bytes 405512 | tf_op jit(solution)/shard_map/ppermute | solution.py:648
  4.5 1.7 %collective-permute-start.2 = (f32[264,128]{1,0:T(8,128)S(1)}, f32[264,128]{1,0:T(8,128)S(1)}, u32[]{:S(2)}, u32[]{:S(2)}) collective-permute-start(f32[264,128]{1,0:T(8,128)S(1)} %get-tuple-element.49.x._.refs_0_.message.charges_f), channel_id=1, source_target_pairs={{28,0},{24,4},{20,8},{16,12},{12,16},{8,20},{4,24},{0,28},{29,1},{... | collective-permute-start | bytes 405512 | tf_op jit(solution)/shard_map/ppermute | solution.py:648
  6.3 0.1 collective-permute-start
  6.3 0.2 collective-permute-start.3
  6.6 0.1 pad_add_fusion.ids
  6.6 5.7 %shard_map.132 = (f32[512,256]{1,0:T(8,128)S(1)}, f32[512,256]{1,0:T(8,128)S(1)}, f32[16,256]{1,0:T(8,128)S(1)}, bf16[512,512]{1,0:T(8,128)(2,1)S(1)}, bf16[512,...) custom-call(s32[2]{0:T(128)S(1)} %pad_add_fusion.ids, ...), custom_call_target="tpu_custom_call" | custom-call | flops 5000000000 | bytes 1048576 | tf_op jit(solution)/shard_map/pallas_call | solution.py:620
  12.3 1.2 %collective-permute-done.x.refs_1_.refs_0_.refs_2_ = f32[264,128]{1,0:T(8,128)S(1)} collective-permute-done((f32[264,128]{1,0:T(8,128)S(1)}, f32[264,128]{1,0:T(8,128)S(1)}, u32[]{:S(2)}, u32[]{:S(2)}) %collective-permute-start) | collective-permute-done | bytes 135200 | tf_op jit(solution)/shard_map/ppermute | solution.py:648
  13.5 0.2 collective-permute-start.4
  13.6 0.5 collective-permute-start.5
  14.1 0.8 %collective-permute-done.4.refs_4_.refs_6_ = f32[264,128]{1,0:T(8,128)S(1)} collective-permute-done((f32[264,128]{1,0:T(8,128)S(1)}, f32[264,128]{1,0:T(8,128)S(1)}, u32[]{:S(2)}, u32[]{:S(2)}) %collective-permute-start.4) | collective-permute-done | bytes 135200 | tf_op jit(solution)/shard_map/ppermute | solution.py:648
  14.9 0.7 %shard_map.136 = (bf16[512,256]{1,0:T(8,128)(2,1)S(1)}, bf16[512,256]{1,0:T(8,128)(2,1)S(1)}) custom-call(f32[512,256]{1,0:T(8,128)S(1)} %get-tuple-element.46.gat, bf16[384,256]{1,0:T(8,128)(2,1)S(1)} %get-tuple-element.47.gh, bf16[384,256]{1,0:T(8,128)(2,1)S(1)} %get-tuple-element.48.gl, f32[264,128]{1,0:T(8,128)S(1)} %collective-permute-done.x.refs_1_.refs_0_.refs_2_, ...), custom_call_target="tpu_custom_call" | custom-call | flops 1000000000 | bytes 1048576 | tf_op jit(solution)/shard_map/pallas_call | solution.py:620
  15.6 1.6 %collective-permute-start.6 = (f32[7,8,128]{2,1,0:T(8,128)S(1)}, f32[7,8,128]{2,1,0:T(8,128)S(1)}, u32[]{:S(2)}, u32[]{:S(2)}) collective-permute-start(f32[7,8,128]{2,1,0:T(8,128)S(1)} %shard_map.138.tiles.x.refs_0_), channel_id=1, source_target_pairs={{1,0},{0,1},{3,2},{2,3},{5,4},{4,5},{7,6},{6,7},{9,8},{8,9},{11,10... | collective-permute-start | bytes 86024 | tf_op jit(solution)/shard_map/ppermute | solution.py:654
  17.2 0.6 %shard_map.137 = (f32[512,256]{1,0:T(8,128)S(1)}, f32[256,128]{1,0:T(8,128)S(1)}) custom-call(f32[512,256]{1,0:T(8,128)S(1)} %get-tuple-element.43.loc, bf16[512,512]{1,0:T(8,128)(2,1)S(1)} %get-tuple-element.44.nh, bf16[512,512]{1,0:T(8,128)(2,1)S(1)} %get-tuple-element.45.nl, bf16[512,256]{1,0:T(8,128)(2,1)S(1)} %get-tuple-element.51.hi, ...), custom_call_target="tpu_custom_call" | custom-call | flops 1000000000 | bytes 1048576 | tf_op jit(solution)/shard_map/pallas_call | solution.py:620
  17.9 1.8 %collective-permute-start.10 = (f32[256,128]{1,0:T(8,128)S(1)}, f32[256,128]{1,0:T(8,128)S(1)}, u32[]{:S(2)}, u32[]{:S(2)}) collective-permute-start(f32[256,128]{1,0:T(8,128)S(1)} %get-tuple-element.68.x), channel_id=1, source_target_pairs={{28,0},{24,4},{20,8},{16,12},{12,16},{8,20},{4,24},{0,28},{29,1},{... | collective-permute-start | bytes 393224 | tf_op jit(solution)/shard_map/ppermute | solution.py:648
  19.7 0.9 %collective-permute-start.9 = (f32[256,128]{1,0:T(8,128)S(1)}, f32[256,128]{1,0:T(8,128)S(1)}, u32[]{:S(2)}, u32[]{:S(2)}) collective-permute-start(f32[256,128]{1,0:T(8,128)S(1)} %get-tuple-element.68.x), channel_id=1, source_target_pairs={{24,0},{28,4},{16,8},{20,12},{8,16},{12,20},{0,24},{4,28},{25,1},{... | collective-permute-start | bytes 393224 | tf_op jit(solution)/shard_map/ppermute | solution.py:648
  20.6 2.7 %collective-permute-start.7 = (f32[14,8,128]{2,1,0:T(8,128)S(1)}, f32[14,8,128]{2,1,0:T(8,128)S(1)}, u32[]{:S(2)}, u32[]{:S(2)}) collective-permute-start(f32[14,8,128]{2,1,0:T(8,128)S(1)} %shard_map.140._), channel_id=1, source_target_pairs={{2,0},{3,1},{0,2},{1,3},{6,4},{7,5},{4,6},{5,7},{10,8},{11,9},{8,1... | collective-permute-start | bytes 172040 | tf_op jit(solution)/shard_map/ppermute | solution.py:654
  23.3 0.5 %collective-permute-start.8 = (f32[256,128]{1,0:T(8,128)S(1)}, f32[256,128]{1,0:T(8,128)S(1)}, u32[]{:S(2)}, u32[]{:S(2)}) collective-permute-start(f32[256,128]{1,0:T(8,128)S(1)} %shard_map.143), channel_id=1, source_target_pairs={{4,0},{0,4},{12,8},{8,12},{20,16},{16,20},{28,24},{24,28},{5,1},{1... | collective-permute-start | bytes 393224 | tf_op jit(solution)/shard_map/ppermute | solution.py:648
  23.8 0.1 shard_map.139
  23.9 0.1 collective-permute-start.11
  24.0 2.4 %collective-permute-done.7.refs_2_ = f32[14,8,128]{2,1,0:T(8,128)S(1)} collective-permute-done((f32[14,8,128]{2,1,0:T(8,128)S(1)}, f32[14,8,128]{2,1,0:T(8,128)S(1)}, u32[]{:S(2)}, u32[]{:S(2)}) %collective-permute-start.7) | collective-permute-done | bytes 57376 | tf_op jit(solution)/shard_map/ppermute | solution.py:654
  26.4 1.0 %shard_map.141 = (f32[512,256]{1,0:T(8,128)S(1)}, f32[8,128]{1,0:T(8,128)S(1)}, f32[3,8,128]{2,1,0:T(8,128)S(1)}) custom-call(f32[512,256]{1,0:T(8,128)S(1)} %get-tuple-element.53.part, bf16[192,1536]{1,0:T(8,128)(2,1)S(1)} %get-tuple-element.54.fh, bf16[192,1536]{1,0:T(8,128)(2,1)S(1)} %get-tuple-element.55.fl, bf16[192,256]{1,0:T(8,128)(2,1)S(1)} %get-tuple-element.57.own, ...), custom_call_target="tpu_custom_call" | custom-call | flops 100000000 | bytes 1048576 | tf_op jit(solution)/shard_map/pallas_call | solution.py:620
  27.4 0.9 %collective-permute-done.8.x.refs_0_ = f32[256,128]{1,0:T(8,128)S(1)} collective-permute-done((f32[256,128]{1,0:T(8,128)S(1)}, f32[256,128]{1,0:T(8,128)S(1)}, u32[]{:S(2)}, u32[]{:S(2)}) %collective-permute-start.8) | collective-permute-done | bytes 131104 | tf_op jit(solution)/shard_map/ppermute | solution.py:648
  28.3 0.1 collective-permute-start.12
  28.4 1.1 %shard_map.142 = (f32[512,256]{1,0:T(8,128)S(1)}, f32[512,256]{1,0:T(8,128)S(1)}, f32[512,256]{1,0:T(8,128)S(1)}, f32[8,128]{1,0:T(8,128)S(1)}) custom-call(f32[512,256]{1,0:T(8,128)S(1)} %get-tuple-element.60.u_in, f32[512,256]{1,0:T(8,128)S(1)} %get-tuple-element.42.f_in, f32[16,256]{1,0:T(8,128)S(1)} %get-tuple-element.50._.refs_4_.rot, ...), custom_call_target="tpu_custom_call" | custom-call | flops 1000000000 | bytes 1048576 | tf_op jit(solution)/shard_map/pallas_call | solution.py:620
  29.5 0.2 collective-permute-done.12.refs_4_
  29.7 0.7 %shard_map.145 = (bf16[512,256]{1,0:T(8,128)(2,1)S(1)}, bf16[512,256]{1,0:T(8,128)(2,1)S(1)}) custom-call(f32[512,256]{1,0:T(8,128)S(1)} %get-tuple-element.66.gat, bf16[384,256]{1,0:T(8,128)(2,1)S(1)} %get-tuple-element.47.gh, bf16[384,256]{1,0:T(8,128)(2,1)S(1)} %get-tuple-element.48.gl, f32[168,128]{1,0:T(8,128)S(1)} %get-tuple-element.59.col, ...), custom_call_target="tpu_custom_call" | custom-call | flops 1000000000 | bytes 1048576 | tf_op jit(solution)/shard_map/pallas_call | solution.py:620
  30.4 1.3 %shard_map.146 = f32[32,8,128]{2,1,0:T(8,128)S(1)} custom-call(f32[512,256]{1,0:T(8,128)S(1)} %get-tuple-element.65.loc, bf16[512,512]{1,0:T(8,128)(2,1)S(1)} %get-tuple-element.44.nh, bf16[512,512]{1,0:T(8,128)(2,1)S(1)} %get-tuple-element.45.nl, bf16[512,256]{1,0:T(8,128)(2,1)S(1)} %get-tuple-element.70.hi, bf16[512,256]{1,0:T(8,128)(2,1)S(1)} %get-tuple-element.71.lo, ...), custom_call_target="tpu_custom_call" | custom-call | flops 1000000000 | bytes 1048576 | tf_op jit(solution)/shard_map/pallas_call | solution.py:620
  31.7 11.3 %all_to_all.5.mine = f32[32,8,128]{2,1,0:T(8,128)S(1)} all-to-all(f32[32,8,128]{2,1,0:T(8,128)S(1)} %shard_map.146), channel_id=1, replica_groups=mesh['gx'=4,'gy'=2,'gz'=4] {'gx','gy','gz'}, dimensions={0} | all-to-all | bytes 262144 | tf_op jit(solution)/shard_map/all_to_all | solution.py:772
  43.0 0.1 collective-permute-start.13
  43.1 1.2 %collective-permute-done.13.other = f32[32,8,128]{2,1,0:T(8,128)S(1)} collective-permute-done((f32[32,8,128]{2,1,0:T(8,128)S(1)}, f32[32,8,128]{2,1,0:T(8,128)S(1)}, u32[]{:S(2)}, u32[]{:S(2)}) %collective-permute-start.13) | collective-permute-done | bytes 131104 | tf_op jit(solution)/shard_map/ppermute | solution.py:648
  44.3 4.4 %shard_map.147 = (f32[486,1,256]{2,1,0:T(1,128)}, f32[1,1]{1,0:T(1,128)}) custom-call(s32[2]{0:T(128)S(1)} %pad_add_fusion.ids, f32[512,256]{1,0:T(8,128)S(1)} %get-tuple-element.42.f_in, f32[512,256]{1,0:T(8,128)S(1)} %get-tuple-element.60.u_in, f32[32,8,128]{2,1,0:T(8,128)S(1)} %all_to_all.5.mine, f32[32,8,128]{2,1,0:T(8,128)S(1)} %collective-permute-done.13.other, ...), custom_call_target="tpu_custom_call" | custom-call | flops 10000000 | bytes 1048576 | tf_op jit(solution)/shard_map/pallas_call | solution.py:620
  (15 shorter events, 0.1 us)
Async XLA Ops:
  2.1 11.6 %collective-permute-start.1 = (f32[264,128]{1,0:T(8,128)S(1)}, f32[264,128]{1,0:T(8,128)S(1)}, u32[]{:S(2)}, u32[]{:S(2)}) collective-permute-start(f32[264,128]{1,0:T(8,128)S(1)} %get-tuple-element.49.x._.refs_0_.message.charges_f), channel_id=1, source_target_pairs={{24,0},{28,4},{16,8},{20,12},{8,16},{12,20},{0,24},{4,28},{25,1},{... | collective-permute-start | bytes 405512 | tf_op jit(solution)/shard_map/ppermute | solution.py:648
  4.5 9.1 %collective-permute-start.2 = (f32[264,128]{1,0:T(8,128)S(1)}, f32[264,128]{1,0:T(8,128)S(1)}, u32[]{:S(2)}, u32[]{:S(2)}) collective-permute-start(f32[264,128]{1,0:T(8,128)S(1)} %get-tuple-element.49.x._.refs_0_.message.charges_f), channel_id=1, source_target_pairs={{28,0},{24,4},{20,8},{16,12},{12,16},{8,20},{4,24},{0,28},{29,1},{... | collective-permute-start | bytes 405512 | tf_op jit(solution)/shard_map/ppermute | solution.py:648
  6.3 7.2 %collective-permute-start = (f32[264,128]{1,0:T(8,128)S(1)}, f32[264,128]{1,0:T(8,128)S(1)}, u32[]{:S(2)}, u32[]{:S(2)}) collective-permute-start(f32[264,128]{1,0:T(8,128)S(1)} %shard_map.133), channel_id=1, source_target_pairs={{4,0},{0,4},{12,8},{8,12},{20,16},{16,20},{28,24},{24,28},{5,1},{1... | collective-permute-start | bytes 405512 | tf_op jit(solution)/shard_map/ppermute | solution.py:648
  6.3 7.8 %collective-permute-start.3 = (f32[264,128]{1,0:T(8,128)S(1)}, f32[264,128]{1,0:T(8,128)S(1)}, u32[]{:S(2)}, u32[]{:S(2)}) collective-permute-start(f32[264,128]{1,0:T(8,128)S(1)} %shard_map.133), channel_id=1, source_target_pairs={{8,0},{12,4},{0,8},{4,12},{24,16},{28,20},{16,24},{20,28},{9,1},{1... | collective-permute-start | bytes 405512 | tf_op jit(solution)/shard_map/ppermute | solution.py:648
  13.5 1.4 %collective-permute-start.4 = (f32[264,128]{1,0:T(8,128)S(1)}, f32[264,128]{1,0:T(8,128)S(1)}, u32[]{:S(2)}, u32[]{:S(2)}) collective-permute-start(f32[264,128]{1,0:T(8,128)S(1)} %shard_map.134), channel_id=1, source_target_pairs={{8,0},{12,4},{0,8},{4,12},{24,16},{28,20},{16,24},{20,28},{9,1},{1... | collective-permute-start | bytes 405512 | tf_op jit(solution)/shard_map/ppermute | solution.py:648
  13.6 1.9 %collective-permute-start.5 = (f32[8,128]{1,0:T(8,128)S(1)}, f32[8,128]{1,0:T(8,128)S(1)}, u32[]{:S(2)}, u32[]{:S(2)}) collective-permute-start(f32[8,128]{1,0:T(8,128)S(1)} %shard_map.135.refs_5_.refs_0_), channel_id=1, source_target_pairs={{8,0},{12,4},{0,8},{4,12},{24,16},{28,20},{16,24},{20,28},{9,1},{1... | collective-permute-start | bytes 12296 | tf_op jit(solution)/shard_map/ppermute | solution.py:648
  15.6 5.0 %collective-permute-start.6 = (f32[7,8,128]{2,1,0:T(8,128)S(1)}, f32[7,8,128]{2,1,0:T(8,128)S(1)}, u32[]{:S(2)}, u32[]{:S(2)}) collective-permute-start(f32[7,8,128]{2,1,0:T(8,128)S(1)} %shard_map.138.tiles.x.refs_0_), channel_id=1, source_target_pairs={{1,0},{0,1},{3,2},{2,3},{5,4},{4,5},{7,6},{6,7},{9,8},{8,9},{11,10... | collective-permute-start | bytes 86024 | tf_op jit(solution)/shard_map/ppermute | solution.py:654
  17.9 11.6 %collective-permute-start.10 = (f32[256,128]{1,0:T(8,128)S(1)}, f32[256,128]{1,0:T(8,128)S(1)}, u32[]{:S(2)}, u32[]{:S(2)}) collective-permute-start(f32[256,128]{1,0:T(8,128)S(1)} %get-tuple-element.68.x), channel_id=1, source_target_pairs={{28,0},{24,4},{20,8},{16,12},{12,16},{8,20},{4,24},{0,28},{29,1},{... | collective-permute-start | bytes 393224 | tf_op jit(solution)/shard_map/ppermute | solution.py:648
  19.7 9.7 %collective-permute-start.9 = (f32[256,128]{1,0:T(8,128)S(1)}, f32[256,128]{1,0:T(8,128)S(1)}, u32[]{:S(2)}, u32[]{:S(2)}) collective-permute-start(f32[256,128]{1,0:T(8,128)S(1)} %get-tuple-element.68.x), channel_id=1, source_target_pairs={{24,0},{28,4},{16,8},{20,12},{8,16},{12,20},{0,24},{4,28},{25,1},{... | collective-permute-start | bytes 393224 | tf_op jit(solution)/shard_map/ppermute | solution.py:648
  20.6 5.8 %collective-permute-start.7 = (f32[14,8,128]{2,1,0:T(8,128)S(1)}, f32[14,8,128]{2,1,0:T(8,128)S(1)}, u32[]{:S(2)}, u32[]{:S(2)}) collective-permute-start(f32[14,8,128]{2,1,0:T(8,128)S(1)} %shard_map.140._), channel_id=1, source_target_pairs={{2,0},{3,1},{0,2},{1,3},{6,4},{7,5},{4,6},{5,7},{10,8},{11,9},{8,1... | collective-permute-start | bytes 172040 | tf_op jit(solution)/shard_map/ppermute | solution.py:654
  23.3 5.0 %collective-permute-start.8 = (f32[256,128]{1,0:T(8,128)S(1)}, f32[256,128]{1,0:T(8,128)S(1)}, u32[]{:S(2)}, u32[]{:S(2)}) collective-permute-start(f32[256,128]{1,0:T(8,128)S(1)} %shard_map.143), channel_id=1, source_target_pairs={{4,0},{0,4},{12,8},{8,12},{20,16},{16,20},{28,24},{24,28},{5,1},{1... | collective-permute-start | bytes 393224 | tf_op jit(solution)/shard_map/ppermute | solution.py:648
  23.9 5.5 %collective-permute-start.11 = (f32[256,128]{1,0:T(8,128)S(1)}, f32[256,128]{1,0:T(8,128)S(1)}, u32[]{:S(2)}, u32[]{:S(2)}) collective-permute-start(f32[256,128]{1,0:T(8,128)S(1)} %shard_map.143), channel_id=1, source_target_pairs={{8,0},{12,4},{0,8},{4,12},{24,16},{28,20},{16,24},{20,28},{9,1},{1... | collective-permute-start | bytes 393224 | tf_op jit(solution)/shard_map/ppermute | solution.py:648
  28.3 1.4 %collective-permute-start.12 = (f32[256,128]{1,0:T(8,128)S(1)}, f32[256,128]{1,0:T(8,128)S(1)}, u32[]{:S(2)}, u32[]{:S(2)}) collective-permute-start(f32[256,128]{1,0:T(8,128)S(1)} %shard_map.144), channel_id=1, source_target_pairs={{8,0},{12,4},{0,8},{4,12},{24,16},{28,20},{16,24},{20,28},{9,1},{1... | collective-permute-start | bytes 393224 | tf_op jit(solution)/shard_map/ppermute | solution.py:648
  43.0 1.3 %collective-permute-start.13 = (f32[32,8,128]{2,1,0:T(8,128)S(1)}, f32[32,8,128]{2,1,0:T(8,128)S(1)}, u32[]{:S(2)}, u32[]{:S(2)}) collective-permute-start(f32[32,8,128]{2,1,0:T(8,128)S(1)} %all_to_all.5.mine), channel_id=1, source_target_pairs={{8,0},{12,4},{0,8},{4,12},{24,16},{28,20},{16,24},{20,28},{9,1},{1... | collective-permute-start | bytes 393224 | tf_op jit(solution)/shard_map/ppermute | solution.py:648

commit v17 on v15

--- a/solution.py
+++ b/solution.py
@@ -502,9 +502,10 @@
         charges.append([a + b for a, b in zip(low, high)])
     own = charges[-1][0]
     whole = own[:8]
-    for column in range(1, s.nx * s.ny):
-        whole = whole + own[8 * column : 8 * column + 8]
-    others = jnp.concatenate([whole] * (s.nx * s.ny), axis=0) - own
+    for at in range(8, own.shape[0], 8):
+        whole = whole + own[at : at + 8]
+    whole = whole + pltpu.roll(whole, 4, 0)
+    others = jnp.concatenate([whole] * (own.shape[0] // 8), axis=0) - own
     potential = apply(mm, [others], root)
     for level in reversed(range(s.levels)):
         beside = apply(mm, charges[level], (siblings[0][level], siblings[1][level]))
@@ -523,9 +524,11 @@
     leaves = []
     for z in range(s.nz):
         wide = []
-        for column in range(columns):
-            tile = firsts[column * s.nz + z]
-            wide.append(jnp.concatenate([tile, pltpu.roll(tile, 4, 0)], axis=1)[:, : s.skel])
+        for column in range(0, columns, 2):
+            a, b = firsts[column * s.nz + z], firsts[(column + 1) * s.nz + z]
+            main = jnp.where(row < 4, a, pltpu.roll(b, 4, 0))
+            tail = jnp.where(row < 4, pltpu.roll(a, 4, 0), b)
+            wide.append(jnp.concatenate([main, tail], axis=1)[:, : s.skel])
         leaves.append(jnp.concatenate(wide, axis=0))
     potential = tree(s, leaves, ups, siblings, root)
     out = []
@@ -533,9 +536,12 @@
         sums = [jnp.zeros((8, LANES), f32) for _ in range(5)]
         for box in range(start, min(s.devices, start + 8)):
             column, z = box // s.nz, box % s.nz
-            phi = potential[z][8 * column : 8 * column + 8]
+            at = 8 * (column // 2)
+            phi = potential[z][at : at + 8]
             main, tail = phi[:, :LANES], phi[:, LANES:]
             tail = jnp.concatenate([tail, tail], axis=1)
+            if column % 2:
+                main, tail = pltpu.roll(main, 4, 0), pltpu.roll(tail, 4, 0)
             first, second = firsts[box], seconds[box]
             both = pltpu.roll(first, 4, 0) * tail
             of_f = jnp.where(row == 0, pltpu.roll(second, 1, 0), jnp.where(row == 1, pltpu.roll(second, 2, 0), pltpu.roll(first, 3, 0)))
@@ -603,12 +609,15 @@
     lsq_out[...] = jnp.abs(s2 * g2)
     on_u = y2 / h21 / beta
     on_f = y1 / beta - on_u * h11
+    moves = []
     for c in range(3):
         part = slice(c * s.step, c * s.step + s.blobs)
         raw[c * s.blobs : (c + 1) * s.blobs, 0, :] = on_f * f_in[part, :] + on_u * u_in[part, :]
-    move = pltpu.make_async_copy(raw, x_out, sem)
-    move.start()
-    move.wait()
+        rows = pl.ds(c * s.blobs, s.blobs)
+        moves.append(pltpu.make_async_copy(raw.at[rows], x_out.at[rows], sem.at[c]))
+        moves[-1].start()
+    for move in moves:
+        move.wait()
 
 
 def call(kernel, outs, args, scalars=0, far_args=0, far_outs=0, scratch=(), flops=0):
@@ -777,7 +786,7 @@
         [ids, f, u, boxes, fetch(boxes, "partner", 0), col, *operators_out],
         scalars=1,
         far_outs=1,
-        scratch=[pltpu.VMEM(flat, f32), pltpu.SemaphoreType.DMA],
+        scratch=[pltpu.VMEM(flat, f32), pltpu.SemaphoreType.DMA((3,))],
         flops=10**7,
     )
     return result.reshape(rhs.shape), lsq.reshape(())

time: 48.3 us -> 48.1 us (level)
  no operation moved by 1% of the time
where the time goes in v17:
time: 48.1 us; the launch traced here: 47.9 us
  Pallas kernels  16.7 us (35%)
  starting transfers between devices  12.7 us (26%)
  blocking collectives  11.2 us (23%)
  waiting for transfers between devices  6.46 us (13%)
  between operations  0.76 us (2%)
    pallas_call x16, Pallas kernels, call(): pl.pallas_call(kernel, out_shape=[jax.ShapeDtypeStruct(shape, kind) for s...  16.7 us
    all_to_all x1, blocking collectives, body(): boxes = lax.all_to_all(packed, ('gx', 'gy', 'gz'), 0, 0)  11.2 us
    ppermute x12, starting transfers between devices, fetch(): return lax.ppermute(x, ('gx', 'gy'), pairs)  8.45 us
    ppermute x2, starting transfers between devices, fetch_layers(): parts.append(lax.ppermute(sent[-1], 'gz', pairs))  4.23 us
    ppermute x12, waiting for transfers between devices, fetch(): return lax.ppermute(x, ('gx', 'gy'), pairs)  3.47 us
    ppermute x2, waiting for transfers between devices, fetch_layers(): parts.append(lax.ppermute(sent[-1], 'gz', pairs))  2.99 us
  transfers between devices with their start and end apart: 14, of which 5 were waited for; matrix products, arithmetic and copies ran while one was open for 0% of the time, Pallas kernels for 19%

profile of v17, /device:TPU:0, one launch (start us, length us, event | category | flops | bytes accessed | tf_op | source)
XLA Modules:
  0.0 47.9 jit_solution(12480584401945778012)
XLA Ops:
  0.6 1.4 %shard_map.131 = (f32[264,128]{1,0:T(8,128)S(1)}, f32[168,128]{1,0:T(8,128)S(1)}, s32[1,1,256]{2,1,0:T(1,128)S(1)}, f32[512,256]{1,0:T(8,128)S(1)}) custom-call(f32[486,1,256]{2,1,0:T(1,128)} %bitcast.9, s32[1,1,256]{2,1,0:T(1,128)} %cells.1, f32[1,162]{1,0:T(1,128)} %bitcast.10), custom_call_target="tpu_custom_call" | custom-call | flops 10000000 | bytes 1048576 | tf_op jit(solution)/shard_map/pallas_call | solution.py:629
  2.1 3.0 %collective-permute-start = (f32[264,128]{1,0:T(8,128)S(1)}, f32[264,128]{1,0:T(8,128)S(1)}, u32[]{:S(2)}, u32[]{:S(2)}) collective-permute-start(f32[264,128]{1,0:T(8,128)S(1)} %get-tuple-element.49.refs_0_.message.charges_f), channel_id=1, source_target_pairs={{4,0},{0,4},{12,8},{8,12},{20,16},{16,20},{28,24},{24,28},{5,1},{1... | collective-permute-start | bytes 405512 | tf_op jit(solution)/shard_map/ppermute | solution.py:657
  5.1 0.7 %collective-permute-start.1 = (f32[264,128]{1,0:T(8,128)S(1)}, f32[264,128]{1,0:T(8,128)S(1)}, u32[]{:S(2)}, u32[]{:S(2)}) collective-permute-start(f32[264,128]{1,0:T(8,128)S(1)} %get-tuple-element.49.refs_0_.message.charges_f), channel_id=1, source_target_pairs={{24,0},{28,4},{16,8},{20,12},{8,16},{12,20},{0,24},{4,28},{25,1},{... | collective-permute-start | bytes 405512 | tf_op jit(solution)/shard_map/ppermute | solution.py:657
  5.7 0.6 %collective-permute-start.2 = (f32[264,128]{1,0:T(8,128)S(1)}, f32[264,128]{1,0:T(8,128)S(1)}, u32[]{:S(2)}, u32[]{:S(2)}) collective-permute-start(f32[264,128]{1,0:T(8,128)S(1)} %get-tuple-element.49.refs_0_.message.charges_f), channel_id=1, source_target_pairs={{28,0},{24,4},{20,8},{16,12},{12,16},{8,20},{4,24},{0,28},{29,1},{... | collective-permute-start | bytes 405512 | tf_op jit(solution)/shard_map/ppermute | solution.py:657
  6.3 0.4 collective-permute-start.3
  6.7 0.1 pad_add_fusion.ids
  6.8 5.6 %shard_map.132 = (f32[512,256]{1,0:T(8,128)S(1)}, f32[512,256]{1,0:T(8,128)S(1)}, f32[16,256]{1,0:T(8,128)S(1)}, bf16[512,512]{1,0:T(8,128)(2,1)S(1)}, bf16[512,...) custom-call(s32[2]{0:T(128)S(1)} %pad_add_fusion.ids, ...), custom_call_target="tpu_custom_call" | custom-call | flops 5000000000 | bytes 1048576 | tf_op jit(solution)/shard_map/pallas_call | solution.py:629
  12.4 0.0 collective-permute-done.x.refs_1_.refs_0_.refs_2_
  12.5 0.2 collective-permute-start.4
  12.7 1.1 %collective-permute-done.1.refs_2_.refs_1_.refs_3_ = f32[264,128]{1,0:T(8,128)S(1)} collective-permute-done((f32[264,128]{1,0:T(8,128)S(1)}, f32[264,128]{1,0:T(8,128)S(1)}, u32[]{:S(2)}, u32[]{:S(2)}) %collective-permute-start.1) | collective-permute-done | bytes 135200 | tf_op jit(solution)/shard_map/ppermute | solution.py:657
  13.8 0.2 collective-permute-start.5
  14.0 0.7 %shard_map.135 = (bf16[512,256]{1,0:T(8,128)(2,1)S(1)}, bf16[512,256]{1,0:T(8,128)(2,1)S(1)}) custom-call(f32[512,256]{1,0:T(8,128)S(1)} %get-tuple-element.46.gat, bf16[384,256]{1,0:T(8,128)(2,1)S(1)} %get-tuple-element.47.gh, bf16[384,256]{1,0:T(8,128)(2,1)S(1)} %get-tuple-element.48.gl, f32[264,128]{1,0:T(8,128)S(1)} %collective-permute-done.x.refs_1_.refs_0_.refs_2_, ...), custom_call_target="tpu_custom_call" | custom-call | flops 1000000000 | bytes 1048576 | tf_op jit(solution)/shard_map/pallas_call | solution.py:629
  14.7 0.4 collective-permute-done.5.refs_1_
  15.0 1.6 %collective-permute-start.6 = (f32[7,8,128]{2,1,0:T(8,128)S(1)}, f32[7,8,128]{2,1,0:T(8,128)S(1)}, u32[]{:S(2)}, u32[]{:S(2)}) collective-permute-start(f32[7,8,128]{2,1,0:T(8,128)S(1)} %shard_map.137.tiles.x.refs_0_), channel_id=1, source_target_pairs={{1,0},{0,1},{3,2},{2,3},{5,4},{4,5},{7,6},{6,7},{9,8},{8,9},{11,10... | collective-permute-start | bytes 86024 | tf_op jit(solution)/shard_map/ppermute | solution.py:663
  16.6 0.6 %shard_map.136 = (f32[512,256]{1,0:T(8,128)S(1)}, f32[256,128]{1,0:T(8,128)S(1)}) custom-call(f32[512,256]{1,0:T(8,128)S(1)} %get-tuple-element.43.loc, bf16[512,512]{1,0:T(8,128)(2,1)S(1)} %get-tuple-element.44.nh, bf16[512,512]{1,0:T(8,128)(2,1)S(1)} %get-tuple-element.45.nl, bf16[512,256]{1,0:T(8,128)(2,1)S(1)} %get-tuple-element.51.hi, ...), custom_call_target="tpu_custom_call" | custom-call | flops 1000000000 | bytes 1048576 | tf_op jit(solution)/shard_map/pallas_call | solution.py:629
  17.2 1.4 %collective-permute-start.8 = (f32[256,128]{1,0:T(8,128)S(1)}, f32[256,128]{1,0:T(8,128)S(1)}, u32[]{:S(2)}, u32[]{:S(2)}) collective-permute-start(f32[256,128]{1,0:T(8,128)S(1)} %get-tuple-element.68.x), channel_id=1, source_target_pairs={{4,0},{0,4},{12,8},{8,12},{20,16},{16,20},{28,24},{24,28},{5,1},{1... | collective-permute-start | bytes 393224 | tf_op jit(solution)/shard_map/ppermute | solution.py:657
  18.7 0.9 %collective-permute-start.10 = (f32[256,128]{1,0:T(8,128)S(1)}, f32[256,128]{1,0:T(8,128)S(1)}, u32[]{:S(2)}, u32[]{:S(2)}) collective-permute-start(f32[256,128]{1,0:T(8,128)S(1)} %get-tuple-element.68.x), channel_id=1, source_target_pairs={{28,0},{24,4},{20,8},{16,12},{12,16},{8,20},{4,24},{0,28},{29,1},{... | collective-permute-start | bytes 393224 | tf_op jit(solution)/shard_map/ppermute | solution.py:657
  19.6 2.7 %collective-permute-start.7 = (f32[14,8,128]{2,1,0:T(8,128)S(1)}, f32[14,8,128]{2,1,0:T(8,128)S(1)}, u32[]{:S(2)}, u32[]{:S(2)}) collective-permute-start(f32[14,8,128]{2,1,0:T(8,128)S(1)} %shard_map.139._), channel_id=1, source_target_pairs={{2,0},{3,1},{0,2},{1,3},{6,4},{7,5},{4,6},{5,7},{10,8},{11,9},{8,1... | collective-permute-start | bytes 172040 | tf_op jit(solution)/shard_map/ppermute | solution.py:663
  22.2 0.1 shard_map.138
  22.3 0.5 %collective-permute-start.11 = (f32[256,128]{1,0:T(8,128)S(1)}, f32[256,128]{1,0:T(8,128)S(1)}, u32[]{:S(2)}, u32[]{:S(2)}) collective-permute-start(f32[256,128]{1,0:T(8,128)S(1)} %shard_map.142), channel_id=1, source_target_pairs={{8,0},{12,4},{0,8},{4,12},{24,16},{28,20},{16,24},{20,28},{9,1},{1... | collective-permute-start | bytes 393224 | tf_op jit(solution)/shard_map/ppermute | solution.py:657
  22.9 0.3 collective-permute-start.9
  23.2 3.0 %collective-permute-done.7.refs_2_ = f32[14,8,128]{2,1,0:T(8,128)S(1)} collective-permute-done((f32[14,8,128]{2,1,0:T(8,128)S(1)}, f32[14,8,128]{2,1,0:T(8,128)S(1)}, u32[]{:S(2)}, u32[]{:S(2)}) %collective-permute-start.7) | collective-permute-done | bytes 57376 | tf_op jit(solution)/shard_map/ppermute | solution.py:663
  26.2 1.0 %shard_map.140 = (f32[512,256]{1,0:T(8,128)S(1)}, f32[8,128]{1,0:T(8,128)S(1)}, f32[3,8,128]{2,1,0:T(8,128)S(1)}) custom-call(f32[512,256]{1,0:T(8,128)S(1)} %get-tuple-element.53.part, bf16[192,1536]{1,0:T(8,128)(2,1)S(1)} %get-tuple-element.54.fh, bf16[192,1536]{1,0:T(8,128)(2,1)S(1)} %get-tuple-element.55.fl, bf16[192,256]{1,0:T(8,128)(2,1)S(1)} %get-tuple-element.57.own, ...), custom_call_target="tpu_custom_call" | custom-call | flops 100000000 | bytes 1048576 | tf_op jit(solution)/shard_map/pallas_call | solution.py:629
  27.2 0.2 collective-permute-start.12
  27.4 1.0 %shard_map.141 = (f32[512,256]{1,0:T(8,128)S(1)}, f32[512,256]{1,0:T(8,128)S(1)}, f32[512,256]{1,0:T(8,128)S(1)}, f32[8,128]{1,0:T(8,128)S(1)}) custom-call(f32[512,256]{1,0:T(8,128)S(1)} %get-tuple-element.60.u_in, f32[512,256]{1,0:T(8,128)S(1)} %get-tuple-element.42.f_in, f32[16,256]{1,0:T(8,128)S(1)} %get-tuple-element.50._.refs_4_.rot, ...), custom_call_target="tpu_custom_call" | custom-call | flops 1000000000 | bytes 1048576 | tf_op jit(solution)/shard_map/pallas_call | solution.py:629
  28.5 0.7 %collective-permute-done.9.refs_1_ = f32[256,128]{1,0:T(8,128)S(1)} collective-permute-done((f32[256,128]{1,0:T(8,128)S(1)}, f32[256,128]{1,0:T(8,128)S(1)}, u32[]{:S(2)}, u32[]{:S(2)}) %collective-permute-start.9) | collective-permute-done | bytes 131104 | tf_op jit(solution)/shard_map/ppermute | solution.py:657
  29.2 0.7 %shard_map.144 = (bf16[512,256]{1,0:T(8,128)(2,1)S(1)}, bf16[512,256]{1,0:T(8,128)(2,1)S(1)}) custom-call(f32[512,256]{1,0:T(8,128)S(1)} %get-tuple-element.66.gat, bf16[384,256]{1,0:T(8,128)(2,1)S(1)} %get-tuple-element.47.gh, bf16[384,256]{1,0:T(8,128)(2,1)S(1)} %get-tuple-element.48.gl, f32[168,128]{1,0:T(8,128)S(1)} %get-tuple-element.59.col, ...), custom_call_target="tpu_custom_call" | custom-call | flops 1000000000 | bytes 1048576 | tf_op jit(solution)/shard_map/pallas_call | solution.py:629
  29.9 1.3 %shard_map.145 = f32[32,8,128]{2,1,0:T(8,128)S(1)} custom-call(f32[512,256]{1,0:T(8,128)S(1)} %get-tuple-element.65.loc, bf16[512,512]{1,0:T(8,128)(2,1)S(1)} %get-tuple-element.44.nh, bf16[512,512]{1,0:T(8,128)(2,1)S(1)} %get-tuple-element.45.nl, bf16[512,256]{1,0:T(8,128)(2,1)S(1)} %get-tuple-element.70.hi, bf16[512,256]{1,0:T(8,128)(2,1)S(1)} %get-tuple-element.71.lo, ...), custom_call_target="tpu_custom_call" | custom-call | flops 1000000000 | bytes 1048576 | tf_op jit(solution)/shard_map/pallas_call | solution.py:629
  31.2 11.2 %all_to_all.5.mine = f32[32,8,128]{2,1,0:T(8,128)S(1)} all-to-all(f32[32,8,128]{2,1,0:T(8,128)S(1)} %shard_map.145), channel_id=1, replica_groups=mesh['gx'=4,'gy'=2,'gz'=4] {'gx','gy','gz'}, dimensions={0} | all-to-all | bytes 262144 | tf_op jit(solution)/shard_map/all_to_all | solution.py:782
  42.4 0.1 collective-permute-start.13
  42.5 1.2 %collective-permute-done.13.other = f32[32,8,128]{2,1,0:T(8,128)S(1)} collective-permute-done((f32[32,8,128]{2,1,0:T(8,128)S(1)}, f32[32,8,128]{2,1,0:T(8,128)S(1)}, u32[]{:S(2)}, u32[]{:S(2)}) %collective-permute-start.13) | collective-permute-done | bytes 131104 | tf_op jit(solution)/shard_map/ppermute | solution.py:657
  43.8 4.1 %shard_map.146 = (f32[486,1,256]{2,1,0:T(1,128)}, f32[1,1]{1,0:T(1,128)}) custom-call(s32[2]{0:T(128)S(1)} %pad_add_fusion.ids, f32[512,256]{1,0:T(8,128)S(1)} %get-tuple-element.42.f_in, f32[512,256]{1,0:T(8,128)S(1)} %get-tuple-element.60.u_in, f32[32,8,128]{2,1,0:T(8,128)S(1)} %all_to_all.5.mine, f32[32,8,128]{2,1,0:T(8,128)S(1)} %collective-permute-done.13.other, ...), custom_call_target="tpu_custom_call" | custom-call | flops 10000000 | bytes 1048576 | tf_op jit(solution)/shard_map/pallas_call | solution.py:629
  (14 shorter events, 0.1 us)
Async XLA Ops:
  2.1 10.4 %collective-permute-start = (f32[264,128]{1,0:T(8,128)S(1)}, f32[264,128]{1,0:T(8,128)S(1)}, u32[]{:S(2)}, u32[]{:S(2)}) collective-permute-start(f32[264,128]{1,0:T(8,128)S(1)} %get-tuple-element.49.refs_0_.message.charges_f), channel_id=1, source_target_pairs={{4,0},{0,4},{12,8},{8,12},{20,16},{16,20},{28,24},{24,28},{5,1},{1... | collective-permute-start | bytes 405512 | tf_op jit(solution)/shard_map/ppermute | solution.py:657
  5.1 8.7 %collective-permute-start.1 = (f32[264,128]{1,0:T(8,128)S(1)}, f32[264,128]{1,0:T(8,128)S(1)}, u32[]{:S(2)}, u32[]{:S(2)}) collective-permute-start(f32[264,128]{1,0:T(8,128)S(1)} %get-tuple-element.49.refs_0_.message.charges_f), channel_id=1, source_target_pairs={{24,0},{28,4},{16,8},{20,12},{8,16},{12,20},{0,24},{4,28},{25,1},{... | collective-permute-start | bytes 405512 | tf_op jit(solution)/shard_map/ppermute | solution.py:657
  5.7 8.0 %collective-permute-start.2 = (f32[264,128]{1,0:T(8,128)S(1)}, f32[264,128]{1,0:T(8,128)S(1)}, u32[]{:S(2)}, u32[]{:S(2)}) collective-permute-start(f32[264,128]{1,0:T(8,128)S(1)} %get-tuple-element.49.refs_0_.message.charges_f), channel_id=1, source_target_pairs={{28,0},{24,4},{20,8},{16,12},{12,16},{8,20},{4,24},{0,28},{29,1},{... | collective-permute-start | bytes 405512 | tf_op jit(solution)/shard_map/ppermute | solution.py:657
  6.3 7.6 %collective-permute-start.3 = (f32[264,128]{1,0:T(8,128)S(1)}, f32[264,128]{1,0:T(8,128)S(1)}, u32[]{:S(2)}, u32[]{:S(2)}) collective-permute-start(f32[264,128]{1,0:T(8,128)S(1)} %get-tuple-element.49.refs_0_.message.charges_f), channel_id=1, source_target_pairs={{8,0},{12,4},{0,8},{4,12},{24,16},{28,20},{16,24},{20,28},{9,1},{1... | collective-permute-start | bytes 405512 | tf_op jit(solution)/shard_map/ppermute | solution.py:657
  12.5 1.5 %collective-permute-start.4 = (f32[264,128]{1,0:T(8,128)S(1)}, f32[264,128]{1,0:T(8,128)S(1)}, u32[]{:S(2)}, u32[]{:S(2)}) collective-permute-start(f32[264,128]{1,0:T(8,128)S(1)} %shard_map.133), channel_id=1, source_target_pairs={{8,0},{12,4},{0,8},{4,12},{24,16},{28,20},{16,24},{20,28},{9,1},{1... | collective-permute-start | bytes 405512 | tf_op jit(solution)/shard_map/ppermute | solution.py:657
  13.8 1.2 %collective-permute-start.5 = (f32[8,128]{1,0:T(8,128)S(1)}, f32[8,128]{1,0:T(8,128)S(1)}, u32[]{:S(2)}, u32[]{:S(2)}) collective-permute-start(f32[8,128]{1,0:T(8,128)S(1)} %shard_map.134.refs_5_.refs_0_), channel_id=1, source_target_pairs={{8,0},{12,4},{0,8},{4,12},{24,16},{28,20},{16,24},{20,28},{9,1},{1... | collective-permute-start | bytes 12296 | tf_op jit(solution)/shard_map/ppermute | solution.py:657
  15.0 4.5 %collective-permute-start.6 = (f32[7,8,128]{2,1,0:T(8,128)S(1)}, f32[7,8,128]{2,1,0:T(8,128)S(1)}, u32[]{:S(2)}, u32[]{:S(2)}) collective-permute-start(f32[7,8,128]{2,1,0:T(8,128)S(1)} %shard_map.137.tiles.x.refs_0_), channel_id=1, source_target_pairs={{1,0},{0,1},{3,2},{2,3},{5,4},{4,5},{7,6},{6,7},{9,8},{8,9},{11,10... | collective-permute-start | bytes 86024 | tf_op jit(solution)/shard_map/ppermute | solution.py:663
  17.2 10.0 %collective-permute-start.8 = (f32[256,128]{1,0:T(8,128)S(1)}, f32[256,128]{1,0:T(8,128)S(1)}, u32[]{:S(2)}, u32[]{:S(2)}) collective-permute-start(f32[256,128]{1,0:T(8,128)S(1)} %get-tuple-element.68.x), channel_id=1, source_target_pairs={{4,0},{0,4},{12,8},{8,12},{20,16},{16,20},{28,24},{24,28},{5,1},{1... | collective-permute-start | bytes 393224 | tf_op jit(solution)/shard_map/ppermute | solution.py:657
  18.7 9.8 %collective-permute-start.10 = (f32[256,128]{1,0:T(8,128)S(1)}, f32[256,128]{1,0:T(8,128)S(1)}, u32[]{:S(2)}, u32[]{:S(2)}) collective-permute-start(f32[256,128]{1,0:T(8,128)S(1)} %get-tuple-element.68.x), channel_id=1, source_target_pairs={{28,0},{24,4},{20,8},{16,12},{12,16},{8,20},{4,24},{0,28},{29,1},{... | collective-permute-start | bytes 393224 | tf_op jit(solution)/shard_map/ppermute | solution.py:657
  19.6 6.6 %collective-permute-start.7 = (f32[14,8,128]{2,1,0:T(8,128)S(1)}, f32[14,8,128]{2,1,0:T(8,128)S(1)}, u32[]{:S(2)}, u32[]{:S(2)}) collective-permute-start(f32[14,8,128]{2,1,0:T(8,128)S(1)} %shard_map.139._), channel_id=1, source_target_pairs={{2,0},{3,1},{0,2},{1,3},{6,4},{7,5},{4,6},{5,7},{10,8},{11,9},{8,1... | collective-permute-start | bytes 172040 | tf_op jit(solution)/shard_map/ppermute | solution.py:663
  22.3 6.1 %collective-permute-start.11 = (f32[256,128]{1,0:T(8,128)S(1)}, f32[256,128]{1,0:T(8,128)S(1)}, u32[]{:S(2)}, u32[]{:S(2)}) collective-permute-start(f32[256,128]{1,0:T(8,128)S(1)} %shard_map.142), channel_id=1, source_target_pairs={{8,0},{12,4},{0,8},{4,12},{24,16},{28,20},{16,24},{20,28},{9,1},{1... | collective-permute-start | bytes 393224 | tf_op jit(solution)/shard_map/ppermute | solution.py:657
  22.9 6.3 %collective-permute-start.9 = (f32[256,128]{1,0:T(8,128)S(1)}, f32[256,128]{1,0:T(8,128)S(1)}, u32[]{:S(2)}, u32[]{:S(2)}) collective-permute-start(f32[256,128]{1,0:T(8,128)S(1)} %shard_map.142), channel_id=1, source_target_pairs={{24,0},{28,4},{16,8},{20,12},{8,16},{12,20},{0,24},{4,28},{25,1},{... | collective-permute-start | bytes 393224 | tf_op jit(solution)/shard_map/ppermute | solution.py:657
  27.2 2.0 %collective-permute-start.12 = (f32[256,128]{1,0:T(8,128)S(1)}, f32[256,128]{1,0:T(8,128)S(1)}, u32[]{:S(2)}, u32[]{:S(2)}) collective-permute-start(f32[256,128]{1,0:T(8,128)S(1)} %shard_map.143), channel_id=1, source_target_pairs={{8,0},{12,4},{0,8},{4,12},{24,16},{28,20},{16,24},{20,28},{9,1},{1... | collective-permute-start | bytes 393224 | tf_op jit(solution)/shard_map/ppermute | solution.py:657
  42.4 1.3 %collective-permute-start.13 = (f32[32,8,128]{2,1,0:T(8,128)S(1)}, f32[32,8,128]{2,1,0:T(8,128)S(1)}, u32[]{:S(2)}, u32[]{:S(2)}) collective-permute-start(f32[32,8,128]{2,1,0:T(8,128)S(1)} %all_to_all.5.mine), channel_id=1, source_target_pairs={{8,0},{12,4},{0,8},{4,12},{24,16},{28,20},{16,24},{20,28},{9,1},{1... | collective-permute-start | bytes 393224 | tf_op jit(solution)/shard_map/ppermute | solution.py:657

commit v18 on v17

--- a/solution.py
+++ b/solution.py
@@ -401,16 +401,13 @@
     hi_out[...], lo_out[...] = split(gathered)
 
 
-def gather_far_kernel(s, gat, gh, gl, col, values, *refs):
-    *messages, hi_out, lo_out = refs
+def gather_far(s, gat, ghost, col, values, messages):
     rims = unpack_rims([message[...] for message in messages], s)
     far = []
     for c in range(3):
         value = jnp.concatenate([values[i, c : c + 1, :] for i in range(values.shape[0])], axis=1)
         far.append(col[:, :1] * value)
-    rims = rims + stacked(far, s)
-    gathered = gat[...] + product(mm, split(rims), (gh[...], gl[...]))
-    hi_out[...], lo_out[...] = split(gathered)
+    return gat[...] + product(mm, split(rims + stacked(far, s)), ghost)
 
 
 def near_kernel(s, loc, nh, nl, hi, lo, out, rim_out):
@@ -419,8 +416,8 @@
     rim_out[...] = pack_rim(part, s)
 
 
-def first_kernel(s, part, fh, fl, own, rims, col, *refs):
-    *layers, u_out, charges_out, values_out = refs
+def first_kernel(s, part, fh, fl, own, rims, col, f_in, rot, sh, sl, oh, ol, *refs):
+    *layers, u_out, charges_out, values_out, loc_out, gat_out, ortho_out, stat_out = refs
     count = 2 + len(s.sources)
     layers = [[part[at + k] for k in range(count)] for part in layers for at in range(0, part.shape[0], count)]
     weight_col = col[:, :1]
@@ -432,18 +429,7 @@
     charges_out[...] = pack_charges(pieces(u, s), weight_col, occ, s)
     for index, value in enumerate(rim_values(s, potentials, rims)):
         values_out[index] = value
-
-
-def order_kernel(x, _, out):
-    out[...] = x[...]
-
-
-def safe_inverse(x):
-    return jnp.where(x > 0.0, 1.0 / jnp.where(x > 0.0, x, 1.0), 0.0)
-
-
-def middle_kernel(s, u_in, f_in, rot, sh, sl, oh, ol, loc_out, gat_out, ortho_out, stat_out):
-    u, f = u_in[...], f_in[...]
+    f = f_in[...]
     loc, gat = local_part(u, s, rot[...], (sh[...], sl[...]), (oh[...], ol[...]))
     loc_out[...] = loc
     gat_out[...] = gat
@@ -457,10 +443,20 @@
     )
 
 
+def order_kernel(x, _, out):
+    out[...] = x[...]
+
+
+def safe_inverse(x):
+    return jnp.where(x > 0.0, 1.0 / jnp.where(x > 0.0, x, 1.0), 0.0)
+
+
 def second_kernel(
-    s, loc, nh, nl, hi, lo, cells, col, f_in, ortho_in, stat, charges_f, charges_u, packed_out
+    s, loc, gat, nh, nl, gh, gl, cells, col, f_in, ortho_in, stat, charges_f, charges_u, values, *refs
 ):
-    part = loc[...] + product(mm, (nh[...], nl[...]), (hi[...], lo[...]))
+    *messages, packed_out = refs
+    gathered = gather_far(s, gat, (gh[...], gl[...]), col, values, messages)
+    part = loc[...] + product(mm, (nh[...], nl[...]), split(gathered))
     f, ortho = f_in[...], ortho_in[...]
     ff, fu, oo = (stat[i : i + 1, :1] for i in range(3))
     fa = total(f * part) * safe_inverse(ff)
@@ -754,29 +750,18 @@
         [cells, tiles],
         flops=2 * 10**10,
     )
-    u, charges, values = call(
+    u, charges, values, loc, gat, ortho, stat = call(
         functools.partial(first_kernel, s),
-        [(full, f32), (tile, f32), ((s.ghosts // LANES,) + tile, f32)],
-        [part, fh, fl, *places, col, *layers],
-        flops=10**8,
-    )
-    loc, gat, ortho, stat = call(
-        functools.partial(middle_kernel, s),
-        [(full, f32), (full, f32), (full, f32), (tile, f32)],
-        [u, f, rot, sh, sl, oh, ol],
+        [(full, f32), (tile, f32), ((s.ghosts // LANES,) + tile, f32)] + [(full, f32)] * 3 + [(tile, f32)],
+        [part, fh, fl, *places, col, f, rot, sh, sl, oh, ol, *layers],
         flops=10**9,
     )
-    forward_rims(got, charges)
-    gathered = call(
-        functools.partial(gather_far_kernel, s),
-        [(full, bf16), (full, bf16)],
-        [gat, gh, gl, col, values] + [got[key] for key in s.sources],
-        flops=10**9,
-    )
+    forward_rims(got, places[1])
     (packed,) = call(
         functools.partial(second_kernel, s),
         [((s.devices, 8, LANES), f32)],
-        [loc, nh, nl, *gathered, cells, col, f, ortho, stat, message, charges],
+        [loc, gat, nh, nl, gh, gl, cells, col, f, ortho, stat, message, charges, values]
+        + [got[key] for key in s.sources],
         flops=10**9,
     )
     boxes = lax.all_to_all(packed, ("gx", "gy", "gz"), 0, 0)

time: 48.1 us -> 48.3 us (level)
    ppermute x2, waiting for transfers between devices: 2.99 us -> 2.49 us  [fetch_layers(): parts.append(lax.ppermute(sent[-1], 'gz', pairs))]
    pallas_call x16 -> x14, Pallas kernels: 16.7 us -> 17 us  [call(): pl.pallas_call(kernel, out_shape=[jax.ShapeDtypeStruct(shape, kind) for s...]
where the time goes in v18:
time: 48.3 us; the launch traced here: 48.1 us
  Pallas kernels  17 us (35%)
  starting transfers between devices  13 us (27%)
  blocking collectives  11 us (23%)
  waiting for transfers between devices  6.28 us (13%)
  between operations  0.73 us (2%)
    pallas_call x14, Pallas kernels, call(): pl.pallas_call(kernel, out_shape=[jax.ShapeDtypeStruct(shape, kind) for s...  17 us
    all_to_all x1, blocking collectives, body(): boxes = lax.all_to_all(packed, ('gx', 'gy', 'gz'), 0, 0)  11 us
    ppermute x12, starting transfers between devices, fetch(): return lax.ppermute(x, ('gx', 'gy'), pairs)  8.77 us
    ppermute x2, starting transfers between devices, fetch_layers(): parts.append(lax.ppermute(sent[-1], 'gz', pairs))  4.23 us
    ppermute x12, waiting for transfers between devices, fetch(): return lax.ppermute(x, ('gx', 'gy'), pairs)  3.78 us
    ppermute x2, waiting for transfers between devices, fetch_layers(): parts.append(lax.ppermute(sent[-1], 'gz', pairs))  2.49 us
  transfers between devices with their start and end apart: 14, of which 5 were waited for; matrix products, arithmetic and copies ran while one was open for 0% of the time, Pallas kernels for 19%

profile of v18, /device:TPU:0, one launch (start us, length us, event | category | flops | bytes accessed | tf_op | source)
XLA Modules:
  0.0 48.1 jit_solution(10611918683113073922)
XLA Ops:
  0.6 1.4 %shard_map.131 = (f32[264,128]{1,0:T(8,128)S(1)}, f32[168,128]{1,0:T(8,128)S(1)}, s32[1,1,256]{2,1,0:T(1,128)S(1)}, f32[512,256]{1,0:T(8,128)S(1)}) custom-call(f32[486,1,256]{2,1,0:T(1,128)} %bitcast.9, s32[1,1,256]{2,1,0:T(1,128)} %cells.1, f32[1,162]{1,0:T(1,128)} %bitcast.10), custom_call_target="tpu_custom_call" | custom-call | flops 10000000 | bytes 1048576 | tf_op jit(solution)/shard_map/pallas_call | solution.py:625
  2.1 3.0 %collective-permute-start = (f32[264,128]{1,0:T(8,128)S(1)}, f32[264,128]{1,0:T(8,128)S(1)}, u32[]{:S(2)}, u32[]{:S(2)}) collective-permute-start(f32[264,128]{1,0:T(8,128)S(1)} %get-tuple-element.47.refs_0_.message.charges_f), channel_id=1, source_target_pairs={{4,0},{0,4},{12,8},{8,12},{20,16},{16,20},{28,24},{24,28},{5,1},{1... | collective-permute-start | bytes 405512 | tf_op jit(solution)/shard_map/ppermute | solution.py:653
  5.1 0.7 %collective-permute-start.1 = (f32[264,128]{1,0:T(8,128)S(1)}, f32[264,128]{1,0:T(8,128)S(1)}, u32[]{:S(2)}, u32[]{:S(2)}) collective-permute-start(f32[264,128]{1,0:T(8,128)S(1)} %get-tuple-element.47.refs_0_.message.charges_f), channel_id=1, source_target_pairs={{24,0},{28,4},{16,8},{20,12},{8,16},{12,20},{0,24},{4,28},{25,1},{... | collective-permute-start | bytes 405512 | tf_op jit(solution)/shard_map/ppermute | solution.py:653
  5.7 0.6 %collective-permute-start.2 = (f32[264,128]{1,0:T(8,128)S(1)}, f32[264,128]{1,0:T(8,128)S(1)}, u32[]{:S(2)}, u32[]{:S(2)}) collective-permute-start(f32[264,128]{1,0:T(8,128)S(1)} %get-tuple-element.47.refs_0_.message.charges_f), channel_id=1, source_target_pairs={{28,0},{24,4},{20,8},{16,12},{12,16},{8,20},{4,24},{0,28},{29,1},{... | collective-permute-start | bytes 405512 | tf_op jit(solution)/shard_map/ppermute | solution.py:653
  6.3 0.4 collective-permute-start.3
  6.7 0.1 pad_add_fusion.ids
  6.8 5.6 %shard_map.132 = (f32[512,256]{1,0:T(8,128)S(1)}, f32[512,256]{1,0:T(8,128)S(1)}, f32[16,256]{1,0:T(8,128)S(1)}, bf16[512,512]{1,0:T(8,128)(2,1)S(1)}, bf16[512,...) custom-call(s32[2]{0:T(128)S(1)} %pad_add_fusion.ids, ...), custom_call_target="tpu_custom_call" | custom-call | flops 5000000000 | bytes 1048576 | tf_op jit(solution)/shard_map/pallas_call | solution.py:625
  12.5 0.2 collective-permute-start.4
  12.7 1.1 %collective-permute-done.1.refs_2_.refs_1_.refs_3_ = f32[264,128]{1,0:T(8,128)S(1)} collective-permute-done((f32[264,128]{1,0:T(8,128)S(1)}, f32[264,128]{1,0:T(8,128)S(1)}, u32[]{:S(2)}, u32[]{:S(2)}) %collective-permute-start.1) | collective-permute-done | bytes 135200 | tf_op jit(solution)/shard_map/ppermute | solution.py:653
  13.8 0.2 collective-permute-start.5
  14.0 0.0 collective-permute-done.4.refs_4_.refs_6_
  14.0 0.7 %shard_map.135 = (bf16[512,256]{1,0:T(8,128)(2,1)S(1)}, bf16[512,256]{1,0:T(8,128)(2,1)S(1)}) custom-call(f32[512,256]{1,0:T(8,128)S(1)} %get-tuple-element.44.gat, bf16[384,256]{1,0:T(8,128)(2,1)S(1)} %get-tuple-element.45.gh, bf16[384,256]{1,0:T(8,128)(2,1)S(1)} %get-tuple-element.46.gl, f32[264,128]{1,0:T(8,128)S(1)} %collective-permute-done.x.refs_1_.refs_0_.refs_2_, ...), custom_call_target="tpu_custom_call" | custom-call | flops 1000000000 | bytes 1048576 | tf_op jit(solution)/shard_map/pallas_call | solution.py:625
  14.7 0.4 collective-permute-done.5.refs_1_
  15.0 1.6 %collective-permute-start.6 = (f32[7,8,128]{2,1,0:T(8,128)S(1)}, f32[7,8,128]{2,1,0:T(8,128)S(1)}, u32[]{:S(2)}, u32[]{:S(2)}) collective-permute-start(f32[7,8,128]{2,1,0:T(8,128)S(1)} %shard_map.137.tiles.x.refs_0_), channel_id=1, source_target_pairs={{1,0},{0,1},{3,2},{2,3},{5,4},{4,5},{7,6},{6,7},{9,8},{8,9},{11,10... | collective-permute-start | bytes 86024 | tf_op jit(solution)/shard_map/ppermute | solution.py:659
  16.6 0.6 %shard_map.136 = (f32[512,256]{1,0:T(8,128)S(1)}, f32[256,128]{1,0:T(8,128)S(1)}) custom-call(f32[512,256]{1,0:T(8,128)S(1)} %get-tuple-element.41.loc, bf16[512,512]{1,0:T(8,128)(2,1)S(1)} %get-tuple-element.42.nh, bf16[512,512]{1,0:T(8,128)(2,1)S(1)} %get-tuple-element.43.nl, bf16[512,256]{1,0:T(8,128)(2,1)S(1)} %get-tuple-element.49.hi, ...), custom_call_target="tpu_custom_call" | custom-call | flops 1000000000 | bytes 1048576 | tf_op jit(solution)/shard_map/pallas_call | solution.py:625
  17.2 1.4 %collective-permute-start.8 = (f32[256,128]{1,0:T(8,128)S(1)}, f32[256,128]{1,0:T(8,128)S(1)}, u32[]{:S(2)}, u32[]{:S(2)}) collective-permute-start(f32[256,128]{1,0:T(8,128)S(1)} %get-tuple-element.69.x), channel_id=1, source_target_pairs={{4,0},{0,4},{12,8},{8,12},{20,16},{16,20},{28,24},{24,28},{5,1},{1... | collective-permute-start | bytes 393224 | tf_op jit(solution)/shard_map/ppermute | solution.py:653
  18.7 0.9 %collective-permute-start.10 = (f32[256,128]{1,0:T(8,128)S(1)}, f32[256,128]{1,0:T(8,128)S(1)}, u32[]{:S(2)}, u32[]{:S(2)}) collective-permute-start(f32[256,128]{1,0:T(8,128)S(1)} %get-tuple-element.69.x), channel_id=1, source_target_pairs={{28,0},{24,4},{20,8},{16,12},{12,16},{8,20},{4,24},{0,28},{29,1},{... | collective-permute-start | bytes 393224 | tf_op jit(solution)/shard_map/ppermute | solution.py:653
  19.6 0.0 collective-permute-done.6.y.refs_1_
  19.6 2.7 %collective-permute-start.7 = (f32[14,8,128]{2,1,0:T(8,128)S(1)}, f32[14,8,128]{2,1,0:T(8,128)S(1)}, u32[]{:S(2)}, u32[]{:S(2)}) collective-permute-start(f32[14,8,128]{2,1,0:T(8,128)S(1)} %shard_map.139._), channel_id=1, source_target_pairs={{2,0},{3,1},{0,2},{1,3},{6,4},{7,5},{4,6},{5,7},{10,8},{11,9},{8,1... | collective-permute-start | bytes 172040 | tf_op jit(solution)/shard_map/ppermute | solution.py:659
  22.2 0.1 shard_map.138
  22.3 0.8 %collective-permute-start.9 = (f32[256,128]{1,0:T(8,128)S(1)}, f32[256,128]{1,0:T(8,128)S(1)}, u32[]{:S(2)}, u32[]{:S(2)}) collective-permute-start(f32[256,128]{1,0:T(8,128)S(1)} %shard_map.141), channel_id=1, source_target_pairs={{24,0},{28,4},{16,8},{20,12},{8,16},{12,20},{0,24},{4,28},{25,1},{... | collective-permute-start | bytes 393224 | tf_op jit(solution)/shard_map/ppermute | solution.py:653
  23.1 0.1 collective-permute-start.11
  23.2 0.5 %collective-permute-start.12 = (f32[256,128]{1,0:T(8,128)S(1)}, f32[256,128]{1,0:T(8,128)S(1)}, u32[]{:S(2)}, u32[]{:S(2)}) collective-permute-start(f32[256,128]{1,0:T(8,128)S(1)} %shard_map.142), channel_id=1, source_target_pairs={{8,0},{12,4},{0,8},{4,12},{24,16},{28,20},{16,24},{20,28},{9,1},{1... | collective-permute-start | bytes 393224 | tf_op jit(solution)/shard_map/ppermute | solution.py:653
  23.7 2.5 %collective-permute-done.7.refs_2_ = f32[14,8,128]{2,1,0:T(8,128)S(1)} collective-permute-done((f32[14,8,128]{2,1,0:T(8,128)S(1)}, f32[14,8,128]{2,1,0:T(8,128)S(1)}, u32[]{:S(2)}, u32[]{:S(2)}) %collective-permute-start.7) | collective-permute-done | bytes 57376 | tf_op jit(solution)/shard_map/ppermute | solution.py:659
  26.2 1.9 %shard_map.140 = (f32[512,256]{1,0:T(8,128)S(1)}, f32[8,128]{1,0:T(8,128)S(1)}, f32[3,8,128]{2,1,0:T(8,128)S(1)}, f32[512,256]{1,0:T(8,128)S(1)}, f32[512,256]{1...) custom-call(f32[512,256]{1,0:T(8,128)S(1)} %get-tuple-element.51.part, ...), custom_call_target="tpu_custom_call" | custom-call | flops 1000000000 | bytes 1048576 | tf_op jit(solution)/shard_map/pallas_call | solution.py:625
  28.1 0.0 collective-permute-done.10.refs_2_
  28.1 1.0 %collective-permute-done.9.refs_1_ = f32[256,128]{1,0:T(8,128)S(1)} collective-permute-done((f32[256,128]{1,0:T(8,128)S(1)}, f32[256,128]{1,0:T(8,128)S(1)}, u32[]{:S(2)}, u32[]{:S(2)}) %collective-permute-start.9) | collective-permute-done | bytes 131104 | tf_op jit(solution)/shard_map/ppermute | solution.py:653
  29.2 2.5 %shard_map.143 = f32[32,8,128]{2,1,0:T(8,128)S(1)} custom-call(f32[512,256]{1,0:T(8,128)S(1)} %get-tuple-element.63.loc, f32[512,256]{1,0:T(8,128)S(1)} %get-tuple-element.64.gat, bf16[512,512]{1,0:T(8,128)(2,1)S(1)} %get-tuple-element.42.nh, bf16[512,512]{1,0:T(8,128)(2,1)S(1)} %get-tuple-element.43.nl, bf16[384,256]{1,0:T(8,128)(2,1)S(1)} %get-tuple-element.45.gh, ...), custom_call_target="tpu_custom_call" | custom-call | flops 1000000000 | bytes 1048576 | tf_op jit(solution)/shard_map/pallas_call | solution.py:625
  31.7 11.0 %all_to_all.5.mine = f32[32,8,128]{2,1,0:T(8,128)S(1)} all-to-all(f32[32,8,128]{2,1,0:T(8,128)S(1)} %shard_map.143), channel_id=1, replica_groups=mesh['gx'=4,'gy'=2,'gz'=4] {'gx','gy','gz'}, dimensions={0} | all-to-all | bytes 262144 | tf_op jit(solution)/shard_map/all_to_all | solution.py:767
  42.6 0.1 collective-permute-start.13
  42.7 1.2 %collective-permute-done.13.other = f32[32,8,128]{2,1,0:T(8,128)S(1)} collective-permute-done((f32[32,8,128]{2,1,0:T(8,128)S(1)}, f32[32,8,128]{2,1,0:T(8,128)S(1)}, u32[]{:S(2)}, u32[]{:S(2)}) %collective-permute-start.13) | collective-permute-done | bytes 131104 | tf_op jit(solution)/shard_map/ppermute | solution.py:653
  44.0 4.1 %shard_map.144 = (f32[486,1,256]{2,1,0:T(1,128)}, f32[1,1]{1,0:T(1,128)}) custom-call(s32[2]{0:T(128)S(1)} %pad_add_fusion.ids, f32[512,256]{1,0:T(8,128)S(1)} %get-tuple-element.40.f_in, f32[512,256]{1,0:T(8,128)S(1)} %get-tuple-element.62.u_in, f32[32,8,128]{2,1,0:T(8,128)S(1)} %all_to_all.5.mine, f32[32,8,128]{2,1,0:T(8,128)S(1)} %collective-permute-done.13.other, ...), custom_call_target="tpu_custom_call" | custom-call | flops 10000000 | bytes 1048576 | tf_op jit(solution)/shard_map/pallas_call | solution.py:625
  (12 shorter events, 0.1 us)
Async XLA Ops:
  2.1 10.4 %collective-permute-start = (f32[264,128]{1,0:T(8,128)S(1)}, f32[264,128]{1,0:T(8,128)S(1)}, u32[]{:S(2)}, u32[]{:S(2)}) collective-permute-start(f32[264,128]{1,0:T(8,128)S(1)} %get-tuple-element.47.refs_0_.message.charges_f), channel_id=1, source_target_pairs={{4,0},{0,4},{12,8},{8,12},{20,16},{16,20},{28,24},{24,28},{5,1},{1... | collective-permute-start | bytes 405512 | tf_op jit(solution)/shard_map/ppermute | solution.py:653
  5.1 8.7 %collective-permute-start.1 = (f32[264,128]{1,0:T(8,128)S(1)}, f32[264,128]{1,0:T(8,128)S(1)}, u32[]{:S(2)}, u32[]{:S(2)}) collective-permute-start(f32[264,128]{1,0:T(8,128)S(1)} %get-tuple-element.47.refs_0_.message.charges_f), channel_id=1, source_target_pairs={{24,0},{28,4},{16,8},{20,12},{8,16},{12,20},{0,24},{4,28},{25,1},{... | collective-permute-start | bytes 405512 | tf_op jit(solution)/shard_map/ppermute | solution.py:653
  5.7 8.0 %collective-permute-start.2 = (f32[264,128]{1,0:T(8,128)S(1)}, f32[264,128]{1,0:T(8,128)S(1)}, u32[]{:S(2)}, u32[]{:S(2)}) collective-permute-start(f32[264,128]{1,0:T(8,128)S(1)} %get-tuple-element.47.refs_0_.message.charges_f), channel_id=1, source_target_pairs={{28,0},{24,4},{20,8},{16,12},{12,16},{8,20},{4,24},{0,28},{29,1},{... | collective-permute-start | bytes 405512 | tf_op jit(solution)/shard_map/ppermute | solution.py:653
  6.3 7.6 %collective-permute-start.3 = (f32[264,128]{1,0:T(8,128)S(1)}, f32[264,128]{1,0:T(8,128)S(1)}, u32[]{:S(2)}, u32[]{:S(2)}) collective-permute-start(f32[264,128]{1,0:T(8,128)S(1)} %get-tuple-element.47.refs_0_.message.charges_f), channel_id=1, source_target_pairs={{8,0},{12,4},{0,8},{4,12},{24,16},{28,20},{16,24},{20,28},{9,1},{1... | collective-permute-start | bytes 405512 | tf_op jit(solution)/shard_map/ppermute | solution.py:653
  12.5 1.5 %collective-permute-start.4 = (f32[264,128]{1,0:T(8,128)S(1)}, f32[264,128]{1,0:T(8,128)S(1)}, u32[]{:S(2)}, u32[]{:S(2)}) collective-permute-start(f32[264,128]{1,0:T(8,128)S(1)} %shard_map.133), channel_id=1, source_target_pairs={{8,0},{12,4},{0,8},{4,12},{24,16},{28,20},{16,24},{20,28},{9,1},{1... | collective-permute-start | bytes 405512 | tf_op jit(solution)/shard_map/ppermute | solution.py:653
  13.8 1.2 %collective-permute-start.5 = (f32[8,128]{1,0:T(8,128)S(1)}, f32[8,128]{1,0:T(8,128)S(1)}, u32[]{:S(2)}, u32[]{:S(2)}) collective-permute-start(f32[8,128]{1,0:T(8,128)S(1)} %shard_map.134.refs_5_.refs_0_), channel_id=1, source_target_pairs={{8,0},{12,4},{0,8},{4,12},{24,16},{28,20},{16,24},{20,28},{9,1},{1... | collective-permute-start | bytes 12296 | tf_op jit(solution)/shard_map/ppermute | solution.py:653
  15.0 4.5 %collective-permute-start.6 = (f32[7,8,128]{2,1,0:T(8,128)S(1)}, f32[7,8,128]{2,1,0:T(8,128)S(1)}, u32[]{:S(2)}, u32[]{:S(2)}) collective-permute-start(f32[7,8,128]{2,1,0:T(8,128)S(1)} %shard_map.137.tiles.x.refs_0_), channel_id=1, source_target_pairs={{1,0},{0,1},{3,2},{2,3},{5,4},{4,5},{7,6},{6,7},{9,8},{8,9},{11,10... | collective-permute-start | bytes 86024 | tf_op jit(solution)/shard_map/ppermute | solution.py:659
  17.2 5.9 %collective-permute-start.8 = (f32[256,128]{1,0:T(8,128)S(1)}, f32[256,128]{1,0:T(8,128)S(1)}, u32[]{:S(2)}, u32[]{:S(2)}) collective-permute-start(f32[256,128]{1,0:T(8,128)S(1)} %get-tuple-element.69.x), channel_id=1, source_target_pairs={{4,0},{0,4},{12,8},{8,12},{20,16},{16,20},{28,24},{24,28},{5,1},{1... | collective-permute-start | bytes 393224 | tf_op jit(solution)/shard_map/ppermute | solution.py:653
  18.7 9.4 %collective-permute-start.10 = (f32[256,128]{1,0:T(8,128)S(1)}, f32[256,128]{1,0:T(8,128)S(1)}, u32[]{:S(2)}, u32[]{:S(2)}) collective-permute-start(f32[256,128]{1,0:T(8,128)S(1)} %get-tuple-element.69.x), channel_id=1, source_target_pairs={{28,0},{24,4},{20,8},{16,12},{12,16},{8,20},{4,24},{0,28},{29,1},{... | collective-permute-start | bytes 393224 | tf_op jit(solution)/shard_map/ppermute | solution.py:653
  19.6 6.6 %collective-permute-start.7 = (f32[14,8,128]{2,1,0:T(8,128)S(1)}, f32[14,8,128]{2,1,0:T(8,128)S(1)}, u32[]{:S(2)}, u32[]{:S(2)}) collective-permute-start(f32[14,8,128]{2,1,0:T(8,128)S(1)} %shard_map.139._), channel_id=1, source_target_pairs={{2,0},{3,1},{0,2},{1,3},{6,4},{7,5},{4,6},{5,7},{10,8},{11,9},{8,1... | collective-permute-start | bytes 172040 | tf_op jit(solution)/shard_map/ppermute | solution.py:659
  22.3 6.8 %collective-permute-start.9 = (f32[256,128]{1,0:T(8,128)S(1)}, f32[256,128]{1,0:T(8,128)S(1)}, u32[]{:S(2)}, u32[]{:S(2)}) collective-permute-start(f32[256,128]{1,0:T(8,128)S(1)} %shard_map.141), channel_id=1, source_target_pairs={{24,0},{28,4},{16,8},{20,12},{8,16},{12,20},{0,24},{4,28},{25,1},{... | collective-permute-start | bytes 393224 | tf_op jit(solution)/shard_map/ppermute | solution.py:653
  23.1 6.1 %collective-permute-start.11 = (f32[256,128]{1,0:T(8,128)S(1)}, f32[256,128]{1,0:T(8,128)S(1)}, u32[]{:S(2)}, u32[]{:S(2)}) collective-permute-start(f32[256,128]{1,0:T(8,128)S(1)} %shard_map.141), channel_id=1, source_target_pairs={{8,0},{12,4},{0,8},{4,12},{24,16},{28,20},{16,24},{20,28},{9,1},{1... | collective-permute-start | bytes 393224 | tf_op jit(solution)/shard_map/ppermute | solution.py:653
  23.2 6.0 %collective-permute-start.12 = (f32[256,128]{1,0:T(8,128)S(1)}, f32[256,128]{1,0:T(8,128)S(1)}, u32[]{:S(2)}, u32[]{:S(2)}) collective-permute-start(f32[256,128]{1,0:T(8,128)S(1)} %shard_map.142), channel_id=1, source_target_pairs={{8,0},{12,4},{0,8},{4,12},{24,16},{28,20},{16,24},{20,28},{9,1},{1... | collective-permute-start | bytes 393224 | tf_op jit(solution)/shard_map/ppermute | solution.py:653
  42.6 1.3 %collective-permute-start.13 = (f32[32,8,128]{2,1,0:T(8,128)S(1)}, f32[32,8,128]{2,1,0:T(8,128)S(1)}, u32[]{:S(2)}, u32[]{:S(2)}) collective-permute-start(f32[32,8,128]{2,1,0:T(8,128)S(1)} %all_to_all.5.mine), channel_id=1, source_target_pairs={{8,0},{12,4},{0,8},{4,12},{24,16},{28,20},{16,24},{20,28},{9,1},{1... | collective-permute-start | bytes 393224 | tf_op jit(solution)/shard_map/ppermute | solution.py:653

commit v19 on v18

--- a/solution.py
+++ b/solution.py
@@ -401,13 +401,15 @@
     hi_out[...], lo_out[...] = split(gathered)
 
 
-def gather_far(s, gat, ghost, col, values, messages):
+def gather_far_kernel(s, gat, gh, gl, col, values, *refs):
+    *messages, hi_out, lo_out = refs
     rims = unpack_rims([message[...] for message in messages], s)
     far = []
     for c in range(3):
         value = jnp.concatenate([values[i, c : c + 1, :] for i in range(values.shape[0])], axis=1)
         far.append(col[:, :1] * value)
-    return gat[...] + product(mm, split(rims + stacked(far, s)), ghost)
+    gathered = gat[...] + product(mm, split(rims + stacked(far, s)), (gh[...], gl[...]))
+    hi_out[...], lo_out[...] = split(gathered)
 
 
 def near_kernel(s, loc, nh, nl, hi, lo, out, rim_out):
@@ -452,11 +454,9 @@
 
 
 def second_kernel(
-    s, loc, gat, nh, nl, gh, gl, cells, col, f_in, ortho_in, stat, charges_f, charges_u, values, *refs
+    s, loc, nh, nl, hi, lo, cells, col, f_in, ortho_in, stat, charges_f, charges_u, packed_out
 ):
-    *messages, packed_out = refs
-    gathered = gather_far(s, gat, (gh[...], gl[...]), col, values, messages)
-    part = loc[...] + product(mm, (nh[...], nl[...]), split(gathered))
+    part = loc[...] + product(mm, (nh[...], nl[...]), (hi[...], lo[...]))
     f, ortho = f_in[...], ortho_in[...]
     ff, fu, oo = (stat[i : i + 1, :1] for i in range(3))
     fa = total(f * part) * safe_inverse(ff)
@@ -757,11 +757,16 @@
         flops=10**9,
     )
     forward_rims(got, places[1])
+    gathered = call(
+        functools.partial(gather_far_kernel, s),
+        [(full, bf16), (full, bf16)],
+        [gat, gh, gl, col, values] + [got[key] for key in s.sources],
+        flops=10**9,
+    )
     (packed,) = call(
         functools.partial(second_kernel, s),
         [((s.devices, 8, LANES), f32)],
-        [loc, gat, nh, nl, gh, gl, cells, col, f, ortho, stat, message, charges, values]
-        + [got[key] for key in s.sources],
+        [loc, nh, nl, *gathered, cells, col, f, ortho, stat, message, charges],
         flops=10**9,
     )
     boxes = lax.all_to_all(packed, ("gx", "gy", "gz"), 0, 0)

time: 48.3 us -> 47.8 us (0.990)
  Pallas kernels: 17 us -> 16.5 us
    pallas_call x14 -> x15, Pallas kernels: 17 us -> 16.5 us  [call(): pl.pallas_call(kernel, out_shape=[jax.ShapeDtypeStruct(shape, kind) for s...]
where the time goes in v19:
time: 47.8 us; the launch traced here: 47.6 us
  Pallas kernels  16.5 us (35%)
  starting transfers between devices  13 us (27%)
  blocking collectives  10.9 us (23%)
  waiting for transfers between devices  6.26 us (13%)
  between operations  0.74 us (2%)
    pallas_call x15, Pallas kernels, call(): pl.pallas_call(kernel, out_shape=[jax.ShapeDtypeStruct(shape, kind) for s...  16.5 us
    all_to_all x1, blocking collectives, body(): boxes = lax.all_to_all(packed, ('gx', 'gy', 'gz'), 0, 0)  10.9 us
    ppermute x12, starting transfers between devices, fetch(): return lax.ppermute(x, ('gx', 'gy'), pairs)  8.8 us
    ppermute x2, starting transfers between devices, fetch_layers(): parts.append(lax.ppermute(sent[-1], 'gz', pairs))  4.23 us
    ppermute x12, waiting for transfers between devices, fetch(): return lax.ppermute(x, ('gx', 'gy'), pairs)  3.78 us
    ppermute x2, waiting for transfers between devices, fetch_layers(): parts.append(lax.ppermute(sent[-1], 'gz', pairs))  2.48 us
  transfers between devices with their start and end apart: 14, of which 5 were waited for; matrix products, arithmetic and copies ran while one was open for 0% of the time, Pallas kernels for 19%

profile of v19, /device:TPU:0, one launch (start us, length us, event | category | flops | bytes accessed | tf_op | source)
XLA Modules:
  0.0 47.6 jit_solution(783091019312587567)
XLA Ops:
  0.6 1.4 %shard_map.131 = (f32[264,128]{1,0:T(8,128)S(1)}, f32[168,128]{1,0:T(8,128)S(1)}, s32[1,1,256]{2,1,0:T(1,128)S(1)}, f32[512,256]{1,0:T(8,128)S(1)}) custom-call(f32[486,1,256]{2,1,0:T(1,128)} %bitcast.9, s32[1,1,256]{2,1,0:T(1,128)} %cells.1, f32[1,162]{1,0:T(1,128)} %bitcast.10), custom_call_target="tpu_custom_call" | custom-call | flops 10000000 | bytes 1048576 | tf_op jit(solution)/shard_map/pallas_call | solution.py:625
  2.1 3.0 %collective-permute-start = (f32[264,128]{1,0:T(8,128)S(1)}, f32[264,128]{1,0:T(8,128)S(1)}, u32[]{:S(2)}, u32[]{:S(2)}) collective-permute-start(f32[264,128]{1,0:T(8,128)S(1)} %get-tuple-element.49.refs_0_.message.charges_f), channel_id=1, source_target_pairs={{4,0},{0,4},{12,8},{8,12},{20,16},{16,20},{28,24},{24,28},{5,1},{1... | collective-permute-start | bytes 405512 | tf_op jit(solution)/shard_map/ppermute | solution.py:653
  5.1 0.7 %collective-permute-start.1 = (f32[264,128]{1,0:T(8,128)S(1)}, f32[264,128]{1,0:T(8,128)S(1)}, u32[]{:S(2)}, u32[]{:S(2)}) collective-permute-start(f32[264,128]{1,0:T(8,128)S(1)} %get-tuple-element.49.refs_0_.message.charges_f), channel_id=1, source_target_pairs={{24,0},{28,4},{16,8},{20,12},{8,16},{12,20},{0,24},{4,28},{25,1},{... | collective-permute-start | bytes 405512 | tf_op jit(solution)/shard_map/ppermute | solution.py:653
  5.7 0.6 %collective-permute-start.2 = (f32[264,128]{1,0:T(8,128)S(1)}, f32[264,128]{1,0:T(8,128)S(1)}, u32[]{:S(2)}, u32[]{:S(2)}) collective-permute-start(f32[264,128]{1,0:T(8,128)S(1)} %get-tuple-element.49.refs_0_.message.charges_f), channel_id=1, source_target_pairs={{28,0},{24,4},{20,8},{16,12},{12,16},{8,20},{4,24},{0,28},{29,1},{... | collective-permute-start | bytes 405512 | tf_op jit(solution)/shard_map/ppermute | solution.py:653
  6.3 0.4 collective-permute-start.3
  6.7 0.1 pad_add_fusion.ids
  6.8 5.6 %shard_map.132 = (f32[512,256]{1,0:T(8,128)S(1)}, f32[512,256]{1,0:T(8,128)S(1)}, f32[16,256]{1,0:T(8,128)S(1)}, bf16[512,512]{1,0:T(8,128)(2,1)S(1)}, bf16[512,...) custom-call(s32[2]{0:T(128)S(1)} %pad_add_fusion.ids, ...), custom_call_target="tpu_custom_call" | custom-call | flops 5000000000 | bytes 1048576 | tf_op jit(solution)/shard_map/pallas_call | solution.py:625
  12.4 0.0 collective-permute-done.x.refs_1_.refs_0_.refs_2_
  12.5 0.2 collective-permute-start.4
  12.7 1.1 %collective-permute-done.1.refs_2_.refs_1_.refs_3_ = f32[264,128]{1,0:T(8,128)S(1)} collective-permute-done((f32[264,128]{1,0:T(8,128)S(1)}, f32[264,128]{1,0:T(8,128)S(1)}, u32[]{:S(2)}, u32[]{:S(2)}) %collective-permute-start.1) | collective-permute-done | bytes 135200 | tf_op jit(solution)/shard_map/ppermute | solution.py:653
  13.8 0.2 collective-permute-start.5
  14.0 0.0 collective-permute-done.4.refs_4_.refs_6_
  14.0 0.7 %shard_map.135 = (bf16[512,256]{1,0:T(8,128)(2,1)S(1)}, bf16[512,256]{1,0:T(8,128)(2,1)S(1)}) custom-call(f32[512,256]{1,0:T(8,128)S(1)} %get-tuple-element.46.gat, bf16[384,256]{1,0:T(8,128)(2,1)S(1)} %get-tuple-element.47.gh, bf16[384,256]{1,0:T(8,128)(2,1)S(1)} %get-tuple-element.48.gl, f32[264,128]{1,0:T(8,128)S(1)} %collective-permute-done.x.refs_1_.refs_0_.refs_2_, ...), custom_call_target="tpu_custom_call" | custom-call | flops 1000000000 | bytes 1048576 | tf_op jit(solution)/shard_map/pallas_call | solution.py:625
  14.7 0.4 collective-permute-done.5.refs_1_
  15.0 1.6 %collective-permute-start.6 = (f32[7,8,128]{2,1,0:T(8,128)S(1)}, f32[7,8,128]{2,1,0:T(8,128)S(1)}, u32[]{:S(2)}, u32[]{:S(2)}) collective-permute-start(f32[7,8,128]{2,1,0:T(8,128)S(1)} %shard_map.137.tiles.x.refs_0_), channel_id=1, source_target_pairs={{1,0},{0,1},{3,2},{2,3},{5,4},{4,5},{7,6},{6,7},{9,8},{8,9},{11,10... | collective-permute-start | bytes 86024 | tf_op jit(solution)/shard_map/ppermute | solution.py:659
  16.6 0.6 %shard_map.136 = (f32[512,256]{1,0:T(8,128)S(1)}, f32[256,128]{1,0:T(8,128)S(1)}) custom-call(f32[512,256]{1,0:T(8,128)S(1)} %get-tuple-element.43.loc, bf16[512,512]{1,0:T(8,128)(2,1)S(1)} %get-tuple-element.44.nh, bf16[512,512]{1,0:T(8,128)(2,1)S(1)} %get-tuple-element.45.nl, bf16[512,256]{1,0:T(8,128)(2,1)S(1)} %get-tuple-element.51.hi, ...), custom_call_target="tpu_custom_call" | custom-call | flops 1000000000 | bytes 1048576 | tf_op jit(solution)/shard_map/pallas_call | solution.py:625
  17.2 1.4 %collective-permute-start.8 = (f32[256,128]{1,0:T(8,128)S(1)}, f32[256,128]{1,0:T(8,128)S(1)}, u32[]{:S(2)}, u32[]{:S(2)}) collective-permute-start(f32[256,128]{1,0:T(8,128)S(1)} %get-tuple-element.68.x), channel_id=1, source_target_pairs={{4,0},{0,4},{12,8},{8,12},{20,16},{16,20},{28,24},{24,28},{5,1},{1... | collective-permute-start | bytes 393224 | tf_op jit(solution)/shard_map/ppermute | solution.py:653
  18.7 0.9 %collective-permute-start.10 = (f32[256,128]{1,0:T(8,128)S(1)}, f32[256,128]{1,0:T(8,128)S(1)}, u32[]{:S(2)}, u32[]{:S(2)}) collective-permute-start(f32[256,128]{1,0:T(8,128)S(1)} %get-tuple-element.68.x), channel_id=1, source_target_pairs={{28,0},{24,4},{20,8},{16,12},{12,16},{8,20},{4,24},{0,28},{29,1},{... | collective-permute-start | bytes 393224 | tf_op jit(solution)/shard_map/ppermute | solution.py:653
  19.6 2.6 %collective-permute-start.7 = (f32[14,8,128]{2,1,0:T(8,128)S(1)}, f32[14,8,128]{2,1,0:T(8,128)S(1)}, u32[]{:S(2)}, u32[]{:S(2)}) collective-permute-start(f32[14,8,128]{2,1,0:T(8,128)S(1)} %shard_map.139._), channel_id=1, source_target_pairs={{2,0},{3,1},{0,2},{1,3},{6,4},{7,5},{4,6},{5,7},{10,8},{11,9},{8,1... | collective-permute-start | bytes 172040 | tf_op jit(solution)/shard_map/ppermute | solution.py:659
  22.2 0.1 shard_map.138
  22.4 0.8 %collective-permute-start.9 = (f32[256,128]{1,0:T(8,128)S(1)}, f32[256,128]{1,0:T(8,128)S(1)}, u32[]{:S(2)}, u32[]{:S(2)}) collective-permute-start(f32[256,128]{1,0:T(8,128)S(1)} %shard_map.141), channel_id=1, source_target_pairs={{24,0},{28,4},{16,8},{20,12},{8,16},{12,20},{0,24},{4,28},{25,1},{... | collective-permute-start | bytes 393224 | tf_op jit(solution)/shard_map/ppermute | solution.py:653
  23.1 0.1 collective-permute-start.11
  23.2 0.5 %collective-permute-start.12 = (f32[256,128]{1,0:T(8,128)S(1)}, f32[256,128]{1,0:T(8,128)S(1)}, u32[]{:S(2)}, u32[]{:S(2)}) collective-permute-start(f32[256,128]{1,0:T(8,128)S(1)} %shard_map.142), channel_id=1, source_target_pairs={{8,0},{12,4},{0,8},{4,12},{24,16},{28,20},{16,24},{20,28},{9,1},{1... | collective-permute-start | bytes 393224 | tf_op jit(solution)/shard_map/ppermute | solution.py:653
  23.7 2.5 %collective-permute-done.7.refs_2_ = f32[14,8,128]{2,1,0:T(8,128)S(1)} collective-permute-done((f32[14,8,128]{2,1,0:T(8,128)S(1)}, f32[14,8,128]{2,1,0:T(8,128)S(1)}, u32[]{:S(2)}, u32[]{:S(2)}) %collective-permute-start.7) | collective-permute-done | bytes 57376 | tf_op jit(solution)/shard_map/ppermute | solution.py:659
  26.2 1.9 %shard_map.140 = (f32[512,256]{1,0:T(8,128)S(1)}, f32[8,128]{1,0:T(8,128)S(1)}, f32[3,8,128]{2,1,0:T(8,128)S(1)}, f32[512,256]{1,0:T(8,128)S(1)}, f32[512,256]{1...) custom-call(f32[512,256]{1,0:T(8,128)S(1)} %get-tuple-element.53.part, ...), custom_call_target="tpu_custom_call" | custom-call | flops 1000000000 | bytes 1048576 | tf_op jit(solution)/shard_map/pallas_call | solution.py:625
  28.1 1.1 %collective-permute-done.9.refs_1_ = f32[256,128]{1,0:T(8,128)S(1)} collective-permute-done((f32[256,128]{1,0:T(8,128)S(1)}, f32[256,128]{1,0:T(8,128)S(1)}, u32[]{:S(2)}, u32[]{:S(2)}) %collective-permute-start.9) | collective-permute-done | bytes 131104 | tf_op jit(solution)/shard_map/ppermute | solution.py:653
  29.2 0.7 %shard_map.143 = (bf16[512,256]{1,0:T(8,128)(2,1)S(1)}, bf16[512,256]{1,0:T(8,128)(2,1)S(1)}) custom-call(f32[512,256]{1,0:T(8,128)S(1)} %get-tuple-element.66.gat, bf16[384,256]{1,0:T(8,128)(2,1)S(1)} %get-tuple-element.47.gh, bf16[384,256]{1,0:T(8,128)(2,1)S(1)} %get-tuple-element.48.gl, f32[168,128]{1,0:T(8,128)S(1)} %get-tuple-element.59.col, ...), custom_call_target="tpu_custom_call" | custom-call | flops 1000000000 | bytes 1048576 | tf_op jit(solution)/shard_map/pallas_call | solution.py:625
  29.9 1.3 %shard_map.144 = f32[32,8,128]{2,1,0:T(8,128)S(1)} custom-call(f32[512,256]{1,0:T(8,128)S(1)} %get-tuple-element.65.loc, bf16[512,512]{1,0:T(8,128)(2,1)S(1)} %get-tuple-element.44.nh, bf16[512,512]{1,0:T(8,128)(2,1)S(1)} %get-tuple-element.45.nl, bf16[512,256]{1,0:T(8,128)(2,1)S(1)} %get-tuple-element.69.hi, bf16[512,256]{1,0:T(8,128)(2,1)S(1)} %get-tuple-element.70.lo, ...), custom_call_target="tpu_custom_call" | custom-call | flops 1000000000 | bytes 1048576 | tf_op jit(solution)/shard_map/pallas_call | solution.py:625
  31.2 10.9 %all_to_all.5.mine = f32[32,8,128]{2,1,0:T(8,128)S(1)} all-to-all(f32[32,8,128]{2,1,0:T(8,128)S(1)} %shard_map.144), channel_id=1, replica_groups=mesh['gx'=4,'gy'=2,'gz'=4] {'gx','gy','gz'}, dimensions={0} | all-to-all | bytes 262144 | tf_op jit(solution)/shard_map/all_to_all | solution.py:772
  42.1 0.1 collective-permute-start.13
  42.2 1.2 %collective-permute-done.13.other = f32[32,8,128]{2,1,0:T(8,128)S(1)} collective-permute-done((f32[32,8,128]{2,1,0:T(8,128)S(1)}, f32[32,8,128]{2,1,0:T(8,128)S(1)}, u32[]{:S(2)}, u32[]{:S(2)}) %collective-permute-start.13) | collective-permute-done | bytes 131104 | tf_op jit(solution)/shard_map/ppermute | solution.py:653
  43.4 4.1 %shard_map.145 = (f32[486,1,256]{2,1,0:T(1,128)}, f32[1,1]{1,0:T(1,128)}) custom-call(s32[2]{0:T(128)S(1)} %pad_add_fusion.ids, f32[512,256]{1,0:T(8,128)S(1)} %get-tuple-element.42.f_in, f32[512,256]{1,0:T(8,128)S(1)} %get-tuple-element.64.u_in, f32[32,8,128]{2,1,0:T(8,128)S(1)} %all_to_all.5.mine, f32[32,8,128]{2,1,0:T(8,128)S(1)} %collective-permute-done.13.other, ...), custom_call_target="tpu_custom_call" | custom-call | flops 10000000 | bytes 1048576 | tf_op jit(solution)/shard_map/pallas_call | solution.py:625
  (13 shorter events, 0.1 us)
Async XLA Ops:
  2.1 10.4 %collective-permute-start = (f32[264,128]{1,0:T(8,128)S(1)}, f32[264,128]{1,0:T(8,128)S(1)}, u32[]{:S(2)}, u32[]{:S(2)}) collective-permute-start(f32[264,128]{1,0:T(8,128)S(1)} %get-tuple-element.49.refs_0_.message.charges_f), channel_id=1, source_target_pairs={{4,0},{0,4},{12,8},{8,12},{20,16},{16,20},{28,24},{24,28},{5,1},{1... | collective-permute-start | bytes 405512 | tf_op jit(solution)/shard_map/ppermute | solution.py:653
  5.1 8.7 %collective-permute-start.1 = (f32[264,128]{1,0:T(8,128)S(1)}, f32[264,128]{1,0:T(8,128)S(1)}, u32[]{:S(2)}, u32[]{:S(2)}) collective-permute-start(f32[264,128]{1,0:T(8,128)S(1)} %get-tuple-element.49.refs_0_.message.charges_f), channel_id=1, source_target_pairs={{24,0},{28,4},{16,8},{20,12},{8,16},{12,20},{0,24},{4,28},{25,1},{... | collective-permute-start | bytes 405512 | tf_op jit(solution)/shard_map/ppermute | solution.py:653
  5.7 8.0 %collective-permute-start.2 = (f32[264,128]{1,0:T(8,128)S(1)}, f32[264,128]{1,0:T(8,128)S(1)}, u32[]{:S(2)}, u32[]{:S(2)}) collective-permute-start(f32[264,128]{1,0:T(8,128)S(1)} %get-tuple-element.49.refs_0_.message.charges_f), channel_id=1, source_target_pairs={{28,0},{24,4},{20,8},{16,12},{12,16},{8,20},{4,24},{0,28},{29,1},{... | collective-permute-start | bytes 405512 | tf_op jit(solution)/shard_map/ppermute | solution.py:653
  6.3 7.6 %collective-permute-start.3 = (f32[264,128]{1,0:T(8,128)S(1)}, f32[264,128]{1,0:T(8,128)S(1)}, u32[]{:S(2)}, u32[]{:S(2)}) collective-permute-start(f32[264,128]{1,0:T(8,128)S(1)} %get-tuple-element.49.refs_0_.message.charges_f), channel_id=1, source_target_pairs={{8,0},{12,4},{0,8},{4,12},{24,16},{28,20},{16,24},{20,28},{9,1},{1... | collective-permute-start | bytes 405512 | tf_op jit(solution)/shard_map/ppermute | solution.py:653
  12.5 1.5 %collective-permute-start.4 = (f32[264,128]{1,0:T(8,128)S(1)}, f32[264,128]{1,0:T(8,128)S(1)}, u32[]{:S(2)}, u32[]{:S(2)}) collective-permute-start(f32[264,128]{1,0:T(8,128)S(1)} %shard_map.133), channel_id=1, source_target_pairs={{8,0},{12,4},{0,8},{4,12},{24,16},{28,20},{16,24},{20,28},{9,1},{1... | collective-permute-start | bytes 405512 | tf_op jit(solution)/shard_map/ppermute | solution.py:653
  13.8 1.2 %collective-permute-start.5 = (f32[8,128]{1,0:T(8,128)S(1)}, f32[8,128]{1,0:T(8,128)S(1)}, u32[]{:S(2)}, u32[]{:S(2)}) collective-permute-start(f32[8,128]{1,0:T(8,128)S(1)} %shard_map.134.refs_5_.refs_0_), channel_id=1, source_target_pairs={{8,0},{12,4},{0,8},{4,12},{24,16},{28,20},{16,24},{20,28},{9,1},{1... | collective-permute-start | bytes 12296 | tf_op jit(solution)/shard_map/ppermute | solution.py:653
  15.0 4.5 %collective-permute-start.6 = (f32[7,8,128]{2,1,0:T(8,128)S(1)}, f32[7,8,128]{2,1,0:T(8,128)S(1)}, u32[]{:S(2)}, u32[]{:S(2)}) collective-permute-start(f32[7,8,128]{2,1,0:T(8,128)S(1)} %shard_map.137.tiles.x.refs_0_), channel_id=1, source_target_pairs={{1,0},{0,1},{3,2},{2,3},{5,4},{4,5},{7,6},{6,7},{9,8},{8,9},{11,10... | collective-permute-start | bytes 86024 | tf_op jit(solution)/shard_map/ppermute | solution.py:659
  17.2 6.0 %collective-permute-start.8 = (f32[256,128]{1,0:T(8,128)S(1)}, f32[256,128]{1,0:T(8,128)S(1)}, u32[]{:S(2)}, u32[]{:S(2)}) collective-permute-start(f32[256,128]{1,0:T(8,128)S(1)} %get-tuple-element.68.x), channel_id=1, source_target_pairs={{4,0},{0,4},{12,8},{8,12},{20,16},{16,20},{28,24},{24,28},{5,1},{1... | collective-permute-start | bytes 393224 | tf_op jit(solution)/shard_map/ppermute | solution.py:653
  18.7 9.4 %collective-permute-start.10 = (f32[256,128]{1,0:T(8,128)S(1)}, f32[256,128]{1,0:T(8,128)S(1)}, u32[]{:S(2)}, u32[]{:S(2)}) collective-permute-start(f32[256,128]{1,0:T(8,128)S(1)} %get-tuple-element.68.x), channel_id=1, source_target_pairs={{28,0},{24,4},{20,8},{16,12},{12,16},{8,20},{4,24},{0,28},{29,1},{... | collective-permute-start | bytes 393224 | tf_op jit(solution)/shard_map/ppermute | solution.py:653
  19.6 6.6 %collective-permute-start.7 = (f32[14,8,128]{2,1,0:T(8,128)S(1)}, f32[14,8,128]{2,1,0:T(8,128)S(1)}, u32[]{:S(2)}, u32[]{:S(2)}) collective-permute-start(f32[14,8,128]{2,1,0:T(8,128)S(1)} %shard_map.139._), channel_id=1, source_target_pairs={{2,0},{3,1},{0,2},{1,3},{6,4},{7,5},{4,6},{5,7},{10,8},{11,9},{8,1... | collective-permute-start | bytes 172040 | tf_op jit(solution)/shard_map/ppermute | solution.py:659
  22.4 6.8 %collective-permute-start.9 = (f32[256,128]{1,0:T(8,128)S(1)}, f32[256,128]{1,0:T(8,128)S(1)}, u32[]{:S(2)}, u32[]{:S(2)}) collective-permute-start(f32[256,128]{1,0:T(8,128)S(1)} %shard_map.141), channel_id=1, source_target_pairs={{24,0},{28,4},{16,8},{20,12},{8,16},{12,20},{0,24},{4,28},{25,1},{... | collective-permute-start | bytes 393224 | tf_op jit(solution)/shard_map/ppermute | solution.py:653
  23.1 6.1 %collective-permute-start.11 = (f32[256,128]{1,0:T(8,128)S(1)}, f32[256,128]{1,0:T(8,128)S(1)}, u32[]{:S(2)}, u32[]{:S(2)}) collective-permute-start(f32[256,128]{1,0:T(8,128)S(1)} %shard_map.141), channel_id=1, source_target_pairs={{8,0},{12,4},{0,8},{4,12},{24,16},{28,20},{16,24},{20,28},{9,1},{1... | collective-permute-start | bytes 393224 | tf_op jit(solution)/shard_map/ppermute | solution.py:653
  23.2 6.0 %collective-permute-start.12 = (f32[256,128]{1,0:T(8,128)S(1)}, f32[256,128]{1,0:T(8,128)S(1)}, u32[]{:S(2)}, u32[]{:S(2)}) collective-permute-start(f32[256,128]{1,0:T(8,128)S(1)} %shard_map.142), channel_id=1, source_target_pairs={{8,0},{12,4},{0,8},{4,12},{24,16},{28,20},{16,24},{20,28},{9,1},{1... | collective-permute-start | bytes 393224 | tf_op jit(solution)/shard_map/ppermute | solution.py:653
  42.1 1.3 %collective-permute-start.13 = (f32[32,8,128]{2,1,0:T(8,128)S(1)}, f32[32,8,128]{2,1,0:T(8,128)S(1)}, u32[]{:S(2)}, u32[]{:S(2)}) collective-permute-start(f32[32,8,128]{2,1,0:T(8,128)S(1)} %all_to_all.5.mine), channel_id=1, source_target_pairs={{8,0},{12,4},{0,8},{4,12},{24,16},{28,20},{16,24},{20,28},{9,1},{1... | collective-permute-start | bytes 393224 | tf_op jit(solution)/shard_map/ppermute | solution.py:653

commit v20 on v19

--- a/solution.py
+++ b/solution.py
@@ -665,12 +665,12 @@
     def fetch_rims(rim, after=None):
         got = {}
         for dy in s.shifts:
-            got["other", dy] = fetch(rim, "other", dy)
-        for dy in s.shifts:
             got["same", dy] = fetch(rim, "same", dy)
+        got["other", 0] = fetch(rim, "other", 0)
         if after is not None:
             (rim,) = call(order_kernel, [(rim.shape, f32)], [rim, after])
-        got["other", 0] = fetch(rim, "other", 0)
+        for dy in s.shifts:
+            got["other", dy] = fetch(rim, "other", dy)
         got["partner", 0] = fetch(rim, "partner", 0)
         return got
 

time: 47.8 us -> 47.4 us (level)
  waiting for transfers between devices: 6.26 us -> 5.16 us
  starting transfers between devices: 13 us -> 13.5 us
    ppermute x12, waiting for transfers between devices: 3.78 us -> 3.14 us  [fetch(): return lax.ppermute(x, ('gx', 'gy'), pairs)]
where the time goes in v20:
time: 47.4 us; the launch traced here: 47.2 us
  Pallas kernels  16.5 us (35%)
  starting transfers between devices  13.5 us (28%)
  blocking collectives  11.1 us (23%)
  waiting for transfers between devices  5.16 us (11%)
  between operations  0.75 us (2%)
    pallas_call x15, Pallas kernels, call(): pl.pallas_call(kernel, out_shape=[jax.ShapeDtypeStruct(shape, kind) for s...  16.5 us
    all_to_all x1, blocking collectives, body(): boxes = lax.all_to_all(packed, ('gx', 'gy', 'gz'), 0, 0)  11.1 us
    ppermute x12, starting transfers between devices, fetch(): return lax.ppermute(x, ('gx', 'gy'), pairs)  9.28 us
    ppermute x2, starting transfers between devices, fetch_layers(): parts.append(lax.ppermute(sent[-1], 'gz', pairs))  4.23 us
    ppermute x12, waiting for transfers between devices, fetch(): return lax.ppermute(x, ('gx', 'gy'), pairs)  3.14 us
    ppermute x2, waiting for transfers between devices, fetch_layers(): parts.append(lax.ppermute(sent[-1], 'gz', pairs))  2.02 us
  transfers between devices with their start and end apart: 14, of which 5 were waited for; matrix products, arithmetic and copies ran while one was open for 0% of the time, Pallas kernels for 19%

profile of v20, /device:TPU:0, one launch (start us, length us, event | category | flops | bytes accessed | tf_op | source)
XLA Modules:
  0.0 47.2 jit_solution(6282148942598967501)
XLA Ops:
  0.6 1.4 %shard_map.131 = (f32[264,128]{1,0:T(8,128)S(1)}, f32[168,128]{1,0:T(8,128)S(1)}, s32[1,1,256]{2,1,0:T(1,128)S(1)}, f32[512,256]{1,0:T(8,128)S(1)}) custom-call(f32[486,1,256]{2,1,0:T(1,128)} %bitcast.9, s32[1,1,256]{2,1,0:T(1,128)} %cells.1, f32[1,162]{1,0:T(1,128)} %bitcast.10), custom_call_target="tpu_custom_call" | custom-call | flops 10000000 | bytes 1048576 | tf_op jit(solution)/shard_map/pallas_call | solution.py:625
  2.1 3.0 %collective-permute-start = (f32[264,128]{1,0:T(8,128)S(1)}, f32[264,128]{1,0:T(8,128)S(1)}, u32[]{:S(2)}, u32[]{:S(2)}) collective-permute-start(f32[264,128]{1,0:T(8,128)S(1)} %get-tuple-element.49.refs_0_.message.charges_f), channel_id=1, source_target_pairs={{4,0},{0,4},{12,8},{8,12},{20,16},{16,20},{28,24},{24,28},{5,1},{1... | collective-permute-start | bytes 405512 | tf_op jit(solution)/shard_map/ppermute | solution.py:653
  5.1 0.7 %collective-permute-start.1 = (f32[264,128]{1,0:T(8,128)S(1)}, f32[264,128]{1,0:T(8,128)S(1)}, u32[]{:S(2)}, u32[]{:S(2)}) collective-permute-start(f32[264,128]{1,0:T(8,128)S(1)} %get-tuple-element.49.refs_0_.message.charges_f), channel_id=1, source_target_pairs={{24,0},{28,4},{16,8},{20,12},{8,16},{12,20},{0,24},{4,28},{25,1},{... | collective-permute-start | bytes 405512 | tf_op jit(solution)/shard_map/ppermute | solution.py:653
  5.7 0.6 %collective-permute-start.2 = (f32[264,128]{1,0:T(8,128)S(1)}, f32[264,128]{1,0:T(8,128)S(1)}, u32[]{:S(2)}, u32[]{:S(2)}) collective-permute-start(f32[264,128]{1,0:T(8,128)S(1)} %get-tuple-element.49.refs_0_.message.charges_f), channel_id=1, source_target_pairs={{28,0},{24,4},{20,8},{16,12},{12,16},{8,20},{4,24},{0,28},{29,1},{... | collective-permute-start | bytes 405512 | tf_op jit(solution)/shard_map/ppermute | solution.py:653
  6.3 0.4 collective-permute-start.3
  6.7 0.1 pad_add_fusion.ids
  6.8 5.6 %shard_map.132 = (f32[512,256]{1,0:T(8,128)S(1)}, f32[512,256]{1,0:T(8,128)S(1)}, f32[16,256]{1,0:T(8,128)S(1)}, bf16[512,512]{1,0:T(8,128)(2,1)S(1)}, bf16[512,...) custom-call(s32[2]{0:T(128)S(1)} %pad_add_fusion.ids, ...), custom_call_target="tpu_custom_call" | custom-call | flops 5000000000 | bytes 1048576 | tf_op jit(solution)/shard_map/pallas_call | solution.py:625
  12.4 0.0 collective-permute-done.x.refs_1_.refs_0_.refs_2_
  12.5 0.2 collective-permute-start.4
  12.7 1.1 %collective-permute-done.1.refs_2_.refs_1_.refs_3_ = f32[264,128]{1,0:T(8,128)S(1)} collective-permute-done((f32[264,128]{1,0:T(8,128)S(1)}, f32[264,128]{1,0:T(8,128)S(1)}, u32[]{:S(2)}, u32[]{:S(2)}) %collective-permute-start.1) | collective-permute-done | bytes 135200 | tf_op jit(solution)/shard_map/ppermute | solution.py:653
  13.8 0.0 collective-permute-done.2.refs_3_.refs_2_.refs_4_
  13.8 0.2 collective-permute-start.5
  14.0 0.7 %shard_map.135 = (bf16[512,256]{1,0:T(8,128)(2,1)S(1)}, bf16[512,256]{1,0:T(8,128)(2,1)S(1)}) custom-call(f32[512,256]{1,0:T(8,128)S(1)} %get-tuple-element.46.gat, bf16[384,256]{1,0:T(8,128)(2,1)S(1)} %get-tuple-element.47.gh, bf16[384,256]{1,0:T(8,128)(2,1)S(1)} %get-tuple-element.48.gl, f32[264,128]{1,0:T(8,128)S(1)} %collective-permute-done.x.refs_1_.refs_0_.refs_2_, ...), custom_call_target="tpu_custom_call" | custom-call | flops 1000000000 | bytes 1048576 | tf_op jit(solution)/shard_map/pallas_call | solution.py:625
  14.7 0.4 collective-permute-done.5.refs_1_
  15.0 1.6 %collective-permute-start.6 = (f32[7,8,128]{2,1,0:T(8,128)S(1)}, f32[7,8,128]{2,1,0:T(8,128)S(1)}, u32[]{:S(2)}, u32[]{:S(2)}) collective-permute-start(f32[7,8,128]{2,1,0:T(8,128)S(1)} %shard_map.137.tiles.x.refs_0_), channel_id=1, source_target_pairs={{1,0},{0,1},{3,2},{2,3},{5,4},{4,5},{7,6},{6,7},{9,8},{8,9},{11,10... | collective-permute-start | bytes 86024 | tf_op jit(solution)/shard_map/ppermute | solution.py:659
  16.6 0.6 %shard_map.136 = (f32[512,256]{1,0:T(8,128)S(1)}, f32[256,128]{1,0:T(8,128)S(1)}) custom-call(f32[512,256]{1,0:T(8,128)S(1)} %get-tuple-element.43.loc, bf16[512,512]{1,0:T(8,128)(2,1)S(1)} %get-tuple-element.44.nh, bf16[512,512]{1,0:T(8,128)(2,1)S(1)} %get-tuple-element.45.nl, bf16[512,256]{1,0:T(8,128)(2,1)S(1)} %get-tuple-element.51.hi, ...), custom_call_target="tpu_custom_call" | custom-call | flops 1000000000 | bytes 1048576 | tf_op jit(solution)/shard_map/pallas_call | solution.py:625
  17.2 1.4 %collective-permute-start.8 = (f32[256,128]{1,0:T(8,128)S(1)}, f32[256,128]{1,0:T(8,128)S(1)}, u32[]{:S(2)}, u32[]{:S(2)}) collective-permute-start(f32[256,128]{1,0:T(8,128)S(1)} %get-tuple-element.68.x), channel_id=1, source_target_pairs={{4,0},{0,4},{12,8},{8,12},{20,16},{16,20},{28,24},{24,28},{5,1},{1... | collective-permute-start | bytes 393224 | tf_op jit(solution)/shard_map/ppermute | solution.py:653
  18.7 0.9 %collective-permute-start.9 = (f32[256,128]{1,0:T(8,128)S(1)}, f32[256,128]{1,0:T(8,128)S(1)}, u32[]{:S(2)}, u32[]{:S(2)}) collective-permute-start(f32[256,128]{1,0:T(8,128)S(1)} %get-tuple-element.68.x), channel_id=1, source_target_pairs={{24,0},{28,4},{16,8},{20,12},{8,16},{12,20},{0,24},{4,28},{25,1},{... | collective-permute-start | bytes 393224 | tf_op jit(solution)/shard_map/ppermute | solution.py:653
  19.6 2.7 %collective-permute-start.7 = (f32[14,8,128]{2,1,0:T(8,128)S(1)}, f32[14,8,128]{2,1,0:T(8,128)S(1)}, u32[]{:S(2)}, u32[]{:S(2)}) collective-permute-start(f32[14,8,128]{2,1,0:T(8,128)S(1)} %shard_map.139._), channel_id=1, source_target_pairs={{2,0},{3,1},{0,2},{1,3},{6,4},{7,5},{4,6},{5,7},{10,8},{11,9},{8,1... | collective-permute-start | bytes 172040 | tf_op jit(solution)/shard_map/ppermute | solution.py:659
  22.2 0.1 shard_map.138
  22.4 0.7 %collective-permute-start.10 = (f32[256,128]{1,0:T(8,128)S(1)}, f32[256,128]{1,0:T(8,128)S(1)}, u32[]{:S(2)}, u32[]{:S(2)}) collective-permute-start(f32[256,128]{1,0:T(8,128)S(1)} %shard_map.141), channel_id=1, source_target_pairs={{28,0},{24,4},{20,8},{16,12},{12,16},{8,20},{4,24},{0,28},{29,1},{... | collective-permute-start | bytes 393224 | tf_op jit(solution)/shard_map/ppermute | solution.py:653
  23.1 1.0 %collective-permute-start.11 = (f32[256,128]{1,0:T(8,128)S(1)}, f32[256,128]{1,0:T(8,128)S(1)}, u32[]{:S(2)}, u32[]{:S(2)}) collective-permute-start(f32[256,128]{1,0:T(8,128)S(1)} %shard_map.141), channel_id=1, source_target_pairs={{8,0},{12,4},{0,8},{4,12},{24,16},{28,20},{16,24},{20,28},{9,1},{1... | collective-permute-start | bytes 393224 | tf_op jit(solution)/shard_map/ppermute | solution.py:653
  24.1 0.1 collective-permute-start.12
  24.2 2.0 %collective-permute-done.7.refs_2_ = f32[14,8,128]{2,1,0:T(8,128)S(1)} collective-permute-done((f32[14,8,128]{2,1,0:T(8,128)S(1)}, f32[14,8,128]{2,1,0:T(8,128)S(1)}, u32[]{:S(2)}, u32[]{:S(2)}) %collective-permute-start.7) | collective-permute-done | bytes 57376 | tf_op jit(solution)/shard_map/ppermute | solution.py:659
  26.2 1.9 %shard_map.140 = (f32[512,256]{1,0:T(8,128)S(1)}, f32[8,128]{1,0:T(8,128)S(1)}, f32[3,8,128]{2,1,0:T(8,128)S(1)}, f32[512,256]{1,0:T(8,128)S(1)}, f32[512,256]{1...) custom-call(f32[512,256]{1,0:T(8,128)S(1)} %get-tuple-element.53.part, ...), custom_call_target="tpu_custom_call" | custom-call | flops 1000000000 | bytes 1048576 | tf_op jit(solution)/shard_map/pallas_call | solution.py:625
  28.2 0.4 collective-permute-done.10.refs_2_
  28.6 0.7 %shard_map.143 = (bf16[512,256]{1,0:T(8,128)(2,1)S(1)}, bf16[512,256]{1,0:T(8,128)(2,1)S(1)}) custom-call(f32[512,256]{1,0:T(8,128)S(1)} %get-tuple-element.66.gat, bf16[384,256]{1,0:T(8,128)(2,1)S(1)} %get-tuple-element.47.gh, bf16[384,256]{1,0:T(8,128)(2,1)S(1)} %get-tuple-element.48.gl, f32[168,128]{1,0:T(8,128)S(1)} %get-tuple-element.59.col, ...), custom_call_target="tpu_custom_call" | custom-call | flops 1000000000 | bytes 1048576 | tf_op jit(solution)/shard_map/pallas_call | solution.py:625
  29.3 1.3 %shard_map.144 = f32[32,8,128]{2,1,0:T(8,128)S(1)} custom-call(f32[512,256]{1,0:T(8,128)S(1)} %get-tuple-element.65.loc, bf16[512,512]{1,0:T(8,128)(2,1)S(1)} %get-tuple-element.44.nh, bf16[512,512]{1,0:T(8,128)(2,1)S(1)} %get-tuple-element.45.nl, bf16[512,256]{1,0:T(8,128)(2,1)S(1)} %get-tuple-element.69.hi, bf16[512,256]{1,0:T(8,128)(2,1)S(1)} %get-tuple-element.70.lo, ...), custom_call_target="tpu_custom_call" | custom-call | flops 1000000000 | bytes 1048576 | tf_op jit(solution)/shard_map/pallas_call | solution.py:625
  30.6 11.1 %all_to_all.5.mine = f32[32,8,128]{2,1,0:T(8,128)S(1)} all-to-all(f32[32,8,128]{2,1,0:T(8,128)S(1)} %shard_map.144), channel_id=1, replica_groups=mesh['gx'=4,'gy'=2,'gz'=4] {'gx','gy','gz'}, dimensions={0} | all-to-all | bytes 262144 | tf_op jit(solution)/shard_map/all_to_all | solution.py:772
  41.7 0.1 collective-permute-start.13
  41.8 1.2 %collective-permute-done.13.other = f32[32,8,128]{2,1,0:T(8,128)S(1)} collective-permute-done((f32[32,8,128]{2,1,0:T(8,128)S(1)}, f32[32,8,128]{2,1,0:T(8,128)S(1)}, u32[]{:S(2)}, u32[]{:S(2)}) %collective-permute-start.13) | collective-permute-done | bytes 131104 | tf_op jit(solution)/shard_map/ppermute | solution.py:653
  43.0 4.1 %shard_map.145 = (f32[486,1,256]{2,1,0:T(1,128)}, f32[1,1]{1,0:T(1,128)}) custom-call(s32[2]{0:T(128)S(1)} %pad_add_fusion.ids, f32[512,256]{1,0:T(8,128)S(1)} %get-tuple-element.42.f_in, f32[512,256]{1,0:T(8,128)S(1)} %get-tuple-element.64.u_in, f32[32,8,128]{2,1,0:T(8,128)S(1)} %all_to_all.5.mine, f32[32,8,128]{2,1,0:T(8,128)S(1)} %collective-permute-done.13.other, ...), custom_call_target="tpu_custom_call" | custom-call | flops 10000000 | bytes 1048576 | tf_op jit(solution)/shard_map/pallas_call | solution.py:625
  (13 shorter events, 0.1 us)
Async XLA Ops:
  2.1 10.4 %collective-permute-start = (f32[264,128]{1,0:T(8,128)S(1)}, f32[264,128]{1,0:T(8,128)S(1)}, u32[]{:S(2)}, u32[]{:S(2)}) collective-permute-start(f32[264,128]{1,0:T(8,128)S(1)} %get-tuple-element.49.refs_0_.message.charges_f), channel_id=1, source_target_pairs={{4,0},{0,4},{12,8},{8,12},{20,16},{16,20},{28,24},{24,28},{5,1},{1... | collective-permute-start | bytes 405512 | tf_op jit(solution)/shard_map/ppermute | solution.py:653
  5.1 8.7 %collective-permute-start.1 = (f32[264,128]{1,0:T(8,128)S(1)}, f32[264,128]{1,0:T(8,128)S(1)}, u32[]{:S(2)}, u32[]{:S(2)}) collective-permute-start(f32[264,128]{1,0:T(8,128)S(1)} %get-tuple-element.49.refs_0_.message.charges_f), channel_id=1, source_target_pairs={{24,0},{28,4},{16,8},{20,12},{8,16},{12,20},{0,24},{4,28},{25,1},{... | collective-permute-start | bytes 405512 | tf_op jit(solution)/shard_map/ppermute | solution.py:653
  5.7 8.0 %collective-permute-start.2 = (f32[264,128]{1,0:T(8,128)S(1)}, f32[264,128]{1,0:T(8,128)S(1)}, u32[]{:S(2)}, u32[]{:S(2)}) collective-permute-start(f32[264,128]{1,0:T(8,128)S(1)} %get-tuple-element.49.refs_0_.message.charges_f), channel_id=1, source_target_pairs={{28,0},{24,4},{20,8},{16,12},{12,16},{8,20},{4,24},{0,28},{29,1},{... | collective-permute-start | bytes 405512 | tf_op jit(solution)/shard_map/ppermute | solution.py:653
  6.3 7.6 %collective-permute-start.3 = (f32[264,128]{1,0:T(8,128)S(1)}, f32[264,128]{1,0:T(8,128)S(1)}, u32[]{:S(2)}, u32[]{:S(2)}) collective-permute-start(f32[264,128]{1,0:T(8,128)S(1)} %get-tuple-element.49.refs_0_.message.charges_f), channel_id=1, source_target_pairs={{8,0},{12,4},{0,8},{4,12},{24,16},{28,20},{16,24},{20,28},{9,1},{1... | collective-permute-start | bytes 405512 | tf_op jit(solution)/shard_map/ppermute | solution.py:653
  12.5 1.5 %collective-permute-start.4 = (f32[264,128]{1,0:T(8,128)S(1)}, f32[264,128]{1,0:T(8,128)S(1)}, u32[]{:S(2)}, u32[]{:S(2)}) collective-permute-start(f32[264,128]{1,0:T(8,128)S(1)} %shard_map.133), channel_id=1, source_target_pairs={{8,0},{12,4},{0,8},{4,12},{24,16},{28,20},{16,24},{20,28},{9,1},{1... | collective-permute-start | bytes 405512 | tf_op jit(solution)/shard_map/ppermute | solution.py:653
  13.8 1.2 %collective-permute-start.5 = (f32[8,128]{1,0:T(8,128)S(1)}, f32[8,128]{1,0:T(8,128)S(1)}, u32[]{:S(2)}, u32[]{:S(2)}) collective-permute-start(f32[8,128]{1,0:T(8,128)S(1)} %shard_map.134.refs_5_.refs_0_), channel_id=1, source_target_pairs={{8,0},{12,4},{0,8},{4,12},{24,16},{28,20},{16,24},{20,28},{9,1},{1... | collective-permute-start | bytes 12296 | tf_op jit(solution)/shard_map/ppermute | solution.py:653
  15.0 4.6 %collective-permute-start.6 = (f32[7,8,128]{2,1,0:T(8,128)S(1)}, f32[7,8,128]{2,1,0:T(8,128)S(1)}, u32[]{:S(2)}, u32[]{:S(2)}) collective-permute-start(f32[7,8,128]{2,1,0:T(8,128)S(1)} %shard_map.137.tiles.x.refs_0_), channel_id=1, source_target_pairs={{1,0},{0,1},{3,2},{2,3},{5,4},{4,5},{7,6},{6,7},{9,8},{8,9},{11,10... | collective-permute-start | bytes 86024 | tf_op jit(solution)/shard_map/ppermute | solution.py:659
  17.2 6.9 %collective-permute-start.8 = (f32[256,128]{1,0:T(8,128)S(1)}, f32[256,128]{1,0:T(8,128)S(1)}, u32[]{:S(2)}, u32[]{:S(2)}) collective-permute-start(f32[256,128]{1,0:T(8,128)S(1)} %get-tuple-element.68.x), channel_id=1, source_target_pairs={{4,0},{0,4},{12,8},{8,12},{20,16},{16,20},{28,24},{24,28},{5,1},{1... | collective-permute-start | bytes 393224 | tf_op jit(solution)/shard_map/ppermute | solution.py:653
  18.7 9.5 %collective-permute-start.9 = (f32[256,128]{1,0:T(8,128)S(1)}, f32[256,128]{1,0:T(8,128)S(1)}, u32[]{:S(2)}, u32[]{:S(2)}) collective-permute-start(f32[256,128]{1,0:T(8,128)S(1)} %get-tuple-element.68.x), channel_id=1, source_target_pairs={{24,0},{28,4},{16,8},{20,12},{8,16},{12,20},{0,24},{4,28},{25,1},{... | collective-permute-start | bytes 393224 | tf_op jit(solution)/shard_map/ppermute | solution.py:653
  19.6 6.6 %collective-permute-start.7 = (f32[14,8,128]{2,1,0:T(8,128)S(1)}, f32[14,8,128]{2,1,0:T(8,128)S(1)}, u32[]{:S(2)}, u32[]{:S(2)}) collective-permute-start(f32[14,8,128]{2,1,0:T(8,128)S(1)} %shard_map.139._), channel_id=1, source_target_pairs={{2,0},{3,1},{0,2},{1,3},{6,4},{7,5},{4,6},{5,7},{10,8},{11,9},{8,1... | collective-permute-start | bytes 172040 | tf_op jit(solution)/shard_map/ppermute | solution.py:659
  22.4 6.2 %collective-permute-start.10 = (f32[256,128]{1,0:T(8,128)S(1)}, f32[256,128]{1,0:T(8,128)S(1)}, u32[]{:S(2)}, u32[]{:S(2)}) collective-permute-start(f32[256,128]{1,0:T(8,128)S(1)} %shard_map.141), channel_id=1, source_target_pairs={{28,0},{24,4},{20,8},{16,12},{12,16},{8,20},{4,24},{0,28},{29,1},{... | collective-permute-start | bytes 393224 | tf_op jit(solution)/shard_map/ppermute | solution.py:653
  23.1 5.5 %collective-permute-start.11 = (f32[256,128]{1,0:T(8,128)S(1)}, f32[256,128]{1,0:T(8,128)S(1)}, u32[]{:S(2)}, u32[]{:S(2)}) collective-permute-start(f32[256,128]{1,0:T(8,128)S(1)} %shard_map.141), channel_id=1, source_target_pairs={{8,0},{12,4},{0,8},{4,12},{24,16},{28,20},{16,24},{20,28},{9,1},{1... | collective-permute-start | bytes 393224 | tf_op jit(solution)/shard_map/ppermute | solution.py:653
  24.1 4.4 %collective-permute-start.12 = (f32[256,128]{1,0:T(8,128)S(1)}, f32[256,128]{1,0:T(8,128)S(1)}, u32[]{:S(2)}, u32[]{:S(2)}) collective-permute-start(f32[256,128]{1,0:T(8,128)S(1)} %shard_map.142), channel_id=1, source_target_pairs={{8,0},{12,4},{0,8},{4,12},{24,16},{28,20},{16,24},{20,28},{9,1},{1... | collective-permute-start | bytes 393224 | tf_op jit(solution)/shard_map/ppermute | solution.py:653
  41.7 1.3 %collective-permute-start.13 = (f32[32,8,128]{2,1,0:T(8,128)S(1)}, f32[32,8,128]{2,1,0:T(8,128)S(1)}, u32[]{:S(2)}, u32[]{:S(2)}) collective-permute-start(f32[32,8,128]{2,1,0:T(8,128)S(1)} %all_to_all.5.mine), channel_id=1, source_target_pairs={{8,0},{12,4},{0,8},{4,12},{24,16},{28,20},{16,24},{20,28},{9,1},{1... | collective-permute-start | bytes 393224 | tf_op jit(solution)/shard_map/ppermute | solution.py:653

commit v21 on v20

--- a/solution.py
+++ b/solution.py
@@ -666,9 +666,9 @@
         got = {}
         for dy in s.shifts:
             got["same", dy] = fetch(rim, "same", dy)
-        got["other", 0] = fetch(rim, "other", 0)
         if after is not None:
             (rim,) = call(order_kernel, [(rim.shape, f32)], [rim, after])
+        got["other", 0] = fetch(rim, "other", 0)
         for dy in s.shifts:
             got["other", dy] = fetch(rim, "other", dy)
         got["partner", 0] = fetch(rim, "partner", 0)

time: 47.4 us -> 48.3 us (1.019)
  waiting for transfers between devices: 5.16 us -> 6.45 us
  blocking collectives: 11.1 us -> 10.4 us
    ppermute x12, waiting for transfers between devices: 3.14 us -> 6.23 us  [fetch(): return lax.ppermute(x, ('gx', 'gy'), pairs)]
    ppermute x2, waiting for transfers between devices: 2.02 us -> 0.23 us  [fetch_layers(): parts.append(lax.ppermute(sent[-1], 'gz', pairs))]
    all_to_all x1, blocking collectives: 11.1 us -> 10.4 us  [body(): boxes = lax.all_to_all(packed, ('gx', 'gy', 'gz'), 0, 0)]
where the time goes in v21:
time: 48.3 us; the launch traced here: 48.1 us
  Pallas kernels  16.5 us (34%)
  starting transfers between devices  13.9 us (29%)
  blocking collectives  10.4 us (22%)
  waiting for transfers between devices  6.45 us (13%)
  between operations  0.73 us (2%)
    pallas_call x15, Pallas kernels, call(): pl.pallas_call(kernel, out_shape=[jax.ShapeDtypeStruct(shape, kind) for s...  16.5 us
    all_to_all x1, blocking collectives, body(): boxes = lax.all_to_all(packed, ('gx', 'gy', 'gz'), 0, 0)  10.4 us
    ppermute x12, starting transfers between devices, fetch(): return lax.ppermute(x, ('gx', 'gy'), pairs)  9.74 us
    ppermute x12, waiting for transfers between devices, fetch(): return lax.ppermute(x, ('gx', 'gy'), pairs)  6.23 us
    ppermute x2, starting transfers between devices, fetch_layers(): parts.append(lax.ppermute(sent[-1], 'gz', pairs))  4.17 us
  transfers between devices with their start and end apart: 14, of which 5 were waited for; matrix products, arithmetic and copies ran while one was open for 0% of the time, Pallas kernels for 19%

profile of v21, /device:TPU:0, one launch (start us, length us, event | category | flops | bytes accessed | tf_op | source)
XLA Modules:
  0.0 48.1 jit_solution(4218915325692616252)
XLA Ops:
  0.6 1.4 %shard_map.131 = (f32[264,128]{1,0:T(8,128)S(1)}, f32[168,128]{1,0:T(8,128)S(1)}, s32[1,1,256]{2,1,0:T(1,128)S(1)}, f32[512,256]{1,0:T(8,128)S(1)}) custom-call(f32[486,1,256]{2,1,0:T(1,128)} %bitcast.9, s32[1,1,256]{2,1,0:T(1,128)} %cells.1, f32[1,162]{1,0:T(1,128)} %bitcast.10), custom_call_target="tpu_custom_call" | custom-call | flops 10000000 | bytes 1048576 | tf_op jit(solution)/shard_map/pallas_call | solution.py:625
  2.1 3.0 %collective-permute-start = (f32[264,128]{1,0:T(8,128)S(1)}, f32[264,128]{1,0:T(8,128)S(1)}, u32[]{:S(2)}, u32[]{:S(2)}) collective-permute-start(f32[264,128]{1,0:T(8,128)S(1)} %get-tuple-element.49.refs_0_.message.charges_f), channel_id=1, source_target_pairs={{4,0},{0,4},{12,8},{8,12},{20,16},{16,20},{28,24},{24,28},{5,1},{1... | collective-permute-start | bytes 405512 | tf_op jit(solution)/shard_map/ppermute | solution.py:653
  5.1 0.7 %collective-permute-start.1 = (f32[264,128]{1,0:T(8,128)S(1)}, f32[264,128]{1,0:T(8,128)S(1)}, u32[]{:S(2)}, u32[]{:S(2)}) collective-permute-start(f32[264,128]{1,0:T(8,128)S(1)} %get-tuple-element.49.refs_0_.message.charges_f), channel_id=1, source_target_pairs={{24,0},{28,4},{16,8},{20,12},{8,16},{12,20},{0,24},{4,28},{25,1},{... | collective-permute-start | bytes 405512 | tf_op jit(solution)/shard_map/ppermute | solution.py:653
  5.7 0.6 %collective-permute-start.2 = (f32[264,128]{1,0:T(8,128)S(1)}, f32[264,128]{1,0:T(8,128)S(1)}, u32[]{:S(2)}, u32[]{:S(2)}) collective-permute-start(f32[264,128]{1,0:T(8,128)S(1)} %get-tuple-element.49.refs_0_.message.charges_f), channel_id=1, source_target_pairs={{28,0},{24,4},{20,8},{16,12},{12,16},{8,20},{4,24},{0,28},{29,1},{... | collective-permute-start | bytes 405512 | tf_op jit(solution)/shard_map/ppermute | solution.py:653
  6.3 0.4 collective-permute-start.3
  6.7 0.1 pad_add_fusion.ids
  6.8 5.6 %shard_map.132 = (f32[512,256]{1,0:T(8,128)S(1)}, f32[512,256]{1,0:T(8,128)S(1)}, f32[16,256]{1,0:T(8,128)S(1)}, bf16[512,512]{1,0:T(8,128)(2,1)S(1)}, bf16[512,...) custom-call(s32[2]{0:T(128)S(1)} %pad_add_fusion.ids, ...), custom_call_target="tpu_custom_call" | custom-call | flops 5000000000 | bytes 1048576 | tf_op jit(solution)/shard_map/pallas_call | solution.py:625
  12.4 0.0 collective-permute-done.x.refs_1_.refs_0_.refs_2_
  12.5 0.2 collective-permute-start.4
  12.7 1.1 %collective-permute-done.1.refs_2_.refs_1_.refs_3_ = f32[264,128]{1,0:T(8,128)S(1)} collective-permute-done((f32[264,128]{1,0:T(8,128)S(1)}, f32[264,128]{1,0:T(8,128)S(1)}, u32[]{:S(2)}, u32[]{:S(2)}) %collective-permute-start.1) | collective-permute-done | bytes 135200 | tf_op jit(solution)/shard_map/ppermute | solution.py:653
  13.8 0.2 collective-permute-start.5
  14.0 0.0 collective-permute-done.4.refs_4_.refs_6_
  14.0 0.7 %shard_map.135 = (bf16[512,256]{1,0:T(8,128)(2,1)S(1)}, bf16[512,256]{1,0:T(8,128)(2,1)S(1)}) custom-call(f32[512,256]{1,0:T(8,128)S(1)} %get-tuple-element.46.gat, bf16[384,256]{1,0:T(8,128)(2,1)S(1)} %get-tuple-element.47.gh, bf16[384,256]{1,0:T(8,128)(2,1)S(1)} %get-tuple-element.48.gl, f32[264,128]{1,0:T(8,128)S(1)} %collective-permute-done.x.refs_1_.refs_0_.refs_2_, ...), custom_call_target="tpu_custom_call" | custom-call | flops 1000000000 | bytes 1048576 | tf_op jit(solution)/shard_map/pallas_call | solution.py:625
  14.7 0.4 collective-permute-done.5.refs_1_
  15.0 1.6 %collective-permute-start.6 = (f32[7,8,128]{2,1,0:T(8,128)S(1)}, f32[7,8,128]{2,1,0:T(8,128)S(1)}, u32[]{:S(2)}, u32[]{:S(2)}) collective-permute-start(f32[7,8,128]{2,1,0:T(8,128)S(1)} %shard_map.137.tiles.x.refs_0_), channel_id=1, source_target_pairs={{1,0},{0,1},{3,2},{2,3},{5,4},{4,5},{7,6},{6,7},{9,8},{8,9},{11,10... | collective-permute-start | bytes 86024 | tf_op jit(solution)/shard_map/ppermute | solution.py:659
  16.6 0.6 %shard_map.136 = (f32[512,256]{1,0:T(8,128)S(1)}, f32[256,128]{1,0:T(8,128)S(1)}) custom-call(f32[512,256]{1,0:T(8,128)S(1)} %get-tuple-element.43.loc, bf16[512,512]{1,0:T(8,128)(2,1)S(1)} %get-tuple-element.44.nh, bf16[512,512]{1,0:T(8,128)(2,1)S(1)} %get-tuple-element.45.nl, bf16[512,256]{1,0:T(8,128)(2,1)S(1)} %get-tuple-element.51.hi, ...), custom_call_target="tpu_custom_call" | custom-call | flops 1000000000 | bytes 1048576 | tf_op jit(solution)/shard_map/pallas_call | solution.py:625
  17.2 1.4 %collective-permute-start.8 = (f32[256,128]{1,0:T(8,128)S(1)}, f32[256,128]{1,0:T(8,128)S(1)}, u32[]{:S(2)}, u32[]{:S(2)}) collective-permute-start(f32[256,128]{1,0:T(8,128)S(1)} %get-tuple-element.68.x), channel_id=1, source_target_pairs={{4,0},{0,4},{12,8},{8,12},{20,16},{16,20},{28,24},{24,28},{5,1},{1... | collective-permute-start | bytes 393224 | tf_op jit(solution)/shard_map/ppermute | solution.py:653
  18.7 0.2 collective-permute-done.6.y.refs_1_
  18.9 2.6 %collective-permute-start.7 = (f32[14,8,128]{2,1,0:T(8,128)S(1)}, f32[14,8,128]{2,1,0:T(8,128)S(1)}, u32[]{:S(2)}, u32[]{:S(2)}) collective-permute-start(f32[14,8,128]{2,1,0:T(8,128)S(1)} %shard_map.139._), channel_id=1, source_target_pairs={{2,0},{3,1},{0,2},{1,3},{6,4},{7,5},{4,6},{5,7},{10,8},{11,9},{8,1... | collective-permute-start | bytes 172040 | tf_op jit(solution)/shard_map/ppermute | solution.py:659
  21.5 0.1 shard_map.138
  21.6 0.5 %collective-permute-start.9 = (f32[256,128]{1,0:T(8,128)S(1)}, f32[256,128]{1,0:T(8,128)S(1)}, u32[]{:S(2)}, u32[]{:S(2)}) collective-permute-start(f32[256,128]{1,0:T(8,128)S(1)} %shard_map.141), channel_id=1, source_target_pairs={{24,0},{28,4},{16,8},{20,12},{8,16},{12,20},{0,24},{4,28},{25,1},{... | collective-permute-start | bytes 393224 | tf_op jit(solution)/shard_map/ppermute | solution.py:653
  22.2 2.1 %collective-permute-start.10 = (f32[256,128]{1,0:T(8,128)S(1)}, f32[256,128]{1,0:T(8,128)S(1)}, u32[]{:S(2)}, u32[]{:S(2)}) collective-permute-start(f32[256,128]{1,0:T(8,128)S(1)} %shard_map.141), channel_id=1, source_target_pairs={{28,0},{24,4},{20,8},{16,12},{12,16},{8,20},{4,24},{0,28},{29,1},{... | collective-permute-start | bytes 393224 | tf_op jit(solution)/shard_map/ppermute | solution.py:653
  24.2 0.6 %collective-permute-start.12 = (f32[256,128]{1,0:T(8,128)S(1)}, f32[256,128]{1,0:T(8,128)S(1)}, u32[]{:S(2)}, u32[]{:S(2)}) collective-permute-start(f32[256,128]{1,0:T(8,128)S(1)} %shard_map.142), channel_id=1, source_target_pairs={{8,0},{12,4},{0,8},{4,12},{24,16},{28,20},{16,24},{20,28},{9,1},{1... | collective-permute-start | bytes 393224 | tf_op jit(solution)/shard_map/ppermute | solution.py:653
  24.8 1.9 %shard_map.140 = (f32[512,256]{1,0:T(8,128)S(1)}, f32[8,128]{1,0:T(8,128)S(1)}, f32[3,8,128]{2,1,0:T(8,128)S(1)}, f32[512,256]{1,0:T(8,128)S(1)}, f32[512,256]{1...) custom-call(f32[512,256]{1,0:T(8,128)S(1)} %get-tuple-element.53.part, ...), custom_call_target="tpu_custom_call" | custom-call | flops 1000000000 | bytes 1048576 | tf_op jit(solution)/shard_map/pallas_call | solution.py:625
  26.7 3.5 %collective-permute-done.9.refs_1_ = f32[256,128]{1,0:T(8,128)S(1)} collective-permute-done((f32[256,128]{1,0:T(8,128)S(1)}, f32[256,128]{1,0:T(8,128)S(1)}, u32[]{:S(2)}, u32[]{:S(2)}) %collective-permute-start.9) | collective-permute-done | bytes 131104 | tf_op jit(solution)/shard_map/ppermute | solution.py:653
  30.2 0.0 collective-permute-done.10.refs_2_
  30.3 0.7 %shard_map.143 = (bf16[512,256]{1,0:T(8,128)(2,1)S(1)}, bf16[512,256]{1,0:T(8,128)(2,1)S(1)}) custom-call(f32[512,256]{1,0:T(8,128)S(1)} %get-tuple-element.66.gat, bf16[384,256]{1,0:T(8,128)(2,1)S(1)} %get-tuple-element.47.gh, bf16[384,256]{1,0:T(8,128)(2,1)S(1)} %get-tuple-element.48.gl, f32[168,128]{1,0:T(8,128)S(1)} %get-tuple-element.59.col, ...), custom_call_target="tpu_custom_call" | custom-call | flops 1000000000 | bytes 1048576 | tf_op jit(solution)/shard_map/pallas_call | solution.py:625
  30.9 1.3 %shard_map.144 = f32[32,8,128]{2,1,0:T(8,128)S(1)} custom-call(f32[512,256]{1,0:T(8,128)S(1)} %get-tuple-element.65.loc, bf16[512,512]{1,0:T(8,128)(2,1)S(1)} %get-tuple-element.44.nh, bf16[512,512]{1,0:T(8,128)(2,1)S(1)} %get-tuple-element.45.nl, bf16[512,256]{1,0:T(8,128)(2,1)S(1)} %get-tuple-element.69.hi, bf16[512,256]{1,0:T(8,128)(2,1)S(1)} %get-tuple-element.70.lo, ...), custom_call_target="tpu_custom_call" | custom-call | flops 1000000000 | bytes 1048576 | tf_op jit(solution)/shard_map/pallas_call | solution.py:625
  32.2 10.4 %all_to_all.5.mine = f32[32,8,128]{2,1,0:T(8,128)S(1)} all-to-all(f32[32,8,128]{2,1,0:T(8,128)S(1)} %shard_map.144), channel_id=1, replica_groups=mesh['gx'=4,'gy'=2,'gz'=4] {'gx','gy','gz'}, dimensions={0} | all-to-all | bytes 262144 | tf_op jit(solution)/shard_map/all_to_all | solution.py:772
  42.6 0.1 collective-permute-start.13
  42.7 1.2 %collective-permute-done.13.other = f32[32,8,128]{2,1,0:T(8,128)S(1)} collective-permute-done((f32[32,8,128]{2,1,0:T(8,128)S(1)}, f32[32,8,128]{2,1,0:T(8,128)S(1)}, u32[]{:S(2)}, u32[]{:S(2)}) %collective-permute-start.13) | collective-permute-done | bytes 131104 | tf_op jit(solution)/shard_map/ppermute | solution.py:653
  44.0 4.1 %shard_map.145 = (f32[486,1,256]{2,1,0:T(1,128)}, f32[1,1]{1,0:T(1,128)}) custom-call(s32[2]{0:T(128)S(1)} %pad_add_fusion.ids, f32[512,256]{1,0:T(8,128)S(1)} %get-tuple-element.42.f_in, f32[512,256]{1,0:T(8,128)S(1)} %get-tuple-element.64.u_in, f32[32,8,128]{2,1,0:T(8,128)S(1)} %all_to_all.5.mine, f32[32,8,128]{2,1,0:T(8,128)S(1)} %collective-permute-done.13.other, ...), custom_call_target="tpu_custom_call" | custom-call | flops 10000000 | bytes 1048576 | tf_op jit(solution)/shard_map/pallas_call | solution.py:625
  (13 shorter events, 0.1 us)
Async XLA Ops:
  2.1 10.4 %collective-permute-start = (f32[264,128]{1,0:T(8,128)S(1)}, f32[264,128]{1,0:T(8,128)S(1)}, u32[]{:S(2)}, u32[]{:S(2)}) collective-permute-start(f32[264,128]{1,0:T(8,128)S(1)} %get-tuple-element.49.refs_0_.message.charges_f), channel_id=1, source_target_pairs={{4,0},{0,4},{12,8},{8,12},{20,16},{16,20},{28,24},{24,28},{5,1},{1... | collective-permute-start | bytes 405512 | tf_op jit(solution)/shard_map/ppermute | solution.py:653
  5.1 8.7 %collective-permute-start.1 = (f32[264,128]{1,0:T(8,128)S(1)}, f32[264,128]{1,0:T(8,128)S(1)}, u32[]{:S(2)}, u32[]{:S(2)}) collective-permute-start(f32[264,128]{1,0:T(8,128)S(1)} %get-tuple-element.49.refs_0_.message.charges_f), channel_id=1, source_target_pairs={{24,0},{28,4},{16,8},{20,12},{8,16},{12,20},{0,24},{4,28},{25,1},{... | collective-permute-start | bytes 405512 | tf_op jit(solution)/shard_map/ppermute | solution.py:653
  5.7 8.0 %collective-permute-start.2 = (f32[264,128]{1,0:T(8,128)S(1)}, f32[264,128]{1,0:T(8,128)S(1)}, u32[]{:S(2)}, u32[]{:S(2)}) collective-permute-start(f32[264,128]{1,0:T(8,128)S(1)} %get-tuple-element.49.refs_0_.message.charges_f), channel_id=1, source_target_pairs={{28,0},{24,4},{20,8},{16,12},{12,16},{8,20},{4,24},{0,28},{29,1},{... | collective-permute-start | bytes 405512 | tf_op jit(solution)/shard_map/ppermute | solution.py:653
  6.3 7.6 %collective-permute-start.3 = (f32[264,128]{1,0:T(8,128)S(1)}, f32[264,128]{1,0:T(8,128)S(1)}, u32[]{:S(2)}, u32[]{:S(2)}) collective-permute-start(f32[264,128]{1,0:T(8,128)S(1)} %get-tuple-element.49.refs_0_.message.charges_f), channel_id=1, source_target_pairs={{8,0},{12,4},{0,8},{4,12},{24,16},{28,20},{16,24},{20,28},{9,1},{1... | collective-permute-start | bytes 405512 | tf_op jit(solution)/shard_map/ppermute | solution.py:653
  12.5 1.5 %collective-permute-start.4 = (f32[264,128]{1,0:T(8,128)S(1)}, f32[264,128]{1,0:T(8,128)S(1)}, u32[]{:S(2)}, u32[]{:S(2)}) collective-permute-start(f32[264,128]{1,0:T(8,128)S(1)} %shard_map.133), channel_id=1, source_target_pairs={{8,0},{12,4},{0,8},{4,12},{24,16},{28,20},{16,24},{20,28},{9,1},{1... | collective-permute-start | bytes 405512 | tf_op jit(solution)/shard_map/ppermute | solution.py:653
  13.8 1.2 %collective-permute-start.5 = (f32[8,128]{1,0:T(8,128)S(1)}, f32[8,128]{1,0:T(8,128)S(1)}, u32[]{:S(2)}, u32[]{:S(2)}) collective-permute-start(f32[8,128]{1,0:T(8,128)S(1)} %shard_map.134.refs_5_.refs_0_), channel_id=1, source_target_pairs={{8,0},{12,4},{0,8},{4,12},{24,16},{28,20},{16,24},{20,28},{9,1},{1... | collective-permute-start | bytes 12296 | tf_op jit(solution)/shard_map/ppermute | solution.py:653
  15.0 3.9 %collective-permute-start.6 = (f32[7,8,128]{2,1,0:T(8,128)S(1)}, f32[7,8,128]{2,1,0:T(8,128)S(1)}, u32[]{:S(2)}, u32[]{:S(2)}) collective-permute-start(f32[7,8,128]{2,1,0:T(8,128)S(1)} %shard_map.137.tiles.x.refs_0_), channel_id=1, source_target_pairs={{1,0},{0,1},{3,2},{2,3},{5,4},{4,5},{7,6},{6,7},{9,8},{8,9},{11,10... | collective-permute-start | bytes 86024 | tf_op jit(solution)/shard_map/ppermute | solution.py:659
  17.2 7.0 %collective-permute-start.8 = (f32[256,128]{1,0:T(8,128)S(1)}, f32[256,128]{1,0:T(8,128)S(1)}, u32[]{:S(2)}, u32[]{:S(2)}) collective-permute-start(f32[256,128]{1,0:T(8,128)S(1)} %get-tuple-element.68.x), channel_id=1, source_target_pairs={{4,0},{0,4},{12,8},{8,12},{20,16},{16,20},{28,24},{24,28},{5,1},{1... | collective-permute-start | bytes 393224 | tf_op jit(solution)/shard_map/ppermute | solution.py:653
  18.9 5.9 %collective-permute-start.7 = (f32[14,8,128]{2,1,0:T(8,128)S(1)}, f32[14,8,128]{2,1,0:T(8,128)S(1)}, u32[]{:S(2)}, u32[]{:S(2)}) collective-permute-start(f32[14,8,128]{2,1,0:T(8,128)S(1)} %shard_map.139._), channel_id=1, source_target_pairs={{2,0},{3,1},{0,2},{1,3},{6,4},{7,5},{4,6},{5,7},{10,8},{11,9},{8,1... | collective-permute-start | bytes 172040 | tf_op jit(solution)/shard_map/ppermute | solution.py:659
  21.6 8.6 %collective-permute-start.9 = (f32[256,128]{1,0:T(8,128)S(1)}, f32[256,128]{1,0:T(8,128)S(1)}, u32[]{:S(2)}, u32[]{:S(2)}) collective-permute-start(f32[256,128]{1,0:T(8,128)S(1)} %shard_map.141), channel_id=1, source_target_pairs={{24,0},{28,4},{16,8},{20,12},{8,16},{12,20},{0,24},{4,28},{25,1},{... | collective-permute-start | bytes 393224 | tf_op jit(solution)/shard_map/ppermute | solution.py:653
  22.2 8.1 %collective-permute-start.10 = (f32[256,128]{1,0:T(8,128)S(1)}, f32[256,128]{1,0:T(8,128)S(1)}, u32[]{:S(2)}, u32[]{:S(2)}) collective-permute-start(f32[256,128]{1,0:T(8,128)S(1)} %shard_map.141), channel_id=1, source_target_pairs={{28,0},{24,4},{20,8},{16,12},{12,16},{8,20},{4,24},{0,28},{29,1},{... | collective-permute-start | bytes 393224 | tf_op jit(solution)/shard_map/ppermute | solution.py:653
  24.2 6.0 %collective-permute-start.11 = (f32[256,128]{1,0:T(8,128)S(1)}, f32[256,128]{1,0:T(8,128)S(1)}, u32[]{:S(2)}, u32[]{:S(2)}) collective-permute-start(f32[256,128]{1,0:T(8,128)S(1)} %shard_map.141), channel_id=1, source_target_pairs={{8,0},{12,4},{0,8},{4,12},{24,16},{28,20},{16,24},{20,28},{9,1},{1... | collective-permute-start | bytes 393224 | tf_op jit(solution)/shard_map/ppermute | solution.py:653
  24.2 6.0 %collective-permute-start.12 = (f32[256,128]{1,0:T(8,128)S(1)}, f32[256,128]{1,0:T(8,128)S(1)}, u32[]{:S(2)}, u32[]{:S(2)}) collective-permute-start(f32[256,128]{1,0:T(8,128)S(1)} %shard_map.142), channel_id=1, source_target_pairs={{8,0},{12,4},{0,8},{4,12},{24,16},{28,20},{16,24},{20,28},{9,1},{1... | collective-permute-start | bytes 393224 | tf_op jit(solution)/shard_map/ppermute | solution.py:653
  42.6 1.3 %collective-permute-start.13 = (f32[32,8,128]{2,1,0:T(8,128)S(1)}, f32[32,8,128]{2,1,0:T(8,128)S(1)}, u32[]{:S(2)}, u32[]{:S(2)}) collective-permute-start(f32[32,8,128]{2,1,0:T(8,128)S(1)} %all_to_all.5.mine), channel_id=1, source_target_pairs={{8,0},{12,4},{0,8},{4,12},{24,16},{28,20},{16,24},{20,28},{9,1},{1... | collective-permute-start | bytes 393224 | tf_op jit(solution)/shard_map/ppermute | solution.py:653
